TPU v7x, 32 devices: a whole 2x2x4 slice. The times are simulated.
32 devices in a mesh: seq: 16 (over z, x, core), fsdp: 2 (over y).
Axes of the slice: x: 2, y: 2, z: 4, core: 2. Of those that a mesh axis runs over, the one named last changes fastest.
Arguments:
- tokens: bfloat16 [2, 2048, 2048], P('fsdp', 'seq'), may hold values from -6 to 6
- cotangent: bfloat16 [2, 2048, 2048], P('fsdp', 'seq'), may hold values from -6 to 6
- segments: int32 [2, 2048], P('fsdp'), may hold values from 0 to 2047, as said below
- routes: int32 [2, 2048, 6], P('fsdp', 'seq'), may hold values from 0 to 15, all different within a row; in each aligned block of 128 rows (0 to 127, 128 to 255, ..., all dimensions but the last counted through in order) at most 64 rows name the same one
- norm_attn: float32 [2048], P(('seq', 'fsdp')), may hold values from 0.5 to 1.5
- w_query: float32 [2048, 3072], P(('seq', 'fsdp')), may hold values from -0.25 to 0.25
- w_latent: float32 [2048, 576], P(('seq', 'fsdp')), may hold values from -0.125 to 0.125
- norm_latent: float32 [512], P(('seq', 'fsdp')), may hold values from 0.5 to 1.5
- w_expand: float32 [512, 4096], P(('seq', 'fsdp')), may hold values from -0.25 to 0.25
- w_output: float32 [2048, 2048], P(('seq', 'fsdp')), may hold values from -0.75 to 0.75
- norm_ffn: float32 [2048], P(('seq', 'fsdp')), may hold values from 0.5 to 1.5
- w_router: float32 [2048, 16], P(('seq', 'fsdp')), may hold values from -0.0625 to 0.0625
- w_shared_gate: float32 [2048, 2816], P('fsdp', 'seq'), may hold values from -0.125 to 0.125
- w_shared_up: float32 [2048, 2816], P('fsdp', 'seq'), may hold values from -0.125 to 0.125
- w_shared_down: float32 [2816, 2048], P(('seq', 'fsdp')), may hold values from -0.15625 to 0.15625
- w_expert_gate: float32 [16, 2048, 1408], P('seq', 'fsdp'), may hold values from -0.125 to 0.125
- w_expert_up: float32 [16, 2048, 1408], P('seq', 'fsdp'), may hold values from -0.125 to 0.125
- w_expert_down: float32 [16, 1408, 2048], P('seq', 'fsdp'), may hold values from -1.25 to 1.25
Outputs:
- output: bfloat16 [2, 2048, 2048], P('fsdp', 'seq')
- input_grad: bfloat16 [2, 2048, 2048], P('fsdp', 'seq')
- grad_norm_attn: float32 [2048], P(('seq', 'fsdp'))
- grad_w_query: float32 [2048, 3072], P(('seq', 'fsdp'))
- grad_w_latent: float32 [2048, 576], P(('seq', 'fsdp'))
- grad_norm_latent: float32 [512], P(('seq', 'fsdp'))
- grad_w_expand: float32 [512, 4096], P(('seq', 'fsdp'))
- grad_w_output: float32 [2048, 2048], P(('seq', 'fsdp'))
- grad_norm_ffn: float32 [2048], P(('seq', 'fsdp'))
- grad_w_router: float32 [2048, 16], P(('seq', 'fsdp'))
- grad_w_shared_gate: float32 [2048, 2816], P('fsdp', 'seq')
- grad_w_shared_up: float32 [2048, 2816], P('fsdp', 'seq')
- grad_w_shared_down: float32 [2816, 2048], P(('seq', 'fsdp'))
- grad_w_expert_gate: float32 [16, 2048, 1408], P('seq', 'fsdp')
- grad_w_expert_up: float32 [16, 2048, 1408], P('seq', 'fsdp')
- grad_w_expert_down: float32 [16, 1408, 2048], P('seq', 'fsdp')
Inputs may be any that keep to these rules, and one draw needn't show every extreme that they name: `routes`: each row names 6 different experts. In the rows of one device (aligned blocks of 128 rows of a sequence) no expert is named by more than 64 rows, a bound that some block reaches. `segments`: never falling along a sequence; equal numbers mark one document.
All inputs are finite; a program needn't handle non-finite values.
Results may differ from a plain program's by a relative error of at most 0.02.
The roundings to bfloat16 on the way count: a program that leaves them out, or rounds other values in their place, can miss the bound.
Values may be sent and summed in bfloat16 or wider, within the bound.
A program may use at most 448 MiB of HBM per device.

v0:
```python
import math

import jax
import jax.numpy as jnp
from jax import lax
from jax.sharding import PartitionSpec as P

H = 16
NOPE = 128
ROPE = 64
VD = 128
LAT = 512
TOP = 6
EXP_DEV = 1


EPSILON = 1e-06
HIGHEST = lax.Precision.HIGHEST


def rotary_tables(count, offset):
    places = (offset + jnp.arange(count, dtype=jnp.int32)).astype(jnp.float32)
    powers = jnp.arange(ROPE // 2, dtype=jnp.int32).astype(jnp.float32) * (2.0 / ROPE)
    inverse = jnp.exp(powers * -math.log(10000.0))
    angles = places[:, None] * inverse[None, :]
    return (jnp.cos(angles), jnp.sin(angles))


def rotate(values, cosine_table, sine_table):
    halfway = values.shape[-1] // 2
    former = values[..., :halfway]
    latter = values[..., halfway:]
    return jnp.concatenate(
        [former * cosine_table - latter * sine_table, latter * cosine_table + former * sine_table],
        axis=-1,
    )


def rotate_back(values, cosine_table, sine_table):
    halfway = values.shape[-1] // 2
    former = values[..., :halfway]
    latter = values[..., halfway:]
    return jnp.concatenate(
        [former * cosine_table + latter * sine_table, latter * cosine_table - former * sine_table],
        axis=-1,
    )


def matmul(left, right):
    return jnp.dot(left, right, preferred_element_type=jnp.float32)


def times_transposed(left, right):
    return lax.dot_general(
        left, right, (((1,), (1,)), ((), ())), preferred_element_type=jnp.float32
    )


def transposed_times(left, right):
    return lax.dot_general(
        left, right, (((0,), (0,)), ((), ())), preferred_element_type=jnp.float32
    )


def exact_transposed_times(left, right):
    return lax.dot_general(
        left, right, (((0,), (0,)), ((), ())), precision=HIGHEST, preferred_element_type=jnp.float32
    )


def exact_times_transposed(left, right):
    return lax.dot_general(
        left, right, (((1,), (1,)), ((), ())), precision=HIGHEST, preferred_element_type=jnp.float32
    )


def norm_forward(values, gain):
    factor = lax.rsqrt(jnp.mean(values * values, axis=-1, keepdims=True) + EPSILON)
    normed = values * factor
    return (normed * gain, normed, factor)


def norm_backward(grad_in, normed, factor, gain):
    inner_grad = grad_in * gain
    gain_grad = jnp.sum(grad_in * normed, axis=0)
    grad_back = factor * (
        inner_grad - normed * jnp.mean(inner_grad * normed, axis=-1, keepdims=True)
    )
    return (grad_back, gain_grad)


def swish_slope(pre_act, sigmoid_act):
    return sigmoid_act * (1.0 + pre_act * (1.0 - sigmoid_act))


def shared_pass(rows_low, grad_rows, gate_w, up_w, down_w):
    gate_proj = matmul(rows_low, gate_w)
    up_proj = matmul(rows_low, up_w)
    gate_sigmoid = jax.nn.sigmoid(gate_proj)
    hidden_low = (gate_proj * gate_sigmoid * up_proj).astype(jnp.bfloat16)
    made_rows = matmul(hidden_low, down_w)
    hidden_grad = times_transposed(grad_rows, down_w)
    gate_grad = (hidden_grad * up_proj * swish_slope(gate_proj, gate_sigmoid)).astype(jnp.bfloat16)
    up_grad = (hidden_grad * gate_proj * gate_sigmoid).astype(jnp.bfloat16)
    rows_grad = times_transposed(gate_grad, gate_w) + times_transposed(up_grad, up_w)
    weight_grads = (
        transposed_times(rows_low, gate_grad),
        transposed_times(rows_low, up_grad),
        transposed_times(hidden_low, grad_rows),
    )
    return (made_rows, rows_grad, weight_grads)


def fetch_dense(norm_attn, w_query, w_latent, norm_latent, w_expand, w_output, norm_ffn, w_router):
    return (
        lax.all_gather(norm_attn.astype(jnp.bfloat16), ("seq", "fsdp"), axis=0, tiled=True),
        lax.all_gather(w_query.astype(jnp.bfloat16), ("seq", "fsdp"), axis=0, tiled=True),
        lax.all_gather(w_latent.astype(jnp.bfloat16), ("seq", "fsdp"), axis=0, tiled=True),
        lax.all_gather(norm_latent.astype(jnp.bfloat16), ("seq", "fsdp"), axis=0, tiled=True),
        lax.all_gather(w_expand.astype(jnp.bfloat16), ("seq", "fsdp"), axis=0, tiled=True),
        lax.all_gather(w_output.astype(jnp.bfloat16), ("seq", "fsdp"), axis=0, tiled=True),
        lax.all_gather(norm_ffn.astype(jnp.bfloat16), ("seq", "fsdp"), axis=0, tiled=True),
        lax.all_gather(w_router.astype(jnp.bfloat16), ("seq", "fsdp"), axis=0, tiled=True),
    )


def body(
    tokens,
    cotangent,
    segments,
    routes,
    norm_attn,
    w_query,
    w_latent,
    norm_latent,
    w_expand,
    w_output,
    norm_ffn,
    w_router,
    w_shared_gate,
    w_shared_up,
    w_shared_down,
    w_expert_gate,
    w_expert_up,
    w_expert_down,
):
    groups = lax.axis_size("seq")
    tok_rows = tokens.shape[1]
    model_width = tokens.shape[2]
    seq_len = segments.shape[1]
    local_heads = H // groups
    query_width = NOPE + ROPE
    expert_count = EXP_DEV * groups
    capacity = tok_rows * TOP * 4 // (3 * expert_count)
    score_scale = query_width ** (-0.5)
    block_rows = min(512, seq_len)
    block_count = seq_len // block_rows
    hidden_in = tokens[0].astype(jnp.float32)
    grad_low = cotangent[0]
    grad_out = grad_low.astype(jnp.float32)
    dense_set = fetch_dense(
        norm_attn, w_query, w_latent, norm_latent, w_expand, w_output, norm_ffn, w_router
    )
    gain_attn, query_w, latent_w, gain_latent, expand_w, output_w, gain_ffn, router_w = dense_set
    expert_set = (
        lax.all_gather(w_expert_gate.astype(jnp.bfloat16), "fsdp", axis=1, tiled=True),
        lax.all_gather(w_expert_up.astype(jnp.bfloat16), "fsdp", axis=1, tiled=True),
        lax.all_gather(w_expert_down.astype(jnp.bfloat16), "fsdp", axis=1, tiled=True),
        lax.all_gather(w_shared_gate.astype(jnp.bfloat16), "fsdp", axis=0, tiled=True),
        lax.all_gather(w_shared_up.astype(jnp.bfloat16), "fsdp", axis=0, tiled=True),
        lax.all_gather(w_shared_down.astype(jnp.bfloat16), "fsdp", axis=0, tiled=True),
    )
    expert_gate_w, expert_up_w, expert_down_w, unit_gate, unit_up, unit_down = expert_set
    scaled_one, normed_one, factor_one = norm_forward(hidden_in, gain_attn.astype(jnp.float32))
    normed_low = scaled_one.astype(jnp.bfloat16)
    query_proj = matmul(normed_low, query_w).reshape(tok_rows, H, query_width)
    latent_proj = matmul(normed_low, latent_w)
    cosine_table, sine_table = rotary_tables(tok_rows, lax.axis_index("seq") * tok_rows)
    queries = jnp.concatenate(
        [
            query_proj[..., :NOPE],
            rotate(query_proj[..., NOPE:], cosine_table[:, None, :], sine_table[:, None, :]),
        ],
        axis=-1,
    ).astype(jnp.bfloat16)
    latent_scaled, latent_normed, latent_factor = norm_forward(
        latent_proj[:, :LAT], gain_latent.astype(jnp.float32)
    )
    latent_low = latent_scaled.astype(jnp.bfloat16)
    expanded = matmul(latent_low, expand_w).reshape(tok_rows, H, NOPE + VD)
    key_rope = rotate(latent_proj[:, LAT:], cosine_table, sine_table)
    key_rows = jnp.concatenate(
        [expanded[..., :NOPE], jnp.broadcast_to(key_rope[:, None, :], (tok_rows, H, ROPE))], axis=-1
    ).astype(jnp.bfloat16)
    value_rows = expanded[..., NOPE:].astype(jnp.bfloat16)
    query_heads, key_heads, value_heads = (
        lax.all_to_all(
            queries.reshape(tok_rows, H * query_width),
            "seq",
            split_axis=1,
            concat_axis=0,
            tiled=True,
        ),
        lax.all_to_all(
            key_rows.reshape(tok_rows, H * query_width),
            "seq",
            split_axis=1,
            concat_axis=0,
            tiled=True,
        ),
        lax.all_to_all(
            value_rows.reshape(tok_rows, H * VD), "seq", split_axis=1, concat_axis=0, tiled=True
        ),
    )
    head_q = query_heads.reshape(seq_len, local_heads, query_width)
    head_k = key_heads.reshape(seq_len, local_heads, query_width)
    head_v = value_heads.reshape(seq_len, local_heads, VD)
    doc_ids = segments[0]
    key_places = jnp.arange(seq_len, dtype=jnp.int32)

    def block_scores(row_start):
        query_block = lax.dynamic_slice_in_dim(head_q, row_start, block_rows, 0)
        doc_block = lax.dynamic_slice_in_dim(doc_ids, row_start, block_rows, 0)
        row_places = row_start + jnp.arange(block_rows, dtype=jnp.int32)
        allowed = (doc_block[:, None] == doc_ids[None, :]) & (
            row_places[:, None] >= key_places[None, :]
        )
        scores = (
            jnp.einsum("qhd,khd->hqk", query_block, head_k, preferred_element_type=jnp.float32)
            * score_scale
        )
        return (jnp.where(allowed[None, :, :], scores, -1e30), query_block)

    def attend(block_index):
        scores, unused_block = block_scores(block_index * block_rows)
        peak = jnp.max(scores, axis=-1, keepdims=True)
        raised = jnp.exp(scores - peak)
        totals = jnp.sum(raised, axis=-1, keepdims=True)
        attention = (raised / totals).astype(jnp.bfloat16)
        block_out = jnp.einsum(
            "hqk,khd->qhd", attention, head_v, preferred_element_type=jnp.float32
        )
        return (block_out.astype(jnp.bfloat16), (peak + jnp.log(totals))[..., 0])

    head_out, log_totals = lax.map(attend, jnp.arange(block_count, dtype=jnp.int32))
    merged = lax.all_to_all(
        head_out.reshape(seq_len, local_heads * VD), "seq", split_axis=0, concat_axis=1, tiled=True
    )
    residual = hidden_in + matmul(merged, output_w)
    scaled_two, normed_two, factor_two = norm_forward(residual, gain_ffn.astype(jnp.float32))
    normed_two_low = scaled_two.astype(jnp.bfloat16)
    logits = matmul(normed_two_low, router_w)
    logit_peak = jnp.max(logits, axis=-1, keepdims=True)
    logit_raised = jnp.exp(logits - logit_peak)
    router_p = logit_raised / jnp.sum(logit_raised, axis=-1, keepdims=True)
    local_routes = routes[0]
    picks = (
        local_routes[:, :, None] == jnp.arange(expert_count, dtype=jnp.int32)[None, None, :]
    ).astype(jnp.float32)
    gate_values = jnp.sum(picks * router_p[:, None, :], axis=-1)
    routed_ids = local_routes.reshape(tok_rows * TOP)
    onehot = (routed_ids[:, None] == jnp.arange(expert_count, dtype=jnp.int32)[None, :]).astype(
        jnp.int32
    )
    slot_rank = jnp.sum((jnp.cumsum(onehot, axis=0) - 1) * onehot, axis=1)
    slot_ids = routed_ids * capacity + slot_rank
    copies = jnp.broadcast_to(normed_two_low[:, None, :], (tok_rows, TOP, model_width)).reshape(
        tok_rows * TOP, model_width
    )
    outgoing = (
        jnp.zeros((expert_count * capacity, model_width), jnp.bfloat16).at[slot_ids].set(copies)
    )
    picked_grad = (
        (gate_values[..., None] * grad_out[:, None, :])
        .reshape(tok_rows * TOP, model_width)
        .astype(jnp.bfloat16)
    )
    sendback = (
        jnp.zeros((expert_count * capacity, model_width), jnp.bfloat16)
        .at[slot_ids]
        .set(picked_grad)
    )
    incoming, made_grad = (
        lax.all_to_all(
            outgoing.reshape(groups, EXP_DEV, capacity, model_width),
            "seq",
            split_axis=0,
            concat_axis=0,
            tiled=True,
        ),
        lax.all_to_all(
            sendback.reshape(groups, EXP_DEV, capacity, model_width),
            "seq",
            split_axis=0,
            concat_axis=0,
            tiled=True,
        ),
    )
    expert_gate = jnp.einsum(
        "secd,edf->secf", incoming, expert_gate_w, preferred_element_type=jnp.float32
    )
    expert_up = jnp.einsum(
        "secd,edf->secf", incoming, expert_up_w, preferred_element_type=jnp.float32
    )
    expert_sigmoid = jax.nn.sigmoid(expert_gate)
    expert_hidden = (expert_gate * expert_sigmoid * expert_up).astype(jnp.bfloat16)
    expert_made = jnp.einsum(
        "secf,efd->secd", expert_hidden, expert_down_w, preferred_element_type=jnp.float32
    ).astype(jnp.bfloat16)
    hidden_grad = jnp.einsum(
        "secd,efd->secf", made_grad, expert_down_w, preferred_element_type=jnp.float32
    )
    grad_expert_down = jnp.einsum(
        "secf,secd->efd", expert_hidden, made_grad, preferred_element_type=jnp.float32
    )
    expert_gate_grad = (hidden_grad * expert_up * swish_slope(expert_gate, expert_sigmoid)).astype(
        jnp.bfloat16
    )
    expert_up_grad = (hidden_grad * expert_gate * expert_sigmoid).astype(jnp.bfloat16)
    grad_expert_gate = jnp.einsum(
        "secd,secf->edf", incoming, expert_gate_grad, preferred_element_type=jnp.float32
    )
    grad_expert_up = jnp.einsum(
        "secd,secf->edf", incoming, expert_up_grad, preferred_element_type=jnp.float32
    )
    incoming_grad = (
        jnp.einsum(
            "secf,edf->secd", expert_gate_grad, expert_gate_w, preferred_element_type=jnp.float32
        )
        + jnp.einsum(
            "secf,edf->secd", expert_up_grad, expert_up_w, preferred_element_type=jnp.float32
        )
    ).astype(jnp.bfloat16)
    returned, returned_grad = (
        lax.all_to_all(expert_made, "seq", split_axis=0, concat_axis=0, tiled=True),
        lax.all_to_all(incoming_grad, "seq", split_axis=0, concat_axis=0, tiled=True),
    )
    full_gate, full_up, full_down = (
        lax.all_gather(unit_gate, "seq", axis=1, tiled=True),
        lax.all_gather(unit_up, "seq", axis=1, tiled=True),
        lax.all_gather(unit_down, "seq", axis=0, tiled=True),
    )
    shared_made, shared_input_grad, whole_grads = shared_pass(
        normed_two_low, grad_low, full_gate, full_up, full_down
    )
    shared_grads = (
        lax.psum_scatter(
            whole_grads[0].astype(jnp.bfloat16), "seq", scatter_dimension=1, tiled=True
        ).astype(jnp.float32),
        lax.psum_scatter(
            whole_grads[1].astype(jnp.bfloat16), "seq", scatter_dimension=1, tiled=True
        ).astype(jnp.float32),
        lax.psum_scatter(
            whole_grads[2].astype(jnp.bfloat16), "seq", scatter_dimension=0, tiled=True
        ).astype(jnp.float32),
    )
    expert_grads = (
        lax.psum_scatter(
            grad_expert_gate.astype(jnp.bfloat16), "fsdp", scatter_dimension=1, tiled=True
        ).astype(jnp.float32),
        lax.psum_scatter(
            grad_expert_up.astype(jnp.bfloat16), "fsdp", scatter_dimension=1, tiled=True
        ).astype(jnp.float32),
        lax.psum_scatter(
            grad_expert_down.astype(jnp.bfloat16), "fsdp", scatter_dimension=1, tiled=True
        ).astype(jnp.float32),
        lax.psum_scatter(
            shared_grads[0].astype(jnp.bfloat16), "fsdp", scatter_dimension=0, tiled=True
        ).astype(jnp.float32),
        lax.psum_scatter(
            shared_grads[1].astype(jnp.bfloat16), "fsdp", scatter_dimension=0, tiled=True
        ).astype(jnp.float32),
        lax.psum_scatter(
            shared_grads[2].astype(jnp.bfloat16), "fsdp", scatter_dimension=0, tiled=True
        ).astype(jnp.float32),
    )
    picked = (
        returned.reshape(expert_count * capacity, model_width)[slot_ids]
        .reshape(tok_rows, TOP, model_width)
        .astype(jnp.float32)
    )
    routed = jnp.sum(gate_values[..., None] * picked, axis=1)
    output = (residual + shared_made + routed).astype(jnp.bfloat16)
    dense_again = fetch_dense(
        norm_attn, w_query, w_latent, norm_latent, w_expand, w_output, norm_ffn, w_router
    )
    gain_attn_b, query_b, latent_b, gain_latent_b, expand_b, output_b, gain_ffn_b, router_b = (
        dense_again
    )
    gate_grad = jnp.sum(grad_out[:, None, :] * picked, axis=-1)
    prob_grad = jnp.sum(picks * gate_grad[..., None], axis=1)
    logit_grad = router_p * (prob_grad - jnp.sum(router_p * prob_grad, axis=-1, keepdims=True))
    normed_two_f = normed_two_low.astype(jnp.float32)
    grad_router = exact_transposed_times(normed_two_f, logit_grad)
    normed_two_grad = shared_input_grad + exact_times_transposed(
        logit_grad, router_b.astype(jnp.float32)
    )
    normed_two_grad = normed_two_grad + jnp.sum(
        returned_grad.reshape(expert_count * capacity, model_width)[slot_ids]
        .reshape(tok_rows, TOP, model_width)
        .astype(jnp.float32),
        axis=1,
    )
    residual_part, grad_gain_ffn = norm_backward(
        normed_two_grad, normed_two, factor_two, gain_ffn_b.astype(jnp.float32)
    )
    residual_grad = grad_out + residual_part
    attn_grad = residual_grad.astype(jnp.bfloat16)
    grad_output = transposed_times(merged, attn_grad)
    merged_grad = times_transposed(attn_grad, output_b).astype(jnp.bfloat16)
    grad_heads = lax.all_to_all(
        merged_grad, "seq", split_axis=1, concat_axis=0, tiled=True
    ).reshape(seq_len, local_heads, VD)

    def attend_back(carry, block_index):
        key_grad, value_grad = carry
        row_start = block_index * block_rows
        scores, query_block = block_scores(row_start)
        grad_block = lax.dynamic_slice_in_dim(grad_heads, row_start, block_rows, 0)
        attention = jnp.exp(scores - log_totals[block_index][:, :, None])
        attention_low = attention.astype(jnp.bfloat16)
        value_grad = value_grad + jnp.einsum(
            "hqk,qhd->khd", attention_low, grad_block, preferred_element_type=jnp.float32
        )
        weight_grad = jnp.einsum(
            "qhd,khd->hqk", grad_block, head_v, preferred_element_type=jnp.float32
        )
        inner_sum = jnp.sum(attention * weight_grad, axis=-1, keepdims=True)
        score_grad = (attention * (weight_grad - inner_sum)).astype(jnp.bfloat16)
        query_grad = (
            jnp.einsum("hqk,khd->qhd", score_grad, head_k, preferred_element_type=jnp.float32)
            * score_scale
        )
        key_grad = (
            key_grad
            + jnp.einsum(
                "hqk,qhd->khd", score_grad, query_block, preferred_element_type=jnp.float32
            )
            * score_scale
        )
        return ((key_grad, value_grad), query_grad)

    start_carry = (
        jnp.zeros((seq_len, local_heads, query_width), jnp.float32),
        jnp.zeros((seq_len, local_heads, VD), jnp.float32),
    )
    (key_grads, value_grads), query_grads = lax.scan(
        attend_back, start_carry, jnp.arange(block_count, dtype=jnp.int32)
    )
    query_tok, key_tok, value_tok = (
        lax.all_to_all(
            query_grads.reshape(seq_len, local_heads * query_width).astype(jnp.bfloat16),
            "seq",
            split_axis=0,
            concat_axis=1,
            tiled=True,
        ),
        lax.all_to_all(
            key_grads.reshape(seq_len, local_heads * query_width).astype(jnp.bfloat16),
            "seq",
            split_axis=0,
            concat_axis=1,
            tiled=True,
        ),
        lax.all_to_all(
            value_grads.reshape(seq_len, local_heads * VD).astype(jnp.bfloat16),
            "seq",
            split_axis=0,
            concat_axis=1,
            tiled=True,
        ),
    )
    query_three = query_tok.reshape(tok_rows, H, query_width)
    query_proj_grad = (
        jnp.concatenate(
            [
                query_three[..., :NOPE].astype(jnp.float32),
                rotate_back(
                    query_three[..., NOPE:].astype(jnp.float32),
                    cosine_table[:, None, :],
                    sine_table[:, None, :],
                ),
            ],
            axis=-1,
        )
        .reshape(tok_rows, H * query_width)
        .astype(jnp.bfloat16)
    )
    key_three = key_tok.reshape(tok_rows, H, query_width)
    key_rope_grad = rotate_back(
        jnp.sum(key_three[..., NOPE:].astype(jnp.float32), axis=1), cosine_table, sine_table
    )
    expand_grad = jnp.concatenate(
        [key_three[..., :NOPE], value_tok.reshape(tok_rows, H, VD)], axis=-1
    ).reshape(tok_rows, H * (NOPE + VD))
    grad_expand = transposed_times(latent_low, expand_grad)
    latent_low_grad = times_transposed(expand_grad, expand_b)
    latent_grad, grad_gain_latent = norm_backward(
        latent_low_grad, latent_normed, latent_factor, gain_latent_b.astype(jnp.float32)
    )
    latent_proj_grad = jnp.concatenate([latent_grad, key_rope_grad], axis=-1).astype(jnp.bfloat16)
    grad_query = transposed_times(normed_low, query_proj_grad)
    grad_latent = transposed_times(normed_low, latent_proj_grad)
    normed_one_grad = times_transposed(query_proj_grad, query_b) + times_transposed(
        latent_proj_grad, latent_b
    )
    input_part, grad_gain_attn = norm_backward(
        normed_one_grad, normed_one, factor_one, gain_attn_b.astype(jnp.float32)
    )
    input_grad = (residual_grad + input_part).astype(jnp.bfloat16)
    dense_grads = (
        lax.psum_scatter(grad_gain_attn, ("seq", "fsdp"), scatter_dimension=0, tiled=True),
        lax.psum_scatter(grad_query, ("seq", "fsdp"), scatter_dimension=0, tiled=True),
        lax.psum_scatter(grad_latent, ("seq", "fsdp"), scatter_dimension=0, tiled=True),
        lax.psum_scatter(grad_gain_latent, ("seq", "fsdp"), scatter_dimension=0, tiled=True),
        lax.psum_scatter(grad_expand, ("seq", "fsdp"), scatter_dimension=0, tiled=True),
        lax.psum_scatter(grad_output, ("seq", "fsdp"), scatter_dimension=0, tiled=True),
        lax.psum_scatter(grad_gain_ffn, ("seq", "fsdp"), scatter_dimension=0, tiled=True),
        lax.psum_scatter(grad_router, ("seq", "fsdp"), scatter_dimension=0, tiled=True),
    )
    return (
        output[None],
        input_grad[None],
        dense_grads[0],
        dense_grads[1],
        dense_grads[2],
        dense_grads[3],
        dense_grads[4],
        dense_grads[5],
        dense_grads[6],
        dense_grads[7],
        expert_grads[3],
        expert_grads[4],
        expert_grads[5],
        expert_grads[0],
        expert_grads[1],
        expert_grads[2],
    )


def solution(mesh):
    return jax.shard_map(
        body,
        mesh=mesh,
        in_specs=(
            P("fsdp", "seq", None),
            P("fsdp", "seq", None),
            P("fsdp", None),
            P("fsdp", "seq", None),
            P(("seq", "fsdp")),
            P(("seq", "fsdp"), None),
            P(("seq", "fsdp"), None),
            P(("seq", "fsdp")),
            P(("seq", "fsdp"), None),
            P(("seq", "fsdp"), None),
            P(("seq", "fsdp")),
            P(("seq", "fsdp"), None),
            P("fsdp", "seq"),
            P("fsdp", "seq"),
            P(("seq", "fsdp"), None),
            P("seq", "fsdp", None),
            P("seq", "fsdp", None),
            P("seq", "fsdp", None),
        ),
        out_specs=(
            P("fsdp", "seq", None),
            P("fsdp", "seq", None),
            P(("seq", "fsdp")),
            P(("seq", "fsdp"), None),
            P(("seq", "fsdp"), None),
            P(("seq", "fsdp")),
            P(("seq", "fsdp"), None),
            P(("seq", "fsdp"), None),
            P(("seq", "fsdp")),
            P(("seq", "fsdp"), None),
            P("fsdp", "seq"),
            P("fsdp", "seq"),
            P(("seq", "fsdp"), None),
            P("seq", "fsdp", None),
            P("seq", "fsdp", None),
            P("seq", "fsdp", None),
        ),
        check_vma=False,
    )
```

profile of v0, /device:TPU:0, one launch (start us, length us, event | category | flops | bytes accessed | tf_op | source)
XLA Modules:
  0.0 2739.7 jit_solution(6918179284606599359)
XLA Ops:
  15.7 12.7 all_gather.66
  28.6 10.4 all_gather.68
  39.1 10.6 all_gather.70
  60.2 40.1 %all-reduce.7 = (bf16[2048]{0:T(1024)(128)(2,1)S(1)}, bf16[512]{0:T(512)(128)(2,1)S(1)}, bf16[2048]{0:T(1024)(128)(2,1)S(1)}) all-reduce(bf16[2048]{0:T(1024)(128)(2,1)S(1)} %dynamic-update-slice, bf16[512]{0:T(512)(128)(2,1)S(1)} %dynamic-update-slice.1, ...), channel_id=1, replica_groups=mesh['seq'=16,'fsdp'=2] {'seq','fsdp'}, use_global_device_ids=true, to_apply=%add | all-reduce | flops 4608 | bytes 18432
  103.7 33.0 %all-gather.16.cloned.1.call-done = bf16[512,4096]{1,0:T(8,128)(2,1)} async-done(((bf16[16,4096]{1,0:T(8,128)(2,1)}), bf16[512,4096]{1,0:T(8,128)(2,1)}) %all-gather.16.cloned.1.call-update) | async-done | bytes 4194320 | tf_op jit(solution)/shard_map/all_gather | solution.py:120
  145.9 98.8 %all-gather.12.cloned.1.call-done = bf16[2048,3072]{1,0:T(8,128)(2,1)} async-done(((bf16[64,3072]{1,0:T(8,128)(2,1)}), bf16[2048,3072]{1,0:T(8,128)(2,1)}) %all-gather.12.cloned.1.call-update) | async-done | bytes 12582928 | tf_op jit(solution)/shard_map/all_gather | solution.py:117
  244.7 16.6 copy.125
  261.3 6.6 fusion.110
  273.9 27.8 %all-to-all-done = bf16[128,16,192]{0,2,1:T(8,128)(2,1)S(1)} async-done(((bf16[128,16,192]{0,2,1:T(8,128)(2,1)}), bf16[128,16,192]{0,2,1:T(8,128)(2,1)S(1)}, u32[]{:S(2)}, u32[]{:S(2)}) %all-to-all-start) | async-done | bytes 786464 | tf_op jit(solution)/shard_map/all_to_all | solution.py:197
  314.8 15.5 all-to-all-done.2
  330.3 27.1 while.28
  357.4 10.0 all-to-all-start.3
  367.4 22.9 all-to-all-done.3
  396.8 54.1 %all-gather.20.cloned.1.call-done = bf16[2048,2816]{0,1:T(8,128)(2,1)} async-done(((bf16[2048,176]{0,1:T(8,128)(2,1)}), bf16[2048,2816]{0,1:T(8,128)(2,1)}) %all-gather.20.cloned.1.call-update) | async-done | bytes 11534352 | tf_op jit(solution)/shard_map/all_gather | solution.py:339
  450.8 9.3 fusion.150
  460.1 85.4 %all-gather.22.cloned.1.call-done = bf16[2048,2816]{0,1:T(8,128)(2,1)} async-done(((bf16[2048,176]{0,1:T(8,128)(2,1)}), bf16[2048,2816]{0,1:T(8,128)(2,1)}) %all-gather.22.cloned.1.call-update) | async-done | bytes 11534352 | tf_op jit(solution)/shard_map/all_gather | solution.py:340
  545.5 9.3 fusion.151
  554.8 85.5 %all-gather.24.cloned.1.call-done = bf16[2816,2048]{1,0:T(8,128)(2,1)} async-done(((bf16[176,2048]{1,0:T(8,128)(2,1)}), bf16[2816,2048]{1,0:T(8,128)(2,1)}) %all-gather.24.cloned.1.call-update) | async-done | bytes 11534352 | tf_op jit(solution)/shard_map/all_gather | solution.py:341
  640.3 9.3 multiply_convert_fusion.3
  649.6 6.3 convolution_convert_fusion.2
  656.4 6.0 convolution_convert_fusion.1
  668.5 6.3 reshape.543
  674.8 10.5 scatter_custom_fusion
  690.0 131.9 %all-gather = bf16[32,64,16]{1,2,0:T(8,128)(2,1)S(1)} all-gather(bf16[1,64,16]{1,2,0:T(8,128)(2,1)S(1)} %convert_bitcast_fusion.3), channel_id=1, replica_groups=mesh['seq'=16,'fsdp'=2] {'seq','fsdp'}, dimensions={0}, use_global_device_ids=true | all-gather | bytes 67584 | tf_op jit(solution)/shard_map/all_gather | solution.py:123
  826.7 8.3 mul.490
  835.6 14.5 scatter_custom_fusion.1
  850.1 12.0 all-to-all-start.6
  862.3 6.0 convolution_convert_fusion
  868.4 11.7 fusion.61
  880.1 12.7 fusion.52
  892.8 79.7 %all-to-all-done.6 = bf16[16,1,64,2048]{3,2,1,0:T(8,128)(2,1)} async-done(((bf16[16,1,64,2048]{3,2,1,0:T(8,128)(2,1)}), bf16[16,1,64,2048]{3,2,1,0:T(8,128)(2,1)}, u32[]{:S(2)}, u32[]{:S(2)}) %all-to-all-start.6) | async-done | bytes 4194336 | tf_op jit(solution)/shard_map/all_to_all | solution.py:291
  972.5 15.9 fusion.42
  988.5 10.2 convert_bitcast_fusion
  998.6 33.1 %all-to-all-start.5 = ((bf16[16,1,64,2048]{3,2,1,0:T(8,128)(2,1)}), bf16[16,1,64,2048]{3,2,1,0:T(8,128)(2,1)}, u32[]{:S(2)}, u32[]{:S(2)}) async-start(bf16[16,1,64,2048]{3,2,1,0:T(8,128)(2,1)} %convert_bitcast_fusion), calls=%async_computation.5 | async-start | bytes 8388608 | tf_op jit(solution)/shard_map/all_to_all | solution.py:335
  1032.2 99.1 %all-to-all-done.5 = bf16[16,1,64,2048]{3,2,1,0:T(8,128)(2,1)} async-done(((bf16[16,1,64,2048]{3,2,1,0:T(8,128)(2,1)}), bf16[16,1,64,2048]{3,2,1,0:T(8,128)(2,1)}, u32[]{:S(2)}, u32[]{:S(2)}) %all-to-all-start.5) | async-done | bytes 4194336 | tf_op jit(solution)/shard_map/all_to_all | solution.py:335
  1131.3 9.8 gather_fusion
  1141.1 6.5 reshape.521
  1147.6 7.2 multiply_reduce_fusion.1
  1157.3 74.4 %reduce-scatter.29.cloned.1.call-done = bf16[2048,176]{0,1:T(8,128)(2,1)} async-done(((bf16[2048,2816]{0,1:T(8,128)(2,1)}), bf16[2048,176]{0,1:T(8,128)(2,1)}) %reduce-scatter.29.cloned.1.call-update) | async-done | bytes 720912 | tf_op jit(solution)/shard_map/reduce_scatter | solution.py:350
  1231.7 130.1 %reduce-scatter.33.cloned.1.call-done = bf16[176,2048]{1,0:T(8,128)(2,1)} async-done(((bf16[2816,2048]{1,0:T(8,128)(2,1)}), bf16[176,2048]{1,0:T(8,128)(2,1)}) %reduce-scatter.33.cloned.1.call-update) | async-done | bytes 720912 | tf_op jit(solution)/shard_map/reduce_scatter | solution.py:353
  1361.9 10.4 fusion.40
  1372.4 9.8 fusion.50
  1382.2 8.3 fusion.63
  1395.6 10.8 fusion.38
  1406.5 6.3 fusion.152
  1417.0 56.8 %all-to-all-done.7 = bf16[16,1,64,2048]{3,2,1,0:T(8,128)(2,1)} async-done(((bf16[16,1,64,2048]{3,2,1,0:T(8,128)(2,1)}), bf16[16,1,64,2048]{3,2,1,0:T(8,128)(2,1)}, u32[]{:S(2)}, u32[]{:S(2)}) %all-to-all-start.7) | async-done | bytes 4194336 | tf_op jit(solution)/shard_map/all_to_all | solution.py:336
  1473.8 9.1 gather_fusion.1
  1486.9 6.2 reduce_sum.193
  1495.0 6.7 fusion.95
  1502.6 22.4 all-to-all-start.8
  1525.0 11.6 fusion.39
  1539.4 86.4 %while.29 = (s32[]{:T(128)}, f32[2048,1,192]{0,2,1:T(8,128)}, f32[2048,1,128]{0,2,1:T(8,128)S(1)}, bf16[4,512,1,192]{1,3,2,0:T(8,128)(2,1)}, s32[4]{0:T(128)S(1)...) while((s32[]{:T(128)}, f32[2048,1,192]{0,2,1:T(8,128)}, ...), condition=%wide.region_23.24_spmd.clone, body=%wide.region_21.23_spmd.clone.sunk | while | flops 1759215616 | bytes 105935416 | solution.py:447
  1634.5 17.4 all-to-all-done.10
  1657.5 14.3 all-to-all-done.11
  1685.9 8.1 fusion.114
  1696.2 24.4 all_to_all.133
  1720.8 10.4 fusion.112
  1732.5 7.6 fusion.85
  1741.5 9.2 fusion.153
  1752.8 39.8 %all-reduce.6 = (f32[2048]{0:T(1024)S(1)}, f32[512]{0:T(512)S(1)}, f32[2048]{0:T(1024)S(1)}) all-reduce(f32[2048]{0:T(1024)S(1)} %get-tuple-element.208, f32[512]{0:T(512)S(1)} %copy-done.68, f32[2048]{0:T(1024)S(1)} %copy-done.57), channel_id=2, replica_groups=mesh['seq'=16,'fsdp'=2] {'seq','fsdp'}, use_global_device_ids=true, to_apply=%region_28.29.clone | all-reduce | flops 4608 | bytes 36864
  1817.1 118.1 %reduce-scatter.19.cloned.1.call-done = f32[64,576]{1,0:T(8,128)} async-done(((f32[2048,576]{1,0:T(8,128)}), f32[64,576]{1,0:T(8,128)}) %reduce-scatter.19.cloned.1.call-update) | async-done | bytes 147472 | tf_op jit(solution)/shard_map/reduce_scatter | solution.py:514
  1935.2 183.4 %reduce-scatter.21.cloned.1.call-done = f32[16,4096]{1,0:T(8,128)} async-done(((f32[512,4096]{1,0:T(8,128)}), f32[16,4096]{1,0:T(8,128)}) %reduce-scatter.21.cloned.1.call-update) | async-done | bytes 262160 | tf_op jit(solution)/shard_map/reduce_scatter | solution.py:516
  2118.6 360.7 %reduce-scatter.23.cloned.1.call-done = f32[64,2048]{1,0:T(8,128)} async-done(((f32[2048,2048]{1,0:T(8,128)}), f32[64,2048]{1,0:T(8,128)}) %reduce-scatter.23.cloned.1.call-update) | async-done | bytes 524304 | tf_op jit(solution)/shard_map/reduce_scatter | solution.py:517
  2479.3 253.4 %reduce-scatter.17.cloned.1.call-done = f32[64,3072]{1,0:T(8,128)} async-done(((f32[2048,3072]{1,0:T(8,128)}), f32[64,3072]{1,0:T(8,128)}) %reduce-scatter.17.cloned.1.call-update) | async-done | bytes 786448 | tf_op jit(solution)/shard_map/reduce_scatter | solution.py:513
  (486 shorter events, 255.1 us)
Async XLA Ops:
  7.2 21.3 copy-start.34
  7.2 93.4 %all-gather.14.cloned.1.call-start = ((), (), s32[]{:S(2)}) async-start(), calls=%async_computation.27 | async-start | bytes 2703360 | tf_op jit(solution)/shard_map/all_gather | solution.py:118
  8.9 127.9 %all-gather.16.cloned.1.call-start = ((), (), s32[]{:S(2)}) async-start(), calls=%async_computation.28 | async-start | bytes 4325376 | tf_op jit(solution)/shard_map/all_gather | solution.py:120
  10.6 28.5 %copy-start.35 = (f32[88,2048]{1,0:T(8,128)S(1)}, f32[88,2048]{1,0:T(8,128)}, u32[]{:S(2)}) copy-start(f32[88,2048]{1,0:T(8,128)} %param.36) | copy-start | bytes 2162692
  10.6 234.1 %all-gather.12.cloned.1.call-start = ((), (), s32[]{:S(2)}) async-start(), calls=%async_computation.26 | async-start | bytes 12976128 | tf_op jit(solution)/shard_map/all_gather | solution.py:117
  12.6 378.0 %all-gather.18.cloned.1.call-start = ((), (), s32[]{:S(2)}) async-start(), calls=%async_computation.29 | async-start | bytes 8650752 | tf_op jit(solution)/shard_map/all_gather | solution.py:121
  14.5 436.3 %all-gather.20.cloned.1.call-start = ((), (), s32[]{:S(2)}) async-start(), calls=%async_computation.30 | async-start | bytes 12255232 | tf_op jit(solution)/shard_map/all_gather | solution.py:339
  28.5 517.0 %all-gather.22.cloned.1.call-start = ((), (), s32[]{:S(2)}) async-start(), calls=%async_computation.31 | async-start | bytes 12255232 | tf_op jit(solution)/shard_map/all_gather | solution.py:340
  39.0 601.3 %all-gather.24.cloned.1.call-start = ((), (), s32[]{:S(2)}) async-start(), calls=%async_computation.32 | async-start | bytes 12255232 | tf_op jit(solution)/shard_map/all_gather | solution.py:341
  49.8 818.6 %all-gather.26.cloned.1.call-start = ((), (), s32[]{:S(2)}) async-start(), calls=%async_computation.33 | async-start | bytes 8650752 | tf_op jit(solution)/shard_map/all_gather | solution.py:166
  54.4 45.9 %copy-start.3 = (bf16[1,128,2048]{2,1,0:T(8,128)(2,1)S(1)}, bf16[1,128,2048]{2,1,0:T(8,128)(2,1)}, u32[]{:S(2)}) copy-start(bf16[1,128,2048]{2,1,0:T(8,128)(2,1)} %param.22) | copy-start | bytes 1572868
  54.4 825.7 %all-gather.28.cloned.1.call-start = ((), (), s32[]{:S(2)}) async-start(), calls=%async_computation.34 | async-start | bytes 8650752 | tf_op jit(solution)/shard_map/all_gather | solution.py:167
  59.4 86.3 %copy-start.62 = (f32[32]{0:T(128)}, f32[32]{0:T(128)S(1)}, u32[]{:S(2)}) copy-start(f32[32]{0:T(128)S(1)} %multiply_exponential_fusion) | copy-start | bytes 388
  100.3 161.0 %copy-start.36 = (f32[2048]{0:T(1024)}, f32[2048]{0:T(1024)S(1)}, u32[]{:S(2)}) copy-start(f32[2048]{0:T(1024)S(1)} %convert_element_type.319) | copy-start | bytes 24580
  100.5 160.8 %copy-start.52 = (f32[128]{0:T(128)}, f32[128]{0:T(128)S(1)}, u32[]{:S(2)}) copy-start(f32[128]{0:T(128)S(1)} %add_rsqrt_fusion.2) | copy-start | bytes 1540
  100.5 39.3 %copy-start.46 = (f32[512]{0:T(512)}, f32[512]{0:T(512)S(1)}, u32[]{:S(2)}) copy-start(f32[512]{0:T(512)S(1)} %convert_element_type.328) | copy-start | bytes 6148
  100.5 45.2 %copy-start.64 = (f32[128]{0:T(128)}, f32[128]{0:T(128)S(1)}, u32[]{:S(2)}) copy-start(f32[128]{0:T(128)S(1)} %add_convert_fusion.2) | copy-start | bytes 1540
  103.5 36.8 %copy-start.17 = (f32[128,576]{0,1:T(8,128)}, f32[128,576]{0,1:T(8,128)S(1)}, u32[]{:S(2)}) copy-start(f32[128,576]{0,1:T(8,128)S(1)} %fusion.121) | copy-start | bytes 884740
  103.7 36.5 %copy-start.60 = (f32[128]{0:T(128)}, f32[128]{0:T(128)S(1)}, u32[]{:S(2)}) copy-start(f32[128]{0:T(128)S(1)} %add_rsqrt_fusion.1) | copy-start | bytes 1540
  141.8 127.3 %all-to-all-start.1 = ((bf16[128,16,192]{0,2,1:T(8,128)(2,1)}), bf16[128,16,192]{0,2,1:T(8,128)(2,1)S(1)}, u32[]{:S(2)}, u32[]{:S(2)}) async-start(bf16[128,16,192]{0,2,1:T(8,128)(2,1)} %pad_maximum_fusion.2), calls=%async_computation.1 | async-start | bytes 1572864 | tf_op jit(solution)/shard_map/all_to_all | solution.py:204
  145.9 122.2 %copy-start.40 = (f32[128,32]{0,1:T(8,128)}, f32[128,32]{0,1:T(8,128)S(1)}, u32[]{:S(2)}) copy-start(f32[128,32]{0,1:T(8,128)S(1)} %get-tuple-element.280) | copy-start | bytes 49156
  145.9 122.2 %copy-start.42 = (f32[128,32]{0,1:T(8,128)}, f32[128,32]{0,1:T(8,128)S(1)}, u32[]{:S(2)}) copy-start(f32[128,32]{0,1:T(8,128)S(1)} %get-tuple-element.281) | copy-start | bytes 49156
  269.1 32.6 %all-to-all-start = ((bf16[128,16,192]{0,2,1:T(8,128)(2,1)}), bf16[128,16,192]{0,2,1:T(8,128)(2,1)S(1)}, u32[]{:S(2)}, u32[]{:S(2)}) async-start(bf16[128,16,192]{0,2,1:T(8,128)(2,1)} %pad_maximum_fusion.1), calls=%async_computation | async-start | bytes 1572864 | tf_op jit(solution)/shard_map/all_to_all | solution.py:197
  301.7 28.6 %all-to-all-start.2 = ((bf16[128,16,128]{2,0,1:T(8,128)(2,1)}), bf16[128,16,128]{2,0,1:T(8,128)(2,1)S(1)}, u32[]{:S(2)}, u32[]{:S(2)}) async-start(bf16[128,16,128]{2,0,1:T(8,128)(2,1)} %copy.154), calls=%async_computation.2 | async-start | bytes 1048576 | tf_op jit(solution)/shard_map/all_to_all | solution.py:211
  307.3 585.5 %all-gather.30.cloned.1.call-start = ((), (), s32[]{:S(2)}) async-start(), calls=%async_computation.35 | async-start | bytes 8650752 | tf_op jit(solution)/shard_map/all_gather | solution.py:168
  312.2 18.1 copy-start.50
  357.4 33.0 %copy-start.28 = (bf16[2048,1,192]{0,2,1:T(8,128)(2,1)}, bf16[2048,1,192]{0,2,1:T(8,128)(2,1)S(1)}, u32[]{:S(2)}) copy-start(bf16[2048,1,192]{0,2,1:T(8,128)(2,1)S(1)} %get-tuple-element.603) | copy-start | bytes 2359300
  357.4 38.2 %copy-start.9 = (bf16[2048,1,128]{2,0,1:T(8,128)(2,1)}, bf16[2048,1,128]{2,0,1:T(8,128)(2,1)S(1)}, u32[]{:S(2)}) copy-start(bf16[2048,1,128]{2,0,1:T(8,128)(2,1)S(1)} %get-tuple-element.559) | copy-start | bytes 1572868
  357.4 33.0 %all-to-all-start.3 = ((bf16[16,128,128]{2,1,0:T(8,128)(2,1)}), bf16[16,128,128]{2,1,0:T(8,128)(2,1)S(1)}, u32[]{:S(2)}, u32[]{:S(2)}) async-start(bf16[16,128,128]{2,1,0:T(8,128)(2,1)} %bitcast.444), calls=%async_computation.3 | async-start | bytes 1048576 | tf_op jit(solution)/shard_map/all_to_all | solution.py:246
  367.3 789.4 %reduce-scatter.25.cloned.1.call-start = ((), (), s32[]{:S(2)}) async-start(), calls=%async_computation.40 | async-start | bytes 12255232 | tf_op jit(solution)/shard_map/reduce_scatter | solution.py:347
  367.4 28.2 %copy-start.44 = (f32[2048]{0:T(1024)}, f32[2048]{0:T(1024)S(1)}, u32[]{:S(2)}) copy-start(f32[2048]{0:T(1024)S(1)} %convert_element_type.333) | copy-start | bytes 24580
  395.6 64.5 %copy-start.66 = (f32[128]{0:T(128)}, f32[128]{0:T(128)S(1)}, u32[]{:S(2)}) copy-start(f32[128]{0:T(128)S(1)} %add_rsqrt_fusion) | copy-start | bytes 1540
  460.1 180.2 %copy-start.22 = (bf16[1,128,2048]{2,1,0:T(8,128)(2,1)S(1)}, bf16[1,128,2048]{2,1,0:T(8,128)(2,1)}, u32[]{:S(2)}) copy-start(bf16[1,128,2048]{2,1,0:T(8,128)(2,1)} %param.23) | copy-start | bytes 1572868
  649.6 212.7 %copy-start.21 = (bf16[128,2816]{1,0:T(8,128)(2,1)}, bf16[128,2816]{1,0:T(8,128)(2,1)S(1)}, u32[]{:S(2)}) copy-start(bf16[128,2816]{1,0:T(8,128)(2,1)S(1)} %get-tuple-element.269) | copy-start | bytes 2162692
  655.9 575.7 %reduce-scatter.29.cloned.1.call-start = ((), (), s32[]{:S(2)}) async-start(), calls=%async_computation.42 | async-start | bytes 12255232 | tf_op jit(solution)/shard_map/reduce_scatter | solution.py:350
  685.3 164.8 %all-to-all-start.4 = ((bf16[16,1,64,2048]{3,2,1,0:T(8,128)(2,1)}), bf16[16,1,64,2048]{3,2,1,0:T(8,128)(2,1)}, u32[]{:S(2)}, u32[]{:S(2)}) async-start(bf16[16,1,64,2048]{3,2,1,0:T(8,128)(2,1)} %bitcast.424), calls=%async_computation.4 | async-start | bytes 8388608 | tf_op jit(solution)/shard_map/all_to_all | solution.py:284
  850.1 122.4 %all-to-all-start.6 = ((bf16[16,1,64,2048]{3,2,1,0:T(8,128)(2,1)}), bf16[16,1,64,2048]{3,2,1,0:T(8,128)(2,1)}, u32[]{:S(2)}, u32[]{:S(2)}) async-start(bf16[16,1,64,2048]{3,2,1,0:T(8,128)(2,1)} %bitcast.423), calls=%async_computation.6 | async-start | bytes 8388608 | tf_op jit(solution)/shard_map/all_to_all | solution.py:291
  862.1 499.8 %reduce-scatter.33.cloned.1.call-start = ((), (), s32[]{:S(2)}) async-start(), calls=%async_computation.44 | async-start | bytes 12255232 | tf_op jit(solution)/shard_map/reduce_scatter | solution.py:353
  972.5 15.9 copy-start.69
  998.6 132.7 %all-to-all-start.5 = ((bf16[16,1,64,2048]{3,2,1,0:T(8,128)(2,1)}), bf16[16,1,64,2048]{3,2,1,0:T(8,128)(2,1)}, u32[]{:S(2)}, u32[]{:S(2)}) async-start(bf16[16,1,64,2048]{3,2,1,0:T(8,128)(2,1)} %convert_bitcast_fusion), calls=%async_computation.5 | async-start | bytes 8388608 | tf_op jit(solution)/shard_map/all_to_all | solution.py:335
  1031.8 708.3 %reduce-scatter.43.cloned.1.call-start = ((), (), s32[]{:S(2)}) async-start(), calls=%async_computation.49 | async-start | bytes 1081344
  1156.7 640.1 %reduce-scatter.27.cloned.1.call-start = ((), (), s32[]{:S(2)}) async-start(), calls=%async_computation.41 | async-start | bytes 1081344 | tf_op jit(solution)/shard_map/reduce_scatter | solution.py:367
  1157.2 641.4 %reduce-scatter.31.cloned.1.call-start = ((), (), s32[]{:S(2)}) async-start(), calls=%async_computation.43 | async-start | bytes 1081344 | tf_op jit(solution)/shard_map/reduce_scatter | solution.py:370
  1231.7 568.9 %reduce-scatter.35.cloned.1.call-start = ((), (), s32[]{:S(2)}) async-start(), calls=%async_computation.45 | async-start | bytes 1081344 | tf_op jit(solution)/shard_map/reduce_scatter | solution.py:373
  1361.9 440.7 %reduce-scatter.41.cloned.1.call-start = ((), (), s32[]{:S(2)}) async-start(), calls=%async_computation.48 | async-start | bytes 8650752 | tf_op jit(solution)/shard_map/reduce_scatter | solution.py:364
  1390.5 83.4 %all-to-all-start.7 = ((bf16[16,1,64,2048]{3,2,1,0:T(8,128)(2,1)}), bf16[16,1,64,2048]{3,2,1,0:T(8,128)(2,1)}, u32[]{:S(2)}, u32[]{:S(2)}) async-start(bf16[16,1,64,2048]{3,2,1,0:T(8,128)(2,1)} %fusion.63), calls=%async_computation.7 | async-start | bytes 8388608 | tf_op jit(solution)/shard_map/all_to_all | solution.py:336
  1395.3 412.3 %reduce-scatter.37.cloned.1.call-start = ((), (), s32[]{:S(2)}) async-start(), calls=%async_computation.46 | async-start | bytes 8650752 | tf_op jit(solution)/shard_map/reduce_scatter | solution.py:358
  1502.6 36.8 %all-to-all-start.8 = ((bf16[128,16,128]{2,0,1:T(8,128)(2,1)}), bf16[128,16,128]{2,0,1:T(8,128)(2,1)S(1)}, u32[]{:S(2)}, u32[]{:S(2)}) async-start(bf16[128,16,128]{2,0,1:T(8,128)(2,1)} %bitcast.371), calls=%async_computation.8 | async-start | bytes 1048576 | tf_op jit(solution)/shard_map/all_to_all | solution.py:411
  1525.0 287.4 %reduce-scatter.39.cloned.1.call-start = ((), (), s32[]{:S(2)}) async-start(), calls=%async_computation.47 | async-start | bytes 8650752 | tf_op jit(solution)/shard_map/reduce_scatter | solution.py:361
  1628.6 43.3 %copy-start.18 = (f32[128,576]{0,1:T(8,128)S(1)}, f32[128,576]{0,1:T(8,128)}, u32[]{:S(2)}) copy-start(f32[128,576]{0,1:T(8,128)} %copy-done.17) | copy-start | bytes 884740
  1628.6 43.3 %copy-start.47 = (f32[512]{0:T(512)S(1)}, f32[512]{0:T(512)}, u32[]{:S(2)}) copy-start(f32[512]{0:T(512)} %copy-done.46) | copy-start | bytes 6148
  1628.6 43.3 %copy-start.61 = (f32[128]{0:T(128)S(1)}, f32[128]{0:T(128)}, u32[]{:S(2)}) copy-start(f32[128]{0:T(128)} %copy-done.60) | copy-start | bytes 1540
  1628.6 23.3 all-to-all-start.10
  1651.9 20.0 all-to-all-start.11
  1657.4 277.9 %reduce-scatter.19.cloned.1.call-start = ((), (), s32[]{:S(2)}) async-start(), calls=%async_computation.37 | async-start | bytes 5406720 | tf_op jit(solution)/shard_map/reduce_scatter | solution.py:514
  1657.5 18.7 copy-start.63
  1657.5 18.6 copy-start.65
  1679.8 438.9 %reduce-scatter.21.cloned.1.call-start = ((), (), s32[]{:S(2)}) async-start(), calls=%async_computation.38 | async-start | bytes 8650752 | tf_op jit(solution)/shard_map/reduce_scatter | solution.py:516
  1684.5 794.8 %reduce-scatter.23.cloned.1.call-start = ((), (), s32[]{:S(2)}) async-start(), calls=%async_computation.39 | async-start | bytes 17301504 | tf_op jit(solution)/shard_map/reduce_scatter | solution.py:517
  1694.0 26.7 copy-start.41
  1694.0 26.7 copy-start.43
  1694.0 1038.7 %reduce-scatter.17.cloned.1.call-start = ((), (), s32[]{:S(2)}) async-start(), calls=%async_computation.36 | async-start | bytes 25952256 | tf_op jit(solution)/shard_map/reduce_scatter | solution.py:513
  1695.7 25.1 copy-start.54
  1750.7 43.7 %copy-start.56 = (f32[128]{0:T(128)S(1)}, f32[128]{0:T(128)}, u32[]{:S(2)}) copy-start(f32[128]{0:T(128)} %copy-done.52) | copy-start | bytes 1540
  (78 other events, 360.9 us)
Sparse Core Ops, SparseCore 0:
  11.5 60.7 all-gather.13
  75.7 61.0 all-gather.15
  140.3 104.4 all-gather.11
  248.2 96.5 all-gather.17
  347.0 103.7 all-gather.19
  453.0 92.4 all-gather.21
  547.8 92.4 all-gather.23
  641.8 72.9 all-gather.25
  716.3 75.6 all-gather.27
  793.4 75.0 all-gather.29
  872.6 205.9 reduce-scatter.24
  1083.1 148.5 reduce-scatter.28
  1235.8 126.0 reduce-scatter.32
  1364.0 142.1 reduce-scatter.42
  1508.3 19.6 reduce-scatter.26
  1530.2 16.7 reduce-scatter.30
  1549.1 16.7 reduce-scatter.34
  1568.7 71.3 reduce-scatter.40
  1643.0 71.3 reduce-scatter.36
  1716.6 72.2 reduce-scatter.38
  1791.8 143.3 reduce-scatter.18
  1938.1 180.4 reduce-scatter.20
  2121.5 357.7 reduce-scatter.22
  2486.1 246.4 reduce-scatter.16
where the time goes:
time: 2750 us; the launch traced here: 2740 us
  waiting for transfers between devices  1810 us (66%)
  matrix products  306 us (11%)
  blocking collectives  270 us (10%)
  local copies, waits for them, and re-layouts  122 us (4%)
  starting transfers between devices  113 us (4%)
  other arithmetic  84.9 us (3%)
    reduce_scatter x1, waiting for transfers between devices, body(): lax.psum_scatter(grad_output, ('seq', 'fsdp'), scatter_dimension=0, tiled...  361 us
    reduce_scatter x1, waiting for transfers between devices, body(): lax.psum_scatter(grad_query, ('seq', 'fsdp'), scatter_dimension=0, tiled=...  253 us
    reduce_scatter x1, waiting for transfers between devices, body(): lax.psum_scatter(grad_expand, ('seq', 'fsdp'), scatter_dimension=0, tiled...  183 us
    all_gather x1, blocking collectives, fetch_dense(): lax.all_gather(w_router.astype(jnp.bfloat16), ('seq', 'fsdp'), axis=0, ti...  132 us
    reduce_scatter x1, waiting for transfers between devices, body(): lax.psum_scatter(whole_grads[2].astype(jnp.bfloat16), 'seq', scatter_dime...  130 us
    reduce_scatter x1, waiting for transfers between devices, body(): lax.psum_scatter(grad_latent, ('seq', 'fsdp'), scatter_dimension=0, tiled...  118 us
    all_to_all x1, waiting for transfers between devices, body(): lax.all_to_all(expert_made, 'seq', split_axis=0, concat_axis=0, tiled=True)  99.1 us
    all_gather x1, waiting for transfers between devices, fetch_dense(): lax.all_gather(w_query.astype(jnp.bfloat16), ('seq', 'fsdp'), axis=0, til...  98.8 us
  transfers between devices with their start and end apart: 35, of which 20 were waited for; matrix products, arithmetic and copies ran while one was open for 18% of the time, Pallas kernels for 0%

commit v1 on v0

v1 whole, which is shorter than its diff:
```python
import math

import jax
import jax.numpy as jnp
from jax import lax
from jax.sharding import PartitionSpec as P

H = 16
NOPE = 128
ROPE = 64
VD = 128
LAT = 512
TOP = 6
EPSILON = 1e-06
HIGHEST = lax.Precision.HIGHEST
LOW = jnp.bfloat16
F32 = jnp.float32


def rotary_tables(count, offset):
    places = (offset + jnp.arange(count, dtype=jnp.int32)).astype(F32)
    powers = jnp.arange(ROPE // 2, dtype=jnp.int32).astype(F32) * (2.0 / ROPE)
    inverse = jnp.exp(powers * -math.log(10000.0))
    angles = places[:, None] * inverse[None, :]
    return jnp.cos(angles), jnp.sin(angles)


def rotate(values, cosine, sine):
    half = values.shape[-1] // 2
    former, latter = values[..., :half], values[..., half:]
    return jnp.concatenate(
        [former * cosine - latter * sine, latter * cosine + former * sine], axis=-1
    )


def rotate_back(values, cosine, sine):
    return rotate(values, cosine, -sine)


def dot(left, right):
    return jnp.dot(left, right, preferred_element_type=F32)


def dot_t(left, right):
    return lax.dot_general(left, right, (((1,), (1,)), ((), ())), preferred_element_type=F32)


def t_dot(left, right):
    return lax.dot_general(left, right, (((0,), (0,)), ((), ())), preferred_element_type=F32)


def exact_t_dot(left, right):
    return lax.dot_general(
        left, right, (((0,), (0,)), ((), ())), precision=HIGHEST, preferred_element_type=F32
    )


def exact_dot_t(left, right):
    return lax.dot_general(
        left, right, (((1,), (1,)), ((), ())), precision=HIGHEST, preferred_element_type=F32
    )


def norm_forward(values, gain):
    factor = lax.rsqrt(jnp.mean(values * values, axis=-1, keepdims=True) + EPSILON)
    normed = values * factor
    return normed * gain, normed, factor


def norm_backward(grad_in, normed, factor, gain):
    inner = grad_in * gain
    gain_grad = jnp.sum(grad_in * normed, axis=0)
    back = factor * (inner - normed * jnp.mean(inner * normed, axis=-1, keepdims=True))
    return back, gain_grad


def swish_slope(value, sigmoid):
    return sigmoid * (1.0 + value * (1.0 - sigmoid))


def gather_rows(block):
    return lax.all_gather(block, "seq", axis=0, tiled=True)


def scatter_rows(partial):
    return lax.psum_scatter(partial, "seq", scatter_dimension=0, tiled=True)


def attend_forward(head_q, head_k, head_v, doc_ids):
    seq_len = head_q.shape[0]
    block_rows = min(512, seq_len)
    places = jnp.arange(seq_len, dtype=jnp.int32)
    scale = (NOPE + ROPE) ** (-0.5)

    def attend(index):
        start = index * block_rows
        query = lax.dynamic_slice_in_dim(head_q, start, block_rows, 0)
        docs = lax.dynamic_slice_in_dim(doc_ids, start, block_rows, 0)
        rows = start + jnp.arange(block_rows, dtype=jnp.int32)
        allowed = (docs[:, None] == doc_ids[None, :]) & (rows[:, None] >= places[None, :])
        scores = jnp.where(allowed, dot_t(query, head_k) * scale, -1e30)
        peak = jnp.max(scores, axis=-1, keepdims=True)
        raised = jnp.exp(scores - peak)
        totals = jnp.sum(raised, axis=-1, keepdims=True)
        out = dot((raised / totals).astype(LOW), head_v)
        return out.astype(LOW), peak + jnp.log(totals)

    out, logs = lax.map(attend, jnp.arange(seq_len // block_rows, dtype=jnp.int32))
    return out.reshape(seq_len, VD), logs.reshape(seq_len, 1)


def attend_backward(head_q, head_k, head_v, doc_ids, logs, head_g):
    seq_len = head_q.shape[0]
    block_rows = min(512, seq_len)
    places = jnp.arange(seq_len, dtype=jnp.int32)
    scale = (NOPE + ROPE) ** (-0.5)

    def back(carry, index):
        key_grad, value_grad = carry
        start = index * block_rows
        query = lax.dynamic_slice_in_dim(head_q, start, block_rows, 0)
        grad = lax.dynamic_slice_in_dim(head_g, start, block_rows, 0)
        log = lax.dynamic_slice_in_dim(logs, start, block_rows, 0)
        docs = lax.dynamic_slice_in_dim(doc_ids, start, block_rows, 0)
        rows = start + jnp.arange(block_rows, dtype=jnp.int32)
        allowed = (docs[:, None] == doc_ids[None, :]) & (rows[:, None] >= places[None, :])
        scores = jnp.where(allowed, dot_t(query, head_k) * scale, -1e30)
        attention = jnp.exp(scores - log)
        value_grad = value_grad + t_dot(attention.astype(LOW), grad)
        weight_grad = dot_t(grad, head_v)
        inner = jnp.sum(attention * weight_grad, axis=-1, keepdims=True)
        score_grad = (attention * (weight_grad - inner)).astype(LOW)
        query_grad = dot(score_grad, head_k) * scale
        key_grad = key_grad + t_dot(score_grad, query) * scale
        return (key_grad, value_grad), query_grad.astype(LOW)

    start = (
        jnp.zeros((seq_len, NOPE + ROPE), F32),
        jnp.zeros((seq_len, VD), F32),
    )
    (key_grad, value_grad), query_grad = lax.scan(
        back, start, jnp.arange(seq_len // block_rows, dtype=jnp.int32)
    )
    return query_grad.reshape(seq_len, NOPE + ROPE), key_grad.astype(LOW), value_grad.astype(LOW)


def body(
    tokens,
    cotangent,
    segments,
    routes,
    norm_attn,
    w_query,
    w_latent,
    norm_latent,
    w_expand,
    w_output,
    norm_ffn,
    w_router,
    w_shared_gate,
    w_shared_up,
    w_shared_down,
    w_expert_gate,
    w_expert_up,
    w_expert_down,
):
    groups = lax.axis_size("seq")
    layers = lax.axis_size("fsdp")
    both = ("seq", "fsdp")
    place = lax.axis_index("seq")
    tok_rows, width = tokens.shape[1], tokens.shape[2]
    seq_len = segments.shape[1]
    own_rows = w_query.shape[0]
    lat_rows = w_expand.shape[0]
    experts = w_router.shape[1]
    capacity = tok_rows // 2
    query_width = NOPE + ROPE
    hidden_own = tokens[0].astype(F32)
    grad_own = cotangent[0].astype(F32)
    doc_ids = segments[0]

    lat_column = jnp.pad(norm_latent[:, None], ((0, own_rows - lat_rows), (0, 0)))
    packed_small = jnp.concatenate(
        [w_latent, w_router, norm_attn[:, None], norm_ffn[:, None], lat_column], axis=1
    ).astype(LOW)
    used = packed_small.shape[1]
    packed_small = jnp.pad(packed_small, ((0, 0), (0, -used % 128)))
    small = lax.all_gather(packed_small, both, axis=0, tiled=True)
    latent_w = small[:, : LAT + ROPE]
    router_w = small[:, LAT + ROPE : LAT + ROPE + experts]
    gains = small[:, LAT + ROPE + experts : LAT + ROPE + experts + 3].astype(F32).T
    gain_attn, gain_ffn = gains[0], gains[1]
    gain_latent = gains[2].reshape(groups * layers, own_rows)[:, :lat_rows].reshape(LAT)

    fold = lat_rows * (NOPE + VD) // own_rows
    query_parts = w_query.astype(LOW).reshape(own_rows, H, query_width).transpose(1, 0, 2)
    expand_parts = (
        w_expand.astype(LOW)
        .reshape(lat_rows, H, NOPE + VD)
        .transpose(1, 0, 2)
        .reshape(H, own_rows, fold)
    )
    head_parts = jnp.concatenate([query_parts, expand_parts], axis=2)
    head_parts = lax.all_to_all(head_parts, "seq", split_axis=0, concat_axis=0, tiled=True)
    head_parts = lax.all_gather(head_parts, "fsdp", axis=1, tiled=False)
    query_w = head_parts[..., :query_width].reshape(width, query_width)
    expand_w = head_parts[..., query_width:].reshape(LAT, NOPE + VD)
    output_w = lax.all_gather(w_output.astype(LOW), "fsdp", axis=0, tiled=True)

    expert_gate_w = lax.all_gather(w_expert_gate[0].astype(LOW), "fsdp", axis=0, tiled=True)
    expert_up_w = lax.all_gather(w_expert_up[0].astype(LOW), "fsdp", axis=0, tiled=True)
    expert_down_w = lax.all_gather(w_expert_down[0].astype(LOW), "fsdp", axis=0, tiled=True)
    shared_in = jnp.concatenate([w_shared_gate, w_shared_up], axis=1).astype(LOW)
    shared_in_w = lax.all_gather(shared_in, "fsdp", axis=0, tiled=True)
    shared_down_w = lax.all_gather(w_shared_down.astype(LOW), "fsdp", axis=0, tiled=True)
    units = w_shared_gate.shape[1]

    hidden_low = gather_rows(tokens[0])
    grad_low = gather_rows(cotangent[0])
    all_routes = gather_rows(routes[0])

    scaled_one, _, _ = norm_forward(hidden_low.astype(F32), gain_attn)
    normed_low = scaled_one.astype(LOW)
    query_proj = dot(normed_low, query_w)
    latent_proj = dot(normed_low, latent_w)
    cosine, sine = rotary_tables(seq_len, 0)
    head_q = jnp.concatenate(
        [query_proj[:, :NOPE], rotate(query_proj[:, NOPE:], cosine, sine)], axis=-1
    ).astype(LOW)
    latent_scaled, _, _ = norm_forward(latent_proj[:, :LAT], gain_latent)
    latent_low = latent_scaled.astype(LOW)
    expanded = dot(latent_low, expand_w)
    key_rope = rotate(latent_proj[:, LAT:], cosine, sine)
    head_k = jnp.concatenate([expanded[:, :NOPE], key_rope], axis=-1).astype(LOW)
    head_v = expanded[:, NOPE:].astype(LOW)

    head_out, logs = attend_forward(head_q, head_k, head_v, doc_ids)
    residual = hidden_own + scatter_rows(dot(head_out, output_w).astype(LOW)).astype(F32)
    scaled_two, normed_two, factor_two = norm_forward(residual, gain_ffn)
    own_two_low = scaled_two.astype(LOW)
    two_low = gather_rows(own_two_low)

    logits = dot(two_low, router_w)
    raised = jnp.exp(logits - jnp.max(logits, axis=-1, keepdims=True))
    router_p = raised / jnp.sum(raised, axis=-1, keepdims=True)
    own_p = lax.dynamic_slice_in_dim(router_p, place * tok_rows, tok_rows, 0)
    mine = (jnp.arange(experts, dtype=jnp.int32) == place).astype(F32)
    gate = jnp.sum(router_p * mine[None, :], axis=-1).reshape(groups, tok_rows)
    named = jnp.any(all_routes == place, axis=-1).reshape(groups, tok_rows)
    rank = jnp.cumsum(named.astype(jnp.int32), axis=1) - 1
    slots = jnp.arange(capacity, dtype=jnp.int32)
    chosen = named[:, None, :] & (rank[:, None, :] == slots[None, :, None])
    chosen_low = chosen.astype(LOW)
    slot_gate = jnp.sum(jnp.where(chosen, gate[:, None, :], 0.0), axis=-1)
    slot_gate = slot_gate.reshape(groups * capacity, 1)

    def dispatch(rows):
        picked = jnp.einsum(
            "brt,btd->brd",
            chosen_low,
            rows.reshape(groups, tok_rows, width),
            preferred_element_type=F32,
        )
        return picked.reshape(groups * capacity, width).astype(LOW)

    def combine(rows):
        spread = jnp.einsum(
            "brt,brd->btd",
            chosen_low,
            rows.reshape(groups, capacity, width),
            preferred_element_type=F32,
        )
        return spread.reshape(seq_len, width)

    expert_in = dispatch(two_low)
    expert_g = dispatch(grad_low)
    made_grad = (slot_gate * expert_g.astype(F32)).astype(LOW)
    gate_proj = dot(expert_in, expert_gate_w)
    up_proj = dot(expert_in, expert_up_w)
    sigmoid = jax.nn.sigmoid(gate_proj)
    inner_low = (gate_proj * sigmoid * up_proj).astype(LOW)
    made = dot(inner_low, expert_down_w).astype(LOW)
    inner_grad = dot_t(made_grad, expert_down_w)
    gate_grad = (inner_grad * up_proj * swish_slope(gate_proj, sigmoid)).astype(LOW)
    up_grad = (inner_grad * gate_proj * sigmoid).astype(LOW)
    row_grad = (dot_t(gate_grad, expert_gate_w) + dot_t(up_grad, expert_up_w)).astype(LOW)
    slot_score = jnp.sum(expert_g.astype(F32) * made.astype(F32), axis=-1)
    score_grad = jnp.sum(
        jnp.where(chosen, slot_score.reshape(groups, capacity, 1), 0.0), axis=1
    )
    prob_grad = lax.all_to_all(score_grad, "seq", split_axis=0, concat_axis=0, tiled=True).T

    shared_proj = dot(two_low, shared_in_w)
    shared_gate, shared_up = shared_proj[:, :units], shared_proj[:, units:]
    shared_sigmoid = jax.nn.sigmoid(shared_gate)
    shared_low = (shared_gate * shared_sigmoid * shared_up).astype(LOW)
    shared_back = dot_t(grad_low, shared_down_w)
    shared_grads = jnp.concatenate(
        [
            shared_back * shared_up * swish_slope(shared_gate, shared_sigmoid),
            shared_back * shared_gate * shared_sigmoid,
        ],
        axis=1,
    ).astype(LOW)

    part_grad = combine(row_grad) + dot_t(shared_grads, shared_in_w)
    two_grad = scatter_rows(part_grad.astype(LOW)).astype(F32)
    part_out = combine((slot_gate * made.astype(F32)).astype(LOW)) + dot(shared_low, shared_down_w)
    ffn_out = scatter_rows(part_out.astype(LOW)).astype(F32)
    output = (residual + ffn_out).astype(LOW)

    def spread_grad(grad):
        return lax.psum_scatter(
            grad.astype(LOW), "fsdp", scatter_dimension=0, tiled=True
        ).astype(F32)

    grad_expert_down = spread_grad(t_dot(inner_low, made_grad))
    grad_expert_gate = spread_grad(t_dot(expert_in, gate_grad))
    grad_expert_up = spread_grad(t_dot(expert_in, up_grad))
    grad_shared_in = spread_grad(t_dot(two_low, shared_grads))
    grad_shared_down = spread_grad(t_dot(shared_low, grad_low))

    logit_grad = own_p * (prob_grad - jnp.sum(own_p * prob_grad, axis=-1, keepdims=True))
    grad_router = exact_t_dot(own_two_low.astype(F32), logit_grad)
    two_grad = two_grad + exact_dot_t(logit_grad, router_w.astype(F32))
    residual_part, grad_gain_ffn = norm_backward(two_grad, normed_two, factor_two, gain_ffn)
    residual_grad = grad_own + residual_part
    attn_grad = gather_rows(residual_grad.astype(LOW))

    grad_output = spread_grad(t_dot(head_out, attn_grad))
    head_g = dot_t(attn_grad, output_w).astype(LOW)
    query_grad, key_grad, value_grad = attend_backward(
        head_q, head_k, head_v, doc_ids, logs, head_g
    )
    query_back = jnp.concatenate(
        [
            query_grad[:, :NOPE],
            rotate_back(query_grad[:, NOPE:].astype(F32), cosine, sine).astype(LOW),
        ],
        axis=-1,
    )
    expand_back = jnp.concatenate([key_grad[:, :NOPE], value_grad], axis=-1)
    part_rows = jnp.concatenate(
        [
            dot_t(query_back, query_w).astype(LOW),
            dot_t(expand_back, expand_w).astype(LOW),
            key_grad[:, NOPE:],
            jnp.zeros((seq_len, 64), LOW),
        ],
        axis=1,
    )
    own_parts = scatter_rows(part_rows).astype(F32)

    grad_query_head = t_dot(normed_low, query_back).reshape(
        groups, layers, own_rows, query_width
    )
    grad_expand_head = t_dot(latent_low, expand_back).reshape(groups, layers, own_rows, fold)
    head_grads = jnp.concatenate([grad_query_head, grad_expand_head], axis=3).astype(LOW)
    head_grads = lax.psum_scatter(head_grads, "fsdp", scatter_dimension=1, tiled=False)
    head_grads = lax.all_to_all(head_grads, "seq", split_axis=0, concat_axis=0, tiled=True)
    grad_query = (
        head_grads[..., :query_width].transpose(1, 0, 2).reshape(own_rows, H * query_width)
    ).astype(F32)
    grad_expand = (
        head_grads[..., query_width:]
        .reshape(H, lat_rows, NOPE + VD)
        .transpose(1, 0, 2)
        .reshape(lat_rows, H * (NOPE + VD))
    ).astype(F32)

    own_low = lax.dynamic_slice_in_dim(normed_low, place * tok_rows, tok_rows, 0)
    own_latent = lax.dynamic_slice_in_dim(latent_proj, place * tok_rows, tok_rows, 0)
    own_cosine = lax.dynamic_slice_in_dim(cosine, place * tok_rows, tok_rows, 0)
    own_sine = lax.dynamic_slice_in_dim(sine, place * tok_rows, tok_rows, 0)
    _, latent_normed, latent_factor = norm_forward(own_latent[:, :LAT], gain_latent)
    latent_back, grad_gain_latent = norm_backward(
        own_parts[:, width : width + LAT], latent_normed, latent_factor, gain_latent
    )
    rope_back = rotate_back(
        own_parts[:, width + LAT : width + LAT + ROPE], own_cosine, own_sine
    )
    latent_grad = jnp.concatenate([latent_back, rope_back], axis=-1).astype(LOW)
    grad_latent = t_dot(own_low, latent_grad)
    one_grad = own_parts[:, :width] + dot_t(latent_grad, latent_w)
    _, normed_one, factor_one = norm_forward(hidden_own, gain_attn)
    input_part, grad_gain_attn = norm_backward(one_grad, normed_one, factor_one, gain_attn)
    input_grad = (residual_grad + input_part).astype(LOW)

    lat_spread = jnp.pad(
        grad_gain_latent.reshape(groups * layers, lat_rows), ((0, 0), (0, own_rows - lat_rows))
    ).reshape(width)
    gain_columns = jnp.stack([grad_gain_attn, grad_gain_ffn, lat_spread]).T
    packed = jnp.concatenate([grad_latent, grad_router, gain_columns], axis=1)
    packed = jnp.pad(packed, ((0, 0), (0, -used % 128)))
    packed = lax.psum_scatter(packed, both, scatter_dimension=0, tiled=True)
    at = LAT + ROPE + experts
    return (
        output[None],
        input_grad[None],
        packed[:, at],
        grad_query,
        packed[:, : LAT + ROPE],
        packed[:lat_rows, at + 2],
        grad_expand,
        grad_output,
        packed[:, at + 1],
        packed[:, LAT + ROPE : at],
        grad_shared_in[:, :units],
        grad_shared_in[:, units:],
        grad_shared_down,
        grad_expert_gate[None],
        grad_expert_up[None],
        grad_expert_down[None],
    )


def solution(mesh):
    flat = P(("seq", "fsdp"))
    rows = P(("seq", "fsdp"), None)
    tokens = P("fsdp", "seq", None)
    expert = P("seq", "fsdp", None)
    weights = (
        flat,
        rows,
        rows,
        flat,
        rows,
        rows,
        flat,
        rows,
        P("fsdp", "seq"),
        P("fsdp", "seq"),
        rows,
        expert,
        expert,
        expert,
    )
    return jax.shard_map(
        body,
        mesh=mesh,
        in_specs=(tokens, tokens, P("fsdp", None), tokens) + weights,
        out_specs=(tokens, tokens) + weights,
        check_vma=False,
    )
```

time: 2750 us -> 1840 us (0.67)
  waiting for transfers between devices: 1810 us -> 1240 us
  blocking collectives: 270 us -> 65.3 us
  starting transfers between devices: 113 us -> 13.2 us
    reduce_scatter x13 -> x6, waiting for transfers between devices: 1120 us -> 240 us  [spread_grad(): lax.psum_scatter(grad.astype(LOW), 'fsdp', scatter_dimension=0, tiled=True)]
    unnamed x25 -> x28, waiting for transfers between devices: 0.89 us -> 496 us
    all_to_all x11 -> x2, waiting for transfers between devices: 336 us -> 5.98 us  [the longest x1 5.98 us: body(): lax.all_to_all(score_grad, 'seq', split_axis=0, concat_axis=0, tiled=True)]
    all_gather x10, waiting for transfers between devices: 357 us -> 499 us  [the longest x4 250 us: gather_rows(): return lax.all_gather(block, 'seq', axis=0, tiled=True)]
    all_gather x4 -> x3, blocking collectives: 166 us -> 43.6 us  [the longest x1 20.2 us: gather_rows(): return lax.all_gather(block, 'seq', axis=0, tiled=True)]
    all_to_all x11 -> x2, starting transfers between devices: 110 us -> 11.6 us  [the longest x1 5.83 us: body(): lax.all_to_all(head_grads, 'seq', split_axis=0, concat_axis=0, tiled=True)]
    unnamed x2 -> x0, blocking collectives: 79.9 us -> none
    unnamed x159 -> x193, local copies, waits for them, and re-layouts: 13 us -> 45.2 us
  transfers between devices with their start and end apart: 35 -> 24, of which waited for: 20 -> 21; matrix products, arithmetic and copies ran while one was open for 18% -> 16% of each run, Pallas kernels for 0% -> 0%
where the time goes in v1:
time: 1840 us
  waiting for transfers between devices  1240 us (67%)
  matrix products  289 us (16%)
  other arithmetic  104 us (6%)
  local copies, waits for them, and re-layouts  102 us (6%)
  blocking collectives  65.3 us (4%)
    unnamed x28, waiting for transfers between devices  496 us
    all_gather x4, waiting for transfers between devices, gather_rows(): return lax.all_gather(block, 'seq', axis=0, tiled=True)  250 us
    reduce_scatter x6, waiting for transfers between devices, spread_grad(): lax.psum_scatter(grad.astype(LOW), 'fsdp', scatter_dimension=0, tiled=True)  240 us
    dot_general x18, matrix products, dot(): return jnp.dot(left, right, preferred_element_type=F32)  89 us
    dot_general x21, matrix products, dot_t(): lax.dot_general(left, right, (((1,), (1,)), ((), ())), preferred_element_...  86.1 us
    dot_general x17, matrix products, t_dot(): lax.dot_general(left, right, (((0,), (0,)), ((), ())), preferred_element_...  77.8 us
    all_gather x1, waiting for transfers between devices, body(): lax.all_gather(w_expert_up[0].astype(LOW), 'fsdp', axis=0, tiled=True)  64.9 us
    all_gather x1, waiting for transfers between devices, body(): lax.all_gather(w_expert_down[0].astype(LOW), 'fsdp', axis=0, tiled=True)  62.9 us
  transfers between devices with their start and end apart: 24, of which 21 were waited for; matrix products, arithmetic and copies ran while one was open for 16% of the time, Pallas kernels for 0%

profile of v1, /device:TPU:0, one launch (start us, length us, event | category | flops | bytes accessed | tf_op | source)
XLA Modules:
  0.0 1835.5 jit_solution(10869645132086318198)
XLA Ops:
  10.8 21.6 %all_to_all.22 = bf16[16,64,256]{2,1,0:T(8,128)(2,1)S(1)} all-to-all(bf16[16,64,256]{2,1,0:T(8,128)(2,1)S(1)} %copy.158), channel_id=1, replica_groups=mesh['seq'=16,'fsdp'=2] {'seq'}, dimensions={0} | all-to-all | bytes 1048576 | tf_op jit(solution)/shard_map/all_to_all | solution.py:204
  35.8 12.1 all_gather.46
  47.9 8.5 all-gather.28.cloned.1.call-done
  59.8 57.9 %all-gather.18.cloned.1.call-done = bf16[2048,640]{1,0:T(8,128)(2,1)} async-done(((bf16[64,640]{1,0:T(8,128)(2,1)}), bf16[2048,640]{1,0:T(8,128)(2,1)}) %all-gather.18.cloned.1.call-update) | async-done | bytes 2621456 | tf_op jit(solution)/shard_map/all_gather | solution.py:188
  120.6 73.1 %all-gather.26.cloned.1.call-done = bf16[1,2048,2048]{2,1,0:T(8,128)(2,1)} async-done(((bf16[1,128,2048]{2,1,0:T(8,128)(2,1)}), bf16[1,2048,2048]{2,1,0:T(8,128)(2,1)}) %all-gather.26.cloned.1.call-update) | async-done | bytes 8388624 | tf_op jit(solution)/shard_map/all_gather | solution.py:82
  193.7 5.1 fusion.27
  198.8 8.6 fusion.29
  207.4 6.4 fusion.141
  215.1 5.6 fusion.60
  230.4 19.8 %while.28 = (s32[]{:T(128)}, bf16[4,512,128]{2,1,0:T(8,128)(2,1)S(1)}, f32[4,512,1]{1,2,0:T(1,128)}, s32[4]{0:T(128)S(1)}, s32[2048]{0:T(1024)S(1)}, /*index=5*/...) while((s32[]{:T(128)}, ...), condition=%wide.region_5.6_spmd.clone, body=%wide.region_2.5_spmd.clone.sunk | while | flops 682688512 | bytes 14588115 | solution.py:108
  250.2 6.9 convolution_convert_fusion.4
  258.5 101.8 %reduce-scatter.37.cloned.1.call-done = bf16[128,2048]{1,0:T(8,128)(2,1)} async-done(((bf16[2048,2048]{1,0:T(8,128)(2,1)}), bf16[128,2048]{1,0:T(8,128)(2,1)}) %reduce-scatter.37.cloned.1.call-update) | async-done | bytes 524304
  367.8 4.8 convert_element_type.326
  378.9 20.2 %all-gather.2 = s32[1,2048,6]{1,0,2:T(1,128)S(1)} all-gather(s32[1,128,6]{1,0,2:T(1,128)S(1)} %copy-done.75), channel_id=4, replica_groups=mesh['seq'=16,'fsdp'=2] {'seq'}, dimensions={1}, use_global_device_ids=true | all-gather | bytes 52224 | tf_op jit(solution)/shard_map/all_gather | solution.py:82
  399.5 11.3 all_gather.53
  410.8 26.4 %all-gather.36.cloned.1.call-done = bf16[1,2048,2048]{2,1,0:T(8,128)(2,1)} async-done(((bf16[1,128,2048]{2,1,0:T(8,128)(2,1)}), bf16[1,2048,2048]{2,1,0:T(8,128)(2,1)}) %all-gather.36.cloned.1.call-update) | async-done | bytes 8388624 | tf_op jit(solution)/shard_map/all_gather | solution.py:82
  437.2 6.6 convolution_convert_fusion.5
  443.8 72.4 %all-gather.20.cloned.1.call-done = bf16[2048,2048]{0,1:T(8,128)(2,1)} async-done(((bf16[128,2048]{0,1:T(8,128)(2,1)}), bf16[2048,2048]{0,1:T(8,128)(2,1)}) %all-gather.20.cloned.1.call-update) | async-done | bytes 8388624 | tf_op jit(solution)/shard_map/all_gather | solution.py:82
  516.2 12.6 copy.185
  528.8 7.2 convolution_convert_fusion.6
  536.0 55.0 %all-gather.30.cloned.1.call-done = bf16[1,2048,1408]{2,1,0:T(8,128)(2,1)} async-done(((bf16[1,1024,1408]{2,1,0:T(8,128)(2,1)}), bf16[1,2048,1408]{2,1,0:T(8,128)(2,1)}) %all-gather.30.cloned.1.call-update) | async-done | bytes 5767184 | tf_op jit(solution)/shard_map/all_gather | solution.py:210
  591.0 11.7 fusion.49
  602.7 64.9 %all-gather.32.cloned.1.call-done = bf16[1,2048,1408]{2,1,0:T(8,128)(2,1)} async-done(((bf16[1,1024,1408]{2,1,0:T(8,128)(2,1)}), bf16[1,2048,1408]{2,1,0:T(8,128)(2,1)}) %all-gather.32.cloned.1.call-update) | async-done | bytes 5767184 | tf_op jit(solution)/shard_map/all_gather | solution.py:211
  667.6 13.1 multiply_convert_fusion.3
  680.7 62.9 %all-gather.34.cloned.1.call-done = bf16[1,1408,2048]{2,1,0:T(8,128)(2,1)} async-done(((bf16[1,704,2048]{2,1,0:T(8,128)(2,1)}), bf16[1,1408,2048]{2,1,0:T(8,128)(2,1)}) %all-gather.34.cloned.1.call-update) | async-done | bytes 5767184 | tf_op jit(solution)/shard_map/all_gather | solution.py:212
  743.7 11.6 fusion.34
  761.2 6.6 fusion.33
  767.7 16.1 multiply_convert_fusion.2
  783.8 9.6 fusion.43
  793.4 8.4 add_convert_fusion
  801.9 8.2 fusion.78
  810.0 6.4 fusion.142
  816.4 7.7 multiply_convert_fusion.6
  825.3 10.2 fusion.30
  835.5 5.8 all-to-all-start.1
  841.6 6.0 all-to-all-done.1
  847.6 92.7 %reduce-scatter.41.cloned.1.call-done = bf16[128,2048]{1,0:T(8,128)(2,1)} async-done(((bf16[2048,2048]{1,0:T(8,128)(2,1)}), bf16[128,2048]{1,0:T(8,128)(2,1)}) %reduce-scatter.41.cloned.1.call-update) | async-done | bytes 524304
  946.9 77.8 %all-gather.24.cloned.1.call-done = bf16[2048,2048]{0,1:T(8,128)(2,1)} async-done(((bf16[128,2048]{0,1:T(8,128)(2,1)}), bf16[2048,2048]{0,1:T(8,128)(2,1)}) %all-gather.24.cloned.1.call-update) | async-done | bytes 8388624 | tf_op jit(solution)/shard_map/all_gather | solution.py:82
  1024.7 6.6 convolution_convert_fusion.12
  1031.4 46.2 %while.29 = (s32[]{:T(128)}, f32[2048,192]{0,1:T(8,128)S(1)}, f32[2048,128]{1,0:T(8,128)}, bf16[4,512,192]{1,2,0:T(8,128)(2,1)}, s32[4]{0:T(128)S(1)}, /*index=5...) while((s32[]{:T(128)}, f32[2048,192]{0,1:T(8,128)S(1)}, ...), condition=%wide.region_23.24_spmd.clone, body=%wide.region_21.23_spmd.clone.sunk | while | flops 1759313920 | bytes 51605844 | solution.py:141
  1087.0 18.9 %maximum_maximum_fusion = bf16[2048,2688]{0,1:T(8,128)(2,1)} fusion(bf16[2048,64]{0,1:T(8,128)(2,1)S(1)} %copy-done.38, bf16[2048,512]{0,1:T(8,128)(2,1)S(1)} %convolution_convert_fusion.7, bf16[2048,2048]{0,1:T(8,128)(2,1)S(1)} %convolution_convert_fusion, bf16[2688]{0:T(1024)(128)(2,1)S(1)} %pad.35.clone), kind=kLoop, calls=%fused_computation.50 | loop fusion | flops 44040192 | bytes 21763328 | tf_op jit(solution)/shard_map/concatenate | solution.py:343
  1105.9 14.0 copy.192
  1121.0 6.4 fusion.56
  1127.5 8.8 convolution_convert_fusion.8
  1136.4 11.7 convolution_convert_fusion.3
  1152.3 5.2 convolution_convert_fusion.10
  1159.5 10.5 convolution_convert_fusion.1
  1170.1 11.1 convolution_convert_fusion.2
  1181.8 10.5 fusion.81
  1192.3 11.7 fusion.31
  1206.5 7.3 convolution_convert_fusion.11
  1213.9 27.1 %reduce-scatter.43.cloned.1.call-done = bf16[128,2688]{1,0:T(8,128)(2,1)} async-done(((bf16[2048,2688]{1,0:T(8,128)(2,1)}), bf16[128,2688]{1,0:T(8,128)(2,1)}) %reduce-scatter.43.cloned.1.call-update) | async-done | bytes 688144
  1254.1 5.8 copy.206
  1259.9 5.2 pad.20.clone
  1268.2 18.8 %reduce-scatter.27.cloned.1.call-done = bf16[1024,352]{0,1:T(8,128)(2,1)} async-done(((bf16[2048,352]{0,1:T(8,128)(2,1)}), bf16[1024,352]{0,1:T(8,128)(2,1)}) %reduce-scatter.27.cloned.1.call-update) | async-done | bytes 720912 | tf_op jit(solution)/shard_map/reduce_scatter | solution.py:313
  1289.4 71.9 %reduce-scatter.31.cloned.1.call-done = bf16[1024,1408]{1,0:T(8,128)(2,1)} async-done(((bf16[2048,1408]{1,0:T(8,128)(2,1)}), bf16[1024,1408]{1,0:T(8,128)(2,1)}) %reduce-scatter.31.cloned.1.call-update) | async-done | bytes 2883600 | tf_op jit(solution)/shard_map/reduce_scatter | solution.py:313
  1366.0 37.5 %all-reduce.7.cloned.1.call-done = bf16[16,2,64,256]{3,2,1,0:T(8,128)(2,1)} async-done(((bf16[16,2,64,256]{3,2,1,0:T(8,128)(2,1)}), bf16[16,2,64,256]{3,2,1,0:T(8,128)(2,1)}) %all-reduce.7.cloned.1.call-update) | async-done | bytes 1048592
  1406.0 5.8 all-to-all-start.2
  1411.8 65.3 %reduce-scatter.35.cloned.1.call-done = bf16[704,2048]{1,0:T(8,128)(2,1)} async-done(((bf16[1408,2048]{1,0:T(8,128)(2,1)}), bf16[704,2048]{1,0:T(8,128)(2,1)}) %reduce-scatter.35.cloned.1.call-update) | async-done | bytes 2883600 | tf_op jit(solution)/shard_map/reduce_scatter | solution.py:313
  1477.1 5.1 bitcast_convert_fusion
  1482.3 69.2 %reduce-scatter.33.cloned.1.call-done = bf16[1024,1408]{1,0:T(8,128)(2,1)} async-done(((bf16[2048,1408]{1,0:T(8,128)(2,1)}), bf16[1024,1408]{1,0:T(8,128)(2,1)}) %reduce-scatter.33.cloned.1.call-update) | async-done | bytes 2883600 | tf_op jit(solution)/shard_map/reduce_scatter | solution.py:313
  1556.1 104.4 %reduce-scatter.39.cloned.1.call-done = bf16[128,2048]{1,0:T(8,128)(2,1)} async-done(((bf16[2048,2048]{1,0:T(8,128)(2,1)}), bf16[128,2048]{1,0:T(8,128)(2,1)}) %reduce-scatter.39.cloned.1.call-update) | async-done | bytes 524304
  1662.7 14.6 reduce-scatter.25.cloned.1.call-done
  1692.9 130.6 %reduce-scatter.45.cloned.1.call-done = f32[64,640]{1,0:T(8,128)} async-done(((f32[2048,640]{1,0:T(8,128)}), f32[64,640]{1,0:T(8,128)}) %reduce-scatter.45.cloned.1.call-update) | async-done | bytes 163856
  (452 shorter events, 185.9 us)
Async XLA Ops:
  7.2 49.2 %all-gather.28.cloned.1.call-start = ((), (), s32[]{:S(2)}) async-start(), calls=%async_computation.25 | async-start | bytes 1572864 | tf_op jit(solution)/shard_map/all_gather | solution.py:205
  8.2 25.4 %copy-start.82 = (f32[16]{0:T(128)S(1)}, f32[16]{0:T(128)}, u32[]{:S(2)}) copy-start(f32[16]{0:T(128)} %param.29) | copy-start | bytes 196
  8.2 25.5 %copy-start.71 = (f32[64,16]{0,1:T(8,128)S(1)}, f32[64,16]{0,1:T(8,128)}, u32[]{:S(2)}) copy-start(f32[64,16]{0,1:T(8,128)} %param.33) | copy-start | bytes 12292
  8.2 25.6 %copy-start.83 = (f32[64]{0:T(128)S(1)}, f32[64]{0:T(128)}, u32[]{:S(2)}) copy-start(f32[64]{0:T(128)} %param.32) | copy-start | bytes 772
  8.2 25.7 %copy-start.84 = (f32[64]{0:T(128)S(1)}, f32[64]{0:T(128)}, u32[]{:S(2)}) copy-start(f32[64]{0:T(128)} %param.26) | copy-start | bytes 772
  8.2 25.8 %copy-start.54 = (f32[64,576]{1,0:T(8,128)S(1)}, f32[64,576]{1,0:T(8,128)}, u32[]{:S(2)}) copy-start(f32[64,576]{1,0:T(8,128)} %param.28) | copy-start | bytes 442372
  8.6 27.1 %copy-start.49 = (f32[64,2048]{1,0:T(8,128)S(1)}, f32[64,2048]{1,0:T(8,128)}, u32[]{:S(2)}) copy-start(f32[64,2048]{1,0:T(8,128)} %param.31) | copy-start | bytes 1572868
  33.5 84.1 %all-gather.18.cloned.1.call-start = ((), (), s32[]{:S(2)}) async-start(), calls=%async_computation.14 | async-start | bytes 2703360 | tf_op jit(solution)/shard_map/all_gather | solution.py:188
  34.9 158.8 %all-gather.26.cloned.1.call-start = ((), (), s32[]{:S(2)}) async-start(), calls=%async_computation.24 | async-start | bytes 8912896 | tf_op jit(solution)/shard_map/all_gather | solution.py:82
  35.6 324.7 %reduce-scatter.37.cloned.1.call-start = ((), (), s32[]{:S(2)}) async-start(), calls=%async_computation.30 | async-start | bytes 8912896
  35.8 188.3 %copy-start.76 = (f32[32]{0:T(128)}, f32[32]{0:T(128)S(1)}, u32[]{:S(2)}) copy-start(f32[32]{0:T(128)S(1)} %multiply_exponential_fusion) | copy-start | bytes 388
  35.8 188.3 %copy-start.60 = (f32[2048]{0:T(1024)}, f32[2048]{0:T(1024)S(1)}, u32[]{:S(2)}) copy-start(f32[2048]{0:T(1024)S(1)} %iota_convert_fusion) | copy-start | bytes 24580
  58.1 163.0 %copy-start.27 = (bf16[512,256]{1,0:T(8,128)(2,1)}, bf16[512,256]{1,0:T(8,128)(2,1)S(1)}, u32[]{:S(2)}) copy-start(bf16[512,256]{1,0:T(8,128)(2,1)S(1)} %reshape.237) | copy-start | bytes 786436
  59.8 147.6 %copy-start.15 = (bf16[16,2,64,192]{3,2,1,0:T(8,128)(2,1)}, bf16[16,2,64,192]{3,2,1,0:T(8,128)(2,1)S(1)}, u32[]{:S(2)}) copy-start(bf16[16,2,64,192]{3,2,1,0:T(8,128)(2,1)S(1)} %copy.198) | copy-start | bytes 2359300
  120.4 78.4 %copy-start.58 = (f32[2048]{0:T(1024)}, f32[2048]{0:T(1024)S(1)}, u32[]{:S(2)}) copy-start(f32[2048]{0:T(1024)S(1)} %get-tuple-element.397) | copy-start | bytes 24580
  120.4 241.6 %copy-start.55 = (f32[2048]{0:T(1024)}, f32[2048]{0:T(1024)S(1)}, u32[]{:S(2)}) copy-start(f32[2048]{0:T(1024)S(1)} %get-tuple-element.395) | copy-start | bytes 24580
  120.6 100.5 %copy-start.66 = (f32[512]{0:T(512)}, f32[512]{0:T(512)S(1)}, u32[]{:S(2)}) copy-start(f32[512]{0:T(512)S(1)} %mul.480) | copy-start | bytes 6148
  257.3 180.0 %all-gather.36.cloned.1.call-start = ((), (), s32[]{:S(2)}) async-start(), calls=%async_computation.29 | async-start | bytes 8912896 | tf_op jit(solution)/shard_map/all_gather | solution.py:82
  257.8 258.3 %all-gather.20.cloned.1.call-start = ((), (), s32[]{:S(2)}) async-start(), calls=%async_computation.15 | async-start | bytes 8912896 | tf_op jit(solution)/shard_map/all_gather | solution.py:82
  258.5 109.2 %copy-start.8 = (bf16[1,128,2048]{1,2,0:T(8,128)(2,1)}, bf16[1,128,2048]{1,2,0:T(8,128)(2,1)S(1)}, u32[]{:S(2)}) copy-start(bf16[1,128,2048]{1,2,0:T(8,128)(2,1)S(1)} %copy.151) | copy-start | bytes 1572868
  363.1 227.8 %all-gather.30.cloned.1.call-start = ((), (), s32[]{:S(2)}) async-start(), calls=%async_computation.26 | async-start | bytes 8650752 | tf_op jit(solution)/shard_map/all_gather | solution.py:210
  367.7 299.9 %all-gather.32.cloned.1.call-start = ((), (), s32[]{:S(2)}) async-start(), calls=%async_computation.27 | async-start | bytes 8650752 | tf_op jit(solution)/shard_map/all_gather | solution.py:211
  372.7 371.0 %all-gather.34.cloned.1.call-start = ((), (), s32[]{:S(2)}) async-start(), calls=%async_computation.28 | async-start | bytes 8650752 | tf_op jit(solution)/shard_map/all_gather | solution.py:212
  377.5 21.9 %copy-start.43 = (f32[88,2048]{1,0:T(8,128)S(1)}, f32[88,2048]{1,0:T(8,128)}, u32[]{:S(2)}) copy-start(f32[88,2048]{1,0:T(8,128)} %param.36) | copy-start | bytes 2162692
  377.5 432.5 %all-gather.22.cloned.1.call-start = ((), (), s32[]{:S(2)}) async-start(), calls=%async_computation.16 | async-start | bytes 2162688 | tf_op jit(solution)/shard_map/all_gather | solution.py:214
  378.8 561.5 %reduce-scatter.41.cloned.1.call-start = ((), (), s32[]{:S(2)}) async-start(), calls=%async_computation.32 | async-start | bytes 8912896
  399.1 402.7 %copy-start.50 = (pred[2048]{0:T(1024)(128)(4,1)}, pred[2048]{0:T(1024)(128)(4,1)S(1)}, u32[]{:S(2)}) copy-start(pred[2048]{0:T(1024)(128)(4,1)S(1)} %compare_reduce_fusion) | copy-start | bytes 6148
  399.4 402.4 %copy-start.35 = (s32[16,128]{1,0:T(8,128)}, s32[16,128]{1,0:T(8,128)S(1)}, u32[]{:S(2)}) copy-start(s32[16,128]{1,0:T(8,128)S(1)} %broadcast_add_fusion) | copy-start | bytes 24580
  410.8 405.6 %copy-start.29 = (bf16[176,2048]{1,0:T(8,128)(2,1)}, bf16[176,2048]{1,0:T(8,128)(2,1)S(1)}, u32[]{:S(2)}) copy-start(bf16[176,2048]{1,0:T(8,128)(2,1)S(1)} %all_gather.53) | copy-start | bytes 2162692
  760.2 181.4 %copy-start.53 = (f32[2048,16]{0,1:T(8,128)}, f32[2048,16]{0,1:T(8,128)S(1)}, u32[]{:S(2)}) copy-start(f32[2048,16]{0,1:T(8,128)S(1)} %get-tuple-element.444) | copy-start | bytes 393220
  761.2 32.2 %slice-start = ((s8[5767168]{0:T(1024)(128)(4,1)}), s8[4194304]{0:T(1024)(128)(4,1)S(1)}, s32[]{:S(2)}) async-start(s8[5767168]{0:T(1024)(128)(4,1)} %bitcast.293), calls=%async_computation.36 | async-start | bytes 8388608
  767.7 16.1 copy-start.22
  767.7 25.7 %slice-start.1 = ((s8[5767168]{0:T(1024)(128)(4,1)}), s8[1572864]{0:T(1024)(128)(4,1)S(1)}, s32[]{:S(2)}) async-start(s8[5767168]{0:T(1024)(128)(4,1)} %bitcast.293), calls=%async_computation.37 | async-start | bytes 3145728
  835.5 106.2 %copy-start.9 = (bf16[1,128,2048]{1,2,0:T(8,128)(2,1)S(1)}, bf16[1,128,2048]{1,2,0:T(8,128)(2,1)}, u32[]{:S(2)}) copy-start(bf16[1,128,2048]{1,2,0:T(8,128)(2,1)} %copy-done.8) | copy-start | bytes 1572868
  835.5 106.2 %copy-start.12 = (bf16[128,2048]{0,1:T(8,128)(2,1)S(1)}, bf16[128,2048]{0,1:T(8,128)(2,1)}, u32[]{:S(2)}) copy-start(bf16[128,2048]{0,1:T(8,128)(2,1)} %copy-done.11) | copy-start | bytes 1572868
  835.5 106.2 %copy-start.56 = (f32[2048]{0:T(1024)S(1)}, f32[2048]{0:T(1024)}, u32[]{:S(2)}) copy-start(f32[2048]{0:T(1024)} %copy-done.55) | copy-start | bytes 24580
  835.5 106.2 %copy-start.73 = (f32[128]{0:T(128)S(1)}, f32[128]{0:T(128)}, u32[]{:S(2)}) copy-start(f32[128]{0:T(128)} %copy-done.72) | copy-start | bytes 1540
  835.5 12.1 all-to-all-start.1
  841.3 183.4 %all-gather.24.cloned.1.call-start = ((), (), s32[]{:S(2)}) async-start(), calls=%async_computation.17 | async-start | bytes 8912896 | tf_op jit(solution)/shard_map/all_gather | solution.py:82
  841.6 105.1 %copy-start.20 = (bf16[1,128,2048]{1,2,0:T(8,128)(2,1)}, bf16[1,128,2048]{1,2,0:T(8,128)(2,1)S(1)}, u32[]{:S(2)}) copy-start(bf16[1,128,2048]{1,2,0:T(8,128)(2,1)S(1)} %copy.168) | copy-start | bytes 1572868
  847.6 99.1 %copy-start.62 = (f32[16,1,128]{2,1,0:T(1,128)}, f32[16,1,128]{2,1,0:T(1,128)S(1)}, u32[]{:S(2)}) copy-start(f32[16,1,128]{2,1,0:T(1,128)S(1)} %all-to-all-done.1) | copy-start | bytes 24580
  847.6 99.1 %copy-start.80 = (f32[128]{0:T(128)}, f32[128]{0:T(128)S(1)}, u32[]{:S(2)}) copy-start(f32[128]{0:T(128)S(1)} %multiply_reduce_fusion.9) | copy-start | bytes 1540
  946.7 294.2 %reduce-scatter.43.cloned.1.call-start = ((), (), s32[]{:S(2)}) async-start(), calls=%async_computation.33 | async-start | bytes 11698176
  946.9 84.5 %copy-start.1 = (bf16[2048,192]{1,0:T(8,128)(2,1)S(1)}, bf16[2048,192]{1,0:T(8,128)(2,1)}, u32[]{:S(2)}) copy-start(bf16[2048,192]{1,0:T(8,128)(2,1)} %copy-done) | copy-start | bytes 2359300
  946.9 84.5 %copy-start.7 = (bf16[2048,128]{1,0:T(8,128)(2,1)S(1)}, bf16[2048,128]{1,0:T(8,128)(2,1)}, u32[]{:S(2)}) copy-start(bf16[2048,128]{1,0:T(8,128)(2,1)} %copy-done.6) | copy-start | bytes 1572868
  946.9 84.5 %copy-start.65 = (s32[1,2048]{1,0:T(1,128)S(1)}, s32[1,2048]{1,0:T(1,128)}, u32[]{:S(2)}) copy-start(s32[1,2048]{1,0:T(1,128)} %param.24) | copy-start | bytes 24580
  1119.9 146.4 %reduce-scatter.29.cloned.1.call-start = ((), (), s32[]{:S(2)}) async-start(), calls=%async_computation.20 | async-start | bytes 1081344 | tf_op jit(solution)/shard_map/reduce_scatter | solution.py:313
  1127.5 159.6 %reduce-scatter.27.cloned.1.call-start = ((), (), s32[]{:S(2)}) async-start(), calls=%async_computation.19 | async-start | bytes 2162688 | tf_op jit(solution)/shard_map/reduce_scatter | solution.py:313
  1136.4 224.9 %reduce-scatter.31.cloned.1.call-start = ((), (), s32[]{:S(2)}) async-start(), calls=%async_computation.21 | async-start | bytes 8650752 | tf_op jit(solution)/shard_map/reduce_scatter | solution.py:313
  1148.1 255.4 %all-reduce.7.cloned.1.call-start = ((), (), s32[]{:S(2)}) async-start(), calls=%async_computation.35 | async-start | bytes 2097152
  1159.4 317.7 %reduce-scatter.35.cloned.1.call-start = ((), (), s32[]{:S(2)}) async-start(), calls=%async_computation.23 | async-start | bytes 8650752 | tf_op jit(solution)/shard_map/reduce_scatter | solution.py:313
  1170.0 381.4 %reduce-scatter.33.cloned.1.call-start = ((), (), s32[]{:S(2)}) async-start(), calls=%async_computation.22 | async-start | bytes 8650752 | tf_op jit(solution)/shard_map/reduce_scatter | solution.py:313
  1181.1 479.4 %reduce-scatter.39.cloned.1.call-start = ((), (), s32[]{:S(2)}) async-start(), calls=%async_computation.31 | async-start | bytes 8912896
  1204.1 473.2 %reduce-scatter.25.cloned.1.call-start = ((), (), s32[]{:S(2)}) async-start(), calls=%async_computation.18 | async-start | bytes 786432 | tf_op jit(solution)/shard_map/reduce_scatter | solution.py:313
  1213.8 31.9 %copy-start.10 = (bf16[1,128,2048]{1,2,0:T(8,128)(2,1)S(1)}, bf16[1,128,2048]{1,2,0:T(8,128)(2,1)}, u32[]{:S(2)}) copy-start(bf16[1,128,2048]{1,2,0:T(8,128)(2,1)} %copy-done.8) | copy-start | bytes 1572868
  1213.8 31.9 %copy-start.59 = (f32[2048]{0:T(1024)S(1)}, f32[2048]{0:T(1024)}, u32[]{:S(2)}) copy-start(f32[2048]{0:T(1024)} %copy-done.58) | copy-start | bytes 24580
  1213.9 609.7 %reduce-scatter.45.cloned.1.call-start = ((), (), s32[]{:S(2)}) async-start(), calls=%async_computation.34 | async-start | bytes 5406720
  1406.0 273.1 %all-to-all-start.2 = ((bf16[16,64,256]{2,1,0:T(8,128)(2,1)}), bf16[16,64,256]{2,1,0:T(8,128)(2,1)S(1)}, u32[]{:S(2)}, u32[]{:S(2)}) async-start(bf16[16,64,256]{2,1,0:T(8,128)(2,1)} %dynamic-slice_bitcast_fusion), calls=%async_computation.2 | async-start | bytes 1048576 | tf_op jit(solution)/shard_map/all_to_all | solution.py:360
  1662.6 23.5 %copy-start.13 = (bf16[128,2048]{0,1:T(8,128)(2,1)S(1)}, bf16[128,2048]{0,1:T(8,128)(2,1)}, u32[]{:S(2)}) copy-start(bf16[128,2048]{0,1:T(8,128)(2,1)} %copy-done.11) | copy-start | bytes 1572868
  1662.6 23.5 %copy-start.21 = (bf16[1,128,2048]{1,2,0:T(8,128)(2,1)S(1)}, bf16[1,128,2048]{1,2,0:T(8,128)(2,1)}, u32[]{:S(2)}) copy-start(bf16[1,128,2048]{1,2,0:T(8,128)(2,1)} %copy-done.20) | copy-start | bytes 1572868
  1662.6 23.5 %copy-start.24 = (f32[128,2048]{0,1:T(8,128)S(1)}, f32[128,2048]{0,1:T(8,128)}, u32[]{:S(2)}) copy-start(f32[128,2048]{0,1:T(8,128)} %copy-done.23) | copy-start | bytes 3145732
  1662.6 23.5 %copy-start.57 = (f32[2048]{0:T(1024)S(1)}, f32[2048]{0:T(1024)}, u32[]{:S(2)}) copy-start(f32[2048]{0:T(1024)} %copy-done.55) | copy-start | bytes 24580
  1662.6 23.5 %copy-start.74 = (f32[128]{0:T(128)S(1)}, f32[128]{0:T(128)}, u32[]{:S(2)}) copy-start(f32[128]{0:T(128)} %copy-done.72) | copy-start | bytes 1540
  1662.7 23.5 %copy-start.79 = (f32[128]{0:T(128)S(1)}, f32[128]{0:T(128)}, u32[]{:S(2)}) copy-start(f32[128]{0:T(128)} %copy-done.78) | copy-start | bytes 1540
  (58 other events, 201.8 us)
Sparse Core Ops, SparseCore 0:
  33.7 22.6 all-gather.27
  59.9 57.7 all-gather.17
  119.8 73.7 all-gather.25
  257.4 102.9 reduce-scatter.36
  362.4 74.8 all-gather.35
  439.8 76.3 all-gather.19
  518.3 72.6 all-gather.29
  593.1 74.4 all-gather.31
  669.2 74.4 all-gather.33
  745.6 25.7 all-gather.21
  835.6 104.6 reduce-scatter.40
  946.8 77.8 all-gather.23
  1120.0 120.8 reduce-scatter.42
  1243.8 16.4 reduce-scatter.28
  1262.3 24.6 reduce-scatter.26
  1289.8 71.3 reduce-scatter.30
  1363.4 40.0 all-reduce.6
  1405.7 71.3 reduce-scatter.34
  1480.0 71.3 reduce-scatter.32
  1555.9 104.6 reduce-scatter.38
  1662.9 14.3 reduce-scatter.24
  1680.1 143.3 reduce-scatter.44

commit v2 on v1

--- a/solution.py
+++ b/solution.py
@@ -1,8 +1,11 @@
+import functools
 import math
 
 import jax
 import jax.numpy as jnp
 from jax import lax
+from jax.experimental import pallas as pl
+from jax.experimental.pallas import tpu as pltpu
 from jax.sharding import PartitionSpec as P
 
 H = 16
@@ -15,6 +18,7 @@
 HIGHEST = lax.Precision.HIGHEST
 LOW = jnp.bfloat16
 F32 = jnp.float32
+MESH = pl.DeviceIdType.MESH
 
 
 def rotary_tables(count, offset):
@@ -78,6 +82,14 @@
     return sigmoid * (1.0 + value * (1.0 - sigmoid))
 
 
+def whole_over_layers(own):
+    if lax.axis_size("fsdp") != 2:
+        return lax.all_gather(own, "fsdp", axis=0, tiled=True)
+    other = lax.ppermute(own, "fsdp", ((0, 1), (1, 0)))
+    first = lax.axis_index("fsdp") == 0
+    return jnp.concatenate([jnp.where(first, own, other), jnp.where(first, other, own)], axis=0)
+
+
 def gather_rows(block):
     return lax.all_gather(block, "seq", axis=0, tiled=True)
 
@@ -86,62 +98,379 @@
     return lax.psum_scatter(partial, "seq", scatter_dimension=0, tiled=True)
 
 
+def ring_places(groups):
+    ring = groups // 2
+    me = lax.axis_index("seq")
+    chip, core = me // 2, lax.rem(me, 2)
+    odd = lax.rem(chip, 2)
+    spot = (1 - odd) * (chip // 2) + odd * (ring - 1 - chip // 2)
+
+    def chip_at(place):
+        place = lax.rem(place + 2 * ring, ring)
+        late = place // (ring // 2)
+        return (1 - late) * (2 * place) + late * (2 * ring - 1 - 2 * place)
+
+    def index_at(place, which):
+        return 2 * chip_at(place) + which
+
+    return spot, core, index_at
+
+
+def enter(neighbours):
+    barrier = pltpu.get_barrier_semaphore()
+    for index in neighbours:
+        pl.semaphore_signal(barrier, inc=1, device_id={"seq": index}, device_id_type=MESH)
+    pl.semaphore_wait(barrier, len(neighbours))
+
+
+class Gather:
+    def __init__(self, groups, chunks, rows, source, out_ref, sems):
+        self.groups, self.chunks, self.size = groups, chunks, rows // chunks
+        self.source, self.out = source, out_ref
+        self.send, self.recv, self.side_send, self.side_recv = sems
+        self.spot, self.core, self.at = ring_places(groups)
+        self.ring = groups // 2
+        self.steps = groups // 4
+        self.started = []
+
+    def block(self, way, step):
+        return self.at(self.spot - step if way == 0 else self.spot + step, self.core)
+
+    def slice(self, ref, chunk):
+        return ref.at[pl.ds(chunk * self.size, self.size)]
+
+    def forward(self, step, chunk, way):
+        index = self.block(way, step)
+        own = self.slice(self.source if step == 0 else self.out.at[index], chunk)
+        copy = pltpu.make_async_remote_copy(
+            src_ref=own,
+            dst_ref=self.slice(self.out.at[index], chunk),
+            send_sem=self.send.at[way, step, chunk],
+            recv_sem=self.recv.at[way, step, chunk],
+            device_id={"seq": self.at(self.spot + (1 if way == 0 else -1), self.core)},
+            device_id_type=MESH,
+        )
+        copy.start()
+        self.started.append(copy)
+
+    def arrived(self, step, chunk, way):
+        index = self.block(way, step + 1)
+        here = self.slice(self.out.at[index], chunk)
+        pltpu.make_async_remote_copy(
+            src_ref=here,
+            dst_ref=here,
+            send_sem=self.send.at[way, step, chunk],
+            recv_sem=self.recv.at[way, step, chunk],
+            device_id={"seq": self.at(self.spot, 1 - self.core)},
+            device_id_type=MESH,
+        ).wait_recv()
+
+    def aside(self, distance, chunk):
+        index = self.at(self.spot - distance, self.core)
+        own = self.slice(self.source if distance == 0 else self.out.at[index], chunk)
+        copy = pltpu.make_async_remote_copy(
+            src_ref=own,
+            dst_ref=self.slice(self.out.at[index], chunk),
+            send_sem=self.side_send.at[distance, chunk],
+            recv_sem=self.side_recv.at[distance, chunk],
+            device_id={"seq": self.at(self.spot, 1 - self.core)},
+            device_id_type=MESH,
+        )
+        copy.start()
+        self.started.append(copy)
+
+    def begin(self, chunk):
+        for way in range(2):
+            if self.steps > 1 or (chunk < self.chunks // 2) == (way == 0):
+                self.forward(0, chunk, way)
+        self.aside(0, chunk)
+
+    def run(self):
+        last = self.steps - 1
+        for step in range(self.steps):
+            for chunk in range(self.chunks):
+                for way in range(2):
+                    half = (chunk < self.chunks // 2) == (way == 0)
+                    if step == last and not half:
+                        continue
+                    self.arrived(step, chunk, way)
+                    if step < last and (step + 1 < last or half):
+                        self.forward(step + 1, chunk, way)
+                    self.aside(step + 1 if way == 0 else self.ring - 1 - step, chunk)
+
+    def finish(self):
+        for distance in range(self.ring):
+            for chunk in range(self.chunks):
+                here = self.slice(self.out.at[self.at(self.spot - distance, 1 - self.core)], chunk)
+                pltpu.make_async_remote_copy(
+                    src_ref=here,
+                    dst_ref=here,
+                    send_sem=self.side_send.at[distance, chunk],
+                    recv_sem=self.side_recv.at[distance, chunk],
+                    device_id={"seq": self.at(self.spot, 1 - self.core)},
+                    device_id_type=MESH,
+                ).wait_recv()
+        for copy in self.started:
+            copy.wait_send()
+
+
+def gather_sems(groups, chunks):
+    steps, ring = groups // 4, groups // 2
+    return [
+        pltpu.SemaphoreType.DMA((2, steps, chunks)),
+        pltpu.SemaphoreType.DMA((2, steps, chunks)),
+        pltpu.SemaphoreType.DMA((ring, chunks)),
+        pltpu.SemaphoreType.DMA((ring, chunks)),
+    ]
+
+
+def gather_kernel(groups, chunks, in_ref, out_ref, own_sem, *sems):
+    ring = Gather(groups, chunks, in_ref.shape[0], in_ref, out_ref, sems)
+    spot, core, at = ring.spot, ring.core, ring.at
+    enter((at(spot - 1, core), at(spot + 1, core), at(spot, 1 - core)))
+    for chunk in range(chunks):
+        ring.begin(chunk)
+    own = pltpu.make_async_copy(in_ref, out_ref.at[at(spot, core)], own_sem)
+    own.start()
+    ring.run()
+    ring.finish()
+    own.wait()
+
+
+def ring_gather(block, groups, collective_id, chunks=4):
+    rows, columns = block.shape
+    gathered = pl.pallas_call(
+        functools.partial(gather_kernel, groups, chunks),
+        out_shape=jax.ShapeDtypeStruct((groups, rows, columns), block.dtype),
+        in_specs=[pl.BlockSpec(memory_space=pl.ANY)],
+        out_specs=pl.BlockSpec(memory_space=pl.ANY),
+        scratch_shapes=[pltpu.SemaphoreType.DMA] + gather_sems(groups, chunks),
+        compiler_params=pltpu.CompilerParams(collective_id=collective_id, has_side_effects=True),
+        cost_estimate=pl.CostEstimate(flops=0, bytes_accessed=150 << 20, transcendentals=0),
+    )(block)
+    return gathered.reshape(groups * rows, columns)
+
+
+def reduce_kernel(groups, chunks, extras, outs, rowfn, gathers, *refs):
+    parts_ref = refs[0]
+    extra_refs = refs[1 : 1 + extras]
+    out_refs = refs[1 + extras : 1 + extras + outs]
+    rest = list(refs[1 + extras + outs :])
+    gather_ref = rest.pop(0) if gathers else None
+    own, side, came, sent = rest[:4]
+    own_sem, side_send, side_recv, send_sem, recv_sem = rest[4:9]
+    ready = rest[9] if gathers else None
+    rows = own.shape[1]
+    size = rows // chunks
+    ring, steps = groups // 2, groups // 4
+    spot, core, at = ring_places(groups)
+    sibling = {"seq": at(spot, 1 - core)}
+    enter((at(spot - 1, core), at(spot + 1, core), at(spot, 1 - core)))
+
+    order = []
+    for step in range(steps):
+        order.append(steps - step)
+        if step:
+            order.append(ring - steps + step)
+    order.append(0)
+    started = []
+    loads = {}
+    for far in order:
+        copy = pltpu.make_async_remote_copy(
+            src_ref=parts_ref.at[at(spot + far, 1 - core)],
+            dst_ref=side.at[far],
+            send_sem=side_send.at[far],
+            recv_sem=side_recv.at[far],
+            device_id=sibling,
+            device_id_type=MESH,
+        )
+        copy.start()
+        started.append(copy)
+        load = pltpu.make_async_copy(
+            parts_ref.at[at(spot + far, core)], own.at[far], own_sem.at[far]
+        )
+        load.start()
+        loads[far] = (load, copy)
+
+    here = set()
+
+    def both(far, chunk):
+        if far not in here:
+            here.add(far)
+            loads[far][0].wait()
+            loads[far][1].wait_recv()
+        part = pl.ds(chunk * size, size)
+        return own[far, part].astype(F32) + side[far, part].astype(F32)
+
+    def neighbour_copy(way, step, chunk):
+        part = pl.ds(chunk * size, size)
+        return pltpu.make_async_remote_copy(
+            src_ref=sent.at[way, step, part],
+            dst_ref=came.at[way, step, part],
+            send_sem=send_sem.at[way, step, chunk],
+            recv_sem=recv_sem.at[way, step, chunk],
+            device_id={"seq": at(spot + (1 if way == 0 else -1), core)},
+            device_id_type=MESH,
+        )
+
+    def half(way, chunk):
+        return (chunk < chunks // 2) == (way == 0)
+
+    for step in range(steps):
+        for chunk in range(chunks):
+            for way in range(2):
+                if step == 0 and not half(way, chunk):
+                    continue
+                far = steps - step if way == 0 else ring - (steps - step)
+                part = pl.ds(chunk * size, size)
+                total = both(far, chunk)
+                if step > 1 or (step == 1 and half(way, chunk)):
+                    neighbour_copy(way, step - 1, chunk).wait_recv()
+                    total = total + came[way, step - 1, part].astype(F32)
+                sent[way, step, part] = total.astype(sent.dtype)
+                copy = neighbour_copy(way, step, chunk)
+                copy.start()
+                started.append(copy)
+    gather = Gather(groups, chunks, rows, ready, gather_ref, rest[10:14]) if gathers else None
+    for chunk in range(chunks):
+        part = pl.ds(chunk * size, size)
+        total = both(0, chunk)
+        for way in range(2):
+            if steps > 1 or half(way, chunk):
+                neighbour_copy(way, steps - 1, chunk).wait_recv()
+                total = total + came[way, steps - 1, part].astype(F32)
+        made = rowfn(total, part, extra_refs, out_refs)
+        if gathers:
+            ready[part] = made
+            gather.begin(chunk)
+    if gathers:
+        local = pltpu.make_async_copy(ready, gather_ref.at[at(spot, core)], rest[14])
+        local.start()
+        gather.run()
+        gather.finish()
+        local.wait()
+    for copy in started:
+        copy.wait_send()
+
+
+def ring_reduce(parts, extras, outs, rowfn, groups, collective_id, gathers=None, chunks=4):
+    _, rows, columns = parts.shape
+    ring, steps = groups // 2, groups // 4
+    scratch = [
+        pltpu.VMEM((ring, rows, columns), LOW),
+        pltpu.VMEM((ring, rows, columns), LOW),
+        pltpu.VMEM((2, steps, rows, columns), LOW),
+        pltpu.VMEM((2, steps, rows, columns), LOW),
+        pltpu.SemaphoreType.DMA((ring,)),
+        pltpu.SemaphoreType.DMA((ring,)),
+        pltpu.SemaphoreType.DMA((ring,)),
+        pltpu.SemaphoreType.DMA((2, steps, chunks)),
+        pltpu.SemaphoreType.DMA((2, steps, chunks)),
+    ]
+    shapes = list(outs)
+    specs = [pl.BlockSpec(memory_space=pltpu.VMEM)] * len(outs)
+    if gathers is not None:
+        shapes.append(jax.ShapeDtypeStruct((groups, rows, gathers), LOW))
+        specs.append(pl.BlockSpec(memory_space=pl.ANY))
+        scratch.append(pltpu.VMEM((rows, gathers), LOW))
+        scratch += gather_sems(groups, chunks)
+        scratch.append(pltpu.SemaphoreType.DMA)
+    return pl.pallas_call(
+        functools.partial(
+            reduce_kernel, groups, chunks, len(extras), len(outs), rowfn, gathers is not None
+        ),
+        out_shape=shapes,
+        in_specs=[pl.BlockSpec(memory_space=pl.ANY)]
+        + [pl.BlockSpec(memory_space=pltpu.VMEM)] * len(extras),
+        out_specs=specs,
+        scratch_shapes=scratch,
+        compiler_params=pltpu.CompilerParams(
+            collective_id=collective_id, has_side_effects=True, vmem_limit_bytes=50 << 20
+        ),
+        cost_estimate=pl.CostEstimate(
+            flops=0, bytes_accessed=(300 if gathers else 150) << 20, transcendentals=0
+        ),
+    )(parts, *extras)
+
+
+def attend_kernel(blocks, q_ref, k_ref, v_ref, col_ref, row_ref, out_ref, log_ref):
+    size = q_ref.shape[0] // blocks
+    scale = (NOPE + ROPE) ** (-0.5)
+    for index in range(blocks):
+        part = pl.ds(index * size, size)
+        reach = (index + 1) * size
+        scores = dot_t(q_ref[part], k_ref[:reach]) * scale
+        rows = index * size + lax.broadcasted_iota(jnp.int32, (size, reach), 0)
+        columns = lax.broadcasted_iota(jnp.int32, (size, reach), 1)
+        allowed = (col_ref[part] == row_ref[:, :reach]) & (rows >= columns)
+        scores = jnp.where(allowed, scores, -1e30)
+        peak = jnp.max(scores, axis=-1, keepdims=True)
+        raised = jnp.exp(scores - peak)
+        total = jnp.sum(raised, axis=-1, keepdims=True)
+        weights = (raised * (1.0 / total)).astype(LOW)
+        out_ref[part] = dot(weights, v_ref[:reach]).astype(LOW)
+        log_ref[part] = peak + jnp.log(total)
+
+
 def attend_forward(head_q, head_k, head_v, doc_ids):
     seq_len = head_q.shape[0]
-    block_rows = min(512, seq_len)
-    places = jnp.arange(seq_len, dtype=jnp.int32)
+    return pl.pallas_call(
+        functools.partial(attend_kernel, seq_len // 256),
+        out_shape=[
+            jax.ShapeDtypeStruct((seq_len, VD), LOW),
+            jax.ShapeDtypeStruct((seq_len, 1), F32),
+        ],
+        compiler_params=pltpu.CompilerParams(vmem_limit_bytes=50 << 20),
+        cost_estimate=pl.CostEstimate(
+            flops=seq_len * seq_len * 400, bytes_accessed=4 << 20, transcendentals=seq_len * seq_len // 2
+        ),
+    )(head_q, head_k, head_v, doc_ids[:, None], doc_ids[None, :])
+
+
+def attend_back_kernel(
+    blocks, q_ref, k_ref, v_ref, g_ref, col_ref, row_ref, log_ref, dq_ref, dk_ref, dv_ref, ksum, vsum
+):
+    size = q_ref.shape[0] // blocks
     scale = (NOPE + ROPE) ** (-0.5)
-
-    def attend(index):
-        start = index * block_rows
-        query = lax.dynamic_slice_in_dim(head_q, start, block_rows, 0)
-        docs = lax.dynamic_slice_in_dim(doc_ids, start, block_rows, 0)
-        rows = start + jnp.arange(block_rows, dtype=jnp.int32)
-        allowed = (docs[:, None] == doc_ids[None, :]) & (rows[:, None] >= places[None, :])
-        scores = jnp.where(allowed, dot_t(query, head_k) * scale, -1e30)
-        peak = jnp.max(scores, axis=-1, keepdims=True)
-        raised = jnp.exp(scores - peak)
-        totals = jnp.sum(raised, axis=-1, keepdims=True)
-        out = dot((raised / totals).astype(LOW), head_v)
-        return out.astype(LOW), peak + jnp.log(totals)
-
-    out, logs = lax.map(attend, jnp.arange(seq_len // block_rows, dtype=jnp.int32))
-    return out.reshape(seq_len, VD), logs.reshape(seq_len, 1)
+    ksum[...] = jnp.zeros_like(ksum)
+    vsum[...] = jnp.zeros_like(vsum)
+    for index in range(blocks):
+        part = pl.ds(index * size, size)
+        reach = (index + 1) * size
+        query, grad = q_ref[part], g_ref[part]
+        scores = dot_t(k_ref[:reach], query) * scale
+        keys = lax.broadcasted_iota(jnp.int32, (reach, size), 0)
+        rows = index * size + lax.broadcasted_iota(jnp.int32, (reach, size), 1)
+        allowed = (col_ref[:reach] == row_ref[:, part]) & (rows >= keys)
+        weights = jnp.exp(jnp.where(allowed, scores, -1e30) - log_ref[:, part])
+        vsum[:reach] += dot(weights.astype(LOW), grad)
+        slopes = dot_t(v_ref[:reach], grad)
+        inner = jnp.sum(weights * slopes, axis=0, keepdims=True)
+        back = (weights * (slopes - inner)).astype(LOW)
+        ksum[:reach] += dot(back, query)
+        dq_ref[part] = (t_dot(back, k_ref[:reach]) * scale).astype(LOW)
+    dk_ref[...] = (ksum[...] * scale).astype(LOW)
+    dv_ref[...] = vsum[...].astype(LOW)
 
 
 def attend_backward(head_q, head_k, head_v, doc_ids, logs, head_g):
     seq_len = head_q.shape[0]
-    block_rows = min(512, seq_len)
-    places = jnp.arange(seq_len, dtype=jnp.int32)
-    scale = (NOPE + ROPE) ** (-0.5)
-
-    def back(carry, index):
-        key_grad, value_grad = carry
-        start = index * block_rows
-        query = lax.dynamic_slice_in_dim(head_q, start, block_rows, 0)
-        grad = lax.dynamic_slice_in_dim(head_g, start, block_rows, 0)
-        log = lax.dynamic_slice_in_dim(logs, start, block_rows, 0)
-        docs = lax.dynamic_slice_in_dim(doc_ids, start, block_rows, 0)
-        rows = start + jnp.arange(block_rows, dtype=jnp.int32)
-        allowed = (docs[:, None] == doc_ids[None, :]) & (rows[:, None] >= places[None, :])
-        scores = jnp.where(allowed, dot_t(query, head_k) * scale, -1e30)
-        attention = jnp.exp(scores - log)
-        value_grad = value_grad + t_dot(attention.astype(LOW), grad)
-        weight_grad = dot_t(grad, head_v)
-        inner = jnp.sum(attention * weight_grad, axis=-1, keepdims=True)
-        score_grad = (attention * (weight_grad - inner)).astype(LOW)
-        query_grad = dot(score_grad, head_k) * scale
-        key_grad = key_grad + t_dot(score_grad, query) * scale
-        return (key_grad, value_grad), query_grad.astype(LOW)
-
-    start = (
-        jnp.zeros((seq_len, NOPE + ROPE), F32),
-        jnp.zeros((seq_len, VD), F32),
-    )
-    (key_grad, value_grad), query_grad = lax.scan(
-        back, start, jnp.arange(seq_len // block_rows, dtype=jnp.int32)
-    )
-    return query_grad.reshape(seq_len, NOPE + ROPE), key_grad.astype(LOW), value_grad.astype(LOW)
+    return pl.pallas_call(
+        functools.partial(attend_back_kernel, seq_len // 256),
+        out_shape=[
+            jax.ShapeDtypeStruct((seq_len, NOPE + ROPE), LOW),
+            jax.ShapeDtypeStruct((seq_len, NOPE + ROPE), LOW),
+            jax.ShapeDtypeStruct((seq_len, VD), LOW),
+        ],
+        scratch_shapes=[
+            pltpu.VMEM((seq_len, NOPE + ROPE), F32),
+            pltpu.VMEM((seq_len, VD), F32),
+        ],
+        compiler_params=pltpu.CompilerParams(vmem_limit_bytes=56 << 20),
+        cost_estimate=pl.CostEstimate(
+            flops=seq_len * seq_len * 1000, bytes_accessed=6 << 20, transcendentals=seq_len * seq_len // 2
+        ),
+    )(head_q, head_k, head_v, head_g, doc_ids[:, None], doc_ids[None, :], logs.reshape(1, seq_len))
 
 
 def body(
@@ -207,15 +536,15 @@
     expand_w = head_parts[..., query_width:].reshape(LAT, NOPE + VD)
     output_w = lax.all_gather(w_output.astype(LOW), "fsdp", axis=0, tiled=True)
 
-    expert_gate_w = lax.all_gather(w_expert_gate[0].astype(LOW), "fsdp", axis=0, tiled=True)
-    expert_up_w = lax.all_gather(w_expert_up[0].astype(LOW), "fsdp", axis=0, tiled=True)
-    expert_down_w = lax.all_gather(w_expert_down[0].astype(LOW), "fsdp", axis=0, tiled=True)
+    expert_gate_w = whole_over_layers(w_expert_gate[0].astype(LOW))
+    expert_up_w = whole_over_layers(w_expert_up[0].astype(LOW))
+    expert_down_w = whole_over_layers(w_expert_down[0].astype(LOW))
     shared_in = jnp.concatenate([w_shared_gate, w_shared_up], axis=1).astype(LOW)
     shared_in_w = lax.all_gather(shared_in, "fsdp", axis=0, tiled=True)
     shared_down_w = lax.all_gather(w_shared_down.astype(LOW), "fsdp", axis=0, tiled=True)
     units = w_shared_gate.shape[1]
 
-    hidden_low = gather_rows(tokens[0])
+    hidden_low = ring_gather(tokens[0], groups, 1)
     grad_low = gather_rows(cotangent[0])
     all_routes = gather_rows(routes[0])
 
@@ -235,10 +564,19 @@
     head_v = expanded[:, NOPE:].astype(LOW)
 
     head_out, logs = attend_forward(head_q, head_k, head_v, doc_ids)
-    residual = hidden_own + scatter_rows(dot(head_out, output_w).astype(LOW)).astype(F32)
-    scaled_two, normed_two, factor_two = norm_forward(residual, gain_ffn)
-    own_two_low = scaled_two.astype(LOW)
-    two_low = gather_rows(own_two_low)
+    part_residual = dot(head_out, output_w).astype(LOW).reshape(groups, tok_rows, width)
+
+    def make_two(total, part, extras, outs):
+        row_sum = extras[0][part].astype(F32) + total
+        outs[0][part] = row_sum
+        return norm_forward(row_sum, extras[1][...])[0].astype(LOW)
+
+    own_shape = jax.ShapeDtypeStruct((tok_rows, width), F32)
+    residual, two_low = ring_reduce(
+        part_residual, [tokens[0], gain_ffn[None]], [own_shape], make_two, groups, 2, width
+    )
+    two_low = two_low.reshape(seq_len, width)
+    own_two_low = lax.dynamic_slice_in_dim(two_low, place * tok_rows, tok_rows, 0)
 
     logits = dot(two_low, router_w)
     raised = jnp.exp(logits - jnp.max(logits, axis=-1, keepdims=True))
@@ -304,15 +642,19 @@
     ).astype(LOW)
 
     part_grad = combine(row_grad) + dot_t(shared_grads, shared_in_w)
-    two_grad = scatter_rows(part_grad.astype(LOW)).astype(F32)
     part_out = combine((slot_gate * made.astype(F32)).astype(LOW)) + dot(shared_low, shared_down_w)
     ffn_out = scatter_rows(part_out.astype(LOW)).astype(F32)
     output = (residual + ffn_out).astype(LOW)
 
     def spread_grad(grad):
-        return lax.psum_scatter(
-            grad.astype(LOW), "fsdp", scatter_dimension=0, tiled=True
-        ).astype(F32)
+        if layers != 2:
+            return lax.psum_scatter(
+                grad.astype(LOW), "fsdp", scatter_dimension=0, tiled=True
+            ).astype(F32)
+        layer, half = lax.axis_index("fsdp"), grad.shape[0] // 2
+        sent = lax.dynamic_slice_in_dim(grad, (1 - layer) * half, half, 0).astype(LOW)
+        kept = lax.dynamic_slice_in_dim(grad, layer * half, half, 0)
+        return kept + lax.ppermute(sent, "fsdp", ((0, 1), (1, 0))).astype(F32)
 
     grad_expert_down = spread_grad(t_dot(inner_low, made_grad))
     grad_expert_gate = spread_grad(t_dot(expert_in, gate_grad))
@@ -322,10 +664,30 @@
 
     logit_grad = own_p * (prob_grad - jnp.sum(own_p * prob_grad, axis=-1, keepdims=True))
     grad_router = exact_t_dot(own_two_low.astype(F32), logit_grad)
-    two_grad = two_grad + exact_dot_t(logit_grad, router_w.astype(F32))
-    residual_part, grad_gain_ffn = norm_backward(two_grad, normed_two, factor_two, gain_ffn)
-    residual_grad = grad_own + residual_part
-    attn_grad = gather_rows(residual_grad.astype(LOW))
+    router_back = exact_dot_t(logit_grad, router_w.astype(F32))
+
+    def make_attn(total, part, extras, outs):
+        grad = total + extras[0][part]
+        gain = extras[1][...]
+        _, normed, factor = norm_forward(extras[2][part], gain)
+        inner = grad * gain
+        back = factor * (inner - normed * jnp.mean(inner * normed, axis=-1, keepdims=True))
+        back = extras[3][part].astype(F32) + back
+        outs[0][part] = back
+        outs[1][part] = grad * normed
+        return back.astype(LOW)
+
+    residual_grad, gain_parts, attn_grad = ring_reduce(
+        part_grad.astype(LOW).reshape(groups, tok_rows, width),
+        [router_back, gain_ffn[None], residual, cotangent[0]],
+        [own_shape, own_shape],
+        make_attn,
+        groups,
+        3,
+        width,
+    )
+    grad_gain_ffn = jnp.sum(gain_parts, axis=0)
+    attn_grad = attn_grad.reshape(seq_len, width)
 
     grad_output = spread_grad(t_dot(head_out, attn_grad))
     head_g = dot_t(attn_grad, output_w).astype(LOW)
@@ -349,7 +711,19 @@
         ],
         axis=1,
     )
-    own_parts = scatter_rows(part_rows).astype(F32)
+
+    def keep(total, part, extras, outs):
+        outs[0][part] = total
+
+    wide = part_rows.shape[1]
+    own_parts = ring_reduce(
+        part_rows.reshape(groups, tok_rows, wide),
+        [],
+        [jax.ShapeDtypeStruct((tok_rows, wide), F32)],
+        keep,
+        groups,
+        4,
+    )[0]
 
     grad_query_head = t_dot(normed_low, query_back).reshape(
         groups, layers, own_rows, query_width

time: 1840 us -> 1230 us (0.67)
  waiting for transfers between devices: 1240 us -> 220 us
  Pallas kernels: 0 us -> 313 us
  blocking collectives: 65.3 us -> 188 us
  matrix products: 289 us -> 220 us
  other arithmetic: 104 us -> 140 us
    unnamed x28 -> x9, waiting for transfers between devices: 496 us -> 0.12 us
    pallas_call x0 -> x6, Pallas kernels: none -> 313 us  [the longest x3 236 us: ring_reduce(): pl.pallas_call(functools.partial(reduce_kernel, groups, chunks, len(extra...]
    all_gather x4 -> x1, waiting for transfers between devices: 250 us -> 0.01 us  [gather_rows(): return lax.all_gather(block, 'seq', axis=0, tiled=True)]
    reduce_scatter x6 -> x1, waiting for transfers between devices: 240 us -> 4.31 us  [scatter_rows(): return lax.psum_scatter(partial, 'seq', scatter_dimension=0, tiled=True)]
    ppermute x0 -> x9, waiting for transfers between devices: none -> 197 us  [the longest x6 197 us: spread_grad(): return kept + lax.ppermute(sent, 'fsdp', ((0, 1), (1, 0))).astype(F32)]
    all_gather x3 -> x0, waiting for transfers between devices: 183 us -> none  [the longest x1 64.9 us: body(): lax.all_gather(w_expert_up[0].astype(LOW), 'fsdp', axis=0, tiled=True)]
    all_gather x1, blocking collectives: 12.1 us -> 135 us  [body(): output_w = lax.all_gather(w_output.astype(LOW), 'fsdp', axis=0, tiled=True)]
    all_gather x1, waiting for transfers between devices: 57.9 us -> 0.01 us  [body(): small = lax.all_gather(packed_small, both, axis=0, tiled=True)]
  transfers between devices with their start and end apart: 24 -> 18, of which waited for: 21 -> 4; matrix products, arithmetic and copies ran while one was open for 16% -> 31% of each run, Pallas kernels for 0% -> 17%
where the time goes in v2:
time: 1230 us; the launch traced here: 1220 us
  Pallas kernels  313 us (25%)
  waiting for transfers between devices  220 us (18%)
  matrix products  220 us (18%)
  blocking collectives  188 us (15%)
  other arithmetic  140 us (11%)
  local copies, waits for them, and re-layouts  103 us (8%)
  starting transfers between devices  18.9 us (2%)
  between operations  15.8 us (1%)
    pallas_call x3, Pallas kernels, ring_reduce(): pl.pallas_call(functools.partial(reduce_kernel, groups, chunks, len(extra...  236 us
    ppermute x6, waiting for transfers between devices, spread_grad(): return kept + lax.ppermute(sent, 'fsdp', ((0, 1), (1, 0))).astype(F32)  197 us
    all_gather x1, blocking collectives, body(): output_w = lax.all_gather(w_output.astype(LOW), 'fsdp', axis=0, tiled=True)  135 us
    dot_general x10, matrix products, dot(): return jnp.dot(left, right, preferred_element_type=F32)  76.1 us
    dot_general x9, matrix products, dot_t(): lax.dot_general(left, right, (((1,), (1,)), ((), ())), preferred_element_...  70.5 us
    pallas_call x1, Pallas kernels, ring_gather(): pl.pallas_call(functools.partial(gather_kernel, groups, chunks), out_shap...  55.1 us
    dot_general x9, matrix products, t_dot(): lax.dot_general(left, right, (((0,), (0,)), ((), ())), preferred_element_...  45.7 us
    unnamed x204, local copies, waits for them, and re-layouts  36.7 us
  transfers between devices with their start and end apart: 18, of which 4 were waited for; matrix products, arithmetic and copies ran while one was open for 31% of the time, Pallas kernels for 17%

profile of v2, /device:TPU:0, one launch (start us, length us, event | category | flops | bytes accessed | tf_op | source)
XLA Modules:
  0.0 1218.1 jit_solution(9062238237546499246)
XLA Ops:
  10.7 21.6 %all_to_all.22 = bf16[16,64,256]{2,1,0:T(8,128)(2,1)S(1)} all-to-all(bf16[16,64,256]{2,1,0:T(8,128)(2,1)S(1)} %copy.127), channel_id=1, replica_groups=mesh['seq'=16,'fsdp'=2] {'seq'}, dimensions={0} | all-to-all | bytes 1048576 | tf_op jit(solution)/shard_map/all_to_all | solution.py:533
  34.9 4.8 convert_bitcast_fusion
  42.3 4.5 convert_bitcast_fusion.1
  47.4 4.5 convert_bitcast_fusion.2
  53.4 20.1 %all-gather.1 = s32[1,2048,6]{1,0,2:T(1,128)S(1)} all-gather(s32[1,128,6]{1,0,2:T(1,128)S(1)} %copy-done.67), channel_id=3, replica_groups=mesh['seq'=16,'fsdp'=2] {'seq'}, dimensions={1}, use_global_device_ids=true | all-gather | bytes 52224 | tf_op jit(solution)/shard_map/all_gather | solution.py:94
  75.4 55.1 %shard_map.297 = bf16[16,128,2048]{2,1,0:T(8,128)(2,1)} custom-call(bf16[128,2048]{1,0:T(8,128)(2,1)} %bitcast.162), custom_call_target="tpu_custom_call" | custom-call | bytes 157286400 | tf_op jit(solution)/shard_map/pallas_call | solution.py:242
  131.2 135.4 %all_gather.27 = bf16[128,2048]{1,0:T(8,128)(2,1)} all-gather(bf16[64,2048]{1,0:T(8,128)(2,1)S(1)} %convert_element_type.298), channel_id=1, replica_groups=mesh['seq'=16,'fsdp'=2] {'fsdp'}, dimensions={0}, use_global_device_ids=true | all-gather | bytes 786432 | tf_op jit(solution)/shard_map/all_gather | solution.py:537
  266.8 11.0 all_gather.30
  278.3 5.1 multiply_reduce_fusion
  287.0 7.0 broadcast_select_fusion.3
  294.0 5.1 broadcast_select_fusion.5
  299.1 4.9 broadcast_select_fusion.1
  305.8 8.7 multiply_convert_fusion
  314.5 6.3 fusion.107
  325.0 9.0 fusion.3
  334.1 8.4 fusion.16
  348.6 12.3 %copy.143 = bf16[2048,2048]{1,0:T(8,128)(2,1)} copy(bf16[2048,2048]{0,1:T(8,128)(2,1)} %bitcast.173) | data formatting | bytes 16777216 | tf_op jit(solution)/shard_map/dot_general | solution.py:53
  363.5 3.2 convolution_convert_fusion.6
  366.9 5.0 fusion.50
  373.5 8.0 shard_map.298
  383.4 6.6 convolution_convert_fusion.1
  390.1 87.6 %shard_map.299 = (f32[128,2048]{1,0:T(8,128)S(1)}, bf16[16,128,2048]{2,1,0:T(8,128)(2,1)}) custom-call(bf16[16,128,2048]{2,1,0:T(8,128)(2,1)} %bitcast.171, bf16[128,2048]{1,0:T(8,128)(2,1)S(1)} %bitcast.163, f32[1,2048]{1,0:T(1,128)S(1)} %get-tuple-element.153.refs_2_), custom_call_target="tpu_custom_call" | custom-call | bytes 314572800 | tf_op jit(solution)/shard_map/pallas_call | solution.py:378
  477.7 6.2 fusion.106
  484.7 3.2 convolution_convert_fusion.4
  487.9 8.7 fusion.108
  496.7 6.7 fusion.14
  505.9 9.8 multiply_convert_fusion.3
  515.7 4.8 convolution_convert_fusion.3
  521.9 8.7 fusion.6
  531.6 3.8 all-to-all-start.1
  535.4 6.5 fusion.5
  541.9 15.8 %multiply_convert_fusion.2 = (bf16[1024,1408]{1,0:T(8,128)(2,1)}, bf16[1024,1408]{1,0:T(8,128)(2,1)}) fusion(f32[1024,1408]{1,0:T(8,128)} %copy-done.78, f32[1024,1408]{1,0:T(8,128)} %get-tuple-element.165, bf16[1024,2048]{1,0:T(8,128)(2,1)S(1)} %get-tuple-element.162, bf16[704,2048]{1,0:T(8,128)(2,1)} %get-tuple-element.127, ...), kind=kOutput, calls=%fused_computation.33 | convolution fusion | flops 5935857664 | bytes 27262976 | tf_op jit(solution)/shard_map/dot_general | solution.py:49
  557.7 11.5 fusion.12
  569.2 11.9 add_convert_fusion
  581.1 8.1 fusion.62
  589.2 4.3 multiply_convert_fusion.6
  594.3 10.5 fusion
  606.8 90.1 %shard_map.300 = (f32[128,2048]{1,0:T(8,128)S(1)}, f32[128,2048]{1,0:T(8,128)S(1)}, bf16[16,128,2048]{2,1,0:T(8,128)(2,1)}) custom-call(bf16[16,128,2048]{2,1,0:T(8,128)(2,1)} %bitcast.170, f32[128,2048]{1,0:T(8,128)S(1)} %fusion.68.refs_1_, f32[1,2048]{1,0:T(1,128)S(1)} %get-tuple-element.153.refs_2_, f32[128,2048]{1,0:T(8,128)} %copy-done.3, ...), custom_call_target="tpu_custom_call" | custom-call | bytes 314572800 | tf_op jit(solution)/shard_map/pallas_call | solution.py:378
  696.9 6.7 convolution_convert_fusion.7.g_ref
  703.6 13.7 %shard_map.301 = (bf16[2048,192]{1,0:T(8,128)(2,1)}, bf16[2048,192]{1,0:T(8,128)(2,1)}, bf16[2048,128]{1,0:T(8,128)(2,1)}) custom-call(bf16[2048,192]{1,0:T(8,128)(2,1)} %copy-done.6, bf16[2048,192]{1,0:T(8,128)(2,1)} %get-tuple-element.172.k_ref, bf16[2048,128]{1,0:T(8,128)(2,1)} %copy-done.7, bf16[2048,128]{1,0:T(8,128)(2,1)} %convolution_convert_fusion.7.g_ref, ...), custom_call_target="tpu_custom_call" | custom-call | flops 4194304000 | bytes 6291456 | tf_op jit(solution)/shard_map/pallas_call | solution.py:458
  730.4 8.1 fusion.42
  738.6 5.9 convolution_convert_fusion
  748.3 19.5 %maximum_maximum_fusion = bf16[2048,2688]{0,1:T(8,128)(2,1)} fusion(bf16[2048,64]{0,1:T(8,128)(2,1)S(1)} %copy.140, bf16[2048,512]{0,1:T(8,128)(2,1)} %convolution_convert_fusion.5, bf16[2048,2048]{0,1:T(8,128)(2,1)} %convolution_convert_fusion, bf16[2688]{0:T(1024)(128)(2,1)S(1)} %copy-done.61), kind=kLoop, calls=%fused_computation.9 | loop fusion | flops 44040192 | bytes 21763328 | tf_op jit(solution)/shard_map/concatenate | solution.py:705
  767.8 14.7 %copy.141 = bf16[2048,2688]{1,0:T(8,128)(2,1)} copy(bf16[2048,2688]{0,1:T(8,128)(2,1)} %maximum_maximum_fusion) | data formatting | bytes 22020096 | tf_op jit(solution)/shard_map/concatenate | solution.py:705
  782.6 58.7 %shard_map.302 = f32[128,2688]{1,0:T(8,128)S(1)} custom-call(bf16[16,128,2688]{2,1,0:T(8,128)(2,1)} %bitcast.172), custom_call_target="tpu_custom_call" | custom-call | bytes 157286400 | tf_op jit(solution)/shard_map/pallas_call | solution.py:378
  851.0 5.8 copy.171
  856.8 5.2 pad.20.clone
  863.2 5.4 fusion.9
  870.9 5.8 fusion.54
  878.6 8.3 fusion.65
  886.8 11.5 fusion.1
  898.4 9.8 fusion.110
  910.1 4.4 copy-done.14
  915.7 8.3 fusion.112
  926.0 4.2 copy-done.16
  931.0 9.4 fusion.111
  948.0 182.5 %collective-permute-done.3 = bf16[64,2048]{1,0:T(8,128)(2,1)S(1)} collective-permute-done((bf16[64,2048]{1,0:T(8,128)(2,1)S(1)}, bf16[64,2048]{1,0:T(8,128)(2,1)S(1)}, u32[]{:S(2)}, u32[]{:S(2)}) %collective-permute-start.3) | collective-permute-done | bytes 262176 | tf_op jit(solution)/shard_map/ppermute | solution.py:657
  1134.1 5.8 all-to-all-start.2
  1144.9 18.1 %all-to-all-done.2 = bf16[16,64,256]{2,1,0:T(8,128)(2,1)S(1)} async-done(((bf16[16,64,256]{2,1,0:T(8,128)(2,1)}), bf16[16,64,256]{2,1,0:T(8,128)(2,1)S(1)}, u32[]{:S(2)}, u32[]{:S(2)}) %all-to-all-start.2) | async-done | bytes 524320 | tf_op jit(solution)/shard_map/all_to_all | solution.py:734
  1166.1 7.5 add_bitcast_fusion
  1173.6 6.7 add_bitcast_fusion.2
  1180.2 14.7 %collective-permute-done.7 = bf16[1024,1408]{1,0:T(8,128)(2,1)} collective-permute-done((bf16[1024,1408]{1,0:T(8,128)(2,1)}, bf16[1024,1408]{1,0:T(8,128)(2,1)}, u32[]{:S(2)}, u32[]{:S(2)}) %collective-permute-start.7) | collective-permute-done | bytes 2883616 | tf_op jit(solution)/shard_map/ppermute | solution.py:657
  1195.0 4.9 add_bitcast_fusion.1
  1204.8 4.3 reduce-scatter.8.cloned.1.call-done
  (354 shorter events, 108.2 us)
Async XLA Ops:
  7.2 276.3 %all-gather.12.cloned.1.call-start = ((), (), s32[]{:S(2)}) async-start(), calls=%async_computation.8 | async-start | bytes 1572864 | tf_op jit(solution)/shard_map/all_gather | solution.py:534
  8.2 25.3 %copy-start.72 = (f32[16]{0:T(128)S(1)}, f32[16]{0:T(128)}, u32[]{:S(2)}) copy-start(f32[16]{0:T(128)} %param.25) | copy-start | bytes 196
  8.2 25.4 %copy-start.64 = (f32[64,16]{0,1:T(8,128)S(1)}, f32[64,16]{0,1:T(8,128)}, u32[]{:S(2)}) copy-start(f32[64,16]{0,1:T(8,128)} %param.29) | copy-start | bytes 12292
  8.2 25.5 %copy-start.73 = (f32[64]{0:T(128)S(1)}, f32[64]{0:T(128)}, u32[]{:S(2)}) copy-start(f32[64]{0:T(128)} %param.28) | copy-start | bytes 772
  8.2 25.7 %copy-start.74 = (f32[64]{0:T(128)S(1)}, f32[64]{0:T(128)}, u32[]{:S(2)}) copy-start(f32[64]{0:T(128)} %param.22) | copy-start | bytes 772
  8.2 25.8 %copy-start.56 = (f32[64,576]{1,0:T(8,128)S(1)}, f32[64,576]{1,0:T(8,128)}, u32[]{:S(2)}) copy-start(f32[64,576]{1,0:T(8,128)} %param.24) | copy-start | bytes 442372
  33.5 270.5 %all-gather.8.cloned.1.call-start = ((), (), s32[]{:S(2)}) async-start(), calls=%async_computation.5 | async-start | bytes 2703360 | tf_op jit(solution)/shard_map/all_gather | solution.py:517
  34.9 453.1 %all-gather.10.cloned.1.call-start = ((), (), s32[]{:S(2)}) async-start(), calls=%async_computation.6 | async-start | bytes 2162688 | tf_op jit(solution)/shard_map/all_gather | solution.py:543
  39.7 259.4 %collective-permute-start.2 = (bf16[704,2048]{1,0:T(8,128)(2,1)}, bf16[704,2048]{1,0:T(8,128)(2,1)}, u32[]{:S(2)}, u32[]{:S(2)}) collective-permute-start(bf16[704,2048]{1,0:T(8,128)(2,1)} %convert_bitcast_fusion), channel_id=1, source_target_pairs={{0,1},{1,0},{2,3},{3,2},{4,5},{5,4},{6,7},{7,6},{8,9},{9,8},{10,11... | collective-permute-start | bytes 8650760 | tf_op jit(solution)/shard_map/ppermute | solution.py:88
  42.2 473.5 %all-gather.14.cloned.1.call-start = ((), (), s32[]{:S(2)}) async-start(), calls=%async_computation.9 | async-start | bytes 8912896 | tf_op jit(solution)/shard_map/all_gather | solution.py:94
  46.8 27.1 %copy-start.53 = (f32[64,2048]{1,0:T(8,128)S(1)}, f32[64,2048]{1,0:T(8,128)}, u32[]{:S(2)}) copy-start(f32[64,2048]{1,0:T(8,128)} %param.27) | copy-start | bytes 1572868
  46.8 27.2 %copy-start.47 = (f32[88,2048]{1,0:T(8,128)S(1)}, f32[88,2048]{1,0:T(8,128)}, u32[]{:S(2)}) copy-start(f32[88,2048]{1,0:T(8,128)} %param.32) | copy-start | bytes 2162692
  46.8 27.2 %copy-start.8 = (s32[1,2048]{1,0:T(1,128)S(1)}, s32[1,2048]{1,0:T(1,128)}, u32[]{:S(2)}) copy-start(s32[1,2048]{1,0:T(1,128)} %row_ref.3) | copy-start | bytes 24580
  46.8 240.2 %collective-permute-start.1 = (bf16[1024,1408]{1,0:T(8,128)(2,1)}, bf16[1024,1408]{1,0:T(8,128)(2,1)}, u32[]{:S(2)}, u32[]{:S(2)}) collective-permute-start(bf16[1024,1408]{1,0:T(8,128)(2,1)} %convert_bitcast_fusion.1), channel_id=1, source_target_pairs={{0,1},{1,0},{2,3},{3,2},{4,5},{5,4},{6,7},{7,6},{8,9},{9,8},{10,11... | collective-permute-start | bytes 8650760 | tf_op jit(solution)/shard_map/ppermute | solution.py:88
  51.9 242.0 %collective-permute-start = (bf16[1024,1408]{1,0:T(8,128)(2,1)}, bf16[1024,1408]{1,0:T(8,128)(2,1)}, u32[]{:S(2)}, u32[]{:S(2)}) collective-permute-start(bf16[1024,1408]{1,0:T(8,128)(2,1)} %convert_bitcast_fusion.2), channel_id=1, source_target_pairs={{0,1},{1,0},{2,3},{3,2},{4,5},{5,4},{6,7},{7,6},{8,9},{9,8},{10,11... | collective-permute-start | bytes 8650760 | tf_op jit(solution)/shard_map/ppermute | solution.py:88
  73.5 293.3 %copy-start.59 = (f32[2048]{0:T(1024)}, f32[2048]{0:T(1024)S(1)}, u32[]{:S(2)}) copy-start(f32[2048]{0:T(1024)S(1)} %iota_convert_fusion) | copy-start | bytes 24580
  73.6 293.2 %copy-start.69 = (f32[32]{0:T(128)}, f32[32]{0:T(128)S(1)}, u32[]{:S(2)}) copy-start(f32[32]{0:T(128)S(1)} %multiply_exponential_fusion) | copy-start | bytes 388
  75.4 191.2 %copy-start = (bf16[1,128,2048]{2,1,0:T(8,128)(2,1)S(1)}, bf16[1,128,2048]{2,1,0:T(8,128)(2,1)}, u32[]{:S(2)}) copy-start(bf16[1,128,2048]{2,1,0:T(8,128)(2,1)} %param.18) | copy-start | bytes 1572868
  285.2 78.2 %copy-start.41 = (bf16[512,256]{1,0:T(8,128)(2,1)}, bf16[512,256]{1,0:T(8,128)(2,1)S(1)}, u32[]{:S(2)}) copy-start(bf16[512,256]{1,0:T(8,128)(2,1)S(1)} %reshape.213) | copy-start | bytes 786436
  285.2 8.7 slice-start.2
  286.9 27.6 %copy-start.23 = (bf16[16,2,64,192]{3,2,1,0:T(8,128)(2,1)}, bf16[16,2,64,192]{3,2,1,0:T(8,128)(2,1)S(1)}, u32[]{:S(2)}) copy-start(bf16[16,2,64,192]{3,2,1,0:T(8,128)(2,1)S(1)} %copy.156) | copy-start | bytes 2359300
  287.0 12.1 slice-start.4
  305.6 19.4 %copy-start.57 = (f32[1,2048]{1,0:T(1,128)}, f32[1,2048]{1,0:T(1,128)S(1)}, u32[]{:S(2)}) copy-start(f32[1,2048]{1,0:T(1,128)S(1)} %get-tuple-element.155) | copy-start | bytes 24580
  305.8 57.6 %copy-start.62 = (f32[512]{0:T(512)}, f32[512]{0:T(512)S(1)}, u32[]{:S(2)}) copy-start(f32[512]{0:T(512)S(1)} %mul.447) | copy-start | bytes 6148
  344.8 139.2 %copy-start.25 = (f32[128,512]{1,0:T(8,128)}, f32[128,512]{1,0:T(8,128)S(1)}, u32[]{:S(2)}) copy-start(f32[128,512]{1,0:T(8,128)S(1)} %copy.164) | copy-start | bytes 786436
  484.7 120.2 %copy-start.55 = (f32[2048,16]{0,1:T(8,128)}, f32[2048,16]{0,1:T(8,128)S(1)}, u32[]{:S(2)}) copy-start(f32[2048,16]{0,1:T(8,128)S(1)} %get-tuple-element.123) | copy-start | bytes 393220
  487.9 8.7 copy-start.32
  487.9 8.7 copy-start.33
  496.7 9.2 copy-start.29
  496.7 9.2 copy-start.31
  520.5 10.1 copy-start.11
  531.6 73.3 %all-to-all-start.1 = ((f32[16,1,128]{2,1,0:T(1,128)}), f32[16,1,128]{2,1,0:T(1,128)S(1)}, u32[]{:S(2)}, u32[]{:S(2)}) async-start(f32[16,1,128]{2,1,0:T(1,128)} %bitcast.32), calls=%async_computation.2 | async-start | bytes 16384 | tf_op jit(solution)/shard_map/all_to_all | solution.py:629
  535.3 596.2 %all-reduce.7.cloned.1.call-start = ((), (), s32[]{:S(2)}) async-start(), calls=%async_computation.11 | async-start | bytes 2097152
  541.9 15.8 %copy-start.18 = (bf16[1024,2048]{1,0:T(8,128)(2,1)}, bf16[1024,2048]{1,0:T(8,128)(2,1)S(1)}, u32[]{:S(2)}) copy-start(bf16[1024,2048]{1,0:T(8,128)(2,1)S(1)} %get-tuple-element.162) | copy-start | bytes 12582916
  541.9 15.8 %copy-start.30 = (bf16[1024,1408]{1,0:T(8,128)(2,1)S(1)}, bf16[1024,1408]{1,0:T(8,128)(2,1)}, u32[]{:S(2)}) copy-start(bf16[1024,1408]{1,0:T(8,128)(2,1)} %get-tuple-element.130) | copy-start | bytes 8650756
  557.7 31.5 %slice-start = ((s8[8388608]{0:T(1024)(128)(4,1)}), s8[4194304]{0:T(1024)(128)(4,1)S(1)}, s32[]{:S(2)}) async-start(s8[8388608]{0:T(1024)(128)(4,1)} %bitcast.176), calls=%async_computation.12 | async-start | bytes 8388608
  569.2 20.0 %slice-start.1 = ((s8[8388608]{0:T(1024)(128)(4,1)}), s8[4194304]{0:T(1024)(128)(4,1)S(1)}, s32[]{:S(2)}) async-start(s8[8388608]{0:T(1024)(128)(4,1)} %bitcast.176), calls=%async_computation.13 | async-start | bytes 8388608
  593.5 11.4 copy-start.48
  594.3 12.4 %copy-start.5 = (bf16[1,128,2048]{2,1,0:T(8,128)(2,1)S(1)}, bf16[1,128,2048]{2,1,0:T(8,128)(2,1)}, u32[]{:S(2)}) copy-start(bf16[1,128,2048]{2,1,0:T(8,128)(2,1)} %param.19) | copy-start | bytes 1572868
  606.8 90.2 %copy-start.37 = (bf16[128,2048]{1,0:T(8,128)(2,1)S(1)}, bf16[128,2048]{1,0:T(8,128)(2,1)}, u32[]{:S(2)}) copy-start(bf16[128,2048]{1,0:T(8,128)(2,1)} %all_gather.27) | copy-start | bytes 1572868
  696.9 26.6 %slice-start.13 = ((s8[4718592]{0:T(1024)(128)(4,1)}), s8[4194304]{0:T(1024)(128)(4,1)S(1)}, s32[]{:S(2)}) async-start(s8[4718592]{0:T(1024)(128)(4,1)} %bitcast.197), calls=%async_computation.25 | async-start | bytes 8388608
  703.6 19.9 %slice-start.14 = ((s8[4718592]{0:T(1024)(128)(4,1)}), s8[524288]{0:T(1024)(128)(4,1)S(1)}, s32[]{:S(2)}) async-start(s8[4718592]{0:T(1024)(128)(4,1)} %bitcast.197), calls=%async_computation.26 | async-start | bytes 1048576
  730.4 14.0 %slice-start.8 = ((s8[8388608]{0:T(1024)(128)(4,1)}), s8[4194304]{0:T(1024)(128)(4,1)S(1)}, s32[]{:S(2)}) async-start(s8[8388608]{0:T(1024)(128)(4,1)} %bitcast.192), calls=%async_computation.20 | async-start | bytes 8388608
  748.3 451.5 %reduce-scatter.10.cloned.1.call-start = ((), (), s32[]{:S(2)}) async-start(), calls=%async_computation.10 | async-start | bytes 5406720
  782.5 58.7 %copy-start.26 = (f32[128,512]{1,0:T(8,128)S(1)}, f32[128,512]{1,0:T(8,128)}, u32[]{:S(2)}) copy-start(f32[128,512]{1,0:T(8,128)} %copy-done.25) | copy-start | bytes 786436
  782.5 58.7 %copy-start.68 = (f32[128]{0:T(128)S(1)}, f32[128]{0:T(128)}, u32[]{:S(2)}) copy-start(f32[128]{0:T(128)} %add_rsqrt_fusion.2) | copy-start | bytes 1540
  782.5 60.0 %copy-start.43 = (bf16[2048,640]{1,0:T(8,128)(2,1)S(1)}, bf16[2048,640]{1,0:T(8,128)(2,1)}, u32[]{:S(2)}) copy-start(bf16[2048,640]{1,0:T(8,128)(2,1)} %all-gather.8.cloned.1.call-done) | copy-start | bytes 7864324
  782.5 60.0 %copy-start.58 = (f32[1,2048]{1,0:T(1,128)S(1)}, f32[1,2048]{1,0:T(1,128)}, u32[]{:S(2)}) copy-start(f32[1,2048]{1,0:T(1,128)} %copy-done.57) | copy-start | bytes 24580
  782.5 60.0 %copy-start.71 = (f32[128]{0:T(128)S(1)}, f32[128]{0:T(128)}, u32[]{:S(2)}) copy-start(f32[128]{0:T(128)} %add_rsqrt_fusion.3) | copy-start | bytes 1540
  862.0 347.1 %reduce-scatter.8.cloned.1.call-start = ((), (), s32[]{:S(2)}) async-start(), calls=%async_computation.7 | async-start | bytes 8912896 | tf_op jit(solution)/shard_map/reduce_scatter | solution.py:98
  869.4 270.6 %collective-permute-start.5 = (bf16[88,2048]{1,0:T(8,128)(2,1)}, bf16[88,2048]{1,0:T(8,128)(2,1)}, u32[]{:S(2)}, u32[]{:S(2)}) collective-permute-start(bf16[88,2048]{1,0:T(8,128)(2,1)} %dynamic-slice_convert_fusion.4), channel_id=1, source_target_pairs={{0,1},{1,0},{2,3},{3,2},{4,5},{5,4},{6,7},{7,6},{8,9},{9,8},{10,11... | collective-permute-start | bytes 1081352 | tf_op jit(solution)/shard_map/ppermute | solution.py:657
  877.8 264.0 %collective-permute-start.4 = (bf16[1024,352]{0,1:T(8,128)(2,1)}, bf16[1024,352]{0,1:T(8,128)(2,1)}, u32[]{:S(2)}, u32[]{:S(2)}) collective-permute-start(bf16[1024,352]{0,1:T(8,128)(2,1)} %dynamic-slice_convert_fusion.3), channel_id=1, source_target_pairs={{0,1},{1,0},{2,3},{3,2},{4,5},{5,4},{6,7},{7,6},{8,9},{9,8},{10,11... | collective-permute-start | bytes 2162696 | tf_op jit(solution)/shard_map/ppermute | solution.py:657
  914.4 259.2 %collective-permute-start.6 = (bf16[1024,1408]{1,0:T(8,128)(2,1)}, bf16[1024,1408]{1,0:T(8,128)(2,1)}, u32[]{:S(2)}, u32[]{:S(2)}) collective-permute-start(bf16[1024,1408]{1,0:T(8,128)(2,1)} %dynamic-slice_convert_fusion.2), channel_id=1, source_target_pairs={{0,1},{1,0},{2,3},{3,2},{4,5},{5,4},{6,7},{7,6},{8,9},{9,8},{10,11... | collective-permute-start | bytes 8650760 | tf_op jit(solution)/shard_map/ppermute | solution.py:657
  915.7 15.2 %copy-start.13 = (bf16[16,64,2048]{2,1,0:T(8,128)(2,1)S(1)}, bf16[16,64,2048]{2,1,0:T(8,128)(2,1)}, u32[]{:S(2)}) copy-start(bf16[16,64,2048]{2,1,0:T(8,128)(2,1)} %convolution_convert_fusion.4) | copy-start | bytes 12582916
  924.0 18.2 %slice-start.6 = ((s8[8388608]{0:T(1024)(128)(4,1)}), s8[4194304]{0:T(1024)(128)(4,1)S(1)}, s32[]{:S(2)}) async-start(s8[8388608]{0:T(1024)(128)(4,1)} %bitcast.183), calls=%async_computation.18 | async-start | bytes 8388608
  930.3 12.0 slice-start.7
  930.3 235.8 %collective-permute-start.8 = (bf16[704,2048]{1,0:T(8,128)(2,1)}, bf16[704,2048]{1,0:T(8,128)(2,1)}, u32[]{:S(2)}, u32[]{:S(2)}) collective-permute-start(bf16[704,2048]{1,0:T(8,128)(2,1)} %dynamic-slice_convert_fusion), channel_id=1, source_target_pairs={{0,1},{1,0},{2,3},{3,2},{4,5},{5,4},{6,7},{7,6},{8,9},{9,8},{10,11... | collective-permute-start | bytes 8650760 | tf_op jit(solution)/shard_map/ppermute | solution.py:657
  945.7 184.7 %collective-permute-start.3 = (bf16[64,2048]{1,0:T(8,128)(2,1)S(1)}, bf16[64,2048]{1,0:T(8,128)(2,1)S(1)}, u32[]{:S(2)}, u32[]{:S(2)}) collective-permute-start(bf16[64,2048]{1,0:T(8,128)(2,1)S(1)} %dynamic-slice_convert_fusion.5), channel_id=1, source_target_pairs={{0,1},{1,0},{2,3},{3,2},{4,5},{5,4},{6,7},{7,6},{8,9},{9,8},{10,11... | collective-permute-start | bytes 786440 | tf_op jit(solution)/shard_map/ppermute | solution.py:657
  1130.5 64.5 %collective-permute-start.7 = (bf16[1024,1408]{1,0:T(8,128)(2,1)}, bf16[1024,1408]{1,0:T(8,128)(2,1)}, u32[]{:S(2)}, u32[]{:S(2)}) collective-permute-start(bf16[1024,1408]{1,0:T(8,128)(2,1)} %dynamic-slice_convert_fusion.1), channel_id=1, source_target_pairs={{0,1},{1,0},{2,3},{3,2},{4,5},{5,4},{6,7},{7,6},{8,9},{9,8},{10,11... | collective-permute-start | bytes 8650760 | tf_op jit(solution)/shard_map/ppermute | solution.py:657
  1134.1 28.9 %all-to-all-start.2 = ((bf16[16,64,256]{2,1,0:T(8,128)(2,1)}), bf16[16,64,256]{2,1,0:T(8,128)(2,1)S(1)}, u32[]{:S(2)}, u32[]{:S(2)}) async-start(bf16[16,64,256]{2,1,0:T(8,128)(2,1)} %dynamic-slice_bitcast_fusion), calls=%async_computation.3 | async-start | bytes 1048576 | tf_op jit(solution)/shard_map/all_to_all | solution.py:734
  1166.1 28.9 %slice-start.10 = ((s8[11534336]{0:T(1024)(128)(4,1)}), s8[4194304]{0:T(1024)(128)(4,1)S(1)}, s32[]{:S(2)}) async-start(s8[11534336]{0:T(1024)(128)(4,1)} %bitcast.195), calls=%async_computation.22 | async-start | bytes 8388608
  1166.1 28.9 %slice-start.11 = ((s8[11534336]{0:T(1024)(128)(4,1)}), s8[4194304]{0:T(1024)(128)(4,1)S(1)}, s32[]{:S(2)}) async-start(s8[11534336]{0:T(1024)(128)(4,1)} %bitcast.195), calls=%async_computation.23 | async-start | bytes 8388608
  1173.6 21.4 %slice-start.12 = ((s8[11534336]{0:T(1024)(128)(4,1)}), s8[3145728]{0:T(1024)(128)(4,1)S(1)}, s32[]{:S(2)}) async-start(s8[11534336]{0:T(1024)(128)(4,1)} %bitcast.195), calls=%async_computation.24 | async-start | bytes 6291456
  1180.2 28.8 %copy-start.4 = (f32[128,2048]{1,0:T(8,128)S(1)}, f32[128,2048]{1,0:T(8,128)}, u32[]{:S(2)}) copy-start(f32[128,2048]{1,0:T(8,128)} %copy-done.3) | copy-start | bytes 3145732
  (48 other events, 251.6 us)
Sparse Core Ops, SparseCore 0:
  33.6 31.9 all-gather.11
  69.1 63.8 all-gather.7
  135.1 40.1 all-gather.9
  177.3 74.8 all-gather.13
  748.4 40.1 all-reduce.6
  862.1 222.5 reduce-scatter.9
  1089.3 119.7 reduce-scatter.7

commit v3 on v2

--- a/solution.py
+++ b/solution.py
@@ -82,12 +82,42 @@
     return sigmoid * (1.0 + value * (1.0 - sigmoid))
 
 
+def after(value, *others):
+    return lax.optimization_barrier((value,) + others)[0]
+
+
+def swap_layers(own):
+    return lax.ppermute(own, "fsdp", ((0, 1), (1, 0)))
+
+
+def layers_in_order(own, other, axis=0):
+    first = lax.axis_index("fsdp") == 0
+    return jnp.concatenate([jnp.where(first, own, other), jnp.where(first, other, own)], axis=axis)
+
+
 def whole_over_layers(own):
     if lax.axis_size("fsdp") != 2:
         return lax.all_gather(own, "fsdp", axis=0, tiled=True)
-    other = lax.ppermute(own, "fsdp", ((0, 1), (1, 0)))
-    first = lax.axis_index("fsdp") == 0
-    return jnp.concatenate([jnp.where(first, own, other), jnp.where(first, other, own)], axis=0)
+    return layers_in_order(own, swap_layers(own))
+
+
+def spread_start(grad, kind=LOW):
+    layers = lax.axis_size("fsdp")
+    if layers != 2:
+        return grad.astype(kind), None
+    layer, half = lax.axis_index("fsdp"), grad.shape[0] // 2
+    sent = lax.dynamic_slice_in_dim(grad, (1 - layer) * half, half, 0).astype(kind)
+    return lax.dynamic_slice_in_dim(grad, layer * half, half, 0), sent
+
+
+def spread_end(kept, sent):
+    if sent is None:
+        return lax.psum_scatter(kept, "fsdp", scatter_dimension=0, tiled=True).astype(F32)
+    return kept + swap_layers(sent).astype(F32)
+
+
+def spread_grad(grad, kind=LOW):
+    return spread_end(*spread_start(grad, kind))
 
 
 def gather_rows(block):
@@ -473,6 +503,314 @@
     )(head_q, head_k, head_v, head_g, doc_ids[:, None], doc_ids[None, :], logs.reshape(1, seq_len))
 
 
+def swapped(values):
+    half = values.shape[-1] // 2
+    return jnp.concatenate([values[:, half:], values[:, :half]], axis=-1)
+
+
+def project_kernel(
+    x_ref, gain_ref, wq_ref, wl_ref, gain_lat_ref, we_ref, table_ref,
+    one_ref, q_ref, k_ref, v_ref, m_ref, c_ref,
+):
+    one = norm_forward(x_ref[...].astype(F32), gain_ref[...])[0].astype(LOW)
+    one_ref[...] = one
+    cosine, sine = table_ref[:, :ROPE], table_ref[:, ROPE:]
+    query = dot(one, wq_ref[...])
+    turned = query[:, NOPE:]
+    q_ref[:, :NOPE] = query[:, :NOPE].astype(LOW)
+    q_ref[:, NOPE:] = (turned * cosine + swapped(turned) * sine).astype(LOW)
+    latent = dot(one, wl_ref[...])
+    turned = latent[:, LAT : LAT + ROPE]
+    k_ref[:, NOPE:] = (turned * cosine + swapped(turned) * sine).astype(LOW)
+    c_ref[...] = latent[:, :LAT]
+    scaled = norm_forward(latent[:, :LAT], gain_lat_ref[...])[0].astype(LOW)
+    m_ref[...] = scaled
+    expanded = dot(scaled, we_ref[...])
+    k_ref[:, :NOPE] = expanded[:, :NOPE].astype(LOW)
+    v_ref[...] = expanded[:, NOPE:].astype(LOW)
+
+
+def project(rows, gain, query_w, small, gain_latent, expand_w, table, tile=256):
+    seq_len, width = rows.shape
+
+    def cut(columns):
+        return pl.BlockSpec((tile, columns), lambda i: (i, 0))
+
+    def whole(array):
+        return pl.BlockSpec(array.shape, lambda i: (0, 0))
+
+    outs = [(width, LOW), (NOPE + ROPE, LOW), (NOPE + ROPE, LOW), (VD, LOW), (LAT, LOW), (LAT, F32)]
+    return pl.pallas_call(
+        project_kernel,
+        grid=(seq_len // tile,),
+        out_shape=[jax.ShapeDtypeStruct((seq_len, c), t) for c, t in outs],
+        in_specs=[
+            cut(width), whole(gain), whole(query_w), whole(small), whole(gain_latent),
+            whole(expand_w), cut(2 * ROPE),
+        ],
+        out_specs=[cut(c) for c, _ in outs],
+        compiler_params=pltpu.CompilerParams(vmem_limit_bytes=50 << 20),
+        cost_estimate=pl.CostEstimate(
+            flops=seq_len * width * 1800, bytes_accessed=28 << 20, transcendentals=0
+        ),
+    )(rows, gain, query_w, small, gain_latent, expand_w, table)
+
+
+def project_back_kernel(
+    dq_ref, dk_ref, dv_ref, table_ref, one_ref, m_ref, wq_ref, we_ref,
+    parts_ref, gq_ref, ge_ref, dq_low, de_low,
+):
+    cosine, sine = table_ref[:, :ROPE], table_ref[:, ROPE:]
+    turned = dq_ref[:, NOPE:].astype(F32)
+    dq_low[:, :NOPE] = dq_ref[:, :NOPE]
+    dq_low[:, NOPE:] = (turned * cosine - swapped(turned) * sine).astype(LOW)
+    de_low[:, :NOPE] = dk_ref[:, :NOPE]
+    de_low[:, NOPE:] = dv_ref[...]
+    blocks, rows, wide = parts_ref.shape
+    width, last = one_ref.shape[1], LAT + ROPE
+    parts_ref[:, :, :width] = dot_t(dq_low[...], wq_ref[...]).astype(LOW).reshape(blocks, rows, width)
+    parts_ref[:, :, width : width + LAT] = (
+        dot_t(de_low[...], we_ref[...]).astype(LOW).reshape(blocks, rows, LAT)
+    )
+    parts_ref[:, :, width + LAT : width + last] = dk_ref[:, NOPE:].reshape(blocks, rows, ROPE)
+    parts_ref[:, :, width + last :] = jnp.zeros((blocks, rows, wide - width - last), LOW)
+
+    @pl.when(pl.program_id(0) == 0)
+    def _():
+        gq_ref[...] = jnp.zeros_like(gq_ref)
+        ge_ref[...] = jnp.zeros_like(ge_ref)
+
+    gq_ref[...] += t_dot(one_ref[...], dq_low[...])
+    ge_ref[...] += t_dot(m_ref[...], de_low[...])
+
+
+def project_back(grads, table, one_low, latent_low, query_w, expand_w, tok_rows, tile=256):
+    seq_len, width = one_low.shape
+    wide = width + LAT + 2 * ROPE
+
+    def cut(columns):
+        return pl.BlockSpec((tile, columns), lambda i: (i, 0))
+
+    def whole(shape):
+        return pl.BlockSpec(shape, lambda i: (0, 0))
+
+    return pl.pallas_call(
+        project_back_kernel,
+        grid=(seq_len // tile,),
+        out_shape=[
+            jax.ShapeDtypeStruct((seq_len // tok_rows, tok_rows, wide), LOW),
+            jax.ShapeDtypeStruct(query_w.shape, F32),
+            jax.ShapeDtypeStruct(expand_w.shape, F32),
+        ],
+        in_specs=[
+            cut(NOPE + ROPE), cut(NOPE + ROPE), cut(VD), cut(2 * ROPE), cut(width), cut(LAT),
+            whole(query_w.shape), whole(expand_w.shape),
+        ],
+        out_specs=[
+            pl.BlockSpec((tile // tok_rows, tok_rows, wide), lambda i: (i, 0, 0)),
+            whole(query_w.shape),
+            whole(expand_w.shape),
+        ],
+        scratch_shapes=[pltpu.VMEM((tile, NOPE + ROPE), LOW), pltpu.VMEM((tile, NOPE + VD), LOW)],
+        compiler_params=pltpu.CompilerParams(vmem_limit_bytes=50 << 20),
+        cost_estimate=pl.CostEstimate(
+            flops=seq_len * width * 1300, bytes_accessed=28 << 20, transcendentals=0
+        ),
+    )(*grads, table, one_low, latent_low, query_w, expand_w)
+
+
+def blocks_of(ref, count):
+    size = ref.shape[0] // count
+    return [pl.ds(block * size, size) for block in range(count)]
+
+
+def two_parts(values):
+    high = values.astype(LOW)
+    return high, (values - high.astype(F32)).astype(LOW)
+
+
+def ffn_kernel(
+    rows_ref, chosen_ref, mine_ref, router_ref, wg_ref, wu_ref, wd_ref, wi_ref, wo_ref,
+    probs_ref, slot_gate_ref, in_ref, gate_ref, up_ref, inner_ref, made_ref, proj_ref, hs_ref, out_ref,
+    spread,
+):
+    count = 4
+    tokens, slots = blocks_of(rows_ref, count), blocks_of(chosen_ref, count)
+    lanes = lax.broadcasted_iota(jnp.int32, mine_ref.shape, 1)
+    logits = jnp.where(mine_ref[1:2] > 0, dot(rows_ref[...], router_ref[...]), -1e30)
+    raised = jnp.exp(logits - jnp.max(logits, axis=-1, keepdims=True))
+    probs = raised / jnp.sum(raised, axis=-1, keepdims=True)
+    probs_ref[...] = probs
+    high, rest = two_parts(jnp.sum(probs * mine_ref[0:1], axis=-1, keepdims=True))
+    high, rest = high.astype(F32), rest.astype(F32)
+    columns = jnp.where(lanes[0:1] == 0, high, jnp.where(lanes[0:1] == 1, rest, 0.0)).astype(LOW)
+    for token, slot in zip(tokens, slots):
+        size = token.size
+        picked = columns[token.start : token.start + size]
+        chosen = chosen_ref[slot]
+        slot_gate_ref[slot] = jnp.sum(dot(chosen, picked), axis=-1, keepdims=True)
+        in_ref[slot] = dot(chosen, rows_ref[token]).astype(LOW)
+    gate = dot(in_ref[...], wg_ref[...])
+    up = dot(in_ref[...], wu_ref[...])
+    gate_ref[...] = gate
+    up_ref[...] = up
+    inner_ref[...] = (gate * jax.nn.sigmoid(gate) * up).astype(LOW)
+    made = dot(inner_ref[...], wd_ref[...]).astype(LOW)
+    made_ref[...] = made
+    spread[...] = (slot_gate_ref[...] * made.astype(F32)).astype(LOW)
+    proj = dot(rows_ref[...], wi_ref[...])
+    proj_ref[...] = proj
+    half = proj.shape[1] // 2
+    gate, up = proj[:, :half], proj[:, half:]
+    hs_ref[...] = (gate * jax.nn.sigmoid(gate) * up).astype(LOW)
+    for token, slot in zip(tokens, slots):
+        total = t_dot(chosen_ref[slot], spread[slot]) + dot(hs_ref[token], wo_ref[...])
+        out_ref[token] = total.astype(LOW)
+
+
+def ffn_back_kernel(
+    grads_ref, chosen_ref, mine_ref, slot_gate_ref, made_ref, gate_ref, up_ref, proj_ref,
+    wg_ref, wu_ref, wd_ref, wi_ref, wo_ref,
+    dy_ref, dgate_ref, dup_ref, dproj_ref, parts_ref, spread,
+):
+    count = 4
+    width = grads_ref.shape[1]
+    tokens, slots = blocks_of(grads_ref, count), blocks_of(chosen_ref, count)
+    mine, shifted = mine_ref[0:1], mine_ref[2:3]
+    for token, slot in zip(tokens, slots):
+        picked = dot(chosen_ref[slot], grads_ref[token])
+        dy_ref[slot] = (slot_gate_ref[slot] * picked).astype(LOW)
+        score = jnp.sum(picked * made_ref[slot].astype(F32), axis=-1, keepdims=True)
+        high, rest = two_parts(score)
+        spread[slot, width:] = (high.astype(F32) * mine + rest.astype(F32) * shifted).astype(LOW)
+    inner = dot_t(dy_ref[...], wd_ref[...])
+    gate = gate_ref[...]
+    sigmoid = jax.nn.sigmoid(gate)
+    dgate_ref[...] = (inner * up_ref[...] * swish_slope(gate, sigmoid)).astype(LOW)
+    dup_ref[...] = (inner * gate * sigmoid).astype(LOW)
+    back = dot_t(dgate_ref[...], wg_ref[...]) + dot_t(dup_ref[...], wu_ref[...])
+    spread[:, :width] = back.astype(LOW)
+    half = proj_ref.shape[1] // 2
+    gate, up = proj_ref[:, :half], proj_ref[:, half:]
+    sigmoid = jax.nn.sigmoid(gate)
+    inner = dot_t(grads_ref[...], wo_ref[...])
+    dproj_ref[:, :half] = (inner * up * swish_slope(gate, sigmoid)).astype(LOW)
+    dproj_ref[:, half:] = (inner * gate * sigmoid).astype(LOW)
+    for block, (token, slot) in enumerate(zip(tokens, slots)):
+        total = t_dot(chosen_ref[slot], spread[slot])
+        parts_ref[block, :, :width] = (
+            total[:, :width] + dot_t(dproj_ref[token], wi_ref[...])
+        ).astype(LOW)
+        parts_ref[block, :, width:] = total[:, width:].astype(LOW)
+
+
+def row_grid(kernel, steps, cuts, outs, scratch, flops):
+    def cut(shape):
+        rest = (0,) * (len(shape) - 1)
+        return pl.BlockSpec((shape[0] // steps,) + tuple(shape[1:]), lambda i: (i,) + rest)
+
+    def whole(shape):
+        rest = (0,) * len(shape)
+        return pl.BlockSpec(tuple(shape), lambda i: rest, pipeline_mode=pl.Buffered(1))
+
+    operands = [array for array, _ in cuts]
+    return pl.pallas_call(
+        kernel,
+        grid=(steps,),
+        out_shape=outs,
+        in_specs=[whole(a.shape) if fixed else cut(a.shape) for a, fixed in cuts],
+        out_specs=[cut(o.shape) for o in outs],
+        scratch_shapes=scratch,
+        compiler_params=pltpu.CompilerParams(vmem_limit_bytes=60 << 20),
+        cost_estimate=pl.CostEstimate(flops=flops, bytes_accessed=60 << 20, transcendentals=0),
+    )(*operands)
+
+
+def grad_in_kernel(layer_ref, rows_ref, grads_ref, sent_ref, kept_ref):
+    made = t_dot(rows_ref[...], grads_ref[...])
+    step, half = pl.program_id(0), pl.num_programs(0) // 2
+
+    @pl.when(step < half)
+    def _():
+        sent_ref[...] = made.astype(LOW)
+
+    @pl.when(step >= half)
+    def _():
+        kept_ref[...] = made
+
+
+def grad_in(rows, grads, tile=512):
+    count, width = rows.shape
+    columns = grads.shape[1]
+    half = width // 2 // tile
+    layer = lax.axis_index("fsdp").reshape(1)
+
+    def source(i, layer_ref):
+        return (0, lax.rem(i + (1 - layer_ref[0]) * half, 2 * half))
+
+    return pl.pallas_call(
+        grad_in_kernel,
+        grid_spec=pltpu.PrefetchScalarGridSpec(
+            num_scalar_prefetch=1,
+            grid=(2 * half,),
+            in_specs=[
+                pl.BlockSpec((count, tile), source),
+                pl.BlockSpec((count, columns), lambda i, _: (0, 0)),
+            ],
+            out_specs=[
+                pl.BlockSpec((tile, columns), lambda i, _: (jnp.minimum(i, half - 1), 0)),
+                pl.BlockSpec((tile, columns), lambda i, _: (jnp.maximum(i - half, 0), 0)),
+            ],
+        ),
+        out_shape=[
+            jax.ShapeDtypeStruct((width // 2, columns), LOW),
+            jax.ShapeDtypeStruct((width // 2, columns), F32),
+        ],
+        compiler_params=pltpu.CompilerParams(vmem_limit_bytes=50 << 20),
+        cost_estimate=pl.CostEstimate(
+            flops=2 * count * width * columns, bytes_accessed=16 << 20, transcendentals=0
+        ),
+    )(layer, rows, grads)
+
+
+def grad_out_kernel(layer_ref, inner_ref, grads_ref, sent_ref, kept_ref, made):
+    half = sent_ref.shape[0]
+    layer = layer_ref[0]
+    made[...] = t_dot(inner_ref[...], grads_ref[...])
+    sent_ref[...] = made[pl.ds(pl.multiple_of((1 - layer) * half, 8), half)].astype(LOW)
+    kept_ref[...] = made[pl.ds(pl.multiple_of(layer * half, 8), half)]
+
+
+def grad_out(inner, grads, tile=512):
+    count, units = inner.shape
+    width = grads.shape[1]
+    layer = lax.axis_index("fsdp").reshape(1)
+    return pl.pallas_call(
+        grad_out_kernel,
+        grid_spec=pltpu.PrefetchScalarGridSpec(
+            num_scalar_prefetch=1,
+            grid=(width // tile,),
+            in_specs=[
+                pl.BlockSpec((count, units), lambda i, _: (0, 0)),
+                pl.BlockSpec((count, tile), lambda i, _: (0, i)),
+            ],
+            out_specs=[
+                pl.BlockSpec((units // 2, tile), lambda i, _: (0, i)),
+                pl.BlockSpec((units // 2, tile), lambda i, _: (0, i)),
+            ],
+            scratch_shapes=[pltpu.VMEM((units, tile), F32)],
+        ),
+        out_shape=[
+            jax.ShapeDtypeStruct((units // 2, width), LOW),
+            jax.ShapeDtypeStruct((units // 2, width), F32),
+        ],
+        compiler_params=pltpu.CompilerParams(vmem_limit_bytes=50 << 20),
+        cost_estimate=pl.CostEstimate(
+            flops=2 * count * width * units, bytes_accessed=16 << 20, transcendentals=0
+        ),
+    )(layer, inner, grads)
+
+
 def body(
     tokens,
     cotangent,
@@ -509,17 +847,24 @@
     doc_ids = segments[0]
 
     lat_column = jnp.pad(norm_latent[:, None], ((0, own_rows - lat_rows), (0, 0)))
-    packed_small = jnp.concatenate(
-        [w_latent, w_router, norm_attn[:, None], norm_ffn[:, None], lat_column], axis=1
-    ).astype(LOW)
-    used = packed_small.shape[1]
-    packed_small = jnp.pad(packed_small, ((0, 0), (0, -used % 128)))
-    small = lax.all_gather(packed_small, both, axis=0, tiled=True)
-    latent_w = small[:, : LAT + ROPE]
-    router_w = small[:, LAT + ROPE : LAT + ROPE + experts]
-    gains = small[:, LAT + ROPE + experts : LAT + ROPE + experts + 3].astype(F32).T
-    gain_attn, gain_ffn = gains[0], gains[1]
-    gain_latent = gains[2].reshape(groups * layers, own_rows)[:, :lat_rows].reshape(LAT)
+    at = LAT + ROPE
+    route_columns = routes.reshape(own_rows, tok_rows * TOP // own_rows).astype(F32)
+    packed = [w_latent, w_router, norm_attn[:, None], norm_ffn[:, None], lat_column, route_columns]
+    packed = jnp.concatenate(packed, axis=1).astype(LOW)
+    used = packed.shape[1]
+    last = at + experts
+    packed = jnp.pad(packed, ((0, 0), (0, -used % 128)))
+    small = lax.all_gather(packed, both, axis=0, tiled=True)
+    router_w = jnp.pad(small[:, at:last], ((0, 0), (0, 128 - experts)))
+    all_routes = small[:, last + 3 : used].reshape(groups, layers, -1)
+    all_routes = lax.dynamic_index_in_dim(all_routes, lax.axis_index("fsdp"), 1, keepdims=False)
+    all_routes = all_routes.reshape(groups, tok_rows, TOP)
+    gains = small[:, last : last + 3].astype(F32).T
+    gain_attn, gain_ffn = gains[0:1], gains[1:2]
+    gain_latent = gains[2].reshape(groups * layers, own_rows)[:, :lat_rows].reshape(1, LAT)
+
+    expert_gate_low = w_expert_gate[0].astype(LOW)
+    expert_gate_w = whole_over_layers(expert_gate_low)
 
     fold = lat_rows * (NOPE + VD) // own_rows
     query_parts = w_query.astype(LOW).reshape(own_rows, H, query_width).transpose(1, 0, 2)
@@ -531,38 +876,29 @@
     )
     head_parts = jnp.concatenate([query_parts, expand_parts], axis=2)
     head_parts = lax.all_to_all(head_parts, "seq", split_axis=0, concat_axis=0, tiled=True)
-    head_parts = lax.all_gather(head_parts, "fsdp", axis=1, tiled=False)
+    head_parts = whole_over_layers(head_parts[None]).transpose(1, 0, 2, 3)
     query_w = head_parts[..., :query_width].reshape(width, query_width)
     expand_w = head_parts[..., query_width:].reshape(LAT, NOPE + VD)
-    output_w = lax.all_gather(w_output.astype(LOW), "fsdp", axis=0, tiled=True)
-
-    expert_gate_w = whole_over_layers(w_expert_gate[0].astype(LOW))
-    expert_up_w = whole_over_layers(w_expert_up[0].astype(LOW))
-    expert_down_w = whole_over_layers(w_expert_down[0].astype(LOW))
-    shared_in = jnp.concatenate([w_shared_gate, w_shared_up], axis=1).astype(LOW)
-    shared_in_w = lax.all_gather(shared_in, "fsdp", axis=0, tiled=True)
-    shared_down_w = lax.all_gather(w_shared_down.astype(LOW), "fsdp", axis=0, tiled=True)
+    output_w = whole_over_layers(w_output.astype(LOW))
     units = w_shared_gate.shape[1]
+    padding = -units % 128
+    spare = ((0, 0), (0, padding))
+    shared_in = jnp.concatenate([jnp.pad(w_shared_gate, spare), jnp.pad(w_shared_up, spare)], axis=1)
+    shared_in_w = whole_over_layers(shared_in.astype(LOW))
+    shared_down_w = jnp.pad(whole_over_layers(w_shared_down.astype(LOW)), ((0, padding), (0, 0)))
 
     hidden_low = ring_gather(tokens[0], groups, 1)
+    expert_up_w = whole_over_layers(after(w_expert_up[0].astype(LOW), expert_gate_w, hidden_low))
+    expert_down_w = whole_over_layers(
+        after(w_expert_down[0].astype(LOW), expert_gate_w, hidden_low)
+    )
     grad_low = gather_rows(cotangent[0])
-    all_routes = gather_rows(routes[0])
-
-    scaled_one, _, _ = norm_forward(hidden_low.astype(F32), gain_attn)
-    normed_low = scaled_one.astype(LOW)
-    query_proj = dot(normed_low, query_w)
-    latent_proj = dot(normed_low, latent_w)
+
     cosine, sine = rotary_tables(seq_len, 0)
-    head_q = jnp.concatenate(
-        [query_proj[:, :NOPE], rotate(query_proj[:, NOPE:], cosine, sine)], axis=-1
-    ).astype(LOW)
-    latent_scaled, _, _ = norm_forward(latent_proj[:, :LAT], gain_latent)
-    latent_low = latent_scaled.astype(LOW)
-    expanded = dot(latent_low, expand_w)
-    key_rope = rotate(latent_proj[:, LAT:], cosine, sine)
-    head_k = jnp.concatenate([expanded[:, :NOPE], key_rope], axis=-1).astype(LOW)
-    head_v = expanded[:, NOPE:].astype(LOW)
-
+    table = jnp.concatenate([cosine, cosine, -sine, sine], axis=1)
+    one_low, head_q, head_k, head_v, latent_low, latent_proj = project(
+        hidden_low, gain_attn, query_w, small, gain_latent, expand_w, table
+    )
     head_out, logs = attend_forward(head_q, head_k, head_v, doc_ids)
     part_residual = dot(head_out, output_w).astype(LOW).reshape(groups, tok_rows, width)
 
@@ -573,101 +909,89 @@
 
     own_shape = jax.ShapeDtypeStruct((tok_rows, width), F32)
     residual, two_low = ring_reduce(
-        part_residual, [tokens[0], gain_ffn[None]], [own_shape], make_two, groups, 2, width
+        part_residual, [tokens[0], gain_ffn], [own_shape], make_two, groups, 2, width
     )
     two_low = two_low.reshape(seq_len, width)
-    own_two_low = lax.dynamic_slice_in_dim(two_low, place * tok_rows, tok_rows, 0)
-
-    logits = dot(two_low, router_w)
-    raised = jnp.exp(logits - jnp.max(logits, axis=-1, keepdims=True))
-    router_p = raised / jnp.sum(raised, axis=-1, keepdims=True)
-    own_p = lax.dynamic_slice_in_dim(router_p, place * tok_rows, tok_rows, 0)
-    mine = (jnp.arange(experts, dtype=jnp.int32) == place).astype(F32)
-    gate = jnp.sum(router_p * mine[None, :], axis=-1).reshape(groups, tok_rows)
-    named = jnp.any(all_routes == place, axis=-1).reshape(groups, tok_rows)
+
+    named = jnp.any(all_routes == place.astype(LOW), axis=-1)
     rank = jnp.cumsum(named.astype(jnp.int32), axis=1) - 1
     slots = jnp.arange(capacity, dtype=jnp.int32)
     chosen = named[:, None, :] & (rank[:, None, :] == slots[None, :, None])
-    chosen_low = chosen.astype(LOW)
-    slot_gate = jnp.sum(jnp.where(chosen, gate[:, None, :], 0.0), axis=-1)
-    slot_gate = slot_gate.reshape(groups * capacity, 1)
-
-    def dispatch(rows):
-        picked = jnp.einsum(
-            "brt,btd->brd",
-            chosen_low,
-            rows.reshape(groups, tok_rows, width),
-            preferred_element_type=F32,
-        )
-        return picked.reshape(groups * capacity, width).astype(LOW)
-
-    def combine(rows):
-        spread = jnp.einsum(
-            "brt,brd->btd",
-            chosen_low,
-            rows.reshape(groups, capacity, width),
-            preferred_element_type=F32,
-        )
-        return spread.reshape(seq_len, width)
-
-    expert_in = dispatch(two_low)
-    expert_g = dispatch(grad_low)
-    made_grad = (slot_gate * expert_g.astype(F32)).astype(LOW)
-    gate_proj = dot(expert_in, expert_gate_w)
-    up_proj = dot(expert_in, expert_up_w)
-    sigmoid = jax.nn.sigmoid(gate_proj)
-    inner_low = (gate_proj * sigmoid * up_proj).astype(LOW)
-    made = dot(inner_low, expert_down_w).astype(LOW)
-    inner_grad = dot_t(made_grad, expert_down_w)
-    gate_grad = (inner_grad * up_proj * swish_slope(gate_proj, sigmoid)).astype(LOW)
-    up_grad = (inner_grad * gate_proj * sigmoid).astype(LOW)
-    row_grad = (dot_t(gate_grad, expert_gate_w) + dot_t(up_grad, expert_up_w)).astype(LOW)
-    slot_score = jnp.sum(expert_g.astype(F32) * made.astype(F32), axis=-1)
-    score_grad = jnp.sum(
-        jnp.where(chosen, slot_score.reshape(groups, capacity, 1), 0.0), axis=1
-    )
-    prob_grad = lax.all_to_all(score_grad, "seq", split_axis=0, concat_axis=0, tiled=True).T
-
-    shared_proj = dot(two_low, shared_in_w)
-    shared_gate, shared_up = shared_proj[:, :units], shared_proj[:, units:]
-    shared_sigmoid = jax.nn.sigmoid(shared_gate)
-    shared_low = (shared_gate * shared_sigmoid * shared_up).astype(LOW)
-    shared_back = dot_t(grad_low, shared_down_w)
-    shared_grads = jnp.concatenate(
+    chosen = chosen.astype(LOW).reshape(groups * capacity, tok_rows)
+    lanes = jnp.arange(128, dtype=jnp.int32)
+    mine = jnp.stack(
+        [(lanes == place), (lanes < experts), (lanes == place + experts)] + [lanes < 0] * 5
+    ).astype(F32)
+    slot_count, unit_count = groups * capacity, expert_gate_w.shape[1]
+    columns = shared_in_w.shape[1]
+
+    def array(rows, columns, kind=LOW):
+        return jax.ShapeDtypeStruct((rows, columns), kind)
+
+    steps = groups // 4
+    routed_flops = 6 * slot_count * width * unit_count
+    probs, slot_gate, expert_in, gate_proj, up_proj, inner_low, made, shared_proj, shared_low, part_out = row_grid(
+        ffn_kernel,
+        steps,
         [
-            shared_back * shared_up * swish_slope(shared_gate, shared_sigmoid),
-            shared_back * shared_gate * shared_sigmoid,
-        ],
-        axis=1,
-    ).astype(LOW)
-
-    part_grad = combine(row_grad) + dot_t(shared_grads, shared_in_w)
-    part_out = combine((slot_gate * made.astype(F32)).astype(LOW)) + dot(shared_low, shared_down_w)
-    ffn_out = scatter_rows(part_out.astype(LOW)).astype(F32)
+            (two_low, False), (chosen, False), (mine, True), (router_w, True),
+            (expert_gate_w, True), (expert_up_w, True), (expert_down_w, True),
+            (shared_in_w, True), (shared_down_w, True),
+        ],
+        [
+            array(seq_len, 128, F32), array(slot_count, 1, F32), array(slot_count, width),
+            array(slot_count, unit_count, F32), array(slot_count, unit_count, F32),
+            array(slot_count, unit_count), array(slot_count, width), array(seq_len, columns, F32),
+            array(seq_len, columns // 2), array(seq_len, width),
+        ],
+        [pltpu.VMEM((slot_count // steps, width), LOW)],
+        routed_flops * 3 // 2,
+    )
+    ffn_out = scatter_rows(part_out).astype(F32)
     output = (residual + ffn_out).astype(LOW)
 
-    def spread_grad(grad):
-        if layers != 2:
-            return lax.psum_scatter(
-                grad.astype(LOW), "fsdp", scatter_dimension=0, tiled=True
-            ).astype(F32)
-        layer, half = lax.axis_index("fsdp"), grad.shape[0] // 2
-        sent = lax.dynamic_slice_in_dim(grad, (1 - layer) * half, half, 0).astype(LOW)
-        kept = lax.dynamic_slice_in_dim(grad, layer * half, half, 0)
-        return kept + lax.ppermute(sent, "fsdp", ((0, 1), (1, 0))).astype(F32)
-
-    grad_expert_down = spread_grad(t_dot(inner_low, made_grad))
-    grad_expert_gate = spread_grad(t_dot(expert_in, gate_grad))
-    grad_expert_up = spread_grad(t_dot(expert_in, up_grad))
+    made_grad, gate_grad, up_grad, shared_grads, part_grad = row_grid(
+        ffn_back_kernel,
+        steps,
+        [
+            (grad_low, False), (chosen, False), (mine, True), (slot_gate, False), (made, False),
+            (gate_proj, False), (up_proj, False), (shared_proj, False),
+            (expert_gate_w, True), (expert_up_w, True), (expert_down_w, True),
+            (shared_in_w, True), (shared_down_w, True),
+        ],
+        [
+            array(slot_count, width), array(slot_count, unit_count), array(slot_count, unit_count),
+            array(seq_len, columns),
+            jax.ShapeDtypeStruct((groups, tok_rows, width + 128), LOW),
+        ],
+        [pltpu.VMEM((slot_count // steps, width + 128), LOW)],
+        routed_flops * 3 // 2,
+    )
+
+    if layers == 2:
+        down_sent, down_kept = grad_out(inner_low, made_grad)
+        gate_sent, gate_kept = grad_in(expert_in, gate_grad)
+        up_sent, up_kept = grad_in(expert_in, up_grad)
+        part_grad = after(part_grad, down_sent, gate_sent, up_sent)
+    else:
+        down_kept, down_sent = spread_start(t_dot(inner_low, made_grad))
+        gate_kept, gate_sent = spread_start(t_dot(expert_in, gate_grad))
+        up_kept, up_sent = spread_start(t_dot(expert_in, up_grad))
+    grad_expert_down = spread_end(down_kept, down_sent)
+    grad_expert_gate = spread_end(gate_kept, gate_sent)
+    grad_expert_up = spread_end(up_kept, up_sent)
     grad_shared_in = spread_grad(t_dot(two_low, shared_grads))
-    grad_shared_down = spread_grad(t_dot(shared_low, grad_low))
-
-    logit_grad = own_p * (prob_grad - jnp.sum(own_p * prob_grad, axis=-1, keepdims=True))
-    grad_router = exact_t_dot(own_two_low.astype(F32), logit_grad)
-    router_back = exact_dot_t(logit_grad, router_w.astype(F32))
+    grad_shared_down = spread_grad(t_dot(shared_low, grad_low)[:units])
+
+    own_probs = lax.dynamic_slice_in_dim(probs, place * tok_rows, tok_rows, 0)
 
     def make_attn(total, part, extras, outs):
-        grad = total + extras[0][part]
+        probs = extras[0][part]
+        score = total[:, width:]
+        score = score + jnp.concatenate([score[:, experts:], score[:, :experts]], axis=1)
+        logit = probs * (score - jnp.sum(probs * score, axis=-1, keepdims=True))
+        high, rest = two_parts(logit)
+        grad = total[:, :width] + dot_t(high, extras[4][...]) + dot_t(rest, extras[4][...])
         gain = extras[1][...]
         _, normed, factor = norm_forward(extras[2][part], gain)
         inner = grad * gain
@@ -675,62 +999,40 @@
         back = extras[3][part].astype(F32) + back
         outs[0][part] = back
         outs[1][part] = grad * normed
-        return back.astype(LOW)
+        rest = rest.astype(F32)
+        rest = jnp.concatenate([rest[:, 128 - experts :], rest[:, : 128 - experts]], axis=1)
+        return jnp.concatenate([back, high.astype(F32) + rest], axis=1).astype(LOW)
 
     residual_grad, gain_parts, attn_grad = ring_reduce(
-        part_grad.astype(LOW).reshape(groups, tok_rows, width),
-        [router_back, gain_ffn[None], residual, cotangent[0]],
+        part_grad,
+        [own_probs, gain_ffn, residual, cotangent[0], router_w],
         [own_shape, own_shape],
         make_attn,
         groups,
         3,
-        width,
+        width + 128,
     )
     grad_gain_ffn = jnp.sum(gain_parts, axis=0)
-    attn_grad = attn_grad.reshape(seq_len, width)
-
-    grad_output = spread_grad(t_dot(head_out, attn_grad))
-    head_g = dot_t(attn_grad, output_w).astype(LOW)
+    attn_grad = attn_grad.reshape(seq_len, width + 128)
+
+    own_width = width // groups
+    two_slice = lax.dynamic_slice_in_dim(two_low, place * own_width, own_width, 1)
+    grad_router = t_dot(two_slice, attn_grad[:, width:])
+    grad_router = grad_router[:, :experts] + grad_router[:, experts : 2 * experts]
+
+    grad_output = spread_grad(t_dot(head_out, attn_grad)[:, :width])
+    head_g = dot_t(attn_grad, jnp.pad(output_w, ((0, 0), (0, 128)))).astype(LOW)
     query_grad, key_grad, value_grad = attend_backward(
         head_q, head_k, head_v, doc_ids, logs, head_g
     )
-    query_back = jnp.concatenate(
-        [
-            query_grad[:, :NOPE],
-            rotate_back(query_grad[:, NOPE:].astype(F32), cosine, sine).astype(LOW),
-        ],
-        axis=-1,
-    )
-    expand_back = jnp.concatenate([key_grad[:, :NOPE], value_grad], axis=-1)
-    part_rows = jnp.concatenate(
-        [
-            dot_t(query_back, query_w).astype(LOW),
-            dot_t(expand_back, expand_w).astype(LOW),
-            key_grad[:, NOPE:],
-            jnp.zeros((seq_len, 64), LOW),
-        ],
-        axis=1,
-    )
-
-    def keep(total, part, extras, outs):
-        outs[0][part] = total
-
-    wide = part_rows.shape[1]
-    own_parts = ring_reduce(
-        part_rows.reshape(groups, tok_rows, wide),
-        [],
-        [jax.ShapeDtypeStruct((tok_rows, wide), F32)],
-        keep,
-        groups,
-        4,
-    )[0]
-
-    grad_query_head = t_dot(normed_low, query_back).reshape(
-        groups, layers, own_rows, query_width
-    )
-    grad_expand_head = t_dot(latent_low, expand_back).reshape(groups, layers, own_rows, fold)
-    head_grads = jnp.concatenate([grad_query_head, grad_expand_head], axis=3).astype(LOW)
-    head_grads = lax.psum_scatter(head_grads, "fsdp", scatter_dimension=1, tiled=False)
+    part_rows, grad_query_head, grad_expand_head = project_back(
+        (query_grad, key_grad, value_grad),
+        table, one_low, latent_low, query_w, expand_w, tok_rows,
+    )
+    grad_query_head = grad_query_head.reshape(groups, layers, own_rows, query_width)
+    grad_expand_head = grad_expand_head.reshape(groups, layers, own_rows, fold)
+    head_grads = jnp.concatenate([grad_query_head, grad_expand_head], axis=3).transpose(1, 0, 2, 3)
+    head_grads = spread_grad(head_grads)[0].astype(LOW)
     head_grads = lax.all_to_all(head_grads, "seq", split_axis=0, concat_axis=0, tiled=True)
     grad_query = (
         head_grads[..., :query_width].transpose(1, 0, 2).reshape(own_rows, H * query_width)
@@ -742,45 +1044,67 @@
         .reshape(lat_rows, H * (NOPE + VD))
     ).astype(F32)
 
-    own_low = lax.dynamic_slice_in_dim(normed_low, place * tok_rows, tok_rows, 0)
     own_latent = lax.dynamic_slice_in_dim(latent_proj, place * tok_rows, tok_rows, 0)
-    own_cosine = lax.dynamic_slice_in_dim(cosine, place * tok_rows, tok_rows, 0)
-    own_sine = lax.dynamic_slice_in_dim(sine, place * tok_rows, tok_rows, 0)
-    _, latent_normed, latent_factor = norm_forward(own_latent[:, :LAT], gain_latent)
-    latent_back, grad_gain_latent = norm_backward(
-        own_parts[:, width : width + LAT], latent_normed, latent_factor, gain_latent
-    )
-    rope_back = rotate_back(
-        own_parts[:, width + LAT : width + LAT + ROPE], own_cosine, own_sine
-    )
-    latent_grad = jnp.concatenate([latent_back, rope_back], axis=-1).astype(LOW)
-    grad_latent = t_dot(own_low, latent_grad)
-    one_grad = own_parts[:, :width] + dot_t(latent_grad, latent_w)
+    own_table = lax.dynamic_slice_in_dim(table, place * tok_rows, tok_rows, 0)
+
+    def make_latent(total, part, extras, outs):
+        gain = extras[1][...]
+        grad = total[:, width : width + LAT]
+        _, normed, factor = norm_forward(extras[0][part], gain)
+        inner = grad * gain
+        back = factor * (inner - normed * jnp.mean(inner * normed, axis=-1, keepdims=True))
+        turned = total[:, width + LAT : width + LAT + ROPE]
+        turned = turned * extras[2][part, :ROPE] - swapped(turned) * extras[2][part, ROPE:]
+        outs[0][part] = total[:, :width]
+        outs[1][part] = grad * normed
+        return jnp.concatenate([back, turned, jnp.zeros_like(turned)], axis=1).astype(LOW)
+
+    one_grad, latent_gains, latent_grad = ring_reduce(
+        part_rows,
+        [own_latent, gain_latent, own_table],
+        [own_shape, jax.ShapeDtypeStruct((tok_rows, LAT), F32)],
+        make_latent,
+        groups,
+        4,
+        LAT + 2 * ROPE,
+    )
+    own_latent_grad = lax.dynamic_index_in_dim(latent_grad, place, 0, keepdims=False)
+    one_grad = one_grad + dot_t(own_latent_grad[:, : LAT + ROPE], small[:, : LAT + ROPE])
     _, normed_one, factor_one = norm_forward(hidden_own, gain_attn)
     input_part, grad_gain_attn = norm_backward(one_grad, normed_one, factor_one, gain_attn)
     input_grad = (residual_grad + input_part).astype(LOW)
 
-    lat_spread = jnp.pad(
-        grad_gain_latent.reshape(groups * layers, lat_rows), ((0, 0), (0, own_rows - lat_rows))
-    ).reshape(width)
-    gain_columns = jnp.stack([grad_gain_attn, grad_gain_ffn, lat_spread]).T
-    packed = jnp.concatenate([grad_latent, grad_router, gain_columns], axis=1)
-    packed = jnp.pad(packed, ((0, 0), (0, -used % 128)))
-    packed = lax.psum_scatter(packed, both, scatter_dimension=0, tiled=True)
-    at = LAT + ROPE + experts
+    one_slice = lax.dynamic_slice_in_dim(one_low, place * own_width, own_width, 1)
+    grad_latent = t_dot(one_slice, latent_grad.reshape(seq_len, LAT + 2 * ROPE))
+    gain_sums = jnp.concatenate(
+        [
+            grad_gain_attn.reshape(groups, own_width),
+            grad_gain_ffn.reshape(groups, own_width),
+            jnp.pad(
+                jnp.sum(latent_gains, axis=0).reshape(groups, layers, lat_rows),
+                ((0, 0), (0, 0), (0, own_rows - lat_rows)),
+            ).reshape(groups, own_width),
+        ],
+        axis=1,
+    )
+    gain_sums = lax.all_to_all(gain_sums, "seq", split_axis=0, concat_axis=0, tiled=True)
+    gain_columns = jnp.sum(gain_sums, axis=0).reshape(3, own_width).T
+    packed = jnp.concatenate([grad_latent[:, :at], grad_router, gain_columns], axis=1)
+    packed = jnp.pad(packed, ((0, 0), (0, -packed.shape[1] % 128)))
+    packed = spread_grad(packed, F32)
     return (
         output[None],
         input_grad[None],
-        packed[:, at],
+        packed[:, last],
         grad_query,
-        packed[:, : LAT + ROPE],
-        packed[:lat_rows, at + 2],
+        packed[:, :at],
+        packed[:lat_rows, last + 2],
         grad_expand,
         grad_output,
-        packed[:, at + 1],
-        packed[:, LAT + ROPE : at],
+        packed[:, last + 1],
+        packed[:, at:last],
         grad_shared_in[:, :units],
-        grad_shared_in[:, units:],
+        grad_shared_in[:, units + padding : 2 * units + padding],
         grad_shared_down,
         grad_expert_gate[None],
         grad_expert_up[None],

time: 1230 us -> 806 us (0.66)
  Pallas kernels: 313 us -> 518 us
  blocking collectives: 188 us -> 0 us
  matrix products: 220 us -> 40.3 us
  waiting for transfers between devices: 220 us -> 67.2 us
  local copies, waits for them, and re-layouts: 103 us -> 37.5 us
  other arithmetic: 140 us -> 90.5 us
  starting transfers between devices: 18.9 us -> 32.7 us
    pallas_call x0 -> x7, Pallas kernels: none -> 170 us  [the longest x2 102 us: row_grid(): pl.pallas_call(kernel, grid=(steps,), out_shape=outs, in_specs=[whole(a.s...]
    all_gather x3 -> x0, blocking collectives: 166 us -> none  [the longest x1 135 us: body(): output_w = lax.all_gather(w_output.astype(LOW), 'fsdp', axis=0, tiled=True)]
    ppermute x9 -> x15, waiting for transfers between devices: 197 us -> 67.1 us  [swap_layers(): return lax.ppermute(own, 'fsdp', ((0, 1), (1, 0)))]
    dot_general x10 -> x1, matrix products: 76.1 us -> 5.54 us  [dot(): return jnp.dot(left, right, preferred_element_type=F32)]
    dot_general x9 -> x2, matrix products: 70.5 us -> 9.97 us  [dot_t(): lax.dot_general(left, right, (((1,), (1,)), ((), ())), preferred_element_...]
    dot_general x6 -> x0, matrix products: 27.6 us -> none  [the longest x2 16.4 us: combine(): jnp.einsum('brt,brd->btd', chosen_low, rows.reshape(groups, capacity, wid...]
    unnamed x204 -> x85, local copies, waits for them, and re-layouts: 36.7 us -> 11.5 us
    all_to_all x1 -> x0, blocking collectives: 21.6 us -> none  [body(): lax.all_to_all(head_parts, 'seq', split_axis=0, concat_axis=0, tiled=True)]
  transfers between devices with their start and end apart: 18 -> 21, of which waited for: 4 -> 5; matrix products, arithmetic and copies ran while one was open for 31% -> 18% of each run, Pallas kernels for 17% -> 65%
where the time goes in v3:
time: 806 us; the launch traced here: 801 us
  Pallas kernels  518 us (64%)
  other arithmetic  90.5 us (11%)
  waiting for transfers between devices  67.2 us (8%)
  matrix products  40.3 us (5%)
  local copies, waits for them, and re-layouts  37.5 us (5%)
  starting transfers between devices  32.7 us (4%)
  between operations  14.8 us (2%)
    pallas_call x3, Pallas kernels, ring_reduce(): pl.pallas_call(functools.partial(reduce_kernel, groups, chunks, len(extra...  257 us
    pallas_call x2, Pallas kernels, row_grid(): pl.pallas_call(kernel, grid=(steps,), out_shape=outs, in_specs=[whole(a.s...  102 us
    pallas_call x1, Pallas kernels, ring_gather(): pl.pallas_call(functools.partial(gather_kernel, groups, chunks), out_shap...  69.2 us
    ppermute x15, waiting for transfers between devices, swap_layers(): return lax.ppermute(own, 'fsdp', ((0, 1), (1, 0)))  67.1 us
    pallas_call x2, Pallas kernels, grad_in(): pl.pallas_call(grad_in_kernel, grid_spec=pltpu.PrefetchScalarGridSpec(num...  25.1 us
    dot_general x5, matrix products, t_dot(): lax.dot_general(left, right, (((0,), (0,)), ((), ())), preferred_element_...  24.8 us
    pallas_call x1, Pallas kernels, project(): pl.pallas_call(project_kernel, grid=(seq_len // tile,), out_shape=[jax.Sh...  17.8 us
    ppermute x15, starting transfers between devices, swap_layers(): return lax.ppermute(own, 'fsdp', ((0, 1), (1, 0)))  16.4 us
  transfers between devices with their start and end apart: 21, of which 5 were waited for; matrix products, arithmetic and copies ran while one was open for 18% of the time, Pallas kernels for 65%

profile of v3, /device:TPU:0, one launch (start us, length us, event | category | flops | bytes accessed | tf_op | source)
XLA Modules:
  0.0 801.3 jit_solution(12913424366443039560)
XLA Ops:
  13.1 1.8 convert_element_type.192
  14.9 3.0 collective-permute-start.1
  17.8 1.9 convert_element_type.204
  21.8 6.5 all-to-all-start
  30.0 1.5 collective-permute-start.5
  31.8 4.5 convert_bitcast_fusion.2
  36.8 3.7 multiply_cosine_fusion
  42.7 4.6 convert_bitcast_fusion.1
  47.3 2.1 convert_bitcast_fusion
  50.1 1.4 copy.96.col_ref
  51.5 69.2 %shard_map.297 = bf16[16,128,2048]{2,1,0:T(8,128)(2,1)} custom-call(bf16[128,2048]{1,0:T(8,128)(2,1)} %bitcast.107), custom_call_target="tpu_custom_call" | custom-call | bytes 157286400 | tf_op jit(solution)/shard_map/pallas_call | solution.py:272
  125.3 1.5 collective-permute-start
  126.8 1.6 broadcast_select_fusion.7
  128.5 1.5 pad_maximum_fusion.3.wi_ref
  130.0 4.2 broadcast_select_fusion.5
  134.1 3.0 pad_maximum_fusion.wg_ref
  137.7 2.2 collective-permute-done
  141.6 2.0 collective-permute-start.4
  149.4 1.4 convert_bitcast_fusion.4
  150.8 1.7 slice_reduce_fusion.1
  152.5 1.6 copy.97.refs_2_
  155.5 17.8 %shard_map.298 = (bf16[2048,2048]{1,0:T(8,128)(2,1)}, bf16[2048,192]{1,0:T(8,128)(2,1)S(1)}, bf16[2048,192]{1,0:T(8,128)(2,1)S(1)}, bf16[2048,128]{1,0:T(8,128)(...) custom-call(bf16[2048,2048]{1,0:T(8,128)(2,1)} %bitcast.115, f32[1,2048]{1,0:T(1,128)S(1)} %copy.95.gain_ref, ...), custom_call_target="tpu_custom_call" | custom-call | flops 7549747200 | bytes 29360128 | tf_op jit(solution)/shard_map/pallas_call | solution.py:543
  174.3 8.5 %shard_map.299 = (bf16[2048,128]{1,0:T(8,128)(2,1)S(1)}, f32[2048,1]{1,0:T(8,128)S(1)}) custom-call(bf16[2048,192]{1,0:T(8,128)(2,1)S(1)} %get-tuple-element.62.q_ref, bf16[2048,192]{1,0:T(8,128)(2,1)} %copy-done.14, bf16[2048,128]{1,0:T(8,128)(2,1)S(1)} %get-tuple-element.64.v_ref, s32[2048,1]{1,0:T(8,128)} %copy.96.col_ref, s32[1,2048]{1,0:T(1,128)S(1)} %copy-done.9), custom_call_target="tpu_custom_call" | custom-call | flops 1677721600 | bytes 4194304 | tf_op jit(solution)/shard_map/pallas_call | solution.py:447
  183.8 5.5 convolution_convert_fusion
  189.3 87.7 %shard_map.300 = (f32[128,2048]{1,0:T(8,128)S(1)}, bf16[16,128,2048]{2,1,0:T(8,128)(2,1)}) custom-call(bf16[16,128,2048]{2,1,0:T(8,128)(2,1)} %bitcast.113, bf16[128,2048]{1,0:T(8,128)(2,1)S(1)} %bitcast.108, f32[1,2048]{1,0:T(1,128)S(1)} %copy.97.refs_2_), custom_call_target="tpu_custom_call" | custom-call | bytes 314572800 | tf_op jit(solution)/shard_map/pallas_call | solution.py:408
  278.3 3.2 broadcast_select_fusion.3
  281.5 3.0 pad_maximum_fusion.1.wu_ref
  284.5 2.2 broadcast_select_fusion.1
  286.6 3.2 pad_maximum_fusion.2.wd_ref
  289.9 49.2 %shard_map.301 = (f32[2048,128]{1,0:T(8,128)}, f32[1024,1]{1,0:T(8,128)}, bf16[1024,2048]{1,0:T(8,128)(2,1)}, f32[1024,1408]{1,0:T(8,128)}, f32[1024,1408]{1,0:T...) custom-call(bf16[2048,2048]{1,0:T(8,128)(2,1)} %bitcast.138, ...), custom_call_target="tpu_custom_call" | custom-call | flops 26575110144 | bytes 62914560 | tf_op jit(solution)/shard_map/pallas_call | solution.py:717
  341.2 5.1 fusion.31
  348.4 52.6 %shard_map.302 = (bf16[1024,2048]{1,0:T(8,128)(2,1)}, bf16[1024,1408]{1,0:T(8,128)(2,1)}, bf16[1024,1408]{1,0:T(8,128)(2,1)}, bf16[2048,512]{1,0:T(8,128)(2,1)}, bf16[16,128,2176]{2,1,0:T(8,128)(2,1)}) custom-call(bf16[2048,2048]{1,0:T(8,128)(2,1)} %bitcast.114, bf16[1024,128]{1,0:T(8,128)(2,1)} %fusion.43.chosen_ref, ...), custom_call_target="tpu_custom_call" | custom-call | flops 26575110144 | bytes 62914560 | tf_op jit(solution)/shard_map/pallas_call | solution.py:717
  401.0 11.0 %shard_map.303 = (bf16[704,2048]{1,0:T(8,128)(2,1)}, f32[704,2048]{1,0:T(8,128)}) custom-call(s32[1]{0:T(128)} %bitcast.21.layer_ref, bf16[1024,1408]{1,0:T(8,128)(2,1)} %get-tuple-element.77.inner_ref, bf16[1024,2048]{1,0:T(8,128)(2,1)} %get-tuple-element.78.grads_ref), custom_call_target="tpu_custom_call" | custom-call | flops 5905580032 | bytes 16777216 | tf_op jit(solution)/shard_map/pallas_call | solution.py:788
  412.0 1.8 collective-permute-start.14
  413.7 12.3 %shard_map.305 = (bf16[1024,1408]{1,0:T(8,128)(2,1)}, f32[1024,1408]{1,0:T(8,128)}) custom-call(s32[1]{0:T(128)} %bitcast.21.layer_ref, bf16[1024,2048]{1,0:T(8,128)(2,1)} %get-tuple-element.80.rows_ref, bf16[1024,1408]{1,0:T(8,128)(2,1)} %get-tuple-element.83.grads_ref), custom_call_target="tpu_custom_call" | custom-call | flops 5905580032 | bytes 16777216 | tf_op jit(solution)/shard_map/pallas_call | solution.py:751
  426.3 12.8 %shard_map.304 = (bf16[1024,1408]{1,0:T(8,128)(2,1)}, f32[1024,1408]{1,0:T(8,128)}) custom-call(s32[1]{0:T(128)} %bitcast.21.layer_ref, bf16[1024,2048]{1,0:T(8,128)(2,1)} %get-tuple-element.80.rows_ref, bf16[1024,1408]{1,0:T(8,128)(2,1)} %get-tuple-element.81.grads_ref), custom_call_target="tpu_custom_call" | custom-call | flops 5905580032 | bytes 16777216 | tf_op jit(solution)/shard_map/pallas_call | solution.py:751
  439.1 94.2 %shard_map.306 = (f32[128,2048]{1,0:T(8,128)S(1)}, f32[128,2048]{1,0:T(8,128)S(1)}, bf16[16,128,2176]{2,1,0:T(8,128)(2,1)}) custom-call(bf16[16,128,2176]{2,1,0:T(8,128)(2,1)} %get-tuple-element.85.refs_0_, f32[128,128]{1,0:T(8,128)S(1)} %constant_dynamic-slice_fusion.3.refs_1_, f32[1,2048]{1,0:T(1,128)S(1)} %copy.97.refs_2_, f32[128,2048]{1,0:T(8,128)} %copy-done.2, ...), custom_call_target="tpu_custom_call" | custom-call | bytes 314572800 | tf_op jit(solution)/shard_map/pallas_call | solution.py:408
  533.2 4.7 fusion
  539.7 1.8 collective-permute-start.9
  542.1 6.9 convolution_convert_fusion.1.g_ref
  549.0 13.7 %shard_map.307 = (bf16[2048,192]{1,0:T(8,128)(2,1)}, bf16[2048,192]{1,0:T(8,128)(2,1)}, bf16[2048,128]{1,0:T(8,128)(2,1)}) custom-call(bf16[2048,192]{1,0:T(8,128)(2,1)} %copy-done.13, bf16[2048,192]{1,0:T(8,128)(2,1)} %copy-done.14, bf16[2048,128]{1,0:T(8,128)(2,1)} %copy-done.15, bf16[2048,128]{1,0:T(8,128)(2,1)} %convolution_convert_fusion.1.g_ref, ...), custom_call_target="tpu_custom_call" | custom-call | flops 4194304000 | bytes 6291456 | tf_op jit(solution)/shard_map/pallas_call | solution.py:488
  566.1 14.7 %shard_map.308 = (bf16[16,128,2688]{2,1,0:T(8,128)(2,1)}, f32[2048,192]{1,0:T(8,128)}, f32[512,256]{1,0:T(8,128)S(1)}) custom-call(bf16[2048,192]{1,0:T(8,128)(2,1)S(1)} %copy-done.16, bf16[2048,192]{1,0:T(8,128)(2,1)S(1)} %copy-done.17, bf16[2048,128]{1,0:T(8,128)(2,1)S(1)} %copy-done.18, f32[2048,128]{1,0:T(8,128)} %copy-done.24, ...), custom_call_target="tpu_custom_call" | custom-call | flops 5452595200 | bytes 29360128 | tf_op jit(solution)/shard_map/pallas_call | solution.py:597
  580.8 74.7 %shard_map.309 = (f32[128,2048]{1,0:T(8,128)S(1)}, f32[128,512]{1,0:T(8,128)S(1)}, bf16[16,128,640]{2,1,0:T(8,128)(2,1)}) custom-call(bf16[16,128,2688]{2,1,0:T(8,128)(2,1)} %get-tuple-element.95.refs_0_, f32[128,512]{1,0:T(8,128)S(1)} %constant_dynamic-slice_fusion.2.refs_1_, f32[1,512]{1,0:T(1,128)S(1)} %copy-done.11, ...), custom_call_target="tpu_custom_call" | custom-call | bytes 314572800 | tf_op jit(solution)/shard_map/pallas_call | solution.py:408
  657.8 3.1 fusion.21
  661.6 3.5 all-to-all-start.1
  665.1 1.6 fusion.38
  666.7 3.9 fusion.2
  671.7 9.5 %fusion.51 = f32[2048,512]{0,1:T(8,128)} fusion(bf16[2048,2048]{1,0:T(8,128)(2,1)} %bitcast.140, bf16[2048,512]{1,0:T(8,128)(2,1)S(1)} %copy-done.34), kind=kOutput, calls=%fused_computation.131 | convolution fusion | flops 4294967296 | bytes 14680064 | tf_op jit(solution)/shard_map/dot_general | solution.py:53
  682.4 2.2 fusion.36
  684.6 1.7 dynamic-slice_convert_fusion
  686.3 5.4 collective-permute-done.7
  695.0 1.4 collective-permute-start.10
  696.4 2.0 convert_add_fusion.2
  698.4 8.5 %collective-permute-done.8 = bf16[1,16,64,256]{3,2,1,0:T(8,128)(2,1)} collective-permute-done((bf16[1,16,64,256]{3,2,1,0:T(8,128)(2,1)}, bf16[1,16,64,256]{3,2,1,0:T(8,128)(2,1)}, u32[]{:S(2)}, u32[]{:S(2)}) %collective-permute-start.8) | collective-permute-done | bytes 524320 | tf_op jit(solution)/shard_map/ppermute | solution.py:90
  707.5 2.4 fusion.35
  709.9 6.0 all-to-all-start.2
  716.0 2.2 convert_add_fusion.1
  718.1 11.2 %collective-permute-done.10 = bf16[1024,512]{0,1:T(8,128)(2,1)S(1)} collective-permute-done((bf16[1024,512]{0,1:T(8,128)(2,1)S(1)}, bf16[1024,512]{0,1:T(8,128)(2,1)S(1)}, u32[]{:S(2)}, u32[]{:S(2)}) %collective-permute-start.10) | collective-permute-done | bytes 1048608 | tf_op jit(solution)/shard_map/ppermute | solution.py:90
  729.3 1.9 convert_add_fusion
  735.4 1.9 fusion.34
  737.4 7.5 add_bitcast_fusion
  744.9 5.0 add_bitcast_fusion.1
  749.9 39.8 %collective-permute-done.12 = bf16[1024,1408]{1,0:T(8,128)(2,1)} collective-permute-done((bf16[1024,1408]{1,0:T(8,128)(2,1)}, bf16[1024,1408]{1,0:T(8,128)(2,1)}, u32[]{:S(2)}, u32[]{:S(2)}) %collective-permute-start.12) | collective-permute-done | bytes 2883616 | tf_op jit(solution)/shard_map/ppermute | solution.py:90
  789.7 4.8 add_bitcast_fusion.2
  (213 shorter events, 53.8 us)
Async XLA Ops:
  7.2 12.5 %copy-start.30 = (f32[16,4096]{1,0:T(8,128)S(1)}, f32[16,4096]{1,0:T(8,128)}, u32[]{:S(2)}) copy-start(f32[16,4096]{1,0:T(8,128)} %param.26) | copy-start | bytes 786436
  7.2 12.8 %copy-start.25 = (f32[64,3072]{1,0:T(8,128)S(1)}, f32[64,3072]{1,0:T(8,128)}, u32[]{:S(2)}) copy-start(f32[64,3072]{1,0:T(8,128)} %param.23) | copy-start | bytes 2359300
  7.2 136.4 %all-gather.4.cloned.1.call-start = ((), (), s32[]{:S(2)}) async-start(), calls=%async_computation.4 | async-start | bytes 2703360 | tf_op jit(solution)/shard_map/all_gather | solution.py:857
  14.9 106.4 %collective-permute-start.1 = (bf16[64,2048]{1,0:T(8,128)(2,1)}, bf16[64,2048]{1,0:T(8,128)(2,1)}, u32[]{:S(2)}, u32[]{:S(2)}) collective-permute-start(bf16[64,2048]{1,0:T(8,128)(2,1)} %convert_element_type.192), channel_id=1, source_target_pairs={{0,1},{1,0},{2,3},{3,2},{4,5},{5,4},{6,7},{7,6},{8,9},{9,8},{10,11... | collective-permute-start | bytes 786440 | tf_op jit(solution)/shard_map/ppermute | solution.py:90
  19.7 103.4 %collective-permute-start.6 = (bf16[88,2048]{1,0:T(8,128)(2,1)}, bf16[88,2048]{1,0:T(8,128)(2,1)}, u32[]{:S(2)}, u32[]{:S(2)}) collective-permute-start(bf16[88,2048]{1,0:T(8,128)(2,1)} %convert_element_type.204), channel_id=1, source_target_pairs={{0,1},{1,0},{2,3},{3,2},{4,5},{5,4},{6,7},{7,6},{8,9},{9,8},{10,11... | collective-permute-start | bytes 1081352 | tf_op jit(solution)/shard_map/ppermute | solution.py:90
  19.8 8.5 %copy-start.26 = (f32[1024,176]{0,1:T(8,128)S(1)}, f32[1024,176]{0,1:T(8,128)}, u32[]{:S(2)}) copy-start(f32[1024,176]{0,1:T(8,128)} %param.30) | copy-start | bytes 2162692
  20.7 7.9 copy-start.27
  21.8 103.5 %all-to-all-start = ((bf16[16,64,256]{2,1,0:T(8,128)(2,1)}), bf16[16,64,256]{2,1,0:T(8,128)(2,1)}, u32[]{:S(2)}, u32[]{:S(2)}) async-start(bf16[16,64,256]{2,1,0:T(8,128)(2,1)} %pad_maximum_fusion.5), calls=%async_computation | async-start | bytes 1048576 | tf_op jit(solution)/shard_map/all_to_all | solution.py:878
  28.3 311.7 %all-gather.6.cloned.1.call-start = ((), (), s32[]{:S(2)}) async-start(), calls=%async_computation.6 | async-start | bytes 8912896 | tf_op jit(solution)/shard_map/all_gather | solution.py:124
  30.0 96.8 %collective-permute-start.5 = (bf16[1024,512]{1,0:T(8,128)(2,1)}, bf16[1024,512]{1,0:T(8,128)(2,1)}, u32[]{:S(2)}, u32[]{:S(2)}) collective-permute-start(bf16[1024,512]{1,0:T(8,128)(2,1)} %fusion.29), channel_id=1, source_target_pairs={{0,1},{1,0},{2,3},{3,2},{4,5},{5,4},{6,7},{7,6},{8,9},{9,8},{10,11... | collective-permute-start | bytes 3145736 | tf_op jit(solution)/shard_map/ppermute | solution.py:90
  31.6 703.9 %reduce-scatter.2.cloned.1.call-start = ((), (), s32[]{:S(2)}) async-start(), calls=%async_computation.5 | async-start | bytes 8912896 | tf_op jit(solution)/shard_map/reduce_scatter | solution.py:128
  36.3 93.7 %collective-permute-start.2 = (bf16[1024,1408]{1,0:T(8,128)(2,1)}, bf16[1024,1408]{1,0:T(8,128)(2,1)}, u32[]{:S(2)}, u32[]{:S(2)}) collective-permute-start(bf16[1024,1408]{1,0:T(8,128)(2,1)} %convert_bitcast_fusion.2), channel_id=1, source_target_pairs={{0,1},{1,0},{2,3},{3,2},{4,5},{5,4},{6,7},{7,6},{8,9},{9,8},{10,11... | collective-permute-start | bytes 8650760 | tf_op jit(solution)/shard_map/ppermute | solution.py:90
  40.6 2.0 copy-start
  40.6 6.8 slice-start.4
  41.5 1.0 copy-start.24
  42.7 4.6 slice-start.5
  47.3 2.8 copy-start.9
  51.5 69.8 %copy-start.23 = (f32[64,2048]{1,0:T(8,128)S(1)}, f32[64,2048]{1,0:T(8,128)}, u32[]{:S(2)}) copy-start(f32[64,2048]{1,0:T(8,128)} %param.27) | copy-start | bytes 1572868
  51.5 71.6 %copy-start.21 = (f32[88,2048]{1,0:T(8,128)S(1)}, f32[88,2048]{1,0:T(8,128)}, u32[]{:S(2)}) copy-start(f32[88,2048]{1,0:T(8,128)} %param.32) | copy-start | bytes 2162692
  125.3 14.5 %collective-permute-start = (bf16[1,16,64,256]{3,2,0,1:T(8,128)(2,1)}, bf16[1,16,64,256]{3,2,0,1:T(8,128)(2,1)S(1)}, u32[]{:S(2)}, u32[]{:S(2)}) collective-permute-start(bf16[1,16,64,256]{3,2,0,1:T(8,128)(2,1)} %bitcast.8), channel_id=1, source_target_pairs={{0,1},{1,0},{2,3},{3,2},{4,5},{5,4},{6,7},{7,6},{8,9},{9,8},{10,11... | collective-permute-start | bytes 1572872 | tf_op jit(solution)/shard_map/ppermute | solution.py:90
  137.1 141.2 %collective-permute-start.3 = (bf16[1024,1408]{1,0:T(8,128)(2,1)}, bf16[1024,1408]{1,0:T(8,128)(2,1)}, u32[]{:S(2)}, u32[]{:S(2)}) collective-permute-start(bf16[1024,1408]{1,0:T(8,128)(2,1)} %convert_bitcast_fusion.1), channel_id=1, source_target_pairs={{0,1},{1,0},{2,3},{3,2},{4,5},{5,4},{6,7},{7,6},{8,9},{9,8},{10,11... | collective-permute-start | bytes 8650760 | tf_op jit(solution)/shard_map/ppermute | solution.py:90
  141.1 14.4 %copy-start.4 = (bf16[16,2,64,256]{3,2,1,0:T(8,128)(2,1)}, bf16[16,2,64,256]{3,2,1,0:T(8,128)(2,1)S(1)}, u32[]{:S(2)}) copy-start(bf16[16,2,64,256]{3,2,1,0:T(8,128)(2,1)S(1)} %maximum_bitcast_fusion) | copy-start | bytes 3145732
  141.6 13.9 %copy-start.7 = (bf16[512,256]{1,0:T(8,128)(2,1)}, bf16[512,256]{1,0:T(8,128)(2,1)S(1)}, u32[]{:S(2)}) copy-start(bf16[512,256]{1,0:T(8,128)(2,1)S(1)} %reshape.194.we_ref) | copy-start | bytes 786436
  141.6 142.8 %collective-permute-start.4 = (bf16[704,2048]{1,0:T(8,128)(2,1)}, bf16[704,2048]{1,0:T(8,128)(2,1)}, u32[]{:S(2)}, u32[]{:S(2)}) collective-permute-start(bf16[704,2048]{1,0:T(8,128)(2,1)} %convert_bitcast_fusion), channel_id=1, source_target_pairs={{0,1},{1,0},{2,3},{3,2},{4,5},{5,4},{6,7},{7,6},{8,9},{9,8},{10,11... | collective-permute-start | bytes 8650760 | tf_op jit(solution)/shard_map/ppermute | solution.py:90
  154.2 19.1 %copy-start.10 = (f32[1,512]{1,0:T(1,128)}, f32[1,512]{1,0:T(1,128)S(1)}, u32[]{:S(2)}) copy-start(f32[1,512]{1,0:T(1,128)S(1)} %reshape.193.gain_lat_ref.refs_2_) | copy-start | bytes 6148
  173.3 1.0 copy-start.14
  174.3 8.5 %copy-start.13 = (bf16[2048,192]{1,0:T(8,128)(2,1)}, bf16[2048,192]{1,0:T(8,128)(2,1)S(1)}, u32[]{:S(2)}) copy-start(bf16[2048,192]{1,0:T(8,128)(2,1)S(1)} %get-tuple-element.62.q_ref) | copy-start | bytes 2359300
  174.3 8.6 %copy-start.15 = (bf16[2048,128]{1,0:T(8,128)(2,1)}, bf16[2048,128]{1,0:T(8,128)(2,1)S(1)}, u32[]{:S(2)}) copy-start(bf16[2048,128]{1,0:T(8,128)(2,1)S(1)} %get-tuple-element.64.v_ref) | copy-start | bytes 1572868
  183.8 5.5 copy-start.1
  277.1 4.4 copy-start.2
  281.5 3.0 copy-start.19
  339.9 1.2 copy-start.22
  346.3 1.1 copy-start.20
  348.1 367.8 %collective-permute-start.11 = (bf16[88,2048]{1,0:T(8,128)(2,1)}, bf16[88,2048]{1,0:T(8,128)(2,1)}, u32[]{:S(2)}, u32[]{:S(2)}) collective-permute-start(bf16[88,2048]{1,0:T(8,128)(2,1)} %dynamic-slice_convert_fusion.1), channel_id=1, source_target_pairs={{0,1},{1,0},{2,3},{3,2},{4,5},{5,4},{6,7},{7,6},{8,9},{9,8},{10,11... | collective-permute-start | bytes 1081352 | tf_op jit(solution)/shard_map/ppermute | solution.py:90
  412.0 325.4 %collective-permute-start.14 = (bf16[704,2048]{1,0:T(8,128)(2,1)}, bf16[704,2048]{1,0:T(8,128)(2,1)}, u32[]{:S(2)}, u32[]{:S(2)}) collective-permute-start(bf16[704,2048]{1,0:T(8,128)(2,1)} %get-tuple-element.79), channel_id=1, source_target_pairs={{0,1},{1,0},{2,3},{3,2},{4,5},{5,4},{6,7},{7,6},{8,9},{9,8},{10,11... | collective-permute-start | bytes 8650760 | tf_op jit(solution)/shard_map/ppermute | solution.py:90
  426.1 318.8 %collective-permute-start.13 = (bf16[1024,1408]{1,0:T(8,128)(2,1)}, bf16[1024,1408]{1,0:T(8,128)(2,1)}, u32[]{:S(2)}, u32[]{:S(2)}) collective-permute-start(bf16[1024,1408]{1,0:T(8,128)(2,1)} %get-tuple-element.84), channel_id=1, source_target_pairs={{0,1},{1,0},{2,3},{3,2},{4,5},{5,4},{6,7},{7,6},{8,9},{9,8},{10,11... | collective-permute-start | bytes 8650760 | tf_op jit(solution)/shard_map/ppermute | solution.py:90
  426.3 12.8 %copy-start.5 = (bf16[1,128,2048]{2,1,0:T(8,128)(2,1)S(1)}, bf16[1,128,2048]{2,1,0:T(8,128)(2,1)}, u32[]{:S(2)}) copy-start(bf16[1,128,2048]{2,1,0:T(8,128)(2,1)} %param.19) | copy-start | bytes 1572868
  426.3 12.8 %copy-start.6 = (bf16[2048,128]{1,0:T(8,128)(2,1)S(1)}, bf16[2048,128]{1,0:T(8,128)(2,1)}, u32[]{:S(2)}) copy-start(bf16[2048,128]{1,0:T(8,128)(2,1)} %pad.40.router_ref.refs_5_) | copy-start | bytes 1572868
  537.9 1.0 copy-start.28
  539.7 155.4 %collective-permute-start.9 = (bf16[64,2048]{1,0:T(8,128)(2,1)}, bf16[64,2048]{1,0:T(8,128)(2,1)}, u32[]{:S(2)}, u32[]{:S(2)}) collective-permute-start(bf16[64,2048]{1,0:T(8,128)(2,1)} %dynamic-slice_convert_fusion.2), channel_id=1, source_target_pairs={{0,1},{1,0},{2,3},{3,2},{4,5},{5,4},{6,7},{7,6},{8,9},{9,8},{10,11... | collective-permute-start | bytes 786440 | tf_op jit(solution)/shard_map/ppermute | solution.py:90
  549.0 13.7 %copy-start.8 = (bf16[512,256]{1,0:T(8,128)(2,1)S(1)}, bf16[512,256]{1,0:T(8,128)(2,1)}, u32[]{:S(2)}) copy-start(bf16[512,256]{1,0:T(8,128)(2,1)} %copy-done.7) | copy-start | bytes 786436
  562.6 1.2 copy-start.16
  563.9 1.2 copy-start.17
  565.1 1.0 copy-start.18
  566.1 14.7 %copy-start.11 = (f32[1,512]{1,0:T(1,128)S(1)}, f32[1,512]{1,0:T(1,128)}, u32[]{:S(2)}) copy-start(f32[1,512]{1,0:T(1,128)} %copy-done.10) | copy-start | bytes 6148
  580.8 76.9 %copy-start.32 = (f32[128]{0:T(128)S(1)}, f32[128]{0:T(128)}, u32[]{:S(2)}) copy-start(f32[128]{0:T(128)} %add_rsqrt_fusion) | copy-start | bytes 1540
  655.6 1.0 copy-start.12
  657.8 3.2 copy-start.31
  660.9 9.6 %copy-start.33 = (f32[128]{0:T(128)S(1)}, f32[128]{0:T(128)}, u32[]{:S(2)}) copy-start(f32[128]{0:T(128)} %add_rsqrt_fusion) | copy-start | bytes 1540
  661.6 19.9 %all-to-all-start.1 = ((f32[16,1,384]{2,1,0:T(1,128)}), f32[16,1,384]{2,1,0:T(1,128)S(1)}, u32[]{:S(2)}, u32[]{:S(2)}) async-start(f32[16,1,384]{2,1,0:T(1,128)} %all_to_all.13), calls=%async_computation.2 | async-start | bytes 49152 | tf_op jit(solution)/shard_map/all_to_all | solution.py:1090
  666.6 5.1 copy-start.34
  671.7 9.8 %copy-start.29 = (f32[128,576]{0,1:T(8,128)S(1)}, f32[128,576]{0,1:T(8,128)}, u32[]{:S(2)}) copy-start(f32[128,576]{0,1:T(8,128)} %fusion.2) | copy-start | bytes 884740
  681.7 10.0 %collective-permute-start.7 = (f32[64,640]{0,1:T(8,128)S(1)}, f32[64,640]{0,1:T(8,128)S(1)}, u32[]{:S(2)}, u32[]{:S(2)}) collective-permute-start(f32[64,640]{0,1:T(8,128)S(1)} %constant_dynamic-slice_fusion), channel_id=1, source_target_pairs={{0,1},{1,0},{2,3},{3,2},{4,5},{5,4},{6,7},{7,6},{8,9},{9,8},{10,11... | collective-permute-start | bytes 491528 | tf_op jit(solution)/shard_map/ppermute | solution.py:90
  691.8 15.2 %collective-permute-start.8 = (bf16[1,16,64,256]{3,2,1,0:T(8,128)(2,1)}, bf16[1,16,64,256]{3,2,1,0:T(8,128)(2,1)}, u32[]{:S(2)}, u32[]{:S(2)}) collective-permute-start(bf16[1,16,64,256]{3,2,1,0:T(8,128)(2,1)} %fusion.36), channel_id=1, source_target_pairs={{0,1},{1,0},{2,3},{3,2},{4,5},{5,4},{6,7},{7,6},{8,9},{9,8},{10,11... | collective-permute-start | bytes 1572872 | tf_op jit(solution)/shard_map/ppermute | solution.py:90
  695.0 34.3 %collective-permute-start.10 = (bf16[1024,512]{0,1:T(8,128)(2,1)S(1)}, bf16[1024,512]{0,1:T(8,128)(2,1)S(1)}, u32[]{:S(2)}, u32[]{:S(2)}) collective-permute-start(bf16[1024,512]{0,1:T(8,128)(2,1)S(1)} %dynamic-slice_convert_fusion), channel_id=1, source_target_pairs={{0,1},{1,0},{2,3},{3,2},{4,5},{5,4},{6,7},{7,6},{8,9},{9,8},{10,11... | collective-permute-start | bytes 3145736 | tf_op jit(solution)/shard_map/ppermute | solution.py:90
  706.9 82.8 %collective-permute-start.12 = (bf16[1024,1408]{1,0:T(8,128)(2,1)}, bf16[1024,1408]{1,0:T(8,128)(2,1)}, u32[]{:S(2)}, u32[]{:S(2)}) collective-permute-start(bf16[1024,1408]{1,0:T(8,128)(2,1)} %get-tuple-element.82), channel_id=1, source_target_pairs={{0,1},{1,0},{2,3},{3,2},{4,5},{5,4},{6,7},{7,6},{8,9},{9,8},{10,11... | collective-permute-start | bytes 8650760 | tf_op jit(solution)/shard_map/ppermute | solution.py:90
  709.9 22.4 %all-to-all-start.2 = ((bf16[16,64,256]{2,1,0:T(8,128)(2,1)}), bf16[16,64,256]{2,1,0:T(8,128)(2,1)S(1)}, u32[]{:S(2)}, u32[]{:S(2)}) async-start(bf16[16,64,256]{2,1,0:T(8,128)(2,1)} %fusion.35), calls=%async_computation.3 | async-start | bytes 1048576 | tf_op jit(solution)/shard_map/all_to_all | solution.py:1036
  732.7 2.7 copy-start.3
  737.4 7.5 slice-start
  737.4 7.5 slice-start.1
  744.9 44.8 %slice-start.2 = ((s8[5767168]{0:T(1024)(128)(4,1)}), s8[4194304]{0:T(1024)(128)(4,1)S(1)}, s32[]{:S(2)}) async-start(s8[5767168]{0:T(1024)(128)(4,1)} %bitcast.120), calls=%async_computation.9 | async-start | bytes 8388608
  744.9 44.8 %slice-start.3 = ((s8[5767168]{0:T(1024)(128)(4,1)}), s8[1572864]{0:T(1024)(128)(4,1)S(1)}, s32[]{:S(2)}) async-start(s8[5767168]{0:T(1024)(128)(4,1)} %bitcast.120), calls=%async_computation.10 | async-start | bytes 3145728
Sparse Core Ops, SparseCore 0:
  13.2 67.3 all-gather.3
  82.7 82.7 all-gather.5
  340.1 103.5 reduce-scatter.1

commit v4 on v3

--- a/solution.py
+++ b/solution.py
@@ -3,6 +3,7 @@
 
 import jax
 import jax.numpy as jnp
+import numpy as np
 from jax import lax
 from jax.experimental import pallas as pl
 from jax.experimental.pallas import tpu as pltpu
@@ -21,24 +22,12 @@
 MESH = pl.DeviceIdType.MESH
 
 
-def rotary_tables(count, offset):
-    places = (offset + jnp.arange(count, dtype=jnp.int32)).astype(F32)
-    powers = jnp.arange(ROPE // 2, dtype=jnp.int32).astype(F32) * (2.0 / ROPE)
-    inverse = jnp.exp(powers * -math.log(10000.0))
-    angles = places[:, None] * inverse[None, :]
-    return jnp.cos(angles), jnp.sin(angles)
-
-
-def rotate(values, cosine, sine):
-    half = values.shape[-1] // 2
-    former, latter = values[..., :half], values[..., half:]
-    return jnp.concatenate(
-        [former * cosine - latter * sine, latter * cosine + former * sine], axis=-1
-    )
-
-
-def rotate_back(values, cosine, sine):
-    return rotate(values, cosine, -sine)
+def rotary_table(count):
+    powers = np.arange(ROPE // 2, dtype=np.float32) * np.float32(2.0 / ROPE)
+    inverse = np.exp(powers * np.float32(-math.log(10000.0)))
+    angles = np.arange(count, dtype=np.float32)[:, None] * inverse[None, :]
+    cosine, sine = np.cos(angles), np.sin(angles)
+    return np.concatenate([cosine, cosine, -sine, sine], axis=1)
 
 
 def dot(left, right):
@@ -86,6 +75,15 @@
     return lax.optimization_barrier((value,) + others)[0]
 
 
+def narrow(array):
+    return jnp.concatenate([array[:, i : i + 512] for i in range(0, array.shape[1], 512)])
+
+
+def widen(array, width):
+    rows = array.shape[0] * 512 // width
+    return jnp.concatenate([array[i * rows : (i + 1) * rows] for i in range(width // 512)], axis=1)
+
+
 def swap_layers(own):
     return lax.ppermute(own, "fsdp", ((0, 1), (1, 0)))
 
@@ -99,6 +97,20 @@
     if lax.axis_size("fsdp") != 2:
         return lax.all_gather(own, "fsdp", axis=0, tiled=True)
     return layers_in_order(own, swap_layers(own))
+
+
+def halves_over_layers(own):
+    if lax.axis_size("fsdp") == 2:
+        return own, swap_layers(own)
+    whole = lax.all_gather(own, "fsdp", axis=0, tiled=True)
+    half = whole.shape[0] // 2
+    return whole[:half], whole[half:]
+
+
+def half_columns(pair, count):
+    first = lax.axis_index("fsdp") if pair else 0
+    size = count // 2
+    return [pl.ds(pl.multiple_of(place * size, 64), size) for place in (first, 1 - first)]
 
 
 def spread_start(grad, kind=LOW):
@@ -215,18 +227,21 @@
                 self.forward(0, chunk, way)
         self.aside(0, chunk)
 
+    def turn(self, step):
+        last = self.steps - 1
+        for chunk in range(self.chunks):
+            for way in range(2):
+                half = (chunk < self.chunks // 2) == (way == 0)
+                if step == last and not half:
+                    continue
+                self.arrived(step, chunk, way)
+                if step < last and (step + 1 < last or half):
+                    self.forward(step + 1, chunk, way)
+                self.aside(step + 1 if way == 0 else self.ring - 1 - step, chunk)
+
     def run(self):
-        last = self.steps - 1
         for step in range(self.steps):
-            for chunk in range(self.chunks):
-                for way in range(2):
-                    half = (chunk < self.chunks // 2) == (way == 0)
-                    if step == last and not half:
-                        continue
-                    self.arrived(step, chunk, way)
-                    if step < last and (step + 1 < last or half):
-                        self.forward(step + 1, chunk, way)
-                    self.aside(step + 1 if way == 0 else self.ring - 1 - step, chunk)
+            self.turn(step)
 
     def finish(self):
         for distance in range(self.ring):
@@ -254,38 +269,216 @@
     ]
 
 
-def gather_kernel(groups, chunks, in_ref, out_ref, own_sem, *sems):
-    ring = Gather(groups, chunks, in_ref.shape[0], in_ref, out_ref, sems)
-    spot, core, at = ring.spot, ring.core, ring.at
-    enter((at(spot - 1, core), at(spot + 1, core), at(spot, 1 - core)))
+class Exchange:
+    def __init__(self, groups, source, place_of, sems):
+        self.groups, self.source, self.place_of = groups, source, place_of
+        self.send, self.recv = sems
+        self.me = lax.axis_index("seq")
+
+    def copy(self, turn):
+        other = lax.rem(self.me + turn, self.groups)
+        return pltpu.make_async_remote_copy(
+            src_ref=self.source.at[other],
+            dst_ref=self.place_of(self.me),
+            send_sem=self.send.at[turn],
+            recv_sem=self.recv.at[turn],
+            device_id={"seq": other},
+            device_id_type=MESH,
+        )
+
+    def begin(self):
+        for turn in range(1, self.groups):
+            self.copy(turn).start()
+
+    def arrived(self, turn):
+        origin = lax.rem(self.me - turn + self.groups, self.groups)
+        pltpu.make_async_remote_copy(
+            src_ref=self.place_of(origin),
+            dst_ref=self.place_of(origin),
+            send_sem=self.send.at[turn],
+            recv_sem=self.recv.at[turn],
+            device_id={"seq": lax.rem(self.me + turn, self.groups)},
+            device_id_type=MESH,
+        ).wait_recv()
+        return origin
+
+    def finish(self):
+        for turn in range(1, self.groups):
+            self.copy(turn).wait_send()
+
+
+def enter_all(groups, pair):
+    barrier = pltpu.get_barrier_semaphore()
+    me = lax.axis_index("seq")
+    for turn in range(1, groups):
+        pl.semaphore_signal(
+            barrier, inc=1, device_id={"seq": lax.rem(me + turn, groups)}, device_id_type=MESH
+        )
+    if pair:
+        other = {"fsdp": 1 - lax.axis_index("fsdp")}
+        pl.semaphore_signal(barrier, inc=1, device_id=other, device_id_type=MESH)
+    pl.semaphore_wait(barrier, groups if pair else groups - 1)
+
+
+def across(source, target, send, recv):
+    return pltpu.make_async_remote_copy(
+        src_ref=source,
+        dst_ref=target,
+        send_sem=send,
+        recv_sem=recv,
+        device_id={"fsdp": 1 - lax.axis_index("fsdp")},
+        device_id_type=MESH,
+    )
+
+
+def start_kernel(
+    groups, chunks, pair, rows_ref, small_ref, heads_ref, *rest,
+):
+    if pair:
+        bulk_ref, rows_out, small_out, heads_out, bulk_out, *rest = rest
+    else:
+        rows_out, small_out, heads_out, *rest = rest
+    local_sems, small_y, head_sems, head_recv, head_y, head_y_recv, *sems = rest
+    me, layer = lax.axis_index("seq"), lax.axis_index("fsdp")
+    mine = layer if pair else 0
+    rows = Gather(groups, chunks, rows_ref.shape[0], rows_ref, rows_out, sems[:4])
+    spare = small_ref.shape[0]
+    block = small_out.at[me]
+    part = block.at[pl.ds(pl.multiple_of(mine * spare, spare), spare)]
+    small = Gather(groups, chunks, small_out.shape[1], block, small_out, sems[4:])
+    heads = Exchange(
+        groups, heads_ref, lambda index: heads_out.at[index, mine], (head_sems, head_recv)
+    )
+    enter_all(groups, pair)
+    locals_ = [
+        pltpu.make_async_copy(small_ref, part, local_sems.at[0]),
+        pltpu.make_async_copy(rows_ref, rows_out.at[me], local_sems.at[1]),
+        pltpu.make_async_copy(heads_ref.at[me], heads_out.at[me, mine], local_sems.at[2]),
+    ]
+    for copy in locals_:
+        copy.start()
+    if pair:
+        across(small_ref, part, small_y.at[0], small_y.at[1]).start()
     for chunk in range(chunks):
-        ring.begin(chunk)
-    own = pltpu.make_async_copy(in_ref, out_ref.at[at(spot, core)], own_sem)
-    own.start()
-    ring.run()
-    ring.finish()
-    own.wait()
-
-
-def ring_gather(block, groups, collective_id, chunks=4):
-    rows, columns = block.shape
-    gathered = pl.pallas_call(
-        functools.partial(gather_kernel, groups, chunks),
-        out_shape=jax.ShapeDtypeStruct((groups, rows, columns), block.dtype),
-        in_specs=[pl.BlockSpec(memory_space=pl.ANY)],
-        out_specs=pl.BlockSpec(memory_space=pl.ANY),
-        scratch_shapes=[pltpu.SemaphoreType.DMA] + gather_sems(groups, chunks),
+        rows.begin(chunk)
+    heads.begin()
+    if pair:
+        across(heads_ref.at[me], heads_out.at[me, mine], head_y.at[0], head_y_recv.at[0]).start()
+        theirs = block.at[pl.ds(pl.multiple_of((1 - mine) * spare, spare), spare)]
+        across(theirs, theirs, small_y.at[0], small_y.at[1]).wait_recv()
+        across(bulk_ref, bulk_out, small_y.at[2], small_y.at[3]).start()
+    locals_[0].wait()
+    for chunk in range(chunks):
+        small.begin(chunk)
+    for step in range(rows.steps):
+        small.turn(step)
+        rows.turn(step)
+        if step == 0:
+            for turn in range(1, groups):
+                origin = heads.arrived(turn)
+                if pair:
+                    own = heads_out.at[origin, mine]
+                    across(own, own, head_y.at[turn], head_y_recv.at[turn]).start()
+    small.finish()
+    rows.finish()
+    heads.finish()
+    for copy in locals_[1:]:
+        copy.wait()
+    if pair:
+        across(small_ref, part, small_y.at[0], small_y.at[1]).wait_send()
+        for turn in range(groups):
+            origin = lax.rem(me - turn + groups, groups)
+            theirs = heads_out.at[origin, 1 - mine]
+            copy = across(theirs, theirs, head_y.at[turn], head_y_recv.at[turn])
+            copy.wait_send()
+            copy.wait_recv()
+        copy = across(bulk_ref, bulk_out, small_y.at[2], small_y.at[3])
+        copy.wait_send()
+        copy.wait_recv()
+
+
+def gather_start(rows, small, heads, bulk, groups, layers, collective_id, chunks=4):
+    pair = layers == 2
+    if not pair:
+        small = lax.all_gather(small, "fsdp", axis=0, tiled=True)
+    height = small.shape[0] * (2 if pair else 1)
+    dma = pltpu.SemaphoreType.DMA
+    any_spec = pl.BlockSpec(memory_space=pl.ANY)
+    bulks = [bulk] if pair else []
+    rows_out, small_out, heads_out, *bulk_out = pl.pallas_call(
+        functools.partial(start_kernel, groups, chunks, pair),
+        out_shape=[
+            jax.ShapeDtypeStruct((groups,) + rows.shape, LOW),
+            jax.ShapeDtypeStruct((groups, height, small.shape[1]), LOW),
+            jax.ShapeDtypeStruct((groups, 2 if pair else 1) + heads.shape[1:], LOW),
+        ]
+        + [jax.ShapeDtypeStruct(array.shape, LOW) for array in bulks],
+        in_specs=[any_spec] * (3 + len(bulks)),
+        out_specs=[any_spec] * (3 + len(bulks)),
+        scratch_shapes=[dma((3,)), dma((4,))]
+        + [dma((groups,))] * 4
+        + gather_sems(groups, chunks)
+        + gather_sems(groups, chunks),
         compiler_params=pltpu.CompilerParams(collective_id=collective_id, has_side_effects=True),
-        cost_estimate=pl.CostEstimate(flops=0, bytes_accessed=150 << 20, transcendentals=0),
-    )(block)
-    return gathered.reshape(groups * rows, columns)
-
-
-def reduce_kernel(groups, chunks, extras, outs, rowfn, gathers, *refs):
+        cost_estimate=pl.CostEstimate(flops=0, bytes_accessed=4 << 20, transcendentals=0),
+    )(rows, small, heads, *bulks)
+    if not pair:
+        heads_out = lax.all_gather(heads_out, "fsdp", axis=1, tiled=True)
+    return (
+        rows_out.reshape(groups * rows.shape[0], rows.shape[1]),
+        small_out.reshape(groups * height, small.shape[1]),
+        heads_out,
+        (bulk, bulk_out[0]) if pair else halves_over_layers(bulk),
+    )
+
+
+class HeadGrads:
+    def __init__(self, groups, pair, grads_ref, out_ref, came, total, y_sems, send, recv, own_sem):
+        self.pair, self.grads, self.out = pair, grads_ref, out_ref
+        self.came, self.total, self.y_sems, self.own_sem = came, total, y_sems, own_sem
+        self.mine = lax.axis_index("fsdp") if pair else 0
+        self.groups = groups
+        self.me = lax.axis_index("seq")
+        self.spread = Exchange(groups, total, lambda index: out_ref.at[index], (send, recv))
+
+    def cross(self):
+        return across(self.grads.at[1 - self.mine], self.came, self.y_sems.at[0], self.y_sems.at[1])
+
+    def begin(self):
+        if self.pair:
+            self.cross().start()
+
+    def middle(self):
+        if self.pair:
+            self.cross().wait_recv()
+            total = self.grads[self.mine].astype(F32) + self.came[...].astype(F32)
+            self.total[...] = total.astype(LOW)
+        else:
+            self.total[...] = self.grads[0]
+        self.spread.begin()
+        self.local = pltpu.make_async_copy(
+            self.total.at[self.me], self.out.at[self.me], self.own_sem
+        )
+        self.local.start()
+
+    def finish(self):
+        for turn in range(1, self.groups):
+            self.spread.arrived(turn)
+        self.spread.finish()
+        self.local.wait()
+        if self.pair:
+            self.cross().wait_send()
+
+
+def reduce_kernel(groups, chunks, extras, outs, rowfn, gathers, heads, *refs):
     parts_ref = refs[0]
     extra_refs = refs[1 : 1 + extras]
+    if heads is not None:
+        heads_ref, refs = refs[1 + extras], refs[: 1 + extras] + refs[2 + extras :]
     out_refs = refs[1 + extras : 1 + extras + outs]
     rest = list(refs[1 + extras + outs :])
+    if heads is not None:
+        head_out = rest.pop(0)
     gather_ref = rest.pop(0) if gathers else None
     own, side, came, sent = rest[:4]
     own_sem, side_send, side_recv, send_sem, recv_sem = rest[4:9]
@@ -295,7 +488,12 @@
     ring, steps = groups // 2, groups // 4
     spot, core, at = ring_places(groups)
     sibling = {"seq": at(spot, 1 - core)}
-    enter((at(spot - 1, core), at(spot + 1, core), at(spot, 1 - core)))
+    if heads is None:
+        enter((at(spot - 1, core), at(spot + 1, core), at(spot, 1 - core)))
+    else:
+        head_grads = HeadGrads(groups, heads, heads_ref, head_out, *rest[-6:])
+        enter_all(groups, heads)
+        head_grads.begin()
 
     order = []
     for step in range(steps):
@@ -361,6 +559,8 @@
                 copy = neighbour_copy(way, step, chunk)
                 copy.start()
                 started.append(copy)
+    if heads is not None:
+        head_grads.middle()
     gather = Gather(groups, chunks, rows, ready, gather_ref, rest[10:14]) if gathers else None
     for chunk in range(chunks):
         part = pl.ds(chunk * size, size)
@@ -379,11 +579,15 @@
         gather.run()
         gather.finish()
         local.wait()
+    if heads is not None:
+        head_grads.finish()
     for copy in started:
         copy.wait_send()
 
 
-def ring_reduce(parts, extras, outs, rowfn, groups, collective_id, gathers=None, chunks=4):
+def ring_reduce(
+    parts, extras, outs, rowfn, groups, collective_id, gathers=None, heads=None, chunks=4
+):
     _, rows, columns = parts.shape
     ring, steps = groups // 2, groups // 4
     scratch = [
@@ -399,15 +603,28 @@
     ]
     shapes = list(outs)
     specs = [pl.BlockSpec(memory_space=pltpu.VMEM)] * len(outs)
+    extras = list(extras)
+    count = len(extras)
+    pair = None
+    if heads is not None:
+        pair = heads.shape[0] == 2
+        extras.append(heads)
+        shapes.append(jax.ShapeDtypeStruct(heads.shape[1:], LOW))
+        specs.append(pl.BlockSpec(memory_space=pltpu.VMEM))
     if gathers is not None:
         shapes.append(jax.ShapeDtypeStruct((groups, rows, gathers), LOW))
         specs.append(pl.BlockSpec(memory_space=pl.ANY))
         scratch.append(pltpu.VMEM((rows, gathers), LOW))
         scratch += gather_sems(groups, chunks)
         scratch.append(pltpu.SemaphoreType.DMA)
+    if heads is not None:
+        scratch += [pltpu.VMEM(heads.shape[1:], LOW)] * 2
+        scratch += [pltpu.SemaphoreType.DMA((2,))]
+        scratch += [pltpu.SemaphoreType.DMA((groups,))] * 2
+        scratch += [pltpu.SemaphoreType.DMA]
     return pl.pallas_call(
         functools.partial(
-            reduce_kernel, groups, chunks, len(extras), len(outs), rowfn, gathers is not None
+            reduce_kernel, groups, chunks, count, len(outs), rowfn, gathers is not None, pair
         ),
         out_shape=shapes,
         in_specs=[pl.BlockSpec(memory_space=pl.ANY)]
@@ -418,7 +635,7 @@
             collective_id=collective_id, has_side_effects=True, vmem_limit_bytes=50 << 20
         ),
         cost_estimate=pl.CostEstimate(
-            flops=0, bytes_accessed=(300 if gathers else 150) << 20, transcendentals=0
+            flops=0, bytes_accessed=4 << 20, transcendentals=0
         ),
     )(parts, *extras)
 
@@ -629,12 +846,23 @@
     return high, (values - high.astype(F32)).astype(LOW)
 
 
+def join_halves(pair, own_ref, other_ref, whole_ref):
+    @pl.when(pl.program_id(0) == 0)
+    def _():
+        own, other = half_columns(pair, whole_ref.shape[0])
+        whole_ref[own] = own_ref[...]
+        whole_ref[other] = other_ref[...]
+
+
 def ffn_kernel(
-    rows_ref, chosen_ref, mine_ref, router_ref, wg_ref, wu_ref, wd_ref, wi_ref, wo_ref,
+    pair, rows_ref, chosen_ref, mine_ref, router_ref, wg_own, wg_other, wu_own, wu_other,
+    wd_own, wd_other, wi_ref, wo_ref,
     probs_ref, slot_gate_ref, in_ref, gate_ref, up_ref, inner_ref, made_ref, proj_ref, hs_ref, out_ref,
-    spread,
+    spread, wd_ref,
 ):
     count = 4
+    width = rows_ref.shape[1]
+    join_halves(pair, wd_own, wd_other, wd_ref)
     tokens, slots = blocks_of(rows_ref, count), blocks_of(chosen_ref, count)
     lanes = lax.broadcasted_iota(jnp.int32, mine_ref.shape, 1)
     logits = jnp.where(mine_ref[1:2] > 0, dot(rows_ref[...], router_ref[...]), -1e30)
@@ -650,8 +878,9 @@
         chosen = chosen_ref[slot]
         slot_gate_ref[slot] = jnp.sum(dot(chosen, picked), axis=-1, keepdims=True)
         in_ref[slot] = dot(chosen, rows_ref[token]).astype(LOW)
-    gate = dot(in_ref[...], wg_ref[...])
-    up = dot(in_ref[...], wu_ref[...])
+    own, other = half_columns(pair, width)
+    gate = dot(in_ref[:, own], wg_own[...]) + dot(in_ref[:, other], wg_other[...])
+    up = dot(in_ref[:, own], wu_own[...]) + dot(in_ref[:, other], wu_other[...])
     gate_ref[...] = gate
     up_ref[...] = up
     inner_ref[...] = (gate * jax.nn.sigmoid(gate) * up).astype(LOW)
@@ -669,12 +898,13 @@
 
 
 def ffn_back_kernel(
-    grads_ref, chosen_ref, mine_ref, slot_gate_ref, made_ref, gate_ref, up_ref, proj_ref,
-    wg_ref, wu_ref, wd_ref, wi_ref, wo_ref,
-    dy_ref, dgate_ref, dup_ref, dproj_ref, parts_ref, spread,
+    pair, grads_ref, chosen_ref, mine_ref, slot_gate_ref, made_ref, gate_ref, up_ref, proj_ref,
+    wg_own, wg_other, wu_own, wu_other, wd_own, wd_other, wi_ref, wo_ref,
+    dy_ref, dgate_ref, dup_ref, dproj_ref, parts_ref, spread, wd_ref,
 ):
     count = 4
     width = grads_ref.shape[1]
+    join_halves(pair, wd_own, wd_other, wd_ref)
     tokens, slots = blocks_of(grads_ref, count), blocks_of(chosen_ref, count)
     mine, shifted = mine_ref[0:1], mine_ref[2:3]
     for token, slot in zip(tokens, slots):
@@ -688,8 +918,11 @@
     sigmoid = jax.nn.sigmoid(gate)
     dgate_ref[...] = (inner * up_ref[...] * swish_slope(gate, sigmoid)).astype(LOW)
     dup_ref[...] = (inner * gate * sigmoid).astype(LOW)
-    back = dot_t(dgate_ref[...], wg_ref[...]) + dot_t(dup_ref[...], wu_ref[...])
-    spread[:, :width] = back.astype(LOW)
+    own, other = half_columns(pair, width)
+    back = dot_t(dgate_ref[...], wg_own[...]) + dot_t(dup_ref[...], wu_own[...])
+    spread[:, own] = back.astype(LOW)
+    back = dot_t(dgate_ref[...], wg_other[...]) + dot_t(dup_ref[...], wu_other[...])
+    spread[:, other] = back.astype(LOW)
     half = proj_ref.shape[1] // 2
     gate, up = proj_ref[:, :half], proj_ref[:, half:]
     sigmoid = jax.nn.sigmoid(gate)
@@ -854,7 +1087,21 @@
     used = packed.shape[1]
     last = at + experts
     packed = jnp.pad(packed, ((0, 0), (0, -used % 128)))
-    small = lax.all_gather(packed, both, axis=0, tiled=True)
+
+    fold = lat_rows * (NOPE + VD) // own_rows
+    query_parts = w_query.astype(LOW).reshape(own_rows, H, query_width).transpose(1, 0, 2)
+    expand_parts = (
+        w_expand.astype(LOW)
+        .reshape(lat_rows, H, NOPE + VD)
+        .transpose(1, 0, 2)
+        .reshape(H, own_rows, fold)
+    )
+    head_parts = jnp.concatenate([query_parts, expand_parts], axis=2)
+    hidden_low, small, head_parts, expert_gate_w = gather_start(
+        tokens[0], packed, head_parts, w_expert_gate[0].astype(LOW), groups, layers, 1
+    )
+    query_w = head_parts[..., :query_width].reshape(width, query_width)
+    expand_w = head_parts[..., query_width:].reshape(LAT, NOPE + VD)
     router_w = jnp.pad(small[:, at:last], ((0, 0), (0, 128 - experts)))
     all_routes = small[:, last + 3 : used].reshape(groups, layers, -1)
     all_routes = lax.dynamic_index_in_dim(all_routes, lax.axis_index("fsdp"), 1, keepdims=False)
@@ -863,39 +1110,32 @@
     gain_attn, gain_ffn = gains[0:1], gains[1:2]
     gain_latent = gains[2].reshape(groups * layers, own_rows)[:, :lat_rows].reshape(1, LAT)
 
-    expert_gate_low = w_expert_gate[0].astype(LOW)
-    expert_gate_w = whole_over_layers(expert_gate_low)
-
-    fold = lat_rows * (NOPE + VD) // own_rows
-    query_parts = w_query.astype(LOW).reshape(own_rows, H, query_width).transpose(1, 0, 2)
-    expand_parts = (
-        w_expand.astype(LOW)
-        .reshape(lat_rows, H, NOPE + VD)
-        .transpose(1, 0, 2)
-        .reshape(H, own_rows, fold)
-    )
-    head_parts = jnp.concatenate([query_parts, expand_parts], axis=2)
-    head_parts = lax.all_to_all(head_parts, "seq", split_axis=0, concat_axis=0, tiled=True)
-    head_parts = whole_over_layers(head_parts[None]).transpose(1, 0, 2, 3)
-    query_w = head_parts[..., :query_width].reshape(width, query_width)
-    expand_w = head_parts[..., query_width:].reshape(LAT, NOPE + VD)
-    output_w = whole_over_layers(w_output.astype(LOW))
     units = w_shared_gate.shape[1]
     padding = -units % 128
     spare = ((0, 0), (0, padding))
     shared_in = jnp.concatenate([jnp.pad(w_shared_gate, spare), jnp.pad(w_shared_up, spare)], axis=1)
-    shared_in_w = whole_over_layers(shared_in.astype(LOW))
-    shared_down_w = jnp.pad(whole_over_layers(w_shared_down.astype(LOW)), ((0, padding), (0, 0)))
-
-    hidden_low = ring_gather(tokens[0], groups, 1)
-    expert_up_w = whole_over_layers(after(w_expert_up[0].astype(LOW), expert_gate_w, hidden_low))
-    expert_down_w = whole_over_layers(
-        after(w_expert_down[0].astype(LOW), expert_gate_w, hidden_low)
-    )
-    grad_low = gather_rows(cotangent[0])
-
-    cosine, sine = rotary_tables(seq_len, 0)
-    table = jnp.concatenate([cosine, cosine, -sine, sine], axis=1)
+    shared_in = shared_in.astype(LOW)
+    shared_in = after(shared_in, hidden_low)
+    down_low, output_low = w_shared_down.astype(LOW), w_output.astype(LOW)
+    if layers == 2:
+        lone = jnp.concatenate([shared_in, narrow(down_low), narrow(output_low)])
+        pair_of = swap_layers(lone)
+        cut = shared_in.shape[0]
+        end = cut + narrow(down_low).shape[0]
+        shared_in_w = layers_in_order(shared_in, pair_of[:cut])
+        shared_down_w = layers_in_order(down_low, widen(pair_of[cut:end], width))
+        output_w = layers_in_order(output_low, widen(pair_of[end:], width))
+    else:
+        shared_in_w = whole_over_layers(shared_in)
+        shared_down_w = whole_over_layers(down_low)
+        output_w = whole_over_layers(output_low)
+    shared_down_w = jnp.pad(shared_down_w, ((0, padding), (0, 0)))
+
+    expert_up_w = halves_over_layers(after(w_expert_up[0].astype(LOW), hidden_low))
+    expert_down_w = halves_over_layers(after(w_expert_down[0].astype(LOW), hidden_low))
+    grad_low = gather_rows(after(cotangent[0], hidden_low))
+
+    table = jnp.asarray(rotary_table(seq_len))
     one_low, head_q, head_k, head_v, latent_low, latent_proj = project(
         hidden_low, gain_attn, query_w, small, gain_latent, expand_w, table
     )
@@ -911,7 +1151,7 @@
     residual, two_low = ring_reduce(
         part_residual, [tokens[0], gain_ffn], [own_shape], make_two, groups, 2, width
     )
-    two_low = two_low.reshape(seq_len, width)
+    two_low = after(two_low, grad_low).reshape(seq_len, width)
 
     named = jnp.any(all_routes == place.astype(LOW), axis=-1)
     rank = jnp.cumsum(named.astype(jnp.int32), axis=1) - 1
@@ -922,7 +1162,8 @@
     mine = jnp.stack(
         [(lanes == place), (lanes < experts), (lanes == place + experts)] + [lanes < 0] * 5
     ).astype(F32)
-    slot_count, unit_count = groups * capacity, expert_gate_w.shape[1]
+    slot_count, unit_count = groups * capacity, w_expert_gate.shape[2]
+    expert_w = [(half, True) for half in expert_gate_w + expert_up_w + expert_down_w]
     columns = shared_in_w.shape[1]
 
     def array(rows, columns, kind=LOW):
@@ -931,12 +1172,11 @@
     steps = groups // 4
     routed_flops = 6 * slot_count * width * unit_count
     probs, slot_gate, expert_in, gate_proj, up_proj, inner_low, made, shared_proj, shared_low, part_out = row_grid(
-        ffn_kernel,
+        functools.partial(ffn_kernel, layers == 2),
         steps,
         [
             (two_low, False), (chosen, False), (mine, True), (router_w, True),
-            (expert_gate_w, True), (expert_up_w, True), (expert_down_w, True),
-            (shared_in_w, True), (shared_down_w, True),
+            *expert_w, (shared_in_w, True), (shared_down_w, True),
         ],
         [
             array(seq_len, 128, F32), array(slot_count, 1, F32), array(slot_count, width),
@@ -944,27 +1184,26 @@
             array(slot_count, unit_count), array(slot_count, width), array(seq_len, columns, F32),
             array(seq_len, columns // 2), array(seq_len, width),
         ],
-        [pltpu.VMEM((slot_count // steps, width), LOW)],
+        [pltpu.VMEM((slot_count // steps, width), LOW), pltpu.VMEM((unit_count, width), LOW)],
         routed_flops * 3 // 2,
     )
     ffn_out = scatter_rows(part_out).astype(F32)
     output = (residual + ffn_out).astype(LOW)
 
     made_grad, gate_grad, up_grad, shared_grads, part_grad = row_grid(
-        ffn_back_kernel,
+        functools.partial(ffn_back_kernel, layers == 2),
         steps,
         [
             (grad_low, False), (chosen, False), (mine, True), (slot_gate, False), (made, False),
             (gate_proj, False), (up_proj, False), (shared_proj, False),
-            (expert_gate_w, True), (expert_up_w, True), (expert_down_w, True),
-            (shared_in_w, True), (shared_down_w, True),
+            *expert_w, (shared_in_w, True), (shared_down_w, True),
         ],
         [
             array(slot_count, width), array(slot_count, unit_count), array(slot_count, unit_count),
             array(seq_len, columns),
             jax.ShapeDtypeStruct((groups, tok_rows, width + 128), LOW),
         ],
-        [pltpu.VMEM((slot_count // steps, width + 128), LOW)],
+        [pltpu.VMEM((slot_count // steps, width + 128), LOW), pltpu.VMEM((unit_count, width), LOW)],
         routed_flops * 3 // 2,
     )
 
@@ -980,8 +1219,8 @@
     grad_expert_down = spread_end(down_kept, down_sent)
     grad_expert_gate = spread_end(gate_kept, gate_sent)
     grad_expert_up = spread_end(up_kept, up_sent)
-    grad_shared_in = spread_grad(t_dot(two_low, shared_grads))
-    grad_shared_down = spread_grad(t_dot(shared_low, grad_low)[:units])
+    shared_in_kept, shared_in_sent = spread_start(t_dot(two_low, shared_grads))
+    shared_down_kept, shared_down_sent = spread_start(t_dot(shared_low, grad_low)[:units])
 
     own_probs = lax.dynamic_slice_in_dim(probs, place * tok_rows, tok_rows, 0)
 
@@ -1020,7 +1259,19 @@
     grad_router = t_dot(two_slice, attn_grad[:, width:])
     grad_router = grad_router[:, :experts] + grad_router[:, experts : 2 * experts]
 
-    grad_output = spread_grad(t_dot(head_out, attn_grad)[:, :width])
+    output_kept, output_sent = spread_start(t_dot(head_out, attn_grad)[:, :width])
+    if layers == 2:
+        lone = jnp.concatenate([shared_in_sent, narrow(shared_down_sent), narrow(output_sent)])
+        pair_of = swap_layers(lone)
+        cut = shared_in_sent.shape[0]
+        end = cut + narrow(shared_down_sent).shape[0]
+        grad_shared_in = shared_in_kept + pair_of[:cut].astype(F32)
+        grad_shared_down = shared_down_kept + widen(pair_of[cut:end], width).astype(F32)
+        grad_output = output_kept + widen(pair_of[end:], width).astype(F32)
+    else:
+        grad_shared_in = spread_end(shared_in_kept, shared_in_sent)
+        grad_shared_down = spread_end(shared_down_kept, shared_down_sent)
+        grad_output = spread_end(output_kept, output_sent)
     head_g = dot_t(attn_grad, jnp.pad(output_w, ((0, 0), (0, 128)))).astype(LOW)
     query_grad, key_grad, value_grad = attend_backward(
         head_q, head_k, head_v, doc_ids, logs, head_g
@@ -1032,18 +1283,9 @@
     grad_query_head = grad_query_head.reshape(groups, layers, own_rows, query_width)
     grad_expand_head = grad_expand_head.reshape(groups, layers, own_rows, fold)
     head_grads = jnp.concatenate([grad_query_head, grad_expand_head], axis=3).transpose(1, 0, 2, 3)
-    head_grads = spread_grad(head_grads)[0].astype(LOW)
-    head_grads = lax.all_to_all(head_grads, "seq", split_axis=0, concat_axis=0, tiled=True)
-    grad_query = (
-        head_grads[..., :query_width].transpose(1, 0, 2).reshape(own_rows, H * query_width)
-    ).astype(F32)
-    grad_expand = (
-        head_grads[..., query_width:]
-        .reshape(H, lat_rows, NOPE + VD)
-        .transpose(1, 0, 2)
-        .reshape(lat_rows, H * (NOPE + VD))
-    ).astype(F32)
-
+    head_grads = head_grads.astype(LOW)
+    if layers != 2:
+        head_grads = lax.psum_scatter(head_grads, "fsdp", scatter_dimension=0, tiled=True)
     own_latent = lax.dynamic_slice_in_dim(latent_proj, place * tok_rows, tok_rows, 0)
     own_table = lax.dynamic_slice_in_dim(table, place * tok_rows, tok_rows, 0)
 
@@ -1059,7 +1301,7 @@
         outs[1][part] = grad * normed
         return jnp.concatenate([back, turned, jnp.zeros_like(turned)], axis=1).astype(LOW)
 
-    one_grad, latent_gains, latent_grad = ring_reduce(
+    one_grad, latent_gains, head_grads, latent_grad = ring_reduce(
         part_rows,
         [own_latent, gain_latent, own_table],
         [own_shape, jax.ShapeDtypeStruct((tok_rows, LAT), F32)],
@@ -1067,7 +1309,18 @@
         groups,
         4,
         LAT + 2 * ROPE,
-    )
+        head_grads,
+    )
+    grad_query = (
+        head_grads[..., :query_width].transpose(1, 0, 2).reshape(own_rows, H * query_width)
+    ).astype(F32)
+    grad_expand = (
+        head_grads[..., query_width:]
+        .reshape(H, lat_rows, NOPE + VD)
+        .transpose(1, 0, 2)
+        .reshape(lat_rows, H * (NOPE + VD))
+    ).astype(F32)
+
     own_latent_grad = lax.dynamic_index_in_dim(latent_grad, place, 0, keepdims=False)
     one_grad = one_grad + dot_t(own_latent_grad[:, : LAT + ROPE], small[:, : LAT + ROPE])
     _, normed_one, factor_one = norm_forward(hidden_own, gain_attn)

time: 806 us -> 740 us (0.918)
  waiting for transfers between devices: 67.2 us -> 9.79 us
  Pallas kernels: 518 us -> 550 us
  other arithmetic: 90.5 us -> 59.4 us
  starting transfers between devices: 32.7 us -> 14 us
  local copies, waits for them, and re-layouts: 37.5 us -> 51.7 us
    ppermute x15 -> x8, waiting for transfers between devices: 67.1 us -> 9.76 us  [swap_layers(): return lax.ppermute(own, 'fsdp', ((0, 1), (1, 0)))]
    pallas_call x4, Pallas kernels: 326 us -> 355 us  [the longest x3 267 us: ring_reduce(): pl.pallas_call(functools.partial(reduce_kernel, groups, chunks, count, le...]
    all_to_all x2 -> x0, starting transfers between devices: 12.5 us -> none  [the longest x1 6.46 us: body(): lax.all_to_all(head_parts, 'seq', split_axis=0, concat_axis=0, tiled=True)]
    select_n x7 -> x3, other arithmetic: 14.4 us -> 2.61 us  [layers_in_order(): jnp.where(first, own, other)]
    concatenate x6 -> x3, other arithmetic: 12.6 us -> 3.41 us  [layers_in_order(): jnp.concatenate([jnp.where(first, own, other), jnp.where(first, other, ow...]
    unnamed x85 -> x89, local copies, waits for them, and re-layouts: 11.5 us -> 20.4 us
    ppermute x15 -> x8, starting transfers between devices: 16.4 us -> 9.14 us  [swap_layers(): return lax.ppermute(own, 'fsdp', ((0, 1), (1, 0)))]
  transfers between devices with their start and end apart: 21 -> 11, of which waited for: 5 -> 2; matrix products, arithmetic and copies ran while one was open for 18% -> 17% of each run, Pallas kernels for 65% -> 56%
where the time goes in v4:
time: 740 us; the launch traced here: 734 us
  Pallas kernels  550 us (74%)
  other arithmetic  59.4 us (8%)
  local copies, waits for them, and re-layouts  51.7 us (7%)
  matrix products  34.2 us (5%)
  between operations  15 us (2%)
  starting transfers between devices  14 us (2%)
  waiting for transfers between devices  9.79 us (1%)
    pallas_call x3, Pallas kernels, ring_reduce(): pl.pallas_call(functools.partial(reduce_kernel, groups, chunks, count, le...  267 us
    pallas_call x2, Pallas kernels, row_grid(): pl.pallas_call(kernel, grid=(steps,), out_shape=outs, in_specs=[whole(a.s...  103 us
    pallas_call x1, Pallas kernels, gather_start(): pl.pallas_call(functools.partial(start_kernel, groups, chunks, pair), out...  87.1 us
    pallas_call x2, Pallas kernels, grad_in(): pl.pallas_call(grad_in_kernel, grid_spec=pltpu.PrefetchScalarGridSpec(num...  24.9 us
    dot_general x5, matrix products, t_dot(): lax.dot_general(left, right, (((0,), (0,)), ((), ())), preferred_element_...  22.3 us
    unnamed x89, local copies, waits for them, and re-layouts  20.4 us
    pallas_call x1, Pallas kernels, project(): pl.pallas_call(project_kernel, grid=(seq_len // tile,), out_shape=[jax.Sh...  17.8 us
  transfers between devices with their start and end apart: 11, of which 2 were waited for; matrix products, arithmetic and copies ran while one was open for 17% of the time, Pallas kernels for 56%

profile of v4, /device:TPU:0, one launch (start us, length us, event | category | flops | bytes accessed | tf_op | source)
XLA Modules:
  0.0 733.8 jit_solution(10417896828466291993)
XLA Ops:
  14.1 1.2 convert_element_type.143
  16.1 4.5 convert_bitcast_fusion.2.rest_0_.wg_own
  21.5 87.1 %shard_map.306 = (bf16[16,128,2048]{2,1,0:T(8,128)(2,1)}, bf16[16,128,640]{2,1,0:T(8,128)(2,1)}, bf16[16,2,64,256]{3,2,1,0:T(8,128)(2,1)}, bf16[1024,1408]{1,0:T(8,128)(2,1)}) custom-call(bf16[128,2048]{1,0:T(8,128)(2,1)} %bitcast.91, bf16[64,640]{1,0:T(8,128)(2,1)} %pad.39.small_ref, bf16[16,64,256]{2,1,0:T(8,128)(2,1)} %pad_maximum_fusion.2.heads_ref, ...), custom_call_target="tpu_custom_call" | custom-call | bytes 4194304 | tf_op jit(solution)/shard_map/pallas_call | solution.py:408
  110.2 1.0 constant_dynamic-update-slice_fusion
  116.4 1.5 collective-permute-start
  117.9 4.5 convert_bitcast_fusion.1.wu_own
  122.9 2.0 convert_bitcast_fusion.wd_own
  124.9 1.5 collective-permute-start.2
  126.5 1.3 slice.281
  127.8 1.2 slice.280
  129.8 1.4 copy.110.col_ref
  134.6 1.3 convert_bitcast_fusion.4
  136.0 1.9 slice_reduce_fusion.1
  137.9 1.6 copy.113.refs_2_
  139.6 1.9 copy.109.gain_ref
  142.4 17.8 %shard_map.307 = (bf16[2048,2048]{1,0:T(8,128)(2,1)}, bf16[2048,192]{1,0:T(8,128)(2,1)S(1)}, bf16[2048,192]{1,0:T(8,128)(2,1)S(1)}, bf16[2048,128]{1,0:T(8,128)(...) custom-call(bf16[2048,2048]{1,0:T(8,128)(2,1)} %bitcast.128, f32[1,2048]{1,0:T(1,128)S(1)} %copy.109.gain_ref, ...), custom_call_target="tpu_custom_call" | custom-call | flops 7549747200 | bytes 29360128 | tf_op jit(solution)/shard_map/pallas_call | solution.py:760
  161.2 8.5 %shard_map.308 = (bf16[2048,128]{1,0:T(8,128)(2,1)S(1)}, f32[2048,1]{1,0:T(8,128)S(1)}) custom-call(bf16[2048,192]{1,0:T(8,128)(2,1)S(1)} %get-tuple-element.73.q_ref, bf16[2048,192]{1,0:T(8,128)(2,1)} %copy-done.11, bf16[2048,128]{1,0:T(8,128)(2,1)S(1)} %get-tuple-element.75.v_ref, s32[2048,1]{1,0:T(8,128)} %copy.110.col_ref, s32[1,2048]{1,0:T(1,128)S(1)} %copy-done.8), custom_call_target="tpu_custom_call" | custom-call | flops 1677721600 | bytes 4194304 | tf_op jit(solution)/shard_map/pallas_call | solution.py:664
  173.7 1.1 broadcast_select_fusion.5
  174.9 5.6 convolution_convert_fusion
  180.4 87.6 %shard_map.309 = (f32[128,2048]{1,0:T(8,128)S(1)}, bf16[16,128,2048]{2,1,0:T(8,128)(2,1)}) custom-call(bf16[16,128,2048]{2,1,0:T(8,128)(2,1)} %bitcast.98, bf16[128,2048]{1,0:T(8,128)(2,1)S(1)} %bitcast.92, f32[1,2048]{1,0:T(1,128)S(1)} %copy.113.refs_2_), custom_call_target="tpu_custom_call" | custom-call | bytes 4194304 | tf_op jit(solution)/shard_map/pallas_call | solution.py:625
  268.1 1.4 fusion.44
  270.5 1.1 fusion.25.wo_ref
  271.6 1.4 broadcast_select_fusion.1
  273.0 1.5 pad_maximum_fusion.wi_ref
  274.4 2.9 collective-permute-done.2.wd_other
  277.4 50.1 %shard_map.310 = (f32[2048,128]{1,0:T(8,128)}, f32[1024,1]{1,0:T(8,128)}, bf16[1024,2048]{1,0:T(8,128)(2,1)}, f32[1024,1408]{1,0:T(8,128)}, f32[1024,1408]{1,0:T...) custom-call(bf16[2048,2048]{1,0:T(8,128)(2,1)} %bitcast.125, ...), custom_call_target="tpu_custom_call" | custom-call | flops 26575110144 | bytes 62914560 | tf_op jit(solution)/shard_map/pallas_call | solution.py:950
  327.4 52.8 %shard_map.311 = (bf16[1024,2048]{1,0:T(8,128)(2,1)}, bf16[1024,1408]{1,0:T(8,128)(2,1)}, bf16[1024,1408]{1,0:T(8,128)(2,1)}, bf16[2048,512]{1,0:T(8,128)(2,1)}, bf16[16,128,2176]{2,1,0:T(8,128)(2,1)}) custom-call(bf16[2048,2048]{1,0:T(8,128)(2,1)} %all-gather.2.cloned.1.call-done.grads_ref, bf16[1024,128]{1,0:T(8,128)(2,1)} %fusion.36.chosen_ref, ...), custom_call_target="tpu_custom_call" | custom-call | flops 26575110144 | bytes 62914560 | tf_op jit(solution)/shard_map/pallas_call | solution.py:950
  380.2 7.7 %fusion.46 = f32[2048,512]{1,0:T(8,128)S(1)} fusion(bf16[2048,2048]{1,0:T(8,128)(2,1)} %bitcast.126, bf16[2048,512]{1,0:T(8,128)(2,1)} %get-tuple-element.119), kind=kOutput, calls=%fused_computation.127 | convolution fusion | flops 4294967296 | bytes 14680064 | tf_op jit(solution)/shard_map/dot_general | solution.py:42
  387.9 12.5 %shard_map.312 = (bf16[704,2048]{1,0:T(8,128)(2,1)}, f32[704,2048]{1,0:T(8,128)}) custom-call(s32[1]{0:T(128)} %bitcast.20.layer_ref, bf16[1024,1408]{1,0:T(8,128)(2,1)} %get-tuple-element.92.inner_ref, bf16[1024,2048]{1,0:T(8,128)(2,1)} %get-tuple-element.93.grads_ref), custom_call_target="tpu_custom_call" | custom-call | flops 5905580032 | bytes 16777216 | tf_op jit(solution)/shard_map/pallas_call | solution.py:1021
  400.4 1.4 collective-permute-start.7
  401.8 12.3 %shard_map.313 = (bf16[1024,1408]{1,0:T(8,128)(2,1)}, f32[1024,1408]{1,0:T(8,128)}) custom-call(s32[1]{0:T(128)} %bitcast.20.layer_ref, bf16[1024,2048]{1,0:T(8,128)(2,1)} %get-tuple-element.95.rows_ref, bf16[1024,1408]{1,0:T(8,128)(2,1)} %get-tuple-element.96.grads_ref), custom_call_target="tpu_custom_call" | custom-call | flops 5905580032 | bytes 16777216 | tf_op jit(solution)/shard_map/pallas_call | solution.py:984
  414.1 12.6 %shard_map.314 = (bf16[1024,1408]{1,0:T(8,128)(2,1)}, f32[1024,1408]{1,0:T(8,128)}) custom-call(s32[1]{0:T(128)} %bitcast.20.layer_ref, bf16[1024,2048]{1,0:T(8,128)(2,1)} %get-tuple-element.95.rows_ref, bf16[1024,1408]{1,0:T(8,128)(2,1)} %get-tuple-element.98.grads_ref), custom_call_target="tpu_custom_call" | custom-call | flops 5905580032 | bytes 16777216 | tf_op jit(solution)/shard_map/pallas_call | solution.py:984
  427.5 1.3 collective-permute-start.5
  428.8 5.2 fusion.26
  434.9 93.4 %shard_map.315 = (f32[128,2048]{1,0:T(8,128)S(1)}, f32[128,2048]{1,0:T(8,128)S(1)}, bf16[16,128,2176]{2,1,0:T(8,128)(2,1)}) custom-call(bf16[16,128,2176]{2,1,0:T(8,128)(2,1)} %get-tuple-element.100.refs_0_, f32[128,128]{1,0:T(8,128)S(1)} %constant_dynamic-slice_fusion.3.refs_1_, f32[1,2048]{1,0:T(1,128)S(1)} %copy.113.refs_2_, f32[128,2048]{1,0:T(8,128)} %copy-done.1, ...), custom_call_target="tpu_custom_call" | custom-call | bytes 4194304 | tf_op jit(solution)/shard_map/pallas_call | solution.py:625
  528.3 1.1 fusion.24
  532.1 4.8 fusion
  540.3 3.3 convolution_convert_fusion.1.g_ref
  543.6 13.9 %shard_map.316 = (bf16[2048,192]{1,0:T(8,128)(2,1)}, bf16[2048,192]{1,0:T(8,128)(2,1)}, bf16[2048,128]{1,0:T(8,128)(2,1)}) custom-call(bf16[2048,192]{1,0:T(8,128)(2,1)} %copy-done.10, bf16[2048,192]{1,0:T(8,128)(2,1)} %copy-done.11, bf16[2048,128]{1,0:T(8,128)(2,1)} %copy-done.12, bf16[2048,128]{1,0:T(8,128)(2,1)} %convolution_convert_fusion.1.g_ref, ...), custom_call_target="tpu_custom_call" | custom-call | flops 4194304000 | bytes 6291456 | tf_op jit(solution)/shard_map/pallas_call | solution.py:705
  557.5 1.2 copy-done.13
  558.7 1.2 copy-done.14
  560.0 1.0 copy-done.15
  561.0 14.7 %shard_map.317 = (bf16[16,128,2688]{2,1,0:T(8,128)(2,1)}, f32[2048,192]{1,0:T(8,128)}, f32[512,256]{1,0:T(8,128)S(1)}) custom-call(bf16[2048,192]{1,0:T(8,128)(2,1)S(1)} %copy-done.13, bf16[2048,192]{1,0:T(8,128)(2,1)S(1)} %copy-done.14, bf16[2048,128]{1,0:T(8,128)(2,1)S(1)} %copy-done.15, f32[2048,128]{1,0:T(8,128)} %constant.60.clone.table_ref, ...), custom_call_target="tpu_custom_call" | custom-call | flops 5452595200 | bytes 29360128 | tf_op jit(solution)/shard_map/pallas_call | solution.py:814
  576.4 1.2 reshape.185
  577.6 2.7 convert.56
  580.5 1.6 copy_bitcast_fusion.refs_4_
  582.0 86.4 %shard_map.318 = (f32[128,2048]{1,0:T(8,128)S(1)}, f32[128,512]{1,0:T(8,128)S(1)}, bf16[16,64,256]{2,1,0:T(8,128)(2,1)S(1)}, bf16[16,128,640]{2,1,0:T(8,128)(2,1)}) custom-call(bf16[16,128,2688]{2,1,0:T(8,128)(2,1)} %get-tuple-element.110.refs_0_, f32[128,512]{1,0:T(8,128)S(1)} %constant_dynamic-slice_fusion.2.refs_1_, ...), custom_call_target="tpu_custom_call" | custom-call | bytes 4194304 | tf_op jit(solution)/shard_map/pallas_call | solution.py:625
  668.4 1.0 copy-done.9
  670.6 3.1 fusion.21
  674.4 4.6 all-to-all-start
  679.0 3.0 fusion.2
  682.0 1.2 fusion.30
  683.2 1.6 fusion.31
  686.0 1.3 collective-permute-start.3
  688.1 1.3 reshape.192
  689.4 6.8 collective-permute-done.3
  698.9 2.2 convert_add_fusion
  701.2 1.2 copy.127
  702.4 1.2 copy.126
  704.5 1.0 fusion.42
  707.4 7.5 %add_bitcast_fusion = f32[1,704,2048]{2,1,0:T(8,128)} fusion(f32[704,2048]{1,0:T(8,128)} %get-tuple-element.123, bf16[704,2048]{1,0:T(8,128)(2,1)} %collective-permute-done.7), kind=kLoop, calls=%fused_computation.3 | loop fusion | flops 2883584 | bytes 14417920 | tf_op jit(solution)/shard_map/broadcast_in_dim | solution.py:1364
  714.9 5.0 add_bitcast_fusion.1
  719.9 4.9 add_bitcast_fusion.2
  724.8 1.9 fusion.29
  (191 shorter events, 44.5 us)
Async XLA Ops:
  7.2 267.3 %all-gather.2.cloned.1.call-start = ((), (), s32[]{:S(2)}) async-start(), calls=%async_computation.2 | async-start | bytes 8912896 | tf_op jit(solution)/shard_map/all_gather | solution.py:136
  20.6 88.4 %copy-start.22 = (f32[64,2048]{1,0:T(8,128)S(1)}, f32[64,2048]{1,0:T(8,128)}, u32[]{:S(2)}) copy-start(f32[64,2048]{1,0:T(8,128)} %param.28) | copy-start | bytes 1572868
  21.5 87.5 %copy-start.18 = (f32[88,2048]{1,0:T(8,128)S(1)}, f32[88,2048]{1,0:T(8,128)}, u32[]{:S(2)}) copy-start(f32[88,2048]{1,0:T(8,128)} %param.33) | copy-start | bytes 2162692
  21.5 87.5 %copy-start.23 = (f32[1024,176]{0,1:T(8,128)S(1)}, f32[1024,176]{0,1:T(8,128)}, u32[]{:S(2)}) copy-start(f32[1024,176]{0,1:T(8,128)} %param.31) | copy-start | bytes 2162692
  108.7 1.1 copy-start.24
  108.7 616.1 %reduce-scatter.2.cloned.1.call-start = ((), (), s32[]{:S(2)}) async-start(), calls=%async_computation.3 | async-start | bytes 8912896 | tf_op jit(solution)/shard_map/reduce_scatter | solution.py:140
  110.2 12.7 %slice-start.4 = ((s8[5767168]{0:T(1024)(128)(4,1)}), s8[4194304]{0:T(1024)(128)(4,1)S(1)}, s32[]{:S(2)}) async-start(s8[5767168]{0:T(1024)(128)(4,1)} %bitcast.103), calls=%async_computation.8 | async-start | bytes 8388608
  116.4 6.5 slice-start.5
  116.4 56.4 %collective-permute-start = (bf16[1632,512]{1,0:T(8,128)(2,1)}, bf16[1632,512]{1,0:T(8,128)(2,1)}, u32[]{:S(2)}, u32[]{:S(2)}) collective-permute-start(bf16[1632,512]{1,0:T(8,128)(2,1)} %slice_dynamic-update-slice_fusion.12), channel_id=1, source_target_pairs={{0,1},{1,0},{2,3},{3,2},{4,5},{5,4},{6,7},{7,6},{8,9},{9,8},{10,11... | collective-permute-start | bytes 5013512 | tf_op jit(solution)/shard_map/ppermute | solution.py:88
  122.4 7.4 %copy-start.8 = (s32[1,2048]{1,0:T(1,128)S(1)}, s32[1,2048]{1,0:T(1,128)}, u32[]{:S(2)}) copy-start(s32[1,2048]{1,0:T(1,128)} %row_ref.3) | copy-start | bytes 24580
  122.4 152.0 %collective-permute-start.1 = (bf16[1024,1408]{1,0:T(8,128)(2,1)}, bf16[1024,1408]{1,0:T(8,128)(2,1)}, u32[]{:S(2)}, u32[]{:S(2)}) collective-permute-start(bf16[1024,1408]{1,0:T(8,128)(2,1)} %convert_bitcast_fusion.1.wu_own), channel_id=1, source_target_pairs={{0,1},{1,0},{2,3},{3,2},{4,5},{5,4},{6,7},{7,6},{8,9},{9,8},{10,11... | collective-permute-start | bytes 8650760 | tf_op jit(solution)/shard_map/ppermute | solution.py:88
  124.9 152.4 %collective-permute-start.2 = (bf16[704,2048]{1,0:T(8,128)(2,1)}, bf16[704,2048]{1,0:T(8,128)(2,1)}, u32[]{:S(2)}, u32[]{:S(2)}) collective-permute-start(bf16[704,2048]{1,0:T(8,128)(2,1)} %convert_bitcast_fusion.wd_own), channel_id=1, source_target_pairs={{0,1},{1,0},{2,3},{3,2},{4,5},{5,4},{6,7},{7,6},{8,9},{9,8},{10,11... | collective-permute-start | bytes 8650760 | tf_op jit(solution)/shard_map/ppermute | solution.py:88
  126.5 7.6 %copy-start.7 = (bf16[16,2,64,256]{3,2,1,0:T(8,128)(2,1)S(1)}, bf16[16,2,64,256]{3,2,1,0:T(8,128)(2,1)}, u32[]{:S(2)}) copy-start(bf16[16,2,64,256]{3,2,1,0:T(8,128)(2,1)} %get-tuple-element.72) | copy-start | bytes 3145732
  134.6 7.8 %copy-start.5 = (bf16[512,256]{1,0:T(8,128)(2,1)}, bf16[512,256]{1,0:T(8,128)(2,1)S(1)}, u32[]{:S(2)}) copy-start(bf16[512,256]{1,0:T(8,128)(2,1)S(1)} %reshape.177.we_ref) | copy-start | bytes 786436
  160.2 1.0 copy-start.11
  161.2 8.6 %copy-start.10 = (bf16[2048,192]{1,0:T(8,128)(2,1)}, bf16[2048,192]{1,0:T(8,128)(2,1)S(1)}, u32[]{:S(2)}) copy-start(bf16[2048,192]{1,0:T(8,128)(2,1)S(1)} %get-tuple-element.73.q_ref) | copy-start | bytes 2359300
  161.2 8.6 %copy-start.12 = (bf16[2048,128]{1,0:T(8,128)(2,1)}, bf16[2048,128]{1,0:T(8,128)(2,1)S(1)}, u32[]{:S(2)}) copy-start(bf16[2048,128]{1,0:T(8,128)(2,1)S(1)} %get-tuple-element.75.v_ref) | copy-start | bytes 1572868
  161.2 11.3 %copy-start = (bf16[1,128,2048]{2,1,0:T(8,128)(2,1)S(1)}, bf16[1,128,2048]{2,1,0:T(8,128)(2,1)}, u32[]{:S(2)}) copy-start(bf16[1,128,2048]{2,1,0:T(8,128)(2,1)} %param.19) | copy-start | bytes 1572868
  180.4 89.9 %copy-start.19 = (f32[88,2048]{1,0:T(8,128)S(1)}, f32[88,2048]{1,0:T(8,128)}, u32[]{:S(2)}) copy-start(f32[88,2048]{1,0:T(8,128)} %param.33) | copy-start | bytes 2162692
  268.1 3.5 copy-start.1
  387.9 140.4 %copy-start.21 = (f32[2048,512]{1,0:T(8,128)}, f32[2048,512]{1,0:T(8,128)S(1)}, u32[]{:S(2)}) copy-start(f32[2048,512]{1,0:T(8,128)S(1)} %fusion.46) | copy-start | bytes 12582916
  400.4 306.9 %collective-permute-start.7 = (bf16[704,2048]{1,0:T(8,128)(2,1)}, bf16[704,2048]{1,0:T(8,128)(2,1)}, u32[]{:S(2)}, u32[]{:S(2)}) collective-permute-start(bf16[704,2048]{1,0:T(8,128)(2,1)} %get-tuple-element.94), channel_id=1, source_target_pairs={{0,1},{1,0},{2,3},{3,2},{4,5},{5,4},{6,7},{7,6},{8,9},{9,8},{10,11... | collective-permute-start | bytes 8650760 | tf_op jit(solution)/shard_map/ppermute | solution.py:88
  414.1 14.7 %copy-start.20 = (bf16[2048,256]{1,0:T(8,128)(2,1)S(1)}, bf16[2048,256]{1,0:T(8,128)(2,1)}, u32[]{:S(2)}) copy-start(bf16[2048,256]{1,0:T(8,128)(2,1)} %get-tuple-element.120) | copy-start | bytes 3145732
  426.7 288.1 %collective-permute-start.6 = (bf16[1024,1408]{1,0:T(8,128)(2,1)}, bf16[1024,1408]{1,0:T(8,128)(2,1)}, u32[]{:S(2)}, u32[]{:S(2)}) collective-permute-start(bf16[1024,1408]{1,0:T(8,128)(2,1)} %get-tuple-element.99), channel_id=1, source_target_pairs={{0,1},{1,0},{2,3},{3,2},{4,5},{5,4},{6,7},{7,6},{8,9},{9,8},{10,11... | collective-permute-start | bytes 8650760 | tf_op jit(solution)/shard_map/ppermute | solution.py:88
  427.5 292.4 %collective-permute-start.5 = (bf16[1024,1408]{1,0:T(8,128)(2,1)}, bf16[1024,1408]{1,0:T(8,128)(2,1)}, u32[]{:S(2)}, u32[]{:S(2)}) collective-permute-start(bf16[1024,1408]{1,0:T(8,128)(2,1)} %get-tuple-element.97), channel_id=1, source_target_pairs={{0,1},{1,0},{2,3},{3,2},{4,5},{5,4},{6,7},{7,6},{8,9},{9,8},{10,11... | collective-permute-start | bytes 8650760 | tf_op jit(solution)/shard_map/ppermute | solution.py:88
  428.8 6.1 copy-start.3
  428.8 6.1 copy-start.4
  434.0 95.5 %copy-start.16 = (f32[176,2048]{1,0:T(8,128)}, f32[176,2048]{1,0:T(8,128)S(1)}, u32[]{:S(2)}) copy-start(f32[176,2048]{1,0:T(8,128)S(1)} %fusion.26) | copy-start | bytes 4325380
  532.1 8.2 %copy-start.27 = (bf16[128,2048]{1,0:T(8,128)(2,1)S(1)}, bf16[128,2048]{1,0:T(8,128)(2,1)}, u32[]{:S(2)}) copy-start(bf16[128,2048]{1,0:T(8,128)(2,1)} %pad_maximum_fusion.3) | copy-start | bytes 1572868
  532.1 8.2 %copy-start.28 = (bf16[16,128,2176]{2,1,0:T(8,128)(2,1)S(1)}, bf16[16,128,2176]{2,1,0:T(8,128)(2,1)}, u32[]{:S(2)}) copy-start(bf16[16,128,2176]{2,1,0:T(8,128)(2,1)} %get-tuple-element.103) | copy-start | bytes 26738692
  536.9 6.6 copy-start.25
  539.5 159.3 %collective-permute-start.4 = (bf16[1632,512]{1,0:T(8,128)(2,1)}, bf16[1632,512]{1,0:T(8,128)(2,1)}, u32[]{:S(2)}, u32[]{:S(2)}) collective-permute-start(bf16[1632,512]{1,0:T(8,128)(2,1)} %slice_dynamic-update-slice_fusion.8), channel_id=1, source_target_pairs={{0,1},{1,0},{2,3},{3,2},{4,5},{5,4},{6,7},{7,6},{8,9},{9,8},{10,11... | collective-permute-start | bytes 5013512 | tf_op jit(solution)/shard_map/ppermute | solution.py:88
  543.6 13.9 %copy-start.6 = (bf16[512,256]{1,0:T(8,128)(2,1)S(1)}, bf16[512,256]{1,0:T(8,128)(2,1)}, u32[]{:S(2)}) copy-start(bf16[512,256]{1,0:T(8,128)(2,1)} %copy-done.5) | copy-start | bytes 786436
  557.5 1.2 copy-start.13
  558.7 1.2 copy-start.14
  560.0 1.0 copy-start.15
  668.4 1.1 copy-start.9
  674.4 11.4 %all-to-all-start = ((f32[16,1,384]{2,1,0:T(1,128)}), f32[16,1,384]{2,1,0:T(1,128)S(1)}, u32[]{:S(2)}, u32[]{:S(2)}) async-start(f32[16,1,384]{2,1,0:T(1,128)} %all_to_all.6), calls=%async_computation.1 | async-start | bytes 49152 | tf_op jit(solution)/shard_map/all_to_all | solution.py:1343
  686.0 10.2 %collective-permute-start.3 = (f32[64,640]{0,1:T(8,128)S(1)}, f32[64,640]{0,1:T(8,128)S(1)}, u32[]{:S(2)}, u32[]{:S(2)}) collective-permute-start(f32[64,640]{0,1:T(8,128)S(1)} %constant_dynamic-slice_fusion), channel_id=1, source_target_pairs={{0,1},{1,0},{2,3},{3,2},{4,5},{5,4},{6,7},{7,6},{8,9},{9,8},{10,11... | collective-permute-start | bytes 491528 | tf_op jit(solution)/shard_map/ppermute | solution.py:88
  701.2 5.2 copy-start.17
  702.4 3.2 copy-start.26
  707.4 7.5 %slice-start.2 = ((s8[5767168]{0:T(1024)(128)(4,1)}), s8[4194304]{0:T(1024)(128)(4,1)S(1)}, s32[]{:S(2)}) async-start(s8[5767168]{0:T(1024)(128)(4,1)} %bitcast.101), calls=%async_computation.6 | async-start | bytes 8388608
  707.4 7.5 %slice-start.3 = ((s8[5767168]{0:T(1024)(128)(4,1)}), s8[1572864]{0:T(1024)(128)(4,1)S(1)}, s32[]{:S(2)}) async-start(s8[5767168]{0:T(1024)(128)(4,1)} %bitcast.101), calls=%async_computation.7 | async-start | bytes 3145728
  714.9 5.0 slice-start
  714.9 5.0 slice-start.1
  719.9 4.9 copy-start.2
Sparse Core Ops, SparseCore 0:
  108.8 72.2 all-gather.1
  327.6 101.9 reduce-scatter.1

commit v5 on v4

--- a/solution.py
+++ b/solution.py
@@ -105,12 +105,6 @@
     whole = lax.all_gather(own, "fsdp", axis=0, tiled=True)
     half = whole.shape[0] // 2
     return whole[:half], whole[half:]
-
-
-def half_columns(pair, count):
-    first = lax.axis_index("fsdp") if pair else 0
-    size = count // 2
-    return [pl.ds(pl.multiple_of(place * size, 64), size) for place in (first, 1 - first)]
 
 
 def spread_start(grad, kind=LOW):
@@ -227,7 +221,7 @@
                 self.forward(0, chunk, way)
         self.aside(0, chunk)
 
-    def turn(self, step):
+    def turn(self, step, beside=None):
         last = self.steps - 1
         for chunk in range(self.chunks):
             for way in range(2):
@@ -238,10 +232,12 @@
                 if step < last and (step + 1 < last or half):
                     self.forward(step + 1, chunk, way)
                 self.aside(step + 1 if way == 0 else self.ring - 1 - step, chunk)
-
-    def run(self):
+                if beside is not None:
+                    beside.step()
+
+    def run(self, beside=None):
         for step in range(self.steps):
-            self.turn(step)
+            self.turn(step, beside)
 
     def finish(self):
         for distance in range(self.ring):
@@ -331,14 +327,71 @@
     )
 
 
-def start_kernel(
-    groups, chunks, pair, rows_ref, small_ref, heads_ref, *rest,
-):
+def cast_cuts(rows):
+    return 4 if rows % 64 == 0 else 1
+
+
+class Cast:
+    def __init__(self, source, target, wide, low, loads, stores):
+        self.source, self.target, self.wide, self.low = source, target, wide, low
+        self.loads, self.stores = loads, stores
+        self.count = cast_cuts(source.shape[0])
+        self.size = source.shape[0] // self.count
+
+    def part(self, piece):
+        return pl.ds(piece * self.size, self.size)
+
+    def load(self, piece):
+        return pltpu.make_async_copy(
+            self.source.at[self.part(piece)], self.wide.at[piece % 2], self.loads.at[piece]
+        )
+
+    def store(self, piece):
+        return pltpu.make_async_copy(
+            self.low.at[piece], self.target.at[self.part(piece)], self.stores.at[piece]
+        )
+
+    def begin(self):
+        for piece in range(min(2, self.count)):
+            self.load(piece).start()
+
+    def step(self, piece):
+        if piece >= self.count:
+            return
+        self.load(piece).wait()
+        self.low[piece] = self.wide[piece % 2].astype(LOW)
+        self.store(piece).start()
+        if piece + 2 < self.count:
+            self.load(piece + 2).start()
+
+    def finish(self):
+        for piece in range(self.count):
+            self.store(piece).wait()
+
+
+def cast_scratch(array):
+    rows, columns = array.shape
+    count = cast_cuts(rows)
+    return [
+        pltpu.VMEM((2, rows // count, columns), F32),
+        pltpu.VMEM((count, rows // count, columns), LOW),
+        pltpu.SemaphoreType.DMA((count,)),
+        pltpu.SemaphoreType.DMA((count,)),
+    ]
+
+
+def start_kernel(groups, chunks, pair, rows_ref, small_ref, heads_ref, *rest):
+    sources, rest = rest[:3], rest[3:]
+    rows_out, small_out, heads_out, *rest = rest
+    targets, rest = rest[:3], rest[3:]
     if pair:
-        bulk_ref, rows_out, small_out, heads_out, bulk_out, *rest = rest
-    else:
-        rows_out, small_out, heads_out, *rest = rest
-    local_sems, small_y, head_sems, head_recv, head_y, head_y_recv, *sems = rest
+        bulk_out, *rest = rest
+    casts = [
+        Cast(source, target, *rest[4 * i : 4 * i + 4])
+        for i, (source, target) in enumerate(zip(sources, targets))
+    ]
+    rest = rest[12:]
+    local_sems, small_y, bulk_y, head_sems, head_recv, head_y, head_y_recv, *sems = rest
     me, layer = lax.axis_index("seq"), lax.axis_index("fsdp")
     mine = layer if pair else 0
     rows = Gather(groups, chunks, rows_ref.shape[0], rows_ref, rows_out, sems[:4])
@@ -349,7 +402,8 @@
     heads = Exchange(
         groups, heads_ref, lambda index: heads_out.at[index, mine], (head_sems, head_recv)
     )
-    enter_all(groups, pair)
+    for cast in casts:
+        cast.begin()
     locals_ = [
         pltpu.make_async_copy(small_ref, part, local_sems.at[0]),
         pltpu.make_async_copy(rows_ref, rows_out.at[me], local_sems.at[1]),
@@ -357,6 +411,18 @@
     ]
     for copy in locals_:
         copy.start()
+
+    def bulk(piece):
+        start = piece * casts[0].size
+        size = min(casts[0].size, bulk_out.shape[0] - start)
+        return across(
+            casts[0].low.at[piece, pl.ds(0, size)],
+            bulk_out.at[pl.ds(start, size)],
+            bulk_y.at[0, piece],
+            bulk_y.at[1, piece],
+        )
+
+    enter_all(groups, pair)
     if pair:
         across(small_ref, part, small_y.at[0], small_y.at[1]).start()
     for chunk in range(chunks):
@@ -366,11 +432,16 @@
         across(heads_ref.at[me], heads_out.at[me, mine], head_y.at[0], head_y_recv.at[0]).start()
         theirs = block.at[pl.ds(pl.multiple_of((1 - mine) * spare, spare), spare)]
         across(theirs, theirs, small_y.at[0], small_y.at[1]).wait_recv()
-        across(bulk_ref, bulk_out, small_y.at[2], small_y.at[3]).start()
     locals_[0].wait()
     for chunk in range(chunks):
         small.begin(chunk)
+    for piece in range(casts[0].count):
+        casts[0].step(piece)
+        if pair:
+            bulk(piece).start()
     for step in range(rows.steps):
+        casts[1].step(step)
+        casts[2].step(step)
         small.turn(step)
         rows.turn(step)
         if step == 0:
@@ -392,44 +463,201 @@
             copy = across(theirs, theirs, head_y.at[turn], head_y_recv.at[turn])
             copy.wait_send()
             copy.wait_recv()
-        copy = across(bulk_ref, bulk_out, small_y.at[2], small_y.at[3])
-        copy.wait_send()
-        copy.wait_recv()
-
-
-def gather_start(rows, small, heads, bulk, groups, layers, collective_id, chunks=4):
+        for piece in range(casts[0].count):
+            bulk(piece).wait_send()
+            bulk(piece).wait_recv()
+    for cast in casts:
+        cast.finish()
+
+
+def gather_start(rows, small, heads, weights, groups, layers, collective_id, chunks=4):
     pair = layers == 2
     if not pair:
         small = lax.all_gather(small, "fsdp", axis=0, tiled=True)
     height = small.shape[0] * (2 if pair else 1)
     dma = pltpu.SemaphoreType.DMA
     any_spec = pl.BlockSpec(memory_space=pl.ANY)
-    bulks = [bulk] if pair else []
-    rows_out, small_out, heads_out, *bulk_out = pl.pallas_call(
+    share = weights[0].shape[0] * 7 // 8
+    outs = [
+        jax.ShapeDtypeStruct((groups,) + rows.shape, LOW),
+        jax.ShapeDtypeStruct((groups, height, small.shape[1]), LOW),
+        jax.ShapeDtypeStruct((groups, 2 if pair else 1) + heads.shape[1:], LOW),
+    ] + [jax.ShapeDtypeStruct(array.shape, LOW) for array in weights]
+    if pair:
+        outs.append(jax.ShapeDtypeStruct((share, weights[0].shape[1]), LOW))
+    rows_out, small_out, heads_out, *lows = pl.pallas_call(
         functools.partial(start_kernel, groups, chunks, pair),
-        out_shape=[
-            jax.ShapeDtypeStruct((groups,) + rows.shape, LOW),
-            jax.ShapeDtypeStruct((groups, height, small.shape[1]), LOW),
-            jax.ShapeDtypeStruct((groups, 2 if pair else 1) + heads.shape[1:], LOW),
-        ]
-        + [jax.ShapeDtypeStruct(array.shape, LOW) for array in bulks],
-        in_specs=[any_spec] * (3 + len(bulks)),
-        out_specs=[any_spec] * (3 + len(bulks)),
-        scratch_shapes=[dma((3,)), dma((4,))]
+        out_shape=outs,
+        in_specs=[any_spec] * 6,
+        out_specs=[any_spec] * len(outs),
+        scratch_shapes=[item for array in weights for item in cast_scratch(array)]
+        + [dma((3,)), dma((2,)), dma((2, cast_cuts(weights[0].shape[0])))]
         + [dma((groups,))] * 4
         + gather_sems(groups, chunks)
         + gather_sems(groups, chunks),
-        compiler_params=pltpu.CompilerParams(collective_id=collective_id, has_side_effects=True),
+        compiler_params=pltpu.CompilerParams(
+            collective_id=collective_id, has_side_effects=True, vmem_limit_bytes=50 << 20
+        ),
         cost_estimate=pl.CostEstimate(flops=0, bytes_accessed=4 << 20, transcendentals=0),
-    )(rows, small, heads, *bulks)
-    if not pair:
+    )(rows, small, heads, *weights)
+    if pair:
+        gate = (lows[0], lows[3], swap_layers(lows[0][share:]))
+    else:
         heads_out = lax.all_gather(heads_out, "fsdp", axis=1, tiled=True)
+        gate = halves_over_layers(lows[0])
     return (
         rows_out.reshape(groups * rows.shape[0], rows.shape[1]),
         small_out.reshape(groups * height, small.shape[1]),
         heads_out,
-        (bulk, bulk_out[0]) if pair else halves_over_layers(bulk),
-    )
+        (gate, halves_over_layers(lows[1]), halves_over_layers(lows[2])),
+    )
+
+
+class Piece:
+    def __init__(self, source, buffer, load_sem, products):
+        self.load = pltpu.make_async_copy(source, buffer, load_sem)
+        self.products = products
+
+
+class Products:
+    def __init__(self, held, pieces):
+        self.held, self.pieces = held, pieces
+        self.jobs = [(piece, which) for piece in pieces for which in range(len(piece.products))]
+        self.at, self.busy = 0, {}
+
+    def begin(self):
+        for copy in self.held:
+            copy.start()
+        for piece in self.pieces[:2]:
+            piece.load.start()
+
+    def step(self):
+        if self.at >= len(self.jobs):
+            return
+        piece, which = self.jobs[self.at]
+        if self.at == 0:
+            for copy in self.held:
+                copy.wait()
+        if which == 0:
+            piece.load.wait()
+        compute, key, stage, store = piece.products[which]
+        if key in self.busy:
+            self.busy[key].wait()
+        stage[...] = compute()
+        store.start()
+        self.busy[key] = store
+        self.at += 1
+        if which == len(piece.products) - 1:
+            later = self.pieces.index(piece) + 2
+            if later < len(self.pieces):
+                self.pieces[later].load.start()
+
+    def finish(self):
+        while self.at < len(self.jobs):
+            self.step()
+        for store in self.busy.values():
+            store.wait()
+
+
+class GradProducts:
+    tile = 256
+
+    def __init__(self, pair, shapes):
+        self.pair = pair
+        self.rows, self.width = shapes[0]
+        self.units, self.tokens, self.columns = shapes[1][1], shapes[3][0], shapes[4][1]
+
+    def outs(self):
+        shared = [(self.width, self.columns), (self.columns // 2, self.width)]
+        experts = [(self.width // 2, self.units)] * 2 if self.pair else []
+        return [jax.ShapeDtypeStruct(shape, F32) for shape in experts + shared]
+
+    def counts(self):
+        experts = self.width // 2 // self.tile if self.pair else 0
+        return experts, self.width // self.tile
+
+    def scratch(self):
+        experts, shared = self.counts()
+        dma, tile = pltpu.SemaphoreType.DMA, self.tile
+        scratch = [
+            pltpu.VMEM((self.tokens, self.columns), LOW),
+            pltpu.VMEM((self.tokens, self.columns // 2), LOW),
+            pltpu.VMEM((2, self.tokens, tile), LOW),
+            pltpu.VMEM((2, tile, self.columns), F32),
+            pltpu.VMEM((2, self.columns // 2, tile), F32),
+            dma((4,)),
+            dma((experts + 2 * shared,)),
+            dma((2 * experts + 2 * shared,)),
+        ]
+        if self.pair:
+            scratch += [
+                pltpu.VMEM((self.rows, self.units), LOW),
+                pltpu.VMEM((self.rows, self.units), LOW),
+                pltpu.VMEM((2, self.rows, tile), LOW),
+                pltpu.VMEM((2, tile, self.units), F32),
+            ]
+        return scratch
+
+    def build(self, ins, outs, scratch):
+        rows_ref, gate_ref, up_ref, two_ref, dproj_ref, hs_ref, grads_ref = ins
+        dproj, hs, pieces_buf, in_stage, out_stage, held_sems, load_sems, store_sems, *rest = scratch
+        tile = self.tile
+        held = [
+            pltpu.make_async_copy(dproj_ref, dproj, held_sems.at[0]),
+            pltpu.make_async_copy(hs_ref, hs, held_sems.at[1]),
+        ]
+        pieces, stored = [], 0
+        experts, shared = self.counts()
+
+        def columns(ref, index, base=0):
+            return ref.at[:, pl.ds(pl.multiple_of(base + index * tile, tile), tile)]
+
+        if self.pair:
+            gate, up, slots, stage = rest
+            held += [
+                pltpu.make_async_copy(gate_ref, gate, held_sems.at[2]),
+                pltpu.make_async_copy(up_ref, up, held_sems.at[3]),
+            ]
+            base = lax.axis_index("fsdp") * (self.width // 2)
+            for index in range(experts):
+                slot = slots.at[index % 2]
+                products = []
+                for number, right in enumerate((gate, up)):
+                    target = outs[number].at[pl.ds(index * tile, tile)]
+                    products.append(
+                        (
+                            functools.partial(lambda a, b: t_dot(a[...], b[...]), slot, right),
+                            ("e", number),
+                            stage.at[number],
+                            pltpu.make_async_copy(stage.at[number], target, store_sems.at[stored]),
+                        )
+                    )
+                    stored += 1
+                pieces.append(
+                    Piece(columns(rows_ref, index, base), slot, load_sems.at[len(pieces)], products)
+                )
+        for index in range(shared):
+            slot, stage = pieces_buf.at[index % 2], in_stage.at[index % 2]
+            target = outs[-2].at[pl.ds(index * tile, tile)]
+            product = (
+                functools.partial(lambda a, b: t_dot(a[...], b[...]), slot, dproj),
+                ("i", index % 2),
+                stage,
+                pltpu.make_async_copy(stage, target, store_sems.at[stored]),
+            )
+            stored += 1
+            pieces.append(Piece(columns(two_ref, index), slot, load_sems.at[len(pieces)], [product]))
+        for index in range(shared):
+            slot, stage = pieces_buf.at[index % 2], out_stage.at[index % 2]
+            product = (
+                functools.partial(lambda a, b: t_dot(b[...], a[...]), slot, hs),
+                ("o", index % 2),
+                stage,
+                pltpu.make_async_copy(stage, columns(outs[-1], index), store_sems.at[stored]),
+            )
+            stored += 1
+            pieces.append(Piece(columns(grads_ref, index), slot, load_sems.at[len(pieces)], [product]))
+        return Products(held, pieces)
 
 
 class HeadGrads:
@@ -470,15 +698,25 @@
             self.cross().wait_send()
 
 
-def reduce_kernel(groups, chunks, extras, outs, rowfn, gathers, heads, *refs):
+def reduce_kernel(groups, chunks, extras, outs, rowfn, gathers, heads, grads, *refs):
     parts_ref = refs[0]
     extra_refs = refs[1 : 1 + extras]
     if heads is not None:
         heads_ref, refs = refs[1 + extras], refs[: 1 + extras] + refs[2 + extras :]
+    beside = None
+    if grads is not None:
+        beside_ins, refs = refs[1 + extras : 8 + extras], refs[: 1 + extras] + refs[8 + extras :]
     out_refs = refs[1 + extras : 1 + extras + outs]
     rest = list(refs[1 + extras + outs :])
     if heads is not None:
         head_out = rest.pop(0)
+    if grads is not None:
+        count = len(grads.outs())
+        beside_outs, rest = rest[:count], rest[count:]
+        count = len(grads.scratch())
+        beside = grads.build(beside_ins, beside_outs, rest[-count:])
+        rest = rest[:-count]
+        beside.begin()
     gather_ref = rest.pop(0) if gathers else None
     own, side, came, sent = rest[:4]
     own_sem, side_send, side_recv, send_sem, recv_sem = rest[4:9]
@@ -559,6 +797,8 @@
                 copy = neighbour_copy(way, step, chunk)
                 copy.start()
                 started.append(copy)
+                if beside is not None and step:
+                    beside.step()
     if heads is not None:
         head_grads.middle()
     gather = Gather(groups, chunks, rows, ready, gather_ref, rest[10:14]) if gathers else None
@@ -576,9 +816,11 @@
     if gathers:
         local = pltpu.make_async_copy(ready, gather_ref.at[at(spot, core)], rest[14])
         local.start()
-        gather.run()
+        gather.run(beside)
         gather.finish()
         local.wait()
+    if beside is not None:
+        beside.finish()
     if heads is not None:
         head_grads.finish()
     for copy in started:
@@ -586,7 +828,8 @@
 
 
 def ring_reduce(
-    parts, extras, outs, rowfn, groups, collective_id, gathers=None, heads=None, chunks=4
+    parts, extras, outs, rowfn, groups, collective_id, gathers=None, heads=None, grads=None,
+    grad_ins=(), chunks=4,
 ):
     _, rows, columns = parts.shape
     ring, steps = groups // 2, groups // 4
@@ -611,6 +854,10 @@
         extras.append(heads)
         shapes.append(jax.ShapeDtypeStruct(heads.shape[1:], LOW))
         specs.append(pl.BlockSpec(memory_space=pltpu.VMEM))
+    any_spec = pl.BlockSpec(memory_space=pl.ANY)
+    if grads is not None:
+        shapes += grads.outs()
+        specs += [any_spec] * len(grads.outs())
     if gathers is not None:
         shapes.append(jax.ShapeDtypeStruct((groups, rows, gathers), LOW))
         specs.append(pl.BlockSpec(memory_space=pl.ANY))
@@ -622,22 +869,25 @@
         scratch += [pltpu.SemaphoreType.DMA((2,))]
         scratch += [pltpu.SemaphoreType.DMA((groups,))] * 2
         scratch += [pltpu.SemaphoreType.DMA]
+    if grads is not None:
+        scratch += grads.scratch()
     return pl.pallas_call(
         functools.partial(
-            reduce_kernel, groups, chunks, count, len(outs), rowfn, gathers is not None, pair
+            reduce_kernel, groups, chunks, count, len(outs), rowfn, gathers is not None, pair, grads
         ),
         out_shape=shapes,
         in_specs=[pl.BlockSpec(memory_space=pl.ANY)]
-        + [pl.BlockSpec(memory_space=pltpu.VMEM)] * len(extras),
+        + [pl.BlockSpec(memory_space=pltpu.VMEM)] * len(extras)
+        + [any_spec] * len(grad_ins),
         out_specs=specs,
         scratch_shapes=scratch,
         compiler_params=pltpu.CompilerParams(
-            collective_id=collective_id, has_side_effects=True, vmem_limit_bytes=50 << 20
+            collective_id=collective_id, has_side_effects=True, vmem_limit_bytes=60 << 20
         ),
         cost_estimate=pl.CostEstimate(
             flops=0, bytes_accessed=4 << 20, transcendentals=0
         ),
-    )(parts, *extras)
+    )(parts, *extras, *grad_ins)
 
 
 def attend_kernel(blocks, q_ref, k_ref, v_ref, col_ref, row_ref, out_ref, log_ref):
@@ -846,23 +1096,46 @@
     return high, (values - high.astype(F32)).astype(LOW)
 
 
-def join_halves(pair, own_ref, other_ref, whole_ref):
-    @pl.when(pl.program_id(0) == 0)
-    def _():
-        own, other = half_columns(pair, whole_ref.shape[0])
-        whole_ref[own] = own_ref[...]
-        whole_ref[other] = other_ref[...]
+class Weights:
+    def __init__(self, pair, counts, refs, wholes, sems):
+        self.copies, at, number = [], 0, 0
+        first = lax.axis_index("fsdp") if pair else 0
+        for whole, pieces in zip(wholes, counts):
+            half, own, copies = whole.shape[0] // 2, refs[at], []
+            start = first * half
+            for piece in [own] + list(refs[at + 1 : at + pieces]):
+                size = piece.shape[0]
+                place = pl.ds(pl.multiple_of(start, 64), size)
+                copies.append(pltpu.make_async_copy(piece, whole.at[place], sems.at[number]))
+                number += 1
+                start = (1 - first) * half if piece is own else start + size
+            self.copies.append(copies)
+            at += pieces
+
+    def on_first(self, act):
+        @pl.when(pl.program_id(0) == 0)
+        def _():
+            act()
+
+    def begin(self, order):
+        self.on_first(lambda: [copy.start() for which in order for copy in self.copies[which]])
+
+    def ready(self, which):
+        self.on_first(lambda: [copy.wait() for copy in self.copies[which]])
 
 
 def ffn_kernel(
-    pair, rows_ref, chosen_ref, mine_ref, router_ref, wg_own, wg_other, wu_own, wu_other,
-    wd_own, wd_other, wi_ref, wo_ref,
-    probs_ref, slot_gate_ref, in_ref, gate_ref, up_ref, inner_ref, made_ref, proj_ref, hs_ref, out_ref,
-    spread, wd_ref,
+    pair, counts, rows_ref, chosen_ref, mine_ref, router_ref, wi_ref, wo_ref, *refs,
 ):
+    pieces = sum(counts)
+    parts, refs = refs[:pieces], refs[pieces:]
+    (
+        probs_ref, slot_gate_ref, in_ref, gate_ref, up_ref, inner_ref, made_ref, proj_ref, hs_ref,
+        out_ref, spread, wg_ref, wu_ref, wd_ref, sems,
+    ) = refs
     count = 4
-    width = rows_ref.shape[1]
-    join_halves(pair, wd_own, wd_other, wd_ref)
+    weights = Weights(pair, counts, parts, (wg_ref, wu_ref, wd_ref), sems)
+    weights.begin((0, 1, 2))
     tokens, slots = blocks_of(rows_ref, count), blocks_of(chosen_ref, count)
     lanes = lax.broadcasted_iota(jnp.int32, mine_ref.shape, 1)
     logits = jnp.where(mine_ref[1:2] > 0, dot(rows_ref[...], router_ref[...]), -1e30)
@@ -878,12 +1151,14 @@
         chosen = chosen_ref[slot]
         slot_gate_ref[slot] = jnp.sum(dot(chosen, picked), axis=-1, keepdims=True)
         in_ref[slot] = dot(chosen, rows_ref[token]).astype(LOW)
-    own, other = half_columns(pair, width)
-    gate = dot(in_ref[:, own], wg_own[...]) + dot(in_ref[:, other], wg_other[...])
-    up = dot(in_ref[:, own], wu_own[...]) + dot(in_ref[:, other], wu_other[...])
+    weights.ready(0)
+    gate = dot(in_ref[...], wg_ref[...])
+    weights.ready(1)
+    up = dot(in_ref[...], wu_ref[...])
     gate_ref[...] = gate
     up_ref[...] = up
     inner_ref[...] = (gate * jax.nn.sigmoid(gate) * up).astype(LOW)
+    weights.ready(2)
     made = dot(inner_ref[...], wd_ref[...]).astype(LOW)
     made_ref[...] = made
     spread[...] = (slot_gate_ref[...] * made.astype(F32)).astype(LOW)
@@ -898,13 +1173,16 @@
 
 
 def ffn_back_kernel(
-    pair, grads_ref, chosen_ref, mine_ref, slot_gate_ref, made_ref, gate_ref, up_ref, proj_ref,
-    wg_own, wg_other, wu_own, wu_other, wd_own, wd_other, wi_ref, wo_ref,
-    dy_ref, dgate_ref, dup_ref, dproj_ref, parts_ref, spread, wd_ref,
+    pair, counts, grads_ref, chosen_ref, mine_ref, slot_gate_ref, made_ref, gate_ref, up_ref,
+    proj_ref, wi_ref, wo_ref, *refs,
 ):
+    pieces = sum(counts)
+    parts, refs = refs[:pieces], refs[pieces:]
+    dy_ref, dgate_ref, dup_ref, dproj_ref, parts_ref, spread, wg_ref, wu_ref, wd_ref, sems = refs
     count = 4
     width = grads_ref.shape[1]
-    join_halves(pair, wd_own, wd_other, wd_ref)
+    weights = Weights(pair, counts, parts, (wg_ref, wu_ref, wd_ref), sems)
+    weights.begin((2, 0, 1))
     tokens, slots = blocks_of(grads_ref, count), blocks_of(chosen_ref, count)
     mine, shifted = mine_ref[0:1], mine_ref[2:3]
     for token, slot in zip(tokens, slots):
@@ -913,16 +1191,16 @@
         score = jnp.sum(picked * made_ref[slot].astype(F32), axis=-1, keepdims=True)
         high, rest = two_parts(score)
         spread[slot, width:] = (high.astype(F32) * mine + rest.astype(F32) * shifted).astype(LOW)
+    weights.ready(2)
     inner = dot_t(dy_ref[...], wd_ref[...])
     gate = gate_ref[...]
     sigmoid = jax.nn.sigmoid(gate)
     dgate_ref[...] = (inner * up_ref[...] * swish_slope(gate, sigmoid)).astype(LOW)
     dup_ref[...] = (inner * gate * sigmoid).astype(LOW)
-    own, other = half_columns(pair, width)
-    back = dot_t(dgate_ref[...], wg_own[...]) + dot_t(dup_ref[...], wu_own[...])
-    spread[:, own] = back.astype(LOW)
-    back = dot_t(dgate_ref[...], wg_other[...]) + dot_t(dup_ref[...], wu_other[...])
-    spread[:, other] = back.astype(LOW)
+    weights.ready(0)
+    weights.ready(1)
+    back = dot_t(dgate_ref[...], wg_ref[...]) + dot_t(dup_ref[...], wu_ref[...])
+    spread[:, :width] = back.astype(LOW)
     half = proj_ref.shape[1] // 2
     gate, up = proj_ref[:, :half], proj_ref[:, half:]
     sigmoid = jax.nn.sigmoid(gate)
@@ -951,7 +1229,12 @@
         kernel,
         grid=(steps,),
         out_shape=outs,
-        in_specs=[whole(a.shape) if fixed else cut(a.shape) for a, fixed in cuts],
+        in_specs=[
+            pl.BlockSpec(memory_space=pl.ANY)
+            if fixed is None
+            else whole(a.shape) if fixed else cut(a.shape)
+            for a, fixed in cuts
+        ],
         out_specs=[cut(o.shape) for o in outs],
         scratch_shapes=scratch,
         compiler_params=pltpu.CompilerParams(vmem_limit_bytes=60 << 20),
@@ -959,17 +1242,8 @@
     )(*operands)
 
 
-def grad_in_kernel(layer_ref, rows_ref, grads_ref, sent_ref, kept_ref):
-    made = t_dot(rows_ref[...], grads_ref[...])
-    step, half = pl.program_id(0), pl.num_programs(0) // 2
-
-    @pl.when(step < half)
-    def _():
-        sent_ref[...] = made.astype(LOW)
-
-    @pl.when(step >= half)
-    def _():
-        kept_ref[...] = made
+def grad_in_kernel(layer_ref, rows_ref, grads_ref, sent_ref):
+    sent_ref[...] = t_dot(rows_ref[...], grads_ref[...]).astype(LOW)
 
 
 def grad_in(rows, grads, tile=512):
@@ -977,31 +1251,21 @@
     columns = grads.shape[1]
     half = width // 2 // tile
     layer = lax.axis_index("fsdp").reshape(1)
-
-    def source(i, layer_ref):
-        return (0, lax.rem(i + (1 - layer_ref[0]) * half, 2 * half))
-
     return pl.pallas_call(
         grad_in_kernel,
         grid_spec=pltpu.PrefetchScalarGridSpec(
             num_scalar_prefetch=1,
-            grid=(2 * half,),
+            grid=(half,),
             in_specs=[
-                pl.BlockSpec((count, tile), source),
+                pl.BlockSpec((count, tile), lambda i, layer: (0, i + (1 - layer[0]) * half)),
                 pl.BlockSpec((count, columns), lambda i, _: (0, 0)),
             ],
-            out_specs=[
-                pl.BlockSpec((tile, columns), lambda i, _: (jnp.minimum(i, half - 1), 0)),
-                pl.BlockSpec((tile, columns), lambda i, _: (jnp.maximum(i - half, 0), 0)),
-            ],
+            out_specs=pl.BlockSpec((tile, columns), lambda i, _: (i, 0)),
         ),
-        out_shape=[
-            jax.ShapeDtypeStruct((width // 2, columns), LOW),
-            jax.ShapeDtypeStruct((width // 2, columns), F32),
-        ],
+        out_shape=jax.ShapeDtypeStruct((width // 2, columns), LOW),
         compiler_params=pltpu.CompilerParams(vmem_limit_bytes=50 << 20),
         cost_estimate=pl.CostEstimate(
-            flops=2 * count * width * columns, bytes_accessed=16 << 20, transcendentals=0
+            flops=count * width * columns, bytes_accessed=10 << 20, transcendentals=0
         ),
     )(layer, rows, grads)
 
@@ -1097,8 +1361,14 @@
         .reshape(H, own_rows, fold)
     )
     head_parts = jnp.concatenate([query_parts, expand_parts], axis=2)
-    hidden_low, small, head_parts, expert_gate_w = gather_start(
-        tokens[0], packed, head_parts, w_expert_gate[0].astype(LOW), groups, layers, 1
+    hidden_low, small, head_parts, expert_sets = gather_start(
+        tokens[0],
+        packed,
+        head_parts,
+        (w_expert_gate[0], w_expert_up[0], w_expert_down[0]),
+        groups,
+        layers,
+        1,
     )
     query_w = head_parts[..., :query_width].reshape(width, query_width)
     expand_w = head_parts[..., query_width:].reshape(LAT, NOPE + VD)
@@ -1131,8 +1401,6 @@
         output_w = whole_over_layers(output_low)
     shared_down_w = jnp.pad(shared_down_w, ((0, padding), (0, 0)))
 
-    expert_up_w = halves_over_layers(after(w_expert_up[0].astype(LOW), hidden_low))
-    expert_down_w = halves_over_layers(after(w_expert_down[0].astype(LOW), hidden_low))
     grad_low = gather_rows(after(cotangent[0], hidden_low))
 
     table = jnp.asarray(rotary_table(seq_len))
@@ -1163,7 +1431,14 @@
         [(lanes == place), (lanes < experts), (lanes == place + experts)] + [lanes < 0] * 5
     ).astype(F32)
     slot_count, unit_count = groups * capacity, w_expert_gate.shape[2]
-    expert_w = [(half, True) for half in expert_gate_w + expert_up_w + expert_down_w]
+    expert_w = [(piece, None) for pieces in expert_sets for piece in pieces]
+    counts = tuple(len(pieces) for pieces in expert_sets)
+    expert_scratch = [
+        pltpu.VMEM((width, unit_count), LOW),
+        pltpu.VMEM((width, unit_count), LOW),
+        pltpu.VMEM((unit_count, width), LOW),
+        pltpu.SemaphoreType.DMA((len(expert_w),)),
+    ]
     columns = shared_in_w.shape[1]
 
     def array(rows, columns, kind=LOW):
@@ -1172,11 +1447,11 @@
     steps = groups // 4
     routed_flops = 6 * slot_count * width * unit_count
     probs, slot_gate, expert_in, gate_proj, up_proj, inner_low, made, shared_proj, shared_low, part_out = row_grid(
-        functools.partial(ffn_kernel, layers == 2),
+        functools.partial(ffn_kernel, layers == 2, counts),
         steps,
         [
             (two_low, False), (chosen, False), (mine, True), (router_w, True),
-            *expert_w, (shared_in_w, True), (shared_down_w, True),
+            (shared_in_w, True), (shared_down_w, True), *expert_w,
         ],
         [
             array(seq_len, 128, F32), array(slot_count, 1, F32), array(slot_count, width),
@@ -1184,44 +1459,38 @@
             array(slot_count, unit_count), array(slot_count, width), array(seq_len, columns, F32),
             array(seq_len, columns // 2), array(seq_len, width),
         ],
-        [pltpu.VMEM((slot_count // steps, width), LOW), pltpu.VMEM((unit_count, width), LOW)],
+        [pltpu.VMEM((slot_count // steps, width), LOW)] + expert_scratch,
         routed_flops * 3 // 2,
     )
     ffn_out = scatter_rows(part_out).astype(F32)
     output = (residual + ffn_out).astype(LOW)
 
     made_grad, gate_grad, up_grad, shared_grads, part_grad = row_grid(
-        functools.partial(ffn_back_kernel, layers == 2),
+        functools.partial(ffn_back_kernel, layers == 2, counts),
         steps,
         [
             (grad_low, False), (chosen, False), (mine, True), (slot_gate, False), (made, False),
             (gate_proj, False), (up_proj, False), (shared_proj, False),
-            *expert_w, (shared_in_w, True), (shared_down_w, True),
+            (shared_in_w, True), (shared_down_w, True), *expert_w,
         ],
         [
             array(slot_count, width), array(slot_count, unit_count), array(slot_count, unit_count),
             array(seq_len, columns),
             jax.ShapeDtypeStruct((groups, tok_rows, width + 128), LOW),
         ],
-        [pltpu.VMEM((slot_count // steps, width + 128), LOW), pltpu.VMEM((unit_count, width), LOW)],
+        [pltpu.VMEM((slot_count // steps, width + 128), LOW)] + expert_scratch,
         routed_flops * 3 // 2,
     )
 
     if layers == 2:
         down_sent, down_kept = grad_out(inner_low, made_grad)
-        gate_sent, gate_kept = grad_in(expert_in, gate_grad)
-        up_sent, up_kept = grad_in(expert_in, up_grad)
+        gate_sent = grad_in(expert_in, gate_grad)
+        up_sent = grad_in(expert_in, up_grad)
         part_grad = after(part_grad, down_sent, gate_sent, up_sent)
     else:
         down_kept, down_sent = spread_start(t_dot(inner_low, made_grad))
         gate_kept, gate_sent = spread_start(t_dot(expert_in, gate_grad))
         up_kept, up_sent = spread_start(t_dot(expert_in, up_grad))
-    grad_expert_down = spread_end(down_kept, down_sent)
-    grad_expert_gate = spread_end(gate_kept, gate_sent)
-    grad_expert_up = spread_end(up_kept, up_sent)
-    shared_in_kept, shared_in_sent = spread_start(t_dot(two_low, shared_grads))
-    shared_down_kept, shared_down_sent = spread_start(t_dot(shared_low, grad_low)[:units])
-
     own_probs = lax.dynamic_slice_in_dim(probs, place * tok_rows, tok_rows, 0)
 
     def make_attn(total, part, extras, outs):
@@ -1242,7 +1511,9 @@
         rest = jnp.concatenate([rest[:, 128 - experts :], rest[:, : 128 - experts]], axis=1)
         return jnp.concatenate([back, high.astype(F32) + rest], axis=1).astype(LOW)
 
-    residual_grad, gain_parts, attn_grad = ring_reduce(
+    grad_ins = (expert_in, gate_grad, up_grad, two_low, shared_grads, shared_low, grad_low)
+    grads = GradProducts(layers == 2, [array.shape for array in grad_ins])
+    residual_grad, gain_parts, *made_grads, attn_grad = ring_reduce(
         part_grad,
         [own_probs, gain_ffn, residual, cotangent[0], router_w],
         [own_shape, own_shape],
@@ -1250,7 +1521,17 @@
         groups,
         3,
         width + 128,
-    )
+        None,
+        grads,
+        grad_ins,
+    )
+    shared_in_kept, shared_in_sent = spread_start(made_grads[-2])
+    shared_down_kept, shared_down_sent = spread_start(made_grads[-1][:units])
+    if layers == 2:
+        gate_kept, up_kept = made_grads[:2]
+    grad_expert_down = spread_end(down_kept, down_sent)
+    grad_expert_gate = spread_end(gate_kept, gate_sent)
+    grad_expert_up = spread_end(up_kept, up_sent)
     grad_gain_ffn = jnp.sum(gain_parts, axis=0)
     attn_grad = attn_grad.reshape(seq_len, width + 128)
 
@@ -1344,7 +1625,14 @@
     gain_columns = jnp.sum(gain_sums, axis=0).reshape(3, own_width).T
     packed = jnp.concatenate([grad_latent[:, :at], grad_router, gain_columns], axis=1)
     packed = jnp.pad(packed, ((0, 0), (0, -packed.shape[1] % 128)))
-    packed = spread_grad(packed, F32)
+    packed_kept, packed_sent = spread_start(packed, F32)
+    if layers == 2:
+        came = after(
+            swap_layers(packed_sent), grad_expert_down, grad_expert_gate, grad_expert_up
+        )
+        packed = packed_kept + came
+    else:
+        packed = spread_end(packed_kept, packed_sent)
     return (
         output[None],
         input_grad[None],

time: 740 us -> 726 us (0.981)
  matrix products: 34.2 us -> 22.9 us
  local copies, waits for them, and re-layouts: 51.7 us -> 61.3 us
    pallas_call x3, Pallas kernels: 267 us -> 286 us  [ring_reduce(): pl.pallas_call(functools.partial(reduce_kernel, groups, chunks, count, le...]
    broadcast_in_dim x3 -> x0, other arithmetic: 17.4 us -> none  [the longest x1 7.5 us: body(): grad_expert_down[None]]
    add x1 -> x3, other arithmetic: 0.15 us -> 17.3 us  [spread_end(): return kept + swap_layers(sent).astype(F32)]
    dot_general x5 -> x3, matrix products: 22.3 us -> 10.1 us  [t_dot(): lax.dot_general(left, right, (((0,), (0,)), ((), ())), preferred_element_...]
    convert_element_type x3 -> x0, other arithmetic: 11 us -> none  [the longest x1 4.52 us: body(): w_expert_up[0].astype(LOW)]
    pallas_call x2, Pallas kernels: 24.9 us -> 14 us  [grad_in(): pl.pallas_call(grad_in_kernel, grid_spec=pltpu.PrefetchScalarGridSpec(num...]
    pallas_call x1, Pallas kernels: 87.1 us -> 79.4 us  [gather_start(): pl.pallas_call(functools.partial(start_kernel, groups, chunks, pair), out...]
    unnamed x89 -> x85, local copies, waits for them, and re-layouts: 20.4 us -> 21.8 us
  transfers between devices with their start and end apart: 11 -> 12, of which waited for: 2 -> 1; matrix products, arithmetic and copies ran while one was open for 17% -> 17% of each run, Pallas kernels for 56% -> 58%
where the time goes in v5:
time: 726 us; the launch traced here: 720 us
  Pallas kernels  546 us (75%)
  local copies, waits for them, and re-layouts  61.3 us (8%)
  other arithmetic  54.5 us (8%)
  matrix products  22.9 us (3%)
  between operations  15.2 us (2%)
  starting transfers between devices  12.5 us (2%)
  waiting for transfers between devices  7.32 us (1%)
    pallas_call x3, Pallas kernels, ring_reduce(): pl.pallas_call(functools.partial(reduce_kernel, groups, chunks, count, le...  286 us
    pallas_call x2, Pallas kernels, row_grid(): pl.pallas_call(kernel, grid=(steps,), out_shape=outs, in_specs=[pl.BlockS...  101 us
    pallas_call x1, Pallas kernels, gather_start(): pl.pallas_call(functools.partial(start_kernel, groups, chunks, pair), out...  79.4 us
    unnamed x85, local copies, waits for them, and re-layouts  21.8 us
    pallas_call x1, Pallas kernels, project(): pl.pallas_call(project_kernel, grid=(seq_len // tile,), out_shape=[jax.Sh...  17.9 us
    add x3, other arithmetic, spread_end(): return kept + swap_layers(sent).astype(F32)  17.3 us
    pallas_call x1, Pallas kernels, project_back(): pl.pallas_call(project_back_kernel, grid=(seq_len // tile,), out_shape=[j...  14.6 us
  transfers between devices with their start and end apart: 12, of which 1 were waited for; matrix products, arithmetic and copies ran while one was open for 17% of the time, Pallas kernels for 58%

profile of v5, /device:TPU:0, one launch (start us, length us, event | category | flops | bytes accessed | tf_op | source)
XLA Modules:
  0.0 719.5 jit_solution(17016589554185927399)
XLA Ops:
  14.6 79.4 %shard_map.306 = (bf16[16,128,2048]{2,1,0:T(8,128)(2,1)}, bf16[16,128,640]{2,1,0:T(8,128)(2,1)}, bf16[16,2,64,256]{3,2,1,0:T(8,128)(2,1)S(1)}, bf16[1024,1408]{1...) custom-call(bf16[128,2048]{1,0:T(8,128)(2,1)S(1)} %bitcast.83, ...), custom_call_target="tpu_custom_call" | custom-call | bytes 4194304 | tf_op jit(solution)/shard_map/pallas_call | solution.py:488
  94.4 2.0 slice.229
  96.3 1.5 collective-permute-start.1
  98.7 1.2 convert.54
  100.1 1.3 convert.55
  102.4 1.3 fusion.23
  103.7 1.1 constant_dynamic-update-slice_fusion
  110.3 1.6 collective-permute-start.2
  112.4 2.0 slice.284
  114.4 1.3 slice.283
  116.4 1.4 copy.104.col_ref
  117.8 1.9 pad.42.router_ref.refs_5_
  122.2 1.2 convert_bitcast_fusion.1
  123.5 1.7 slice_reduce_fusion.1
  125.2 2.5 copy.107.refs_2_
  129.1 17.9 %shard_map.307 = (bf16[2048,2048]{1,0:T(8,128)(2,1)}, bf16[2048,192]{1,0:T(8,128)(2,1)S(1)}, bf16[2048,192]{1,0:T(8,128)(2,1)S(1)}, bf16[2048,128]{1,0:T(8,128)(...) custom-call(bf16[2048,2048]{1,0:T(8,128)(2,1)} %bitcast.123, f32[1,2048]{1,0:T(1,128)S(1)} %copy.103.gain_ref, ...), custom_call_target="tpu_custom_call" | custom-call | flops 7549747200 | bytes 29360128 | tf_op jit(solution)/shard_map/pallas_call | solution.py:1010
  148.1 8.5 %shard_map.308 = (bf16[2048,128]{1,0:T(8,128)(2,1)S(1)}, f32[2048,1]{1,0:T(8,128)S(1)}) custom-call(bf16[2048,192]{1,0:T(8,128)(2,1)S(1)} %get-tuple-element.75.q_ref, bf16[2048,192]{1,0:T(8,128)(2,1)} %copy-done.6, bf16[2048,128]{1,0:T(8,128)(2,1)S(1)} %get-tuple-element.77.v_ref, s32[2048,1]{1,0:T(8,128)} %copy.104.col_ref, s32[1,2048]{1,0:T(1,128)S(1)} %copy-done.3), custom_call_target="tpu_custom_call" | custom-call | flops 1677721600 | bytes 4194304 | tf_op jit(solution)/shard_map/pallas_call | solution.py:914
  157.6 1.5 constant_dynamic-slice_fusion.1.refs_3_
  159.0 1.7 constant_dynamic-slice_fusion.2.refs_1_
  161.9 1.1 fusion.42
  164.2 2.4 broadcast_select_fusion.1
  166.7 5.6 convolution_convert_fusion
  172.4 89.4 %shard_map.309 = (f32[128,2048]{1,0:T(8,128)}, bf16[16,128,2048]{2,1,0:T(8,128)(2,1)}) custom-call(bf16[16,128,2048]{2,1,0:T(8,128)(2,1)} %bitcast.87, bf16[128,2048]{1,0:T(8,128)(2,1)} %bitcast.82, f32[1,2048]{1,0:T(1,128)} %copy.107.refs_2_), custom_call_target="tpu_custom_call" | custom-call | bytes 4194304 | tf_op jit(solution)/shard_map/pallas_call | solution.py:874
  261.8 1.4 pad_maximum_fusion.wi_ref
  263.3 7.3 %collective-permute-done.3.refs_6_ = bf16[704,2048]{1,0:T(8,128)(2,1)} collective-permute-done((bf16[704,2048]{1,0:T(8,128)(2,1)}, bf16[704,2048]{1,0:T(8,128)(2,1)}, u32[]{:S(2)}, u32[]{:S(2)}) %collective-permute-start.3) | collective-permute-done | bytes 2883616 | tf_op jit(solution)/shard_map/ppermute | solution.py:88
  270.5 47.1 %shard_map.310 = (f32[2048,128]{1,0:T(8,128)}, f32[1024,1]{1,0:T(8,128)}, bf16[1024,2048]{1,0:T(8,128)(2,1)}, f32[1024,1408]{1,0:T(8,128)}, f32[1024,1408]{1,0:T...) custom-call(bf16[2048,2048]{1,0:T(8,128)(2,1)} %bitcast.88, ...), custom_call_target="tpu_custom_call" | custom-call | flops 26575110144 | bytes 62914560 | tf_op jit(solution)/shard_map/pallas_call | solution.py:1228
  317.7 1.5 constant_dynamic-slice_fusion.3.refs_1_
  319.2 53.7 %shard_map.311 = (bf16[1024,2048]{1,0:T(8,128)(2,1)}, bf16[1024,1408]{1,0:T(8,128)(2,1)}, bf16[1024,1408]{1,0:T(8,128)(2,1)}, bf16[2048,512]{1,0:T(8,128)(2,1)}, bf16[16,128,2176]{2,1,0:T(8,128)(2,1)}) custom-call(bf16[2048,2048]{1,0:T(8,128)(2,1)} %all-gather.2.cloned.1.call-done.grads_ref.refs_12_, bf16[1024,128]{1,0:T(8,128)(2,1)} %fusion.34.chosen_ref, ...), custom_call_target="tpu_custom_call" | custom-call | flops 26575110144 | bytes 62914560 | tf_op jit(solution)/shard_map/pallas_call | solution.py:1228
  372.9 7.0 shard_map.313
  379.9 7.0 shard_map.314
  387.3 11.3 %shard_map.312 = (bf16[704,2048]{1,0:T(8,128)(2,1)}, f32[704,2048]{1,0:T(8,128)}) custom-call(s32[1]{0:T(128)} %bitcast.20.layer_ref, bf16[1024,1408]{1,0:T(8,128)(2,1)} %get-tuple-element.95.inner_ref, bf16[1024,2048]{1,0:T(8,128)(2,1)} %get-tuple-element.96.grads_ref), custom_call_target="tpu_custom_call" | custom-call | flops 5905580032 | bytes 16777216 | tf_op jit(solution)/shard_map/pallas_call | solution.py:1285
  398.6 1.7 collective-permute-start.5
  400.7 105.6 %shard_map.315 = (f32[128,2048]{1,0:T(8,128)}, f32[128,2048]{1,0:T(8,128)}, f32[1024,1408]{1,0:T(8,128)}, f32[1024,1408]{1,0:T(8,128)}, f32[2048,512]{1,0:T(8,12...) custom-call(bf16[16,128,2176]{2,1,0:T(8,128)(2,1)} %get-tuple-element.101.refs_0_, ...), custom_call_target="tpu_custom_call" | custom-call | bytes 4194304 | tf_op jit(solution)/shard_map/pallas_call | solution.py:874
  506.3 1.5 slice.242
  507.8 2.7 fusion.24
  513.1 4.8 fusion
  520.5 1.5 collective-permute-start.8
  522.0 3.3 convolution_convert_fusion.1.g_ref
  525.2 13.7 %shard_map.316 = (bf16[2048,192]{1,0:T(8,128)(2,1)}, bf16[2048,192]{1,0:T(8,128)(2,1)}, bf16[2048,128]{1,0:T(8,128)(2,1)}) custom-call(bf16[2048,192]{1,0:T(8,128)(2,1)} %copy-done.5, bf16[2048,192]{1,0:T(8,128)(2,1)} %copy-done.6, bf16[2048,128]{1,0:T(8,128)(2,1)} %copy-done.7, bf16[2048,128]{1,0:T(8,128)(2,1)} %convolution_convert_fusion.1.g_ref, ...), custom_call_target="tpu_custom_call" | custom-call | flops 4194304000 | bytes 6291456 | tf_op jit(solution)/shard_map/pallas_call | solution.py:955
  538.9 1.2 copy-done.8
  540.1 1.2 copy-done.9
  542.4 14.6 %shard_map.317 = (bf16[16,128,2688]{2,1,0:T(8,128)(2,1)}, f32[2048,192]{1,0:T(8,128)}, f32[512,256]{1,0:T(8,128)S(1)}) custom-call(bf16[2048,192]{1,0:T(8,128)(2,1)S(1)} %copy-done.8, bf16[2048,192]{1,0:T(8,128)(2,1)S(1)} %copy-done.9, bf16[2048,128]{1,0:T(8,128)(2,1)S(1)} %copy-done.10, f32[2048,128]{1,0:T(8,128)} %constant.60.clone.table_ref, ...), custom_call_target="tpu_custom_call" | custom-call | flops 5452595200 | bytes 29360128 | tf_op jit(solution)/shard_map/pallas_call | solution.py:1064
  557.2 1.7 convert.56
  558.9 1.3 copy_bitcast_fusion.refs_4_
  560.2 90.7 %shard_map.318 = (f32[128,2048]{1,0:T(8,128)}, f32[128,512]{1,0:T(8,128)}, bf16[16,64,256]{2,1,0:T(8,128)(2,1)}, bf16[16,128,640]{2,1,0:T(8,128)(2,1)}) custom-call(bf16[16,128,2688]{2,1,0:T(8,128)(2,1)} %get-tuple-element.113.refs_0_, f32[128,512]{1,0:T(8,128)} %constant_dynamic-slice_fusion.2.refs_1_, f32[1,512]{1,0:T(1,128)} %copy-done.4, ...), custom_call_target="tpu_custom_call" | custom-call | bytes 4194304 | tf_op jit(solution)/shard_map/pallas_call | solution.py:874
  652.0 1.6 fusion.29
  654.7 3.8 fusion.21
  658.5 1.3 reduce_sum.57
  660.1 1.1 convert_bitcast_fusion
  661.8 3.6 all-to-all-start
  665.4 3.8 fusion.2
  669.2 2.7 fusion.28
  672.8 1.9 copy.115
  674.7 1.3 reshape.189
  677.5 2.2 convert_add_fusion.3
  679.7 1.1 fusion.39
  680.8 2.4 copy.119
  683.2 1.2 copy.118
  686.4 1.9 convert_add_fusion.5
  689.2 6.6 convert_add_fusion
  695.9 5.0 convert_add_fusion.1
  700.9 5.7 convert_add_fusion.2
  706.6 1.2 dynamic-slice_add_fusion
  710.3 1.9 fusion.27
  (185 shorter events, 42.9 us)
Async XLA Ops:
  7.2 6.4 copy-start.23
  7.2 256.1 %all-gather.2.cloned.1.call-start = ((), (), s32[]{:S(2)}) async-start(), calls=%async_computation.2 | async-start | bytes 8912896 | tf_op jit(solution)/shard_map/all_gather | solution.py:130
  13.6 1.0 copy-start
  14.6 83.2 %copy-start.19 = (f32[64,2048]{1,0:T(8,128)S(1)}, f32[64,2048]{1,0:T(8,128)}, u32[]{:S(2)}) copy-start(f32[64,2048]{1,0:T(8,128)} %param.28) | copy-start | bytes 1572868
  94.0 35.1 %copy-start.2 = (bf16[16,2,64,256]{3,2,1,0:T(8,128)(2,1)}, bf16[16,2,64,256]{3,2,1,0:T(8,128)(2,1)S(1)}, u32[]{:S(2)}) copy-start(bf16[16,2,64,256]{3,2,1,0:T(8,128)(2,1)S(1)} %get-tuple-element.74) | copy-start | bytes 3145732
  94.0 3.9 copy-start.17
  94.0 616.3 %reduce-scatter.2.cloned.1.call-start = ((), (), s32[]{:S(2)}) async-start(), calls=%async_computation.3 | async-start | bytes 8912896 | tf_op jit(solution)/shard_map/reduce_scatter | solution.py:134
  96.3 166.9 %collective-permute-start.1 = (bf16[128,1408]{1,0:T(8,128)(2,1)}, bf16[128,1408]{1,0:T(8,128)(2,1)}, u32[]{:S(2)}, u32[]{:S(2)}) collective-permute-start(bf16[128,1408]{1,0:T(8,128)(2,1)} %slice.229), channel_id=1, source_target_pairs={{0,1},{1,0},{2,3},{3,2},{4,5},{5,4},{6,7},{7,6},{8,9},{9,8},{10,11... | collective-permute-start | bytes 1081352 | tf_op jit(solution)/shard_map/ppermute | solution.py:88
  102.4 2.4 copy-start.21
  103.7 10.7 %copy-start.11 = (bf16[1024,512]{1,0:T(8,128)(2,1)}, bf16[1024,512]{1,0:T(8,128)(2,1)S(1)}, u32[]{:S(2)}) copy-start(bf16[1024,512]{1,0:T(8,128)(2,1)S(1)} %fusion.23) | copy-start | bytes 3145732
  104.8 11.6 %copy-start.3 = (s32[1,2048]{1,0:T(1,128)S(1)}, s32[1,2048]{1,0:T(1,128)}, u32[]{:S(2)}) copy-start(s32[1,2048]{1,0:T(1,128)} %row_ref.3) | copy-start | bytes 24580
  109.9 51.0 %collective-permute-start = (bf16[1632,512]{1,0:T(8,128)(2,1)}, bf16[1632,512]{1,0:T(8,128)(2,1)}, u32[]{:S(2)}, u32[]{:S(2)}) collective-permute-start(bf16[1632,512]{1,0:T(8,128)(2,1)} %slice_dynamic-update-slice_fusion.12), channel_id=1, source_target_pairs={{0,1},{1,0},{2,3},{3,2},{4,5},{5,4},{6,7},{7,6},{8,9},{9,8},{10,11... | collective-permute-start | bytes 5013512 | tf_op jit(solution)/shard_map/ppermute | solution.py:88
  110.3 152.9 %collective-permute-start.2 = (bf16[1024,1408]{1,0:T(8,128)(2,1)}, bf16[1024,1408]{1,0:T(8,128)(2,1)}, u32[]{:S(2)}, u32[]{:S(2)}) collective-permute-start(bf16[1024,1408]{1,0:T(8,128)(2,1)} %get-tuple-element.86.refs_3_), channel_id=1, source_target_pairs={{0,1},{1,0},{2,3},{3,2},{4,5},{5,4},{6,7},{7,6},{8,9},{9,8},{10,11... | collective-permute-start | bytes 8650760 | tf_op jit(solution)/shard_map/ppermute | solution.py:88
  111.9 158.6 %collective-permute-start.3 = (bf16[704,2048]{1,0:T(8,128)(2,1)}, bf16[704,2048]{1,0:T(8,128)(2,1)}, u32[]{:S(2)}, u32[]{:S(2)}) collective-permute-start(bf16[704,2048]{1,0:T(8,128)(2,1)} %get-tuple-element.87.refs_5_), channel_id=1, source_target_pairs={{0,1},{1,0},{2,3},{3,2},{4,5},{5,4},{6,7},{7,6},{8,9},{9,8},{10,11... | collective-permute-start | bytes 8650760 | tf_op jit(solution)/shard_map/ppermute | solution.py:88
  127.8 19.2 %copy-start.4 = (f32[1,512]{1,0:T(1,128)}, f32[1,512]{1,0:T(1,128)S(1)}, u32[]{:S(2)}) copy-start(f32[1,512]{1,0:T(1,128)S(1)} %reshape.173.gain_lat_ref.refs_2_) | copy-start | bytes 6148
  147.0 1.0 copy-start.6
  148.1 8.5 %copy-start.5 = (bf16[2048,192]{1,0:T(8,128)(2,1)}, bf16[2048,192]{1,0:T(8,128)(2,1)S(1)}, u32[]{:S(2)}) copy-start(bf16[2048,192]{1,0:T(8,128)(2,1)S(1)} %get-tuple-element.75.q_ref) | copy-start | bytes 2359300
  148.1 8.6 %copy-start.7 = (bf16[2048,128]{1,0:T(8,128)(2,1)}, bf16[2048,128]{1,0:T(8,128)(2,1)S(1)}, u32[]{:S(2)}) copy-start(bf16[2048,128]{1,0:T(8,128)(2,1)S(1)} %get-tuple-element.77.v_ref) | copy-start | bytes 1572868
  156.6 6.4 copy-start.18
  161.9 2.3 copy-start.12
  164.2 2.4 copy-start.20
  172.4 89.4 %copy-start.14 = (bf16[1024,512]{1,0:T(8,128)(2,1)S(1)}, bf16[1024,512]{1,0:T(8,128)(2,1)}, u32[]{:S(2)}) copy-start(bf16[1024,512]{1,0:T(8,128)(2,1)} %get-tuple-element.197) | copy-start | bytes 3145732
  386.9 302.3 %collective-permute-start.7 = (bf16[1024,1408]{1,0:T(8,128)(2,1)}, bf16[1024,1408]{1,0:T(8,128)(2,1)}, u32[]{:S(2)}, u32[]{:S(2)}) collective-permute-start(bf16[1024,1408]{1,0:T(8,128)(2,1)} %shard_map.314), channel_id=1, source_target_pairs={{0,1},{1,0},{2,3},{3,2},{4,5},{5,4},{6,7},{7,6},{8,9},{9,8},{10,11... | collective-permute-start | bytes 8650760 | tf_op jit(solution)/shard_map/ppermute | solution.py:88
  398.6 302.3 %collective-permute-start.5 = (bf16[704,2048]{1,0:T(8,128)(2,1)}, bf16[704,2048]{1,0:T(8,128)(2,1)}, u32[]{:S(2)}, u32[]{:S(2)}) collective-permute-start(bf16[704,2048]{1,0:T(8,128)(2,1)} %get-tuple-element.97), channel_id=1, source_target_pairs={{0,1},{1,0},{2,3},{3,2},{4,5},{5,4},{6,7},{7,6},{8,9},{9,8},{10,11... | collective-permute-start | bytes 8650760 | tf_op jit(solution)/shard_map/ppermute | solution.py:88
  400.3 295.6 %collective-permute-start.6 = (bf16[1024,1408]{1,0:T(8,128)(2,1)}, bf16[1024,1408]{1,0:T(8,128)(2,1)}, u32[]{:S(2)}, u32[]{:S(2)}) collective-permute-start(bf16[1024,1408]{1,0:T(8,128)(2,1)} %shard_map.313), channel_id=1, source_target_pairs={{0,1},{1,0},{2,3},{3,2},{4,5},{5,4},{6,7},{7,6},{8,9},{9,8},{10,11... | collective-permute-start | bytes 8650760 | tf_op jit(solution)/shard_map/ppermute | solution.py:88
  513.1 8.8 %copy-start.27 = (bf16[16,128,2176]{2,1,0:T(8,128)(2,1)S(1)}, bf16[16,128,2176]{2,1,0:T(8,128)(2,1)}, u32[]{:S(2)}) copy-start(bf16[16,128,2176]{2,1,0:T(8,128)(2,1)} %get-tuple-element.106) | copy-start | bytes 26738692
  517.9 7.3 %copy-start.24 = (f32[128,2048]{1,0:T(8,128)}, f32[128,2048]{1,0:T(8,128)S(1)}, u32[]{:S(2)}) copy-start(f32[128,2048]{1,0:T(8,128)S(1)} %fusion) | copy-start | bytes 3145732
  520.5 157.0 %collective-permute-start.8 = (bf16[1632,512]{1,0:T(8,128)(2,1)}, bf16[1632,512]{1,0:T(8,128)(2,1)}, u32[]{:S(2)}, u32[]{:S(2)}) collective-permute-start(bf16[1632,512]{1,0:T(8,128)(2,1)} %slice_dynamic-update-slice_fusion.8), channel_id=1, source_target_pairs={{0,1},{1,0},{2,3},{3,2},{4,5},{5,4},{6,7},{7,6},{8,9},{9,8},{10,11... | collective-permute-start | bytes 5013512 | tf_op jit(solution)/shard_map/ppermute | solution.py:88
  538.9 1.2 copy-start.8
  540.1 1.2 copy-start.9
  541.3 1.0 copy-start.10
  650.9 3.8 copy-start.1
  650.9 3.7 copy-start.28
  654.7 5.1 copy-start.26
  654.7 5.4 copy-start.22
  661.8 14.1 %all-to-all-start = ((f32[16,1,384]{2,1,0:T(1,128)}), f32[16,1,384]{2,1,0:T(1,128)S(1)}, u32[]{:S(2)}, u32[]{:S(2)}) async-start(f32[16,1,384]{2,1,0:T(1,128)} %all_to_all.6), calls=%async_computation.1 | async-start | bytes 49152 | tf_op jit(solution)/shard_map/all_to_all | solution.py:1624
  672.8 3.2 copy-start.25
  676.0 1.5 copy-start.15
  676.9 29.7 %collective-permute-start.4 = (f32[64,640]{0,1:T(8,128)}, f32[64,640]{0,1:T(8,128)}, u32[]{:S(2)}, u32[]{:S(2)}) collective-permute-start(f32[64,640]{0,1:T(8,128)} %constant_dynamic-slice_fusion), channel_id=1, source_target_pairs={{0,1},{1,0},{2,3},{3,2},{4,5},{5,4},{6,7},{7,6},{8,9},{9,8},{10,11... | collective-permute-start | bytes 491528 | tf_op jit(solution)/shard_map/ppermute | solution.py:88
  689.2 6.7 slice-start.2
  689.2 6.7 slice-start.3
  695.9 5.0 slice-start
  695.9 5.0 slice-start.1
  700.9 5.7 copy-start.16
  706.6 3.7 copy-start.13
Sparse Core Ops, SparseCore 0:
  94.2 72.2 all-gather.1
  317.8 108.2 reduce-scatter.1

commit v6 on v5

--- a/solution.py
+++ b/solution.py
@@ -73,15 +73,6 @@
 
 def after(value, *others):
     return lax.optimization_barrier((value,) + others)[0]
-
-
-def narrow(array):
-    return jnp.concatenate([array[:, i : i + 512] for i in range(0, array.shape[1], 512)])
-
-
-def widen(array, width):
-    rows = array.shape[0] * 512 // width
-    return jnp.concatenate([array[i * rows : (i + 1) * rows] for i in range(width // 512)], axis=1)
 
 
 def swap_layers(own):
@@ -347,9 +338,13 @@
         )
 
     def store(self, piece):
-        return pltpu.make_async_copy(
-            self.low.at[piece], self.target.at[self.part(piece)], self.stores.at[piece]
-        )
+        if isinstance(self.target, tuple):
+            first = self.target[0].shape[0] // self.size
+            target = self.target[0 if piece < first else 1]
+            place = pl.ds((piece if piece < first else piece - first) * self.size, self.size)
+        else:
+            target, place = self.target, self.part(piece)
+        return pltpu.make_async_copy(self.low.at[piece], target.at[place], self.stores.at[piece])
 
     def begin(self):
         for piece in range(min(2, self.count)):
@@ -380,18 +375,21 @@
     ]
 
 
-def start_kernel(groups, chunks, pair, rows_ref, small_ref, heads_ref, *rest):
-    sources, rest = rest[:3], rest[3:]
+def start_kernel(groups, chunks, pair, count, rows_ref, small_ref, heads_ref, *rest):
+    sources, rest = rest[:count], rest[count:]
     rows_out, small_out, heads_out, *rest = rest
-    targets, rest = rest[:3], rest[3:]
+    targets, rest = rest[:count], rest[count:]
     if pair:
         bulk_out, *rest = rest
+        lone_outs, rest = rest[: count - 3], rest[count - 3 :]
+        gate_rest, *rest = rest
+        targets = ((targets[0], gate_rest),) + tuple(targets[1:])
     casts = [
         Cast(source, target, *rest[4 * i : 4 * i + 4])
         for i, (source, target) in enumerate(zip(sources, targets))
     ]
-    rest = rest[12:]
-    local_sems, small_y, bulk_y, head_sems, head_recv, head_y, head_y_recv, *sems = rest
+    rest = rest[4 * count :]
+    local_sems, small_y, bulk_y, lone_y, head_sems, head_recv, head_y, head_y_recv, *sems = rest
     me, layer = lax.axis_index("seq"), lax.axis_index("fsdp")
     mine = layer if pair else 0
     rows = Gather(groups, chunks, rows_ref.shape[0], rows_ref, rows_out, sems[:4])
@@ -413,14 +411,17 @@
         copy.start()
 
     def bulk(piece):
-        start = piece * casts[0].size
-        size = min(casts[0].size, bulk_out.shape[0] - start)
+        size = casts[0].size
         return across(
-            casts[0].low.at[piece, pl.ds(0, size)],
-            bulk_out.at[pl.ds(start, size)],
+            casts[0].low.at[piece],
+            bulk_out.at[pl.ds(piece * size, size)],
             bulk_y.at[0, piece],
             bulk_y.at[1, piece],
         )
+
+    def lone(index):
+        low = casts[3 + index].low
+        return across(low, lone_outs[index], lone_y.at[0, index], lone_y.at[1, index])
 
     enter_all(groups, pair)
     if pair:
@@ -435,9 +436,15 @@
     locals_[0].wait()
     for chunk in range(chunks):
         small.begin(chunk)
+    for index, cast in enumerate(casts[3:]):
+        for piece in range(cast.count):
+            cast.step(piece)
+        if pair:
+            lone(index).start()
+    shared = range(bulk_out.shape[0] // casts[0].size) if pair else ()
     for piece in range(casts[0].count):
         casts[0].step(piece)
-        if pair:
+        if piece in shared:
             bulk(piece).start()
     for step in range(rows.steps):
         casts[1].step(step)
@@ -463,9 +470,12 @@
             copy = across(theirs, theirs, head_y.at[turn], head_y_recv.at[turn])
             copy.wait_send()
             copy.wait_recv()
-        for piece in range(casts[0].count):
+        for piece in shared:
             bulk(piece).wait_send()
             bulk(piece).wait_recv()
+        for index in range(count - 3):
+            lone(index).wait_send()
+            lone(index).wait_recv()
     for cast in casts:
         cast.finish()
 
@@ -477,21 +487,30 @@
     height = small.shape[0] * (2 if pair else 1)
     dma = pltpu.SemaphoreType.DMA
     any_spec = pl.BlockSpec(memory_space=pl.ANY)
-    share = weights[0].shape[0] * 7 // 8
+    share = weights[0].shape[0] // 4
+    count = len(weights)
     outs = [
         jax.ShapeDtypeStruct((groups,) + rows.shape, LOW),
         jax.ShapeDtypeStruct((groups, height, small.shape[1]), LOW),
         jax.ShapeDtypeStruct((groups, 2 if pair else 1) + heads.shape[1:], LOW),
     ] + [jax.ShapeDtypeStruct(array.shape, LOW) for array in weights]
+    gate_shape = weights[0].shape
     if pair:
-        outs.append(jax.ShapeDtypeStruct((share, weights[0].shape[1]), LOW))
+        outs[3] = jax.ShapeDtypeStruct((share, gate_shape[1]), LOW)
+        outs.append(outs[3])
+        for array in weights[3:]:
+            cuts = cast_cuts(array.shape[0])
+            outs.append(
+                jax.ShapeDtypeStruct((cuts, array.shape[0] // cuts, array.shape[1]), LOW)
+            )
+        outs.append(jax.ShapeDtypeStruct((gate_shape[0] - share, gate_shape[1]), LOW))
     rows_out, small_out, heads_out, *lows = pl.pallas_call(
-        functools.partial(start_kernel, groups, chunks, pair),
+        functools.partial(start_kernel, groups, chunks, pair, count),
         out_shape=outs,
-        in_specs=[any_spec] * 6,
+        in_specs=[any_spec] * (3 + count),
         out_specs=[any_spec] * len(outs),
         scratch_shapes=[item for array in weights for item in cast_scratch(array)]
-        + [dma((3,)), dma((2,)), dma((2, cast_cuts(weights[0].shape[0])))]
+        + [dma((3,)), dma((2,)), dma((2, cast_cuts(weights[0].shape[0]))), dma((2, count))]
         + [dma((groups,))] * 4
         + gather_sems(groups, chunks)
         + gather_sems(groups, chunks),
@@ -501,8 +520,13 @@
         cost_estimate=pl.CostEstimate(flops=0, bytes_accessed=4 << 20, transcendentals=0),
     )(rows, small, heads, *weights)
     if pair:
-        gate = (lows[0], lows[3], swap_layers(lows[0][share:]))
+        gate = (lows[0], lows[-1], lows[count], swap_layers(lows[-1]))
+        lone = [
+            layers_in_order(own, other.reshape(own.shape))
+            for own, other in zip(lows[3:count], lows[count + 1 : -1])
+        ]
     else:
+        lone = [whole_over_layers(own) for own in lows[3:]]
         heads_out = lax.all_gather(heads_out, "fsdp", axis=1, tiled=True)
         gate = halves_over_layers(lows[0])
     return (
@@ -510,6 +534,7 @@
         small_out.reshape(groups * height, small.shape[1]),
         heads_out,
         (gate, halves_over_layers(lows[1]), halves_over_layers(lows[2])),
+        lone,
     )
 
 
@@ -660,8 +685,25 @@
         return Products(held, pieces)
 
 
+class Later:
+    def __init__(self, laterfn, chunks, size, extras, outs, ready):
+        self.todo = [pl.ds(chunk * size, size) for chunk in range(chunks)]
+        self.run = functools.partial(laterfn, extras=extras, outs=outs, ready=ready)
+
+    def step(self):
+        if self.todo:
+            self.run(self.todo.pop(0))
+
+    def finish(self):
+        while self.todo:
+            self.step()
+
+
 class HeadGrads:
-    def __init__(self, groups, pair, grads_ref, out_ref, came, total, y_sems, send, recv, own_sem):
+    def __init__(
+        self, groups, pair, swaps, grads_ref, out_ref, came, total, y_sems, send, recv, own_sem, swap_sems
+    ):
+        self.swaps, self.swap_sems = swaps, swap_sems
         self.pair, self.grads, self.out = pair, grads_ref, out_ref
         self.came, self.total, self.y_sems, self.own_sem = came, total, y_sems, own_sem
         self.mine = lax.axis_index("fsdp") if pair else 0
@@ -672,9 +714,15 @@
     def cross(self):
         return across(self.grads.at[1 - self.mine], self.came, self.y_sems.at[0], self.y_sems.at[1])
 
+    def swap(self, index):
+        source, target = self.swaps[index]
+        return across(source, target, self.swap_sems.at[0, index], self.swap_sems.at[1, index])
+
     def begin(self):
         if self.pair:
             self.cross().start()
+            for index in range(len(self.swaps)):
+                self.swap(index).start()
 
     def middle(self):
         if self.pair:
@@ -696,13 +744,22 @@
         self.local.wait()
         if self.pair:
             self.cross().wait_send()
-
-
-def reduce_kernel(groups, chunks, extras, outs, rowfn, gathers, heads, grads, *refs):
+            for index in range(len(self.swaps)):
+                self.swap(index).wait_send()
+                self.swap(index).wait_recv()
+
+
+def reduce_kernel(
+    groups, chunks, extras, outs, rowfn, laterfn, gathers, heads, grads, swap_count, product, *refs
+):
     parts_ref = refs[0]
+    if product:
+        right_ref, refs = refs[1], refs[:1] + refs[2:]
     extra_refs = refs[1 : 1 + extras]
     if heads is not None:
         heads_ref, refs = refs[1 + extras], refs[: 1 + extras] + refs[2 + extras :]
+        swap_ins = refs[1 + extras : 1 + extras + swap_count]
+        refs = refs[: 1 + extras] + refs[1 + extras + swap_count :]
     beside = None
     if grads is not None:
         beside_ins, refs = refs[1 + extras : 8 + extras], refs[: 1 + extras] + refs[8 + extras :]
@@ -710,6 +767,9 @@
     rest = list(refs[1 + extras + outs :])
     if heads is not None:
         head_out = rest.pop(0)
+        swaps, rest = list(zip(swap_ins, rest[:swap_count])), rest[swap_count:]
+    if product:
+        side_made = rest.pop()
     if grads is not None:
         count = len(grads.outs())
         beside_outs, rest = rest[:count], rest[count:]
@@ -729,7 +789,7 @@
     if heads is None:
         enter((at(spot - 1, core), at(spot + 1, core), at(spot, 1 - core)))
     else:
-        head_grads = HeadGrads(groups, heads, heads_ref, head_out, *rest[-6:])
+        head_grads = HeadGrads(groups, heads, swaps, heads_ref, head_out, *rest[-7:])
         enter_all(groups, heads)
         head_grads.begin()
 
@@ -741,9 +801,20 @@
     order.append(0)
     started = []
     loads = {}
-    for far in order:
+
+    def prepare(far):
+        if product:
+
+            def block(index):
+                part = pl.ds(pl.multiple_of(index * rows, rows), rows)
+                return dot(parts_ref[part], right_ref[...]).astype(LOW)
+
+            side_made[far] = block(at(spot + far, 1 - core))
+            source = side_made.at[far]
+        else:
+            source = parts_ref.at[at(spot + far, 1 - core)]
         copy = pltpu.make_async_remote_copy(
-            src_ref=parts_ref.at[at(spot + far, 1 - core)],
+            src_ref=source,
             dst_ref=side.at[far],
             send_sem=side_send.at[far],
             recv_sem=side_recv.at[far],
@@ -752,18 +823,26 @@
         )
         copy.start()
         started.append(copy)
+        if product:
+            own[far] = block(at(spot + far, core))
+            loads[far] = (None, copy)
+            return
         load = pltpu.make_async_copy(
             parts_ref.at[at(spot + far, core)], own.at[far], own_sem.at[far]
         )
         load.start()
         loads[far] = (load, copy)
 
+    if not product:
+        for far in order:
+            prepare(far)
     here = set()
 
     def both(far, chunk):
         if far not in here:
             here.add(far)
-            loads[far][0].wait()
+            if loads[far][0] is not None:
+                loads[far][0].wait()
             loads[far][1].wait_recv()
         part = pl.ds(chunk * size, size)
         return own[far, part].astype(F32) + side[far, part].astype(F32)
@@ -782,7 +861,12 @@
     def half(way, chunk):
         return (chunk < chunks // 2) == (way == 0)
 
+    if product:
+        prepare(steps)
     for step in range(steps):
+        if product and step:
+            prepare(steps - step)
+            prepare(ring - steps + step)
         for chunk in range(chunks):
             for way in range(2):
                 if step == 0 and not half(way, chunk):
@@ -797,8 +881,10 @@
                 copy = neighbour_copy(way, step, chunk)
                 copy.start()
                 started.append(copy)
-                if beside is not None and step:
+                if beside is not None and step and chunk == chunks - 1:
                     beside.step()
+    if product:
+        prepare(0)
     if heads is not None:
         head_grads.middle()
     gather = Gather(groups, chunks, rows, ready, gather_ref, rest[10:14]) if gathers else None
@@ -816,6 +902,8 @@
     if gathers:
         local = pltpu.make_async_copy(ready, gather_ref.at[at(spot, core)], rest[14])
         local.start()
+        if laterfn is not None:
+            beside = Later(laterfn, chunks, size, extra_refs, out_refs, ready)
         gather.run(beside)
         gather.finish()
         local.wait()
@@ -829,9 +917,12 @@
 
 def ring_reduce(
     parts, extras, outs, rowfn, groups, collective_id, gathers=None, heads=None, grads=None,
-    grad_ins=(), chunks=4,
+    grad_ins=(), swaps=(), right=None, laterfn=None, chunks=4,
 ):
-    _, rows, columns = parts.shape
+    if right is None:
+        _, rows, columns = parts.shape
+    else:
+        rows, columns = parts.shape[0] // groups, right.shape[1]
     ring, steps = groups // 2, groups // 4
     scratch = [
         pltpu.VMEM((ring, rows, columns), LOW),
@@ -855,6 +946,9 @@
         shapes.append(jax.ShapeDtypeStruct(heads.shape[1:], LOW))
         specs.append(pl.BlockSpec(memory_space=pltpu.VMEM))
     any_spec = pl.BlockSpec(memory_space=pl.ANY)
+    for array in swaps:
+        shapes.append(jax.ShapeDtypeStruct(array.shape, LOW))
+        specs.append(any_spec)
     if grads is not None:
         shapes += grads.outs()
         specs += [any_spec] * len(grads.outs())
@@ -868,26 +962,31 @@
         scratch += [pltpu.VMEM(heads.shape[1:], LOW)] * 2
         scratch += [pltpu.SemaphoreType.DMA((2,))]
         scratch += [pltpu.SemaphoreType.DMA((groups,))] * 2
-        scratch += [pltpu.SemaphoreType.DMA]
+        scratch += [pltpu.SemaphoreType.DMA, pltpu.SemaphoreType.DMA((2, max(1, len(swaps))))]
     if grads is not None:
         scratch += grads.scratch()
+    if right is not None:
+        scratch.append(pltpu.VMEM((ring, rows, columns), LOW))
     return pl.pallas_call(
         functools.partial(
-            reduce_kernel, groups, chunks, count, len(outs), rowfn, gathers is not None, pair, grads
+            reduce_kernel, groups, chunks, count, len(outs), rowfn, laterfn, gathers is not None, pair, grads,
+            len(swaps), right is not None,
         ),
         out_shape=shapes,
-        in_specs=[pl.BlockSpec(memory_space=pl.ANY)]
+        in_specs=(
+            [any_spec] if right is None else [pl.BlockSpec(memory_space=pltpu.VMEM)] * 2
+        )
         + [pl.BlockSpec(memory_space=pltpu.VMEM)] * len(extras)
-        + [any_spec] * len(grad_ins),
+        + [any_spec] * (len(swaps) + len(grad_ins)),
         out_specs=specs,
         scratch_shapes=scratch,
         compiler_params=pltpu.CompilerParams(
-            collective_id=collective_id, has_side_effects=True, vmem_limit_bytes=60 << 20
+            collective_id=collective_id, has_side_effects=True, vmem_limit_bytes=50 << 20
         ),
         cost_estimate=pl.CostEstimate(
             flops=0, bytes_accessed=4 << 20, transcendentals=0
         ),
-    )(parts, *extras, *grad_ins)
+    )(parts, *([] if right is None else [right]), *extras, *swaps, *grad_ins)
 
 
 def attend_kernel(blocks, q_ref, k_ref, v_ref, col_ref, row_ref, out_ref, log_ref):
@@ -982,7 +1081,7 @@
     one = norm_forward(x_ref[...].astype(F32), gain_ref[...])[0].astype(LOW)
     one_ref[...] = one
     cosine, sine = table_ref[:, :ROPE], table_ref[:, ROPE:]
-    query = dot(one, wq_ref[...])
+    query = dot(one, wq_ref[:, : NOPE + ROPE])
     turned = query[:, NOPE:]
     q_ref[:, :NOPE] = query[:, :NOPE].astype(LOW)
     q_ref[:, NOPE:] = (turned * cosine + swapped(turned) * sine).astype(LOW)
@@ -1035,7 +1134,7 @@
     de_low[:, NOPE:] = dv_ref[...]
     blocks, rows, wide = parts_ref.shape
     width, last = one_ref.shape[1], LAT + ROPE
-    parts_ref[:, :, :width] = dot_t(dq_low[...], wq_ref[...]).astype(LOW).reshape(blocks, rows, width)
+    parts_ref[:, :, :width] = dot_t(dq_low[...], wq_ref[:, : NOPE + ROPE]).astype(LOW).reshape(blocks, rows, width)
     parts_ref[:, :, width : width + LAT] = (
         dot_t(de_low[...], we_ref[...]).astype(LOW).reshape(blocks, rows, LAT)
     )
@@ -1066,7 +1165,7 @@
         grid=(seq_len // tile,),
         out_shape=[
             jax.ShapeDtypeStruct((seq_len // tok_rows, tok_rows, wide), LOW),
-            jax.ShapeDtypeStruct(query_w.shape, F32),
+            jax.ShapeDtypeStruct((width, NOPE + ROPE), F32),
             jax.ShapeDtypeStruct(expand_w.shape, F32),
         ],
         in_specs=[
@@ -1075,7 +1174,7 @@
         ],
         out_specs=[
             pl.BlockSpec((tile // tok_rows, tok_rows, wide), lambda i: (i, 0, 0)),
-            whole(query_w.shape),
+            whole((width, NOPE + ROPE)),
             whole(expand_w.shape),
         ],
         scratch_shapes=[pltpu.VMEM((tile, NOPE + ROPE), LOW), pltpu.VMEM((tile, NOPE + VD), LOW)],
@@ -1101,14 +1200,14 @@
         self.copies, at, number = [], 0, 0
         first = lax.axis_index("fsdp") if pair else 0
         for whole, pieces in zip(wholes, counts):
-            half, own, copies = whole.shape[0] // 2, refs[at], []
-            start = first * half
-            for piece in [own] + list(refs[at + 1 : at + pieces]):
-                size = piece.shape[0]
-                place = pl.ds(pl.multiple_of(start, 64), size)
+            half, done, copies = whole.shape[0] // 2, 0, []
+            for piece in refs[at : at + pieces]:
+                side, offset = done // half, done % half
+                start = (first if side == 0 else 1 - first) * half + offset
+                place = pl.ds(pl.multiple_of(start, 64), piece.shape[0])
                 copies.append(pltpu.make_async_copy(piece, whole.at[place], sems.at[number]))
                 number += 1
-                start = (1 - first) * half if piece is own else start + size
+                done += piece.shape[0]
             self.copies.append(copies)
             at += pieces
 
@@ -1361,16 +1460,19 @@
         .reshape(H, own_rows, fold)
     )
     head_parts = jnp.concatenate([query_parts, expand_parts], axis=2)
-    hidden_low, small, head_parts, expert_sets = gather_start(
+    hidden_low, small, head_parts, expert_sets, lone = gather_start(
         tokens[0],
         packed,
         head_parts,
-        (w_expert_gate[0], w_expert_up[0], w_expert_down[0]),
+        (
+            w_expert_gate[0], w_expert_up[0], w_expert_down[0],
+            w_shared_gate, w_shared_up, w_shared_down, w_output,
+        ),
         groups,
         layers,
         1,
     )
-    query_w = head_parts[..., :query_width].reshape(width, query_width)
+    query_w = head_parts.reshape(width, query_width + fold)
     expand_w = head_parts[..., query_width:].reshape(LAT, NOPE + VD)
     router_w = jnp.pad(small[:, at:last], ((0, 0), (0, 128 - experts)))
     all_routes = small[:, last + 3 : used].reshape(groups, layers, -1)
@@ -1383,22 +1485,8 @@
     units = w_shared_gate.shape[1]
     padding = -units % 128
     spare = ((0, 0), (0, padding))
-    shared_in = jnp.concatenate([jnp.pad(w_shared_gate, spare), jnp.pad(w_shared_up, spare)], axis=1)
-    shared_in = shared_in.astype(LOW)
-    shared_in = after(shared_in, hidden_low)
-    down_low, output_low = w_shared_down.astype(LOW), w_output.astype(LOW)
-    if layers == 2:
-        lone = jnp.concatenate([shared_in, narrow(down_low), narrow(output_low)])
-        pair_of = swap_layers(lone)
-        cut = shared_in.shape[0]
-        end = cut + narrow(down_low).shape[0]
-        shared_in_w = layers_in_order(shared_in, pair_of[:cut])
-        shared_down_w = layers_in_order(down_low, widen(pair_of[cut:end], width))
-        output_w = layers_in_order(output_low, widen(pair_of[end:], width))
-    else:
-        shared_in_w = whole_over_layers(shared_in)
-        shared_down_w = whole_over_layers(down_low)
-        output_w = whole_over_layers(output_low)
+    shared_gate_w, shared_up_w, shared_down_w, output_w = lone
+    shared_in_w = jnp.concatenate([jnp.pad(shared_gate_w, spare), jnp.pad(shared_up_w, spare)], axis=1)
     shared_down_w = jnp.pad(shared_down_w, ((0, padding), (0, 0)))
 
     grad_low = gather_rows(after(cotangent[0], hidden_low))
@@ -1408,8 +1496,6 @@
         hidden_low, gain_attn, query_w, small, gain_latent, expand_w, table
     )
     head_out, logs = attend_forward(head_q, head_k, head_v, doc_ids)
-    part_residual = dot(head_out, output_w).astype(LOW).reshape(groups, tok_rows, width)
-
     def make_two(total, part, extras, outs):
         row_sum = extras[0][part].astype(F32) + total
         outs[0][part] = row_sum
@@ -1417,7 +1503,7 @@
 
     own_shape = jax.ShapeDtypeStruct((tok_rows, width), F32)
     residual, two_low = ring_reduce(
-        part_residual, [tokens[0], gain_ffn], [own_shape], make_two, groups, 2, width
+        head_out, [tokens[0], gain_ffn], [own_shape], make_two, groups, 2, width, right=output_w
     )
     two_low = after(two_low, grad_low).reshape(seq_len, width)
 
@@ -1506,17 +1592,18 @@
         back = factor * (inner - normed * jnp.mean(inner * normed, axis=-1, keepdims=True))
         back = extras[3][part].astype(F32) + back
         outs[0][part] = back
-        outs[1][part] = grad * normed
+        gain_sum = jnp.sum(grad * normed, axis=0, keepdims=True)
+        outs[1][...] = gain_sum if part.start == 0 else outs[1][...] + gain_sum
         rest = rest.astype(F32)
         rest = jnp.concatenate([rest[:, 128 - experts :], rest[:, : 128 - experts]], axis=1)
         return jnp.concatenate([back, high.astype(F32) + rest], axis=1).astype(LOW)
 
     grad_ins = (expert_in, gate_grad, up_grad, two_low, shared_grads, shared_low, grad_low)
     grads = GradProducts(layers == 2, [array.shape for array in grad_ins])
-    residual_grad, gain_parts, *made_grads, attn_grad = ring_reduce(
+    residual_grad, grad_gain_ffn, *made_grads, attn_grad = ring_reduce(
         part_grad,
         [own_probs, gain_ffn, residual, cotangent[0], router_w],
-        [own_shape, own_shape],
+        [own_shape, jax.ShapeDtypeStruct((1, width), F32)],
         make_attn,
         groups,
         3,
@@ -1532,7 +1619,6 @@
     grad_expert_down = spread_end(down_kept, down_sent)
     grad_expert_gate = spread_end(gate_kept, gate_sent)
     grad_expert_up = spread_end(up_kept, up_sent)
-    grad_gain_ffn = jnp.sum(gain_parts, axis=0)
     attn_grad = attn_grad.reshape(seq_len, width + 128)
 
     own_width = width // groups
@@ -1541,18 +1627,6 @@
     grad_router = grad_router[:, :experts] + grad_router[:, experts : 2 * experts]
 
     output_kept, output_sent = spread_start(t_dot(head_out, attn_grad)[:, :width])
-    if layers == 2:
-        lone = jnp.concatenate([shared_in_sent, narrow(shared_down_sent), narrow(output_sent)])
-        pair_of = swap_layers(lone)
-        cut = shared_in_sent.shape[0]
-        end = cut + narrow(shared_down_sent).shape[0]
-        grad_shared_in = shared_in_kept + pair_of[:cut].astype(F32)
-        grad_shared_down = shared_down_kept + widen(pair_of[cut:end], width).astype(F32)
-        grad_output = output_kept + widen(pair_of[end:], width).astype(F32)
-    else:
-        grad_shared_in = spread_end(shared_in_kept, shared_in_sent)
-        grad_shared_down = spread_end(shared_down_kept, shared_down_sent)
-        grad_output = spread_end(output_kept, output_sent)
     head_g = dot_t(attn_grad, jnp.pad(output_w, ((0, 0), (0, 128)))).astype(LOW)
     query_grad, key_grad, value_grad = attend_backward(
         head_q, head_k, head_v, doc_ids, logs, head_g
@@ -1579,19 +1653,47 @@
         turned = total[:, width + LAT : width + LAT + ROPE]
         turned = turned * extras[2][part, :ROPE] - swapped(turned) * extras[2][part, ROPE:]
         outs[0][part] = total[:, :width]
-        outs[1][part] = grad * normed
+        gain_sum = jnp.sum(grad * normed, axis=0, keepdims=True)
+        outs[1][...] = gain_sum if part.start == 0 else outs[1][...] + gain_sum
         return jnp.concatenate([back, turned, jnp.zeros_like(turned)], axis=1).astype(LOW)
 
-    one_grad, latent_gains, head_grads, latent_grad = ring_reduce(
+    def make_input(part, extras, outs, ready):
+        grad = outs[0][part] + dot_t(ready[part], extras[3][...])
+        gain = extras[4][...]
+        _, normed, factor = norm_forward(extras[5][part].astype(F32), gain)
+        inner = grad * gain
+        back = factor * (inner - normed * jnp.mean(inner * normed, axis=-1, keepdims=True))
+        outs[2][part] = (extras[6][part] + back).astype(LOW)
+        gain_sum = jnp.sum(grad * normed, axis=0, keepdims=True)
+        outs[3][...] = gain_sum if part.start == 0 else outs[3][...] + gain_sum
+
+    swaps = (shared_in_sent, shared_down_sent, output_sent) if layers == 2 else ()
+    _, latent_gains, input_grad, grad_gain_attn, head_grads, *swapped_grads, latent_grad = ring_reduce(
         part_rows,
-        [own_latent, gain_latent, own_table],
-        [own_shape, jax.ShapeDtypeStruct((tok_rows, LAT), F32)],
+        [
+            own_latent, gain_latent, own_table,
+            small[:, : LAT + 2 * ROPE], gain_attn, tokens[0], residual_grad,
+        ],
+        [
+            own_shape,
+            jax.ShapeDtypeStruct((1, LAT), F32),
+            jax.ShapeDtypeStruct((tok_rows, width), LOW),
+            jax.ShapeDtypeStruct((1, width), F32),
+        ],
         make_latent,
         groups,
         4,
         LAT + 2 * ROPE,
         head_grads,
-    )
+        swaps=swaps,
+        laterfn=make_input,
+    )
+    shared_kept = (shared_in_kept, shared_down_kept, output_kept)
+    if layers == 2:
+        shared_all = [kept + came.astype(F32) for kept, came in zip(shared_kept, swapped_grads)]
+    else:
+        shared_all = [spread_end(kept, None) for kept in shared_kept]
+    grad_shared_in, grad_shared_down, grad_output = shared_all
     grad_query = (
         head_grads[..., :query_width].transpose(1, 0, 2).reshape(own_rows, H * query_width)
     ).astype(F32)
@@ -1602,12 +1704,6 @@
         .reshape(lat_rows, H * (NOPE + VD))
     ).astype(F32)
 
-    own_latent_grad = lax.dynamic_index_in_dim(latent_grad, place, 0, keepdims=False)
-    one_grad = one_grad + dot_t(own_latent_grad[:, : LAT + ROPE], small[:, : LAT + ROPE])
-    _, normed_one, factor_one = norm_forward(hidden_own, gain_attn)
-    input_part, grad_gain_attn = norm_backward(one_grad, normed_one, factor_one, gain_attn)
-    input_grad = (residual_grad + input_part).astype(LOW)
-
     one_slice = lax.dynamic_slice_in_dim(one_low, place * own_width, own_width, 1)
     grad_latent = t_dot(one_slice, latent_grad.reshape(seq_len, LAT + 2 * ROPE))
     gain_sums = jnp.concatenate(
@@ -1615,7 +1711,7 @@
             grad_gain_attn.reshape(groups, own_width),
             grad_gain_ffn.reshape(groups, own_width),
             jnp.pad(
-                jnp.sum(latent_gains, axis=0).reshape(groups, layers, lat_rows),
+                latent_gains.reshape(groups, layers, lat_rows),
                 ((0, 0), (0, 0), (0, own_rows - lat_rows)),
             ).reshape(groups, own_width),
         ],

time: 726 us -> 721 us (level)
  Pallas kernels: 546 us -> 558 us
  local copies, waits for them, and re-layouts: 61.3 us -> 49.7 us
  other arithmetic: 54.5 us -> 43 us
  waiting for transfers between devices: 7.32 us -> 15.5 us
    pallas_call x3, Pallas kernels: 286 us -> 298 us  [ring_reduce(): pl.pallas_call(functools.partial(reduce_kernel, groups, chunks, count, le...]
    ppermute x9 -> x7, waiting for transfers between devices: 7.28 us -> 15.5 us  [swap_layers(): return lax.ppermute(own, 'fsdp', ((0, 1), (1, 0)))]
    unnamed x85 -> x81, local copies, waits for them, and re-layouts: 21.8 us -> 17.9 us
  transfers between devices with their start and end apart: 12 -> 10, of which waited for: 1 -> 1; matrix products, arithmetic and copies ran while one was open for 17% -> 12% of each run, Pallas kernels for 58% -> 61%
where the time goes in v6:
time: 721 us; the launch traced here: 711 us
  Pallas kernels  558 us (77%)
  local copies, waits for them, and re-layouts  49.7 us (7%)
  other arithmetic  43 us (6%)
  matrix products  17.7 us (2%)
  waiting for transfers between devices  15.5 us (2%)
  between operations  15.1 us (2%)
  starting transfers between devices  12.3 us (2%)
    pallas_call x3, Pallas kernels, ring_reduce(): pl.pallas_call(functools.partial(reduce_kernel, groups, chunks, count, le...  298 us
    pallas_call x2, Pallas kernels, row_grid(): pl.pallas_call(kernel, grid=(steps,), out_shape=outs, in_specs=[pl.BlockS...  101 us
    pallas_call x1, Pallas kernels, gather_start(): pl.pallas_call(functools.partial(start_kernel, groups, chunks, pair, coun...  78.5 us
    unnamed x81, local copies, waits for them, and re-layouts  17.9 us
    pallas_call x1, Pallas kernels, project(): pl.pallas_call(project_kernel, grid=(seq_len // tile,), out_shape=[jax.Sh...  17.9 us
    add x3, other arithmetic, spread_end(): return kept + swap_layers(sent).astype(F32)  17.3 us
    ppermute x7, waiting for transfers between devices, swap_layers(): return lax.ppermute(own, 'fsdp', ((0, 1), (1, 0)))  15.5 us
    pallas_call x1, Pallas kernels, project_back(): pl.pallas_call(project_back_kernel, grid=(seq_len // tile,), out_shape=[j...  14.6 us
  transfers between devices with their start and end apart: 10, of which 1 were waited for; matrix products, arithmetic and copies ran while one was open for 12% of the time, Pallas kernels for 61%

profile of v6, /device:TPU:0, one launch (start us, length us, event | category | flops | bytes accessed | tf_op | source)
XLA Modules:
  0.0 711.2 jit_solution(8038158822975864988)
XLA Ops:
  11.3 0.9 convert.38
  12.4 1.0 convert_element_type.111
  13.6 1.2 convert_element_type.110
  15.6 1.3 copy.111.rest_3_
  16.9 1.3 copy.112.rest_4_
  18.2 1.0 pad_maximum_fusion.2.heads_ref
  19.2 78.5 %shard_map.306 = (bf16[16,128,2048]{2,1,0:T(8,128)(2,1)}, bf16[16,128,640]{2,1,0:T(8,128)(2,1)}, bf16[16,2,64,256]{3,2,1,0:T(8,128)(2,1)}, bf16[256,1408]{1,0:T(...) custom-call(bf16[128,2048]{1,0:T(8,128)(2,1)S(1)} %bitcast.83, ...), custom_call_target="tpu_custom_call" | custom-call | bytes 4194304 | tf_op jit(solution)/shard_map/pallas_call | solution.py:507
  99.3 1.6 collective-permute-start
  101.4 1.5 collective-permute-start.2
  102.9 2.1 slice.99
  105.0 2.1 slice.100
  107.8 1.4 copy.115.col_ref
  109.1 1.8 reshape.174
  112.0 1.9 pad.38.clone.router_ref.refs_5_
  113.9 1.3 slice.73
  115.5 1.3 slice_convert_fusion
  118.4 1.2 copy-done.17
  119.6 17.9 %shard_map.307 = (bf16[2048,2048]{1,0:T(8,128)(2,1)}, bf16[2048,192]{1,0:T(8,128)(2,1)S(1)}, bf16[2048,192]{1,0:T(8,128)(2,1)S(1)}, bf16[2048,128]{1,0:T(8,128)(...) custom-call(bf16[2048,2048]{1,0:T(8,128)(2,1)} %bitcast.125, ...), custom_call_target="tpu_custom_call" | custom-call | flops 7549747200 | bytes 29360128 | tf_op jit(solution)/shard_map/pallas_call | solution.py:1109
  137.6 1.0 copy-done.20
  138.6 8.5 %shard_map.308 = (bf16[2048,128]{1,0:T(8,128)(2,1)S(1)}, f32[2048,1]{1,0:T(8,128)S(1)}) custom-call(bf16[2048,192]{1,0:T(8,128)(2,1)S(1)} %get-tuple-element.87.q_ref, bf16[2048,192]{1,0:T(8,128)(2,1)} %copy-done.20, bf16[2048,128]{1,0:T(8,128)(2,1)S(1)} %get-tuple-element.89.v_ref, s32[2048,1]{1,0:T(8,128)} %copy.115.col_ref, s32[1,2048]{1,0:T(1,128)S(1)} %copy-done.18), custom_call_target="tpu_custom_call" | custom-call | flops 1677721600 | bytes 4194304 | tf_op jit(solution)/shard_map/pallas_call | solution.py:1013
  147.9 0.9 reduce.2
  148.9 1.0 copy-done.7
  149.9 99.0 %shard_map.309 = (f32[128,2048]{1,0:T(8,128)S(1)}, bf16[16,128,2048]{2,1,0:T(8,128)(2,1)}) custom-call(bf16[2048,128]{1,0:T(8,128)(2,1)S(1)} %copy-done.7, bf16[128,2048]{1,0:T(8,128)(2,1)S(1)} %pad_maximum_fusion.3.refs_1_, bf16[128,2048]{1,0:T(8,128)(2,1)S(1)} %bitcast.84, f32[1,2048]{1,0:T(1,128)S(1)} %get-tuple-element.228.refs_3_.refs_2_), custom_call_target="tpu_custom_call" | custom-call | bytes 4194304 | tf_op jit(solution)/shard_map/pallas_call | solution.py:970
  249.8 1.0 constant_dynamic-slice_fusion.2.refs_1_
  250.8 1.4 bitcast_select_fusion.1
  252.5 1.1 fusion.12.wo_ref
  253.9 1.5 pad_maximum_fusion.wi_ref
  255.4 15.4 %collective-permute-done.2.refs_7_ = bf16[704,2048]{1,0:T(8,128)(2,1)} collective-permute-done((bf16[704,2048]{1,0:T(8,128)(2,1)}, bf16[704,2048]{1,0:T(8,128)(2,1)}, u32[]{:S(2)}, u32[]{:S(2)}) %collective-permute-start.2) | collective-permute-done | bytes 2883616 | tf_op jit(solution)/shard_map/ppermute | solution.py:79
  270.8 47.3 %shard_map.310 = (f32[2048,128]{1,0:T(8,128)}, f32[1024,1]{1,0:T(8,128)}, bf16[1024,2048]{1,0:T(8,128)(2,1)}, f32[1024,1408]{1,0:T(8,128)}, f32[1024,1408]{1,0:T...) custom-call(bf16[2048,2048]{1,0:T(8,128)(2,1)} %bitcast.94, ...), custom_call_target="tpu_custom_call" | custom-call | flops 26575110144 | bytes 62914560 | tf_op jit(solution)/shard_map/pallas_call | solution.py:1327
  318.2 53.2 %shard_map.311 = (bf16[1024,2048]{1,0:T(8,128)(2,1)}, bf16[1024,1408]{1,0:T(8,128)(2,1)}, bf16[1024,1408]{1,0:T(8,128)(2,1)}, bf16[2048,512]{1,0:T(8,128)(2,1)}, bf16[16,128,2176]{2,1,0:T(8,128)(2,1)}) custom-call(bf16[2048,2048]{1,0:T(8,128)(2,1)} %all-gather.2.cloned.1.call-done.grads_ref.refs_12_, bf16[1024,128]{1,0:T(8,128)(2,1)} %fusion.20.chosen_ref, ...), custom_call_target="tpu_custom_call" | custom-call | flops 26575110144 | bytes 62914560 | tf_op jit(solution)/shard_map/pallas_call | solution.py:1327
  371.4 7.0 shard_map.314
  378.4 1.5 collective-permute-start.6
  379.9 11.0 %shard_map.312 = (bf16[704,2048]{1,0:T(8,128)(2,1)}, f32[704,2048]{1,0:T(8,128)}) custom-call(s32[1]{0:T(128)} %bitcast.23.layer_ref, bf16[1024,1408]{1,0:T(8,128)(2,1)} %get-tuple-element.115.inner_ref, bf16[1024,2048]{1,0:T(8,128)(2,1)} %get-tuple-element.116.grads_ref), custom_call_target="tpu_custom_call" | custom-call | flops 5905580032 | bytes 16777216 | tf_op jit(solution)/shard_map/pallas_call | solution.py:1384
  391.5 7.5 %shard_map.313 = bf16[1024,1408]{1,0:T(8,128)(2,1)} custom-call(s32[1]{0:T(128)} %bitcast.23.layer_ref, bf16[1024,2048]{1,0:T(8,128)(2,1)} %get-tuple-element.118.rows_ref.refs_6_, bf16[1024,1408]{1,0:T(8,128)(2,1)} %get-tuple-element.119.grads_ref.refs_7_), custom_call_target="tpu_custom_call" | custom-call | flops 2952790016 | bytes 10485760 | tf_op jit(solution)/shard_map/pallas_call | solution.py:1353
  399.0 1.5 collective-permute-start.5
  401.3 105.5 %shard_map.315 = (f32[128,2048]{1,0:T(8,128)S(1)}, f32[1,2048]{1,0:T(1,128)S(1)}, f32[1024,1408]{1,0:T(8,128)}, f32[1024,1408]{1,0:T(8,128)}, f32[2048,512]{1,0:...) custom-call(bf16[16,128,2176]{2,1,0:T(8,128)(2,1)} %get-tuple-element.121.refs_0_, ...), custom_call_target="tpu_custom_call" | custom-call | bytes 4194304 | tf_op jit(solution)/shard_map/pallas_call | solution.py:970
  506.8 3.0 slice.77
  509.8 6.8 convolution_convert_fusion.g_ref
  516.7 13.7 %shard_map.316 = (bf16[2048,192]{1,0:T(8,128)(2,1)}, bf16[2048,192]{1,0:T(8,128)(2,1)}, bf16[2048,128]{1,0:T(8,128)(2,1)}) custom-call(bf16[2048,192]{1,0:T(8,128)(2,1)} %copy-done.19, bf16[2048,192]{1,0:T(8,128)(2,1)} %copy-done.20, bf16[2048,128]{1,0:T(8,128)(2,1)} %copy-done.21, bf16[2048,128]{1,0:T(8,128)(2,1)} %convolution_convert_fusion.g_ref, ...), custom_call_target="tpu_custom_call" | custom-call | flops 4194304000 | bytes 6291456 | tf_op jit(solution)/shard_map/pallas_call | solution.py:1054
  530.4 1.2 copy-done.22
  531.6 1.2 copy-done.23
  532.9 1.0 copy-done.24
  533.9 14.6 %shard_map.317 = (bf16[16,128,2688]{2,1,0:T(8,128)(2,1)}, f32[2048,192]{1,0:T(8,128)}, f32[512,256]{1,0:T(8,128)S(1)}) custom-call(bf16[2048,192]{1,0:T(8,128)(2,1)S(1)} %copy-done.22, bf16[2048,192]{1,0:T(8,128)(2,1)S(1)} %copy-done.23, bf16[2048,128]{1,0:T(8,128)(2,1)S(1)} %copy-done.24, f32[2048,128]{1,0:T(8,128)} %constant.50.clone.table_ref, ...), custom_call_target="tpu_custom_call" | custom-call | flops 5452595200 | bytes 29360128 | tf_op jit(solution)/shard_map/pallas_call | solution.py:1163
  548.8 1.7 convert.44
  550.5 2.8 dynamic-slice_convert_fusion.refs_9_
  553.3 1.3 copy_bitcast_fusion.refs_8_
  554.6 4.7 fusion
  559.3 1.5 dynamic-slice_convert_fusion.1.refs_10_
  560.8 93.9 %shard_map.318 = (f32[128,2048]{1,0:T(8,128)}, f32[1,512]{1,0:T(1,128)S(1)}, bf16[128,2048]{1,0:T(8,128)(2,1)S(1)}, f32[1,2048]{1,0:T(1,128)S(1)}, bf16[16,64,25...) custom-call(bf16[16,128,2688]{2,1,0:T(8,128)(2,1)} %get-tuple-elemen, ...), custom_call_target="tpu_custom_call" | custom-call | bytes 4194304 | tf_op jit(solution)/shard_map/pallas_call | solution.py:970
  657.5 3.7 all-to-all-start
  661.4 1.1 convert_bitcast_fusion
  662.4 4.5 fusion.2
  667.3 1.7 fusion.15
  669.0 1.1 fusion.24
  670.2 0.9 convert_add_fusion.4
  672.0 1.2 copy.130
  674.1 1.9 copy.126
  676.0 1.3 reshape.189
  677.2 2.4 copy.129
  679.9 1.3 collective-permute-start.3
  681.2 6.6 convert_add_fusion
  687.9 5.0 convert_add_fusion.1
  692.8 5.7 convert_add_fusion.2
  701.1 1.9 fusion.14
  (157 shorter events, 23.4 us)
Async XLA Ops:
  7.2 8.4 %copy-start.28 = (f32[1024,176]{0,1:T(8,128)S(1)}, f32[1024,176]{0,1:T(8,128)}, u32[]{:S(2)}) copy-start(f32[1024,176]{0,1:T(8,128)} %param.31) | copy-start | bytes 2162692
  7.2 248.2 %all-gather.2.cloned.1.call-start = ((), (), s32[]{:S(2)}) async-start(), calls=%async_computation.2 | async-start | bytes 8912896 | tf_op jit(solution)/shard_map/all_gather | solution.py:121
  13.4 3.5 copy-start.29
  15.4 3.8 copy-start
  19.2 88.6 %copy-start.18 = (s32[1,2048]{1,0:T(1,128)S(1)}, s32[1,2048]{1,0:T(1,128)}, u32[]{:S(2)}) copy-start(s32[1,2048]{1,0:T(1,128)} %row_ref.3) | copy-start | bytes 24580
  97.7 0.7 copy-start.9
  98.5 0.7 copy-start.11
  99.2 14.7 %copy-start.4 = (bf16[4,256,176]{2,1,0:T(8,128)(2,1)}, bf16[4,256,176]{2,1,0:T(8,128)(2,1)S(1)}, u32[]{:S(2)}) copy-start(bf16[4,256,176]{2,1,0:T(8,128)(2,1)S(1)} %get-tuple-element.98) | copy-start | bytes 1081348
  99.2 14.7 %copy-start.5 = (bf16[4,256,176]{2,1,0:T(8,128)(2,1)}, bf16[4,256,176]{2,1,0:T(8,128)(2,1)S(1)}, u32[]{:S(2)}) copy-start(bf16[4,256,176]{2,1,0:T(8,128)(2,1)S(1)} %get-tuple-element.100) | copy-start | bytes 1081348
  99.2 601.9 %reduce-scatter.2.cloned.1.call-start = ((), (), s32[]{:S(2)}) async-start(), calls=%async_computation.3 | async-start | bytes 8912896 | tf_op jit(solution)/shard_map/reduce_scatter | solution.py:125
  99.3 156.1 %collective-permute-start = (bf16[768,1408]{1,0:T(8,128)(2,1)}, bf16[768,1408]{1,0:T(8,128)(2,1)}, u32[]{:S(2)}, u32[]{:S(2)}) collective-permute-start(bf16[768,1408]{1,0:T(8,128)(2,1)} %get-tuple-element.104.refs_1_), channel_id=1, source_target_pairs={{0,1},{1,0},{2,3},{3,2},{4,5},{5,4},{6,7},{7,6},{8,9},{9,8},{10,11... | collective-permute-start | bytes 6488072 | tf_op jit(solution)/shard_map/ppermute | solution.py:79
  100.9 154.5 %collective-permute-start.1 = (bf16[1024,1408]{1,0:T(8,128)(2,1)}, bf16[1024,1408]{1,0:T(8,128)(2,1)}, u32[]{:S(2)}, u32[]{:S(2)}) collective-permute-start(bf16[1024,1408]{1,0:T(8,128)(2,1)} %get-tuple-element.106.refs_4_), channel_id=1, source_target_pairs={{0,1},{1,0},{2,3},{3,2},{4,5},{5,4},{6,7},{7,6},{8,9},{9,8},{10,11... | collective-permute-start | bytes 8650760 | tf_op jit(solution)/shard_map/ppermute | solution.py:79
  101.4 169.5 %collective-permute-start.2 = (bf16[704,2048]{1,0:T(8,128)(2,1)}, bf16[704,2048]{1,0:T(8,128)(2,1)}, u32[]{:S(2)}, u32[]{:S(2)}) collective-permute-start(bf16[704,2048]{1,0:T(8,128)(2,1)} %get-tuple-element.107.refs_6_), channel_id=1, source_target_pairs={{0,1},{1,0},{2,3},{3,2},{4,5},{5,4},{6,7},{7,6},{8,9},{9,8},{10,11... | collective-permute-start | bytes 8650760 | tf_op jit(solution)/shard_map/ppermute | solution.py:79
  115.5 22.1 %copy-start.15 = (bf16[512,256]{1,0:T(8,128)(2,1)}, bf16[512,256]{1,0:T(8,128)(2,1)S(1)}, u32[]{:S(2)}) copy-start(bf16[512,256]{1,0:T(8,128)(2,1)S(1)} %reshape.171.we_ref) | copy-start | bytes 786436
  118.4 1.2 copy-start.17
  137.6 1.0 copy-start.20
  138.6 8.5 %copy-start.19 = (bf16[2048,192]{1,0:T(8,128)(2,1)}, bf16[2048,192]{1,0:T(8,128)(2,1)S(1)}, u32[]{:S(2)}) copy-start(bf16[2048,192]{1,0:T(8,128)(2,1)S(1)} %get-tuple-element.87.q_ref) | copy-start | bytes 2359300
  138.6 8.6 %copy-start.21 = (bf16[2048,128]{1,0:T(8,128)(2,1)}, bf16[2048,128]{1,0:T(8,128)(2,1)S(1)}, u32[]{:S(2)}) copy-start(bf16[2048,128]{1,0:T(8,128)(2,1)S(1)} %get-tuple-element.89.v_ref) | copy-start | bytes 1572868
  147.1 0.8 copy-start.6
  148.9 1.0 copy-start.7
  250.7 1.7 copy-start.10
  250.7 1.7 copy-start.12
  378.4 302.8 %collective-permute-start.6 = (bf16[1024,1408]{1,0:T(8,128)(2,1)}, bf16[1024,1408]{1,0:T(8,128)(2,1)}, u32[]{:S(2)}, u32[]{:S(2)}) collective-permute-start(bf16[1024,1408]{1,0:T(8,128)(2,1)} %shard_map.314), channel_id=1, source_target_pairs={{0,1},{1,0},{2,3},{3,2},{4,5},{5,4},{6,7},{7,6},{8,9},{9,8},{10,11... | collective-permute-start | bytes 8650760 | tf_op jit(solution)/shard_map/ppermute | solution.py:79
  390.9 301.9 %collective-permute-start.4 = (bf16[704,2048]{1,0:T(8,128)(2,1)}, bf16[704,2048]{1,0:T(8,128)(2,1)}, u32[]{:S(2)}, u32[]{:S(2)}) collective-permute-start(bf16[704,2048]{1,0:T(8,128)(2,1)} %get-tuple-element.117), channel_id=1, source_target_pairs={{0,1},{1,0},{2,3},{3,2},{4,5},{5,4},{6,7},{7,6},{8,9},{9,8},{10,11... | collective-permute-start | bytes 8650760 | tf_op jit(solution)/shard_map/ppermute | solution.py:79
  391.5 9.8 %copy-start.1 = (bf16[1,128,2048]{2,1,0:T(8,128)(2,1)S(1)}, bf16[1,128,2048]{2,1,0:T(8,128)(2,1)}, u32[]{:S(2)}) copy-start(bf16[1,128,2048]{2,1,0:T(8,128)(2,1)} %param.20) | copy-start | bytes 1572868
  391.5 9.8 %copy-start.2 = (bf16[2048,128]{1,0:T(8,128)(2,1)S(1)}, bf16[2048,128]{1,0:T(8,128)(2,1)}, u32[]{:S(2)}) copy-start(bf16[2048,128]{1,0:T(8,128)(2,1)} %pad.38.clone.router_ref.refs_5_) | copy-start | bytes 1572868
  399.0 288.9 %collective-permute-start.5 = (bf16[1024,1408]{1,0:T(8,128)(2,1)}, bf16[1024,1408]{1,0:T(8,128)(2,1)}, u32[]{:S(2)}, u32[]{:S(2)}) collective-permute-start(bf16[1024,1408]{1,0:T(8,128)(2,1)} %shard_map.313), channel_id=1, source_target_pairs={{0,1},{1,0},{2,3},{3,2},{4,5},{5,4},{6,7},{7,6},{8,9},{9,8},{10,11... | collective-permute-start | bytes 8650760 | tf_op jit(solution)/shard_map/ppermute | solution.py:79
  506.8 9.8 %copy-start.3 = (f32[128,2048]{1,0:T(8,128)}, f32[128,2048]{1,0:T(8,128)S(1)}, u32[]{:S(2)}) copy-start(f32[128,2048]{1,0:T(8,128)S(1)} %get-tuple-element.134.refs_7_) | copy-start | bytes 3145732
  516.7 13.7 %copy-start.16 = (bf16[512,256]{1,0:T(8,128)(2,1)S(1)}, bf16[512,256]{1,0:T(8,128)(2,1)}, u32[]{:S(2)}) copy-start(bf16[512,256]{1,0:T(8,128)(2,1)} %copy-done.15) | copy-start | bytes 786436
  530.4 1.2 copy-start.22
  531.6 1.2 copy-start.23
  532.8 1.0 copy-start.24
  550.5 4.1 copy-start.8
  559.3 1.6 copy-start.30
  654.7 0.7 copy-start.13
  657.5 22.1 %all-to-all-start = ((f32[16,1,384]{2,1,0:T(1,128)}), f32[16,1,384]{2,1,0:T(1,128)S(1)}, u32[]{:S(2)}, u32[]{:S(2)}) async-start(f32[16,1,384]{2,1,0:T(1,128)} %all_to_all.6), calls=%async_computation.1 | async-start | bytes 49152 | tf_op jit(solution)/shard_map/all_to_all | solution.py:1720
  661.3 5.6 copy-start.26
  661.4 5.6 copy-start.27
  667.3 2.9 copy-start.14
  667.3 2.9 copy-start.25
  669.0 2.1 copy-start.31
  674.1 5.6 copy-start.32
  679.9 18.6 %collective-permute-start.3 = (f32[64,640]{0,1:T(8,128)S(1)}, f32[64,640]{0,1:T(8,128)S(1)}, u32[]{:S(2)}, u32[]{:S(2)}) collective-permute-start(f32[64,640]{0,1:T(8,128)S(1)} %constant_dynamic-slice_fusion), channel_id=1, source_target_pairs={{0,1},{1,0},{2,3},{3,2},{4,5},{5,4},{6,7},{7,6},{8,9},{9,8},{10,11... | collective-permute-start | bytes 491528 | tf_op jit(solution)/shard_map/ppermute | solution.py:79
  681.2 6.7 slice-start.2
  681.2 6.7 slice-start.3
  687.8 5.0 slice-start
  687.8 5.0 slice-start.1
Sparse Core Ops, SparseCore 0:
  99.3 79.9 all-gather.1
  318.3 112.3 reduce-scatter.1

commit v7 on v6

--- a/solution.py
+++ b/solution.py
@@ -1466,7 +1466,7 @@
         head_parts,
         (
             w_expert_gate[0], w_expert_up[0], w_expert_down[0],
-            w_shared_gate, w_shared_up, w_shared_down, w_output,
+            jnp.concatenate([w_shared_gate, w_shared_up], axis=1), w_shared_down, w_output,
         ),
         groups,
         layers,
@@ -1485,7 +1485,8 @@
     units = w_shared_gate.shape[1]
     padding = -units % 128
     spare = ((0, 0), (0, padding))
-    shared_gate_w, shared_up_w, shared_down_w, output_w = lone
+    shared_pair_w, shared_down_w, output_w = lone
+    shared_gate_w, shared_up_w = shared_pair_w[:, :units], shared_pair_w[:, units:]
     shared_in_w = jnp.concatenate([jnp.pad(shared_gate_w, spare), jnp.pad(shared_up_w, spare)], axis=1)
     shared_down_w = jnp.pad(shared_down_w, ((0, padding), (0, 0)))
 

time: 721 us -> 727 us (level)
    unnamed x81 -> x73, local copies, waits for them, and re-layouts: 17.9 us -> 18.2 us
where the time goes in v7:
time: 727 us; the launch traced here: 717 us
  Pallas kernels  558 us (77%)
  local copies, waits for them, and re-layouts  51.6 us (7%)
  other arithmetic  46.9 us (6%)
  matrix products  17 us (2%)
  waiting for transfers between devices  15.4 us (2%)
  between operations  15.1 us (2%)
  starting transfers between devices  12.3 us (2%)
    pallas_call x3, Pallas kernels, ring_reduce(): pl.pallas_call(functools.partial(reduce_kernel, groups, chunks, count, le...  303 us
    pallas_call x2, Pallas kernels, row_grid(): pl.pallas_call(kernel, grid=(steps,), out_shape=outs, in_specs=[pl.BlockS...  100 us
    pallas_call x1, Pallas kernels, gather_start(): pl.pallas_call(functools.partial(start_kernel, groups, chunks, pair, coun...  75.4 us
    unnamed x73, local copies, waits for them, and re-layouts  18.2 us
    pallas_call x1, Pallas kernels, project(): pl.pallas_call(project_kernel, grid=(seq_len // tile,), out_shape=[jax.Sh...  17.9 us
    add x3, other arithmetic, spread_end(): return kept + swap_layers(sent).astype(F32)  17.3 us
    ppermute x7, waiting for transfers between devices, swap_layers(): return lax.ppermute(own, 'fsdp', ((0, 1), (1, 0)))  15.3 us
    pallas_call x1, Pallas kernels, project_back(): pl.pallas_call(project_back_kernel, grid=(seq_len // tile,), out_shape=[j...  14.6 us
  transfers between devices with their start and end apart: 10, of which 1 were waited for; matrix products, arithmetic and copies ran while one was open for 12% of the time, Pallas kernels for 61%

profile of v7, /device:TPU:0, one launch (start us, length us, event | category | flops | bytes accessed | tf_op | source)
XLA Modules:
  0.0 716.5 jit_solution(2530793410340102311)
XLA Ops:
  12.3 1.0 convert_element_type.111
  13.5 1.2 convert_element_type.110
  15.3 1.0 copy.143
  16.2 1.4 copy.111
  17.7 2.4 copy.112
  20.1 1.3 pad_maximum_fusion.3.heads_ref
  21.4 2.7 pad_maximum_fusion.1.rest_3_
  24.1 75.4 %shard_map.306 = (bf16[16,128,2048]{2,1,0:T(8,128)(2,1)}, bf16[16,128,640]{2,1,0:T(8,128)(2,1)}, bf16[16,2,64,256]{3,2,1,0:T(8,128)(2,1)}, bf16[256,1408]{1,0:T(...) custom-call(bf16[128,2048]{1,0:T(8,128)(2,1)S(1)} %bitcast.80, ...), custom_call_target="tpu_custom_call" | custom-call | bytes 4194304 | tf_op jit(solution)/shard_map/pallas_call | solution.py:507
  101.2 1.6 collective-permute-start
  103.3 1.5 collective-permute-start.2
  104.8 2.0 slice.108
  106.9 2.1 slice.109
  109.7 1.4 copy.115.col_ref
  111.1 1.8 reshape.171
  113.9 1.9 pad.38.clone.router_ref.refs_5_
  115.9 1.0 slice.80
  116.9 1.5 reshape.168.we_ref
  118.3 2.3 slice_convert_fusion
  120.6 1.6 copy.139
  123.4 17.9 %shard_map.307 = (bf16[2048,2048]{1,0:T(8,128)(2,1)}, bf16[2048,192]{1,0:T(8,128)(2,1)S(1)}, bf16[2048,192]{1,0:T(8,128)(2,1)S(1)}, bf16[2048,128]{1,0:T(8,128)(...) custom-call(bf16[2048,2048]{1,0:T(8,128)(2,1)} %bitcast.122, ...), custom_call_target="tpu_custom_call" | custom-call | flops 7549747200 | bytes 29360128 | tf_op jit(solution)/shard_map/pallas_call | solution.py:1109
  142.3 8.6 %shard_map.308 = (bf16[2048,128]{1,0:T(8,128)(2,1)S(1)}, f32[2048,1]{1,0:T(8,128)S(1)}) custom-call(bf16[2048,192]{1,0:T(8,128)(2,1)S(1)} %get-tuple-element.85.q_ref, bf16[2048,192]{1,0:T(8,128)(2,1)} %copy-done.16, bf16[2048,128]{1,0:T(8,128)(2,1)S(1)} %get-tuple-element.87.v_ref, s32[2048,1]{1,0:T(8,128)} %copy.115.col_ref, s32[1,2048]{1,0:T(1,128)S(1)} %copy-done.13), custom_call_target="tpu_custom_call" | custom-call | flops 1677721600 | bytes 4194304 | tf_op jit(solution)/shard_map/pallas_call | solution.py:1013
  150.9 0.9 reduce.2
  151.9 101.0 %shard_map.309 = (f32[128,2048]{1,0:T(8,128)S(1)}, bf16[16,128,2048]{2,1,0:T(8,128)(2,1)}) custom-call(bf16[2048,128]{1,0:T(8,128)(2,1)S(1)} %get-tuple-element.88.refs_0_, bf16[128,2048]{1,0:T(8,128)(2,1)S(1)} %pad_maximum_fusion.4.refs_1_, bf16[128,2048]{1,0:T(8,128)(2,1)S(1)} %bitcast.81, f32[1,2048]{1,0:T(1,128)S(1)} %get-tuple-element.224.refs_3_.refs_2_), custom_call_target="tpu_custom_call" | custom-call | bytes 4194304 | tf_op jit(solution)/shard_map/pallas_call | solution.py:970
  253.8 1.0 constant_dynamic-slice_fusion.2.refs_1_
  254.7 1.0 bitcast_select_fusion.3
  255.8 1.1 fusion.11.wo_ref
  257.8 1.5 pad_maximum_fusion.wi_ref
  259.3 15.3 %collective-permute-done.2.refs_7_ = bf16[704,2048]{1,0:T(8,128)(2,1)} collective-permute-done((bf16[704,2048]{1,0:T(8,128)(2,1)}, bf16[704,2048]{1,0:T(8,128)(2,1)}, u32[]{:S(2)}, u32[]{:S(2)}) %collective-permute-start.2) | collective-permute-done | bytes 2883616 | tf_op jit(solution)/shard_map/ppermute | solution.py:79
  274.6 47.3 %shard_map.310 = (f32[2048,128]{1,0:T(8,128)}, f32[1024,1]{1,0:T(8,128)}, bf16[1024,2048]{1,0:T(8,128)(2,1)}, f32[1024,1408]{1,0:T(8,128)}, f32[1024,1408]{1,0:T...) custom-call(bf16[2048,2048]{1,0:T(8,128)(2,1)} %bitcast.91, ...), custom_call_target="tpu_custom_call" | custom-call | flops 26575110144 | bytes 62914560 | tf_op jit(solution)/shard_map/pallas_call | solution.py:1327
  322.0 52.7 %shard_map.311 = (bf16[1024,2048]{1,0:T(8,128)(2,1)}, bf16[1024,1408]{1,0:T(8,128)(2,1)}, bf16[1024,1408]{1,0:T(8,128)(2,1)}, bf16[2048,512]{1,0:T(8,128)(2,1)}, bf16[16,128,2176]{2,1,0:T(8,128)(2,1)}) custom-call(bf16[2048,2048]{1,0:T(8,128)(2,1)} %all-gather.2.cloned.1.call-done.grads_ref.refs_12_, bf16[1024,128]{1,0:T(8,128)(2,1)} %fusion.19.chosen_ref, ...), custom_call_target="tpu_custom_call" | custom-call | flops 26575110144 | bytes 62914560 | tf_op jit(solution)/shard_map/pallas_call | solution.py:1327
  374.7 6.9 shard_map.314
  381.6 1.5 collective-permute-start.6
  383.1 10.9 %shard_map.312 = (bf16[704,2048]{1,0:T(8,128)(2,1)}, f32[704,2048]{1,0:T(8,128)}) custom-call(s32[1]{0:T(128)} %bitcast.22.layer_ref, bf16[1024,1408]{1,0:T(8,128)(2,1)} %get-tuple-element.111.inner_ref, bf16[1024,2048]{1,0:T(8,128)(2,1)} %get-tuple-element.112.grads_ref), custom_call_target="tpu_custom_call" | custom-call | flops 5905580032 | bytes 16777216 | tf_op jit(solution)/shard_map/pallas_call | solution.py:1384
  394.7 7.4 %shard_map.313 = bf16[1024,1408]{1,0:T(8,128)(2,1)} custom-call(s32[1]{0:T(128)} %bitcast.22.layer_ref, bf16[1024,2048]{1,0:T(8,128)(2,1)} %get-tuple-element.114.rows_ref.refs_6_, bf16[1024,1408]{1,0:T(8,128)(2,1)} %get-tuple-element.115.grads_ref.refs_7_), custom_call_target="tpu_custom_call" | custom-call | flops 2952790016 | bytes 10485760 | tf_op jit(solution)/shard_map/pallas_call | solution.py:1353
  402.1 1.4 collective-permute-start.5
  404.4 107.8 %shard_map.315 = (f32[128,2048]{1,0:T(8,128)S(1)}, f32[1,2048]{1,0:T(1,128)S(1)}, f32[1024,1408]{1,0:T(8,128)}, f32[1024,1408]{1,0:T(8,128)}, f32[2048,512]{1,0:...) custom-call(bf16[16,128,2176]{2,1,0:T(8,128)(2,1)} %get-tuple-element.117.refs_0_, ...), custom_call_target="tpu_custom_call" | custom-call | bytes 4194304 | tf_op jit(solution)/shard_map/pallas_call | solution.py:970
  512.2 3.1 slice.86
  515.3 6.8 convolution_convert_fusion.g_ref
  522.1 13.7 %shard_map.316 = (bf16[2048,192]{1,0:T(8,128)(2,1)}, bf16[2048,192]{1,0:T(8,128)(2,1)}, bf16[2048,128]{1,0:T(8,128)(2,1)}) custom-call(bf16[2048,192]{1,0:T(8,128)(2,1)} %copy-done.15, bf16[2048,192]{1,0:T(8,128)(2,1)} %copy-done.16, bf16[2048,128]{1,0:T(8,128)(2,1)} %copy-done.17, bf16[2048,128]{1,0:T(8,128)(2,1)} %convolution_convert_fusion.g_ref, ...), custom_call_target="tpu_custom_call" | custom-call | flops 4194304000 | bytes 6291456 | tf_op jit(solution)/shard_map/pallas_call | solution.py:1054
  535.8 1.2 copy-done.18
  537.0 1.2 copy-done.19
  538.3 1.0 copy-done.20
  539.3 14.6 %shard_map.317 = (bf16[16,128,2688]{2,1,0:T(8,128)(2,1)}, f32[2048,192]{1,0:T(8,128)}, f32[512,256]{1,0:T(8,128)S(1)}) custom-call(bf16[2048,192]{1,0:T(8,128)(2,1)S(1)} %copy-done.18, bf16[2048,192]{1,0:T(8,128)(2,1)S(1)} %copy-done.19, bf16[2048,128]{1,0:T(8,128)(2,1)S(1)} %copy-done.20, f32[2048,128]{1,0:T(8,128)} %constant.52.clone.table_ref, ...), custom_call_target="tpu_custom_call" | custom-call | flops 5452595200 | bytes 29360128 | tf_op jit(solution)/shard_map/pallas_call | solution.py:1163
  554.2 1.7 convert.44
  555.9 2.7 dynamic-slice_convert_fusion.refs_9_
  558.6 1.3 copy_bitcast_fusion.refs_8_
  559.9 4.7 fusion
  564.6 1.5 dynamic-slice_convert_fusion.1.refs_10_
  566.1 93.9 %shard_map.318 = (f32[128,2048]{1,0:T(8,128)}, f32[1,512]{1,0:T(1,128)S(1)}, bf16[128,2048]{1,0:T(8,128)(2,1)S(1)}, f32[1,2048]{1,0:T(1,128)S(1)}, bf16[16,64,25...) custom-call(bf16[16,128,2688]{2,1,0:T(8,128)(2,1)} %get-tuple-elemen, ...), custom_call_target="tpu_custom_call" | custom-call | bytes 4194304 | tf_op jit(solution)/shard_map/pallas_call | solution.py:970
  663.5 3.9 all-to-all-start
  667.6 1.1 convert_bitcast_fusion
  668.6 3.8 fusion.2
  672.8 1.7 fusion.14
  674.5 1.1 fusion.23
  675.7 0.9 convert_add_fusion.4
  677.5 1.2 copy.130
  679.6 1.8 copy.126
  681.4 1.3 reshape.185
  682.7 2.4 copy.129
  685.3 1.2 collective-permute-start.3
  686.5 6.6 convert_add_fusion
  693.2 5.0 convert_add_fusion.1
  698.2 5.7 convert_add_fusion.2
  706.5 1.9 fusion.13
  (149 shorter events, 24.9 us)
Async XLA Ops:
  7.2 252.1 %all-gather.2.cloned.1.call-start = ((), (), s32[]{:S(2)}) async-start(), calls=%async_computation.2 | async-start | bytes 8912896 | tf_op jit(solution)/shard_map/all_gather | solution.py:121
  20.1 4.0 copy-start
  20.1 4.0 copy-start.4
  24.1 85.6 %copy-start.13 = (s32[1,2048]{1,0:T(1,128)S(1)}, s32[1,2048]{1,0:T(1,128)}, u32[]{:S(2)}) copy-start(s32[1,2048]{1,0:T(1,128)} %row_ref.3) | copy-start | bytes 24580
  99.5 0.7 copy-start.5
  100.3 0.9 copy-start.14
  101.2 14.7 %copy-start.12 = (bf16[16,2,64,256]{3,2,1,0:T(8,128)(2,1)S(1)}, bf16[16,2,64,256]{3,2,1,0:T(8,128)(2,1)}, u32[]{:S(2)}) copy-start(bf16[16,2,64,256]{3,2,1,0:T(8,128)(2,1)} %get-tuple-element.84) | copy-start | bytes 3145732
  101.2 605.3 %reduce-scatter.2.cloned.1.call-start = ((), (), s32[]{:S(2)}) async-start(), calls=%async_computation.3 | async-start | bytes 8912896 | tf_op jit(solution)/shard_map/reduce_scatter | solution.py:125
  101.2 158.1 %collective-permute-start = (bf16[768,1408]{1,0:T(8,128)(2,1)}, bf16[768,1408]{1,0:T(8,128)(2,1)}, u32[]{:S(2)}, u32[]{:S(2)}) collective-permute-start(bf16[768,1408]{1,0:T(8,128)(2,1)} %get-tuple-element.100.refs_1_), channel_id=1, source_target_pairs={{0,1},{1,0},{2,3},{3,2},{4,5},{5,4},{6,7},{7,6},{8,9},{9,8},{10,11... | collective-permute-start | bytes 6488072 | tf_op jit(solution)/shard_map/ppermute | solution.py:79
  102.8 156.5 %collective-permute-start.1 = (bf16[1024,1408]{1,0:T(8,128)(2,1)}, bf16[1024,1408]{1,0:T(8,128)(2,1)}, u32[]{:S(2)}, u32[]{:S(2)}) collective-permute-start(bf16[1024,1408]{1,0:T(8,128)(2,1)} %get-tuple-element.102.refs_4_), channel_id=1, source_target_pairs={{0,1},{1,0},{2,3},{3,2},{4,5},{5,4},{6,7},{7,6},{8,9},{9,8},{10,11... | collective-permute-start | bytes 8650760 | tf_op jit(solution)/shard_map/ppermute | solution.py:79
  103.3 171.3 %collective-permute-start.2 = (bf16[704,2048]{1,0:T(8,128)(2,1)}, bf16[704,2048]{1,0:T(8,128)(2,1)}, u32[]{:S(2)}, u32[]{:S(2)}) collective-permute-start(bf16[704,2048]{1,0:T(8,128)(2,1)} %get-tuple-element.103.refs_6_), channel_id=1, source_target_pairs={{0,1},{1,0},{2,3},{3,2},{4,5},{5,4},{6,7},{7,6},{8,9},{9,8},{10,11... | collective-permute-start | bytes 8650760 | tf_op jit(solution)/shard_map/ppermute | solution.py:79
  118.3 23.1 %copy-start.8 = (bf16[512,256]{1,0:T(8,128)(2,1)}, bf16[512,256]{1,0:T(8,128)(2,1)S(1)}, u32[]{:S(2)}) copy-start(bf16[512,256]{1,0:T(8,128)(2,1)S(1)} %reshape.168.we_ref) | copy-start | bytes 786436
  141.4 1.0 copy-start.16
  142.3 8.6 %copy-start.15 = (bf16[2048,192]{1,0:T(8,128)(2,1)}, bf16[2048,192]{1,0:T(8,128)(2,1)S(1)}, u32[]{:S(2)}) copy-start(bf16[2048,192]{1,0:T(8,128)(2,1)S(1)} %get-tuple-element.85.q_ref) | copy-start | bytes 2359300
  142.3 8.6 %copy-start.17 = (bf16[2048,128]{1,0:T(8,128)(2,1)}, bf16[2048,128]{1,0:T(8,128)(2,1)S(1)}, u32[]{:S(2)}) copy-start(bf16[2048,128]{1,0:T(8,128)(2,1)S(1)} %get-tuple-element.87.v_ref) | copy-start | bytes 1572868
  151.9 105.0 %copy-start.24 = (bf16[1024,352]{1,0:T(8,128)(2,1)S(1)}, bf16[1024,352]{1,0:T(8,128)(2,1)}, u32[]{:S(2)}) copy-start(bf16[1024,352]{1,0:T(8,128)(2,1)} %get-tuple-element.95) | copy-start | bytes 2162692
  151.9 105.0 %copy-start.25 = (bf16[4,256,352]{2,1,0:T(8,128)(2,1)S(1)}, bf16[4,256,352]{2,1,0:T(8,128)(2,1)}, u32[]{:S(2)}) copy-start(bf16[4,256,352]{2,1,0:T(8,128)(2,1)} %get-tuple-element.96) | copy-start | bytes 2162692
  254.7 2.4 copy-start.28
  381.6 304.9 %collective-permute-start.6 = (bf16[1024,1408]{1,0:T(8,128)(2,1)}, bf16[1024,1408]{1,0:T(8,128)(2,1)}, u32[]{:S(2)}, u32[]{:S(2)}) collective-permute-start(bf16[1024,1408]{1,0:T(8,128)(2,1)} %shard_map.314), channel_id=1, source_target_pairs={{0,1},{1,0},{2,3},{3,2},{4,5},{5,4},{6,7},{7,6},{8,9},{9,8},{10,11... | collective-permute-start | bytes 8650760 | tf_op jit(solution)/shard_map/ppermute | solution.py:79
  394.0 304.2 %collective-permute-start.4 = (bf16[704,2048]{1,0:T(8,128)(2,1)}, bf16[704,2048]{1,0:T(8,128)(2,1)}, u32[]{:S(2)}, u32[]{:S(2)}) collective-permute-start(bf16[704,2048]{1,0:T(8,128)(2,1)} %get-tuple-element.113), channel_id=1, source_target_pairs={{0,1},{1,0},{2,3},{3,2},{4,5},{5,4},{6,7},{7,6},{8,9},{9,8},{10,11... | collective-permute-start | bytes 8650760 | tf_op jit(solution)/shard_map/ppermute | solution.py:79
  394.7 9.6 %copy-start.1 = (bf16[1,128,2048]{2,1,0:T(8,128)(2,1)S(1)}, bf16[1,128,2048]{2,1,0:T(8,128)(2,1)}, u32[]{:S(2)}) copy-start(bf16[1,128,2048]{2,1,0:T(8,128)(2,1)} %param.20) | copy-start | bytes 1572868
  394.7 9.6 %copy-start.2 = (bf16[2048,128]{1,0:T(8,128)(2,1)S(1)}, bf16[2048,128]{1,0:T(8,128)(2,1)}, u32[]{:S(2)}) copy-start(bf16[2048,128]{1,0:T(8,128)(2,1)} %pad.38.clone.router_ref.refs_5_) | copy-start | bytes 1572868
  402.1 291.1 %collective-permute-start.5 = (bf16[1024,1408]{1,0:T(8,128)(2,1)}, bf16[1024,1408]{1,0:T(8,128)(2,1)}, u32[]{:S(2)}, u32[]{:S(2)}) collective-permute-start(bf16[1024,1408]{1,0:T(8,128)(2,1)} %shard_map.313), channel_id=1, source_target_pairs={{0,1},{1,0},{2,3},{3,2},{4,5},{5,4},{6,7},{7,6},{8,9},{9,8},{10,11... | collective-permute-start | bytes 8650760 | tf_op jit(solution)/shard_map/ppermute | solution.py:79
  512.2 9.9 %copy-start.3 = (f32[128,2048]{1,0:T(8,128)}, f32[128,2048]{1,0:T(8,128)S(1)}, u32[]{:S(2)}) copy-start(f32[128,2048]{1,0:T(8,128)S(1)} %get-tuple-element.130.refs_7_) | copy-start | bytes 3145732
  522.1 13.7 %copy-start.9 = (bf16[512,256]{1,0:T(8,128)(2,1)S(1)}, bf16[512,256]{1,0:T(8,128)(2,1)}, u32[]{:S(2)}) copy-start(bf16[512,256]{1,0:T(8,128)(2,1)} %copy-done.8) | copy-start | bytes 786436
  535.8 1.2 copy-start.18
  537.0 1.2 copy-start.19
  538.3 1.0 copy-start.20
  564.6 1.6 copy-start.26
  660.1 0.7 copy-start.6
  660.8 0.7 copy-start.10
  663.5 21.6 %all-to-all-start = ((f32[16,1,384]{2,1,0:T(1,128)}), f32[16,1,384]{2,1,0:T(1,128)S(1)}, u32[]{:S(2)}, u32[]{:S(2)}) async-start(f32[16,1,384]{2,1,0:T(1,128)} %all_to_all.6), calls=%async_computation.1 | async-start | bytes 49152 | tf_op jit(solution)/shard_map/all_to_all | solution.py:1721
  667.5 4.9 copy-start.22
  667.5 4.9 copy-start.23
  672.8 2.9 copy-start.7
  672.8 2.9 copy-start.21
  674.5 2.1 copy-start.11
  674.5 2.1 copy-start.27
  685.3 18.6 %collective-permute-start.3 = (f32[64,640]{0,1:T(8,128)S(1)}, f32[64,640]{0,1:T(8,128)S(1)}, u32[]{:S(2)}, u32[]{:S(2)}) collective-permute-start(f32[64,640]{0,1:T(8,128)S(1)} %constant_dynamic-slice_fusion), channel_id=1, source_target_pairs={{0,1},{1,0},{2,3},{3,2},{4,5},{5,4},{6,7},{7,6},{8,9},{9,8},{10,11... | collective-permute-start | bytes 491528 | tf_op jit(solution)/shard_map/ppermute | solution.py:79
  686.5 6.7 slice-start.2
  686.5 6.7 slice-start.3
  693.2 5.0 slice-start
  693.2 5.0 slice-start.1
Sparse Core Ops, SparseCore 0:
  101.3 83.6 all-gather.1
  322.1 115.1 reduce-scatter.1
